TPU v7x, 128 devices: a whole 4x4x4 slice. The times are simulated.
128 devices in a mesh: dp: 32 (over y, z, core), mp: 4 (over x).
Axes of the slice: x: 4, y: 4, z: 4, core: 2. Of those that a mesh axis runs over, the one named last changes fastest.
Arguments:
- hidden_states: bfloat16 [32768, 8192], P('dp'), may hold values from -6 to 6
- norm_gain: float32 [8192], replicated, may hold values from 0.6 to 9
- w_query: bfloat16 [8192, 4096], P('dp', 'mp'), may hold values from -0.0625 to 0.0625
- w_keyval: bfloat16 [8192, 1024], P('dp', 'mp'), may hold values from -0.0625 to 0.0625
- query_bias: float32 [4096], P('mp'), may hold values from -3 to 3
- keyval_bias: float32 [1024], P('mp'), may hold values from -3 to 3
- group_dest: int32 [32, 16], replicated, may hold values from 0 to 31, as said below
- group_offset: int32 [32, 16], replicated, may hold values from 0 to 960, as said below
- group_length: int32 [32, 16], replicated, may hold values from 8 to 64, as said below
Outputs:
- attention_out: bfloat16 [32768, 4096], P(('dp', 'mp'))
Inputs may be any that keep to these rules, and one draw needn't show every extreme that they name: `group_dest`: the 16 groups of one rollout pack go to different training packs, and every training pack receives exactly 16 groups. `group_offset`: multiples of 64; the groups that one training pack receives have different offsets. `group_length`: each value is 64, 32, 16 or 8, and each of the four occurs in every draw.
All inputs are finite; a program needn't handle non-finite values.
Results may differ from a plain program's by a relative error of at most 0.006.
The roundings to bfloat16 on the way count: a program that leaves them out, or rounds other values in their place, can miss the bound.
Values may be sent and summed in bfloat16 or wider, within the bound.
No kernel may reach another device: no remote copies, remote signals or barrier semaphores. Data moves between devices by JAX's collectives and lax.ppermute only.
A program may use at most 128 MiB of HBM per device.

v0:
```python
import jax
import jax.numpy as jnp
from jax import lax
from jax.sharding import PartitionSpec as P

HD = 128


rope_base = 1000000.0
norm_epsilon = 1e-06


def rotary(values_in, position):
    half_width = values_in.shape[-1] // 2
    frequency = rope_base ** (
        -(jnp.arange(half_width, dtype=jnp.float32) * 2.0) / values_in.shape[-1]
    )
    angles = position.astype(jnp.float32)[:, None] * frequency[None, :]
    cosine = jnp.cos(angles)[:, None, :]
    sine_part = jnp.sin(angles)[:, None, :]
    first_half = values_in[..., :half_width]
    second_half = values_in[..., half_width:]
    return jnp.concatenate(
        [
            first_half * cosine - second_half * sine_part,
            second_half * cosine + first_half * sine_part,
        ],
        -1,
    )


def positions(lengths, group_rows):
    within = jnp.arange(group_rows, dtype=jnp.int32)
    return (within[None, :] % lengths[:, None]).reshape(-1)


def attend(query_flat, keyval_flat, lengths, kv_local, group_rows):
    row_count = query_flat.shape[0]
    groups = row_count // group_rows
    repeat = query_flat.shape[1] // (HD * kv_local)
    query_heads = query_flat.reshape(groups, group_rows, kv_local, repeat, HD)
    keyval_heads = keyval_flat.reshape(groups, group_rows, kv_local, 2, HD)
    score_scale = HD ** (-0.5)
    scores = (
        jnp.einsum(
            "gqhrd,gkhd->ghrqk",
            query_heads,
            keyval_heads[:, :, :, 0],
            preferred_element_type=jnp.float32,
        )
        * score_scale
    )
    within = jnp.arange(group_rows, dtype=jnp.int32)
    segment = within[None, :] // lengths[:, None]
    allowed = (segment[:, :, None] == segment[:, None, :]) & (within[None, :] <= within[:, None])[
        None
    ]
    scores = jnp.where(allowed[:, None, None], scores, -jnp.inf)
    row_max = jnp.max(scores, -1, keepdims=True)
    weights = jnp.exp(scores - row_max)
    weights = (weights / jnp.sum(weights, -1, keepdims=True)).astype(jnp.bfloat16)
    context = jnp.einsum(
        "ghrqk,gkhd->gqhrd", weights, keyval_heads[:, :, :, 1], preferred_element_type=jnp.float32
    )
    return context.astype(jnp.bfloat16).reshape(row_count, query_flat.shape[1])


def per_device(
    hidden_states,
    norm_gain,
    w_query,
    w_keyval,
    query_bias,
    keyval_bias,
    group_dest,
    group_offset,
    group_length,
):
    pack_count = lax.axis_size("dp")
    own_index = lax.axis_index("dp")
    row_count = hidden_states.shape[0]
    groups = group_dest.shape[1]
    group_rows = row_count // groups
    kv_local = w_keyval.shape[1] // (2 * HD)
    widened = hidden_states.astype(jnp.float32)
    mean_square = jnp.mean(widened * widened, -1, keepdims=True)
    normed = (widened * lax.rsqrt(mean_square + norm_epsilon) * norm_gain).astype(jnp.bfloat16)

    def add_rows(piece):
        return jnp.dot(normed, piece, preferred_element_type=jnp.float32)

    query = add_rows(lax.all_gather(w_query, "dp", axis=0, tiled=True))
    keyval = add_rows(lax.all_gather(w_keyval, "dp", axis=0, tiled=True))
    query = query + query_bias
    keyval = (keyval + keyval_bias).reshape(row_count, kv_local, 2, HD)
    own_lengths = lax.dynamic_index_in_dim(group_length, own_index, 0, keepdims=False)
    own_dest = lax.dynamic_index_in_dim(group_dest, own_index, 0, keepdims=False)
    position = positions(own_lengths, group_rows)
    query_rot = (
        rotary(query.reshape(row_count, -1, HD), position)
        .astype(jnp.bfloat16)
        .reshape(row_count, -1)
    )
    key_rot = rotary(keyval[:, :, 0], position).astype(jnp.bfloat16)
    value_part = keyval[:, :, 1].astype(jnp.bfloat16)
    keyval_rot = jnp.stack([key_rot, value_part], 2).reshape(row_count, -1)
    chooser = (own_dest[None, :] == jnp.arange(pack_count, dtype=jnp.int32)[:, None]).astype(
        jnp.bfloat16
    )
    arrivals = group_dest == own_index
    slot_index = group_offset // group_rows
    matches = (slot_index[None] == jnp.arange(groups, dtype=jnp.int32)[:, None, None]) & arrivals[
        None
    ]
    placement = jnp.sum(matches.astype(jnp.int32), -1).astype(jnp.bfloat16)

    def outgoing(source_rows):
        flattened = source_rows.reshape(groups, -1)
        sending = jnp.dot(chooser, flattened, preferred_element_type=jnp.float32).astype(
            jnp.bfloat16
        )
        return sending.reshape(pack_count, group_rows, -1)

    def incoming(received):
        flattened = received.reshape(pack_count, -1)
        placed = jnp.dot(placement, flattened, preferred_element_type=jnp.float32).astype(
            jnp.bfloat16
        )
        return placed.reshape(row_count, -1)

    query_recv, keyval_recv = (
        lax.all_to_all(outgoing(query_rot), "dp", split_axis=0, concat_axis=0, tiled=True),
        lax.all_to_all(outgoing(keyval_rot), "dp", split_axis=0, concat_axis=0, tiled=True),
    )
    balanced_lengths = jnp.sum(jnp.where(matches, group_length[None], 0), (1, 2))
    balanced = attend(
        incoming(query_recv), incoming(keyval_recv), balanced_lengths, kv_local, group_rows
    )
    return lax.all_to_all(balanced, "mp", split_axis=0, concat_axis=1, tiled=True)


def solution(mesh):
    return jax.shard_map(
        per_device,
        mesh=mesh,
        in_specs=(
            P("dp", None),
            P(),
            P("dp", "mp"),
            P("dp", "mp"),
            P("mp"),
            P("mp"),
            P(),
            P(),
            P(),
        ),
        out_specs=P(("dp", "mp"), None),
        check_vma=False,
    )
```

profile of v0, /device:TPU:1, one launch (start us, length us, event | category | flops | bytes accessed | tf_op | source)
XLA Modules:
  0.0 306.5 jit_solution(18395869973068619279)
XLA Ops:
  6.5 0.7 all-gather.3.cloned.1.call-update
  7.3 0.7 all-gather.5.cloned.1.call-update
  8.0 0.9 dynamic-slice_reduce_fusion
  9.3 7.2 %fusion = f32[1024]{0:T(1024)S(1)} fusion(bf16[1024,8192]{1,0:T(8,128)(2,1)} %param.9), kind=kLoop, calls=%fused_computation.4 | loop fusion | flops 25164800 | bytes 16781312 | tf_op jit(solution)/shard_map/reduce_sum | solution.py:86
  16.7 3.1 %multiply_cosine_fusion = (f32[1024,64]{1,0:T(8,128)}, f32[1024,64]{1,0:T(8,128)}) fusion(f32[64]{0:T(128)S(1)} %multiply_power_fusion, f32[1024]{0:T(1024)S(1)} %fusion.42), kind=kLoop, calls=%fused_computation.32 | loop fusion | flops 65536 | bytes 528640 | tf_op jit(solution)/shard_map/cos | solution.py:19
  19.8 39.9 %all-gather.3.cloned.1.call-done = bf16[8192,256]{1,0:T(8,128)(2,1)} async-done(((bf16[256,256]{1,0:T(8,128)(2,1)}), bf16[8192,256]{1,0:T(8,128)(2,1)}) %all-gather.3.cloned.1.call-update) | async-done | bytes 4194320 | tf_op jit(solution)/shard_map/all_gather | solution.py:93
  59.7 10.5 %fusion.23 = f32[1024,256]{0,1:T(8,128)S(1)} fusion(bf16[8192,256]{1,0:T(8,128)(2,1)} %all-gather.3.cloned.1.call-done, bf16[1024,8192]{1,0:T(8,128)(2,1)} %param.9, f32[8192]{0:T(1024)S(1)} %copy-done.3, f32[1024]{0:T(1024)S(1)} %add_rsqrt_fusion, f32[256]{0:T(256)S(1)} %copy-done.5), kind=kOutput, calls=%fused_computation.30 | convolution fusion | flops 4328783872 | bytes 22057984 | tf_op jit(solution)/shard_map/dot_general | solution.py:90
  70.3 1.2 fusion.35
  72.8 1.2 copy.60
  74.0 5.3 %all-to-all-start = ((bf16[32,64,256]{2,1,0:T(8,128)(2,1)}), bf16[32,64,256]{2,1,0:T(8,128)(2,1)S(1)}, u32[]{:S(2)}, u32[]{:S(2)}) async-start(bf16[32,64,256]{2,1,0:T(8,128)(2,1)} %bitcast.26), calls=%async_computation | async-start | bytes 2097152 | tf_op jit(solution)/shard_map/all_to_all | solution.py:133
  79.3 65.1 %all-gather.5.cloned.1.call-done = bf16[8192,1024]{1,0:T(8,128)(2,1)} async-done(((bf16[256,1024]{1,0:T(8,128)(2,1)}), bf16[8192,1024]{1,0:T(8,128)(2,1)}) %all-gather.5.cloned.1.call-update) | async-done | bytes 16777232 | tf_op jit(solution)/shard_map/all_gather | solution.py:92
  144.4 24.4 %fusion.9 = f32[1024,1024]{0,1:T(8,128)S(1)} fusion(bf16[8192,1024]{1,0:T(8,128)(2,1)} %all-gather.5.cloned.1.call-done, bf16[1024,8192]{1,0:T(8,128)(2,1)} %param.9, f32[8192]{0:T(1024)S(1)} %copy-done.3, f32[1024]{0:T(1024)S(1)} %add_rsqrt_fusion, f32[1024]{0:T(1024)S(1)} %copy-done.4), kind=kOutput, calls=%fused_computation.18 | convolution fusion | flops 17214472192 | bytes 37789696 | tf_op jit(solution)/shard_map/dot_general | solution.py:90
  168.8 1.7 fusion.47
  170.5 3.8 %copy.59 = f32[1024,8,64]{2,1,0:T(8,128)} copy(f32[1024,8,64]{0,2,1:T(8,128)} %get-tuple-element.9) | data formatting | bytes 4194304
  174.3 2.8 copy.58
  177.1 4.2 %subtract_convert_fusion = (bf16[1024,8,64]{2,1,0:T(8,128)(2,1)S(1)}, bf16[1024,8,64]{2,1,0:T(8,128)(2,1)S(1)}) fusion(f32[1024,8,64]{2,1,0:T(8,128)} %copy.59, f32[1024,8,64]{2,1,0:T(8,128)} %copy.58, f32[1024,64]{1,0:T(8,128)} %get-tuple-element.16, f32[1024,64]{1,0:T(8,128)} %get-tuple-element.15), kind=kLoop, calls=%fused_computation.15 | loop fusion | flops 4194304 | bytes 6815744 | tf_op jit(solution)/shard_map/convert
  181.3 1.2 pad_maximum_fusion
  182.5 1.9 convert_element_type.71
  184.3 2.8 convolution_convert_fusion
  187.2 4.3 %copy.62 = bf16[4,8,64,1024]{3,2,1,0:T(8,128)(2,1)} copy(bf16[4,8,64,1024]{3,1,2,0:T(8,128)(2,1)S(1)} %bitcast.75) | data formatting | bytes 8388608
  191.4 5.8 %all-to-all-start.1 = ((bf16[32,64,1024]{2,1,0:T(8,128)(2,1)}), bf16[32,64,1024]{2,1,0:T(8,128)(2,1)}, u32[]{:S(2)}, u32[]{:S(2)}) async-start(bf16[32,64,1024]{2,1,0:T(8,128)(2,1)} %bitcast.74), calls=%async_computation.1 | async-start | bytes 8388608 | tf_op jit(solution)/shard_map/all_to_all | solution.py:132
  199.4 1.1 fusion.48
  200.6 48.7 %all-to-all-done.1 = bf16[32,64,1024]{2,1,0:T(8,128)(2,1)} async-done(((bf16[32,64,1024]{2,1,0:T(8,128)(2,1)}), bf16[32,64,1024]{2,1,0:T(8,128)(2,1)}, u32[]{:S(2)}, u32[]{:S(2)}) %all-to-all-start.1) | async-done | bytes 4194336 | tf_op jit(solution)/shard_map/all_to_all | solution.py:132
  249.3 4.5 %copy.63 = bf16[4,8,64,1024]{3,1,2,0:T(8,128)(2,1)S(1)} copy(bf16[4,8,64,1024]{3,2,1,0:T(8,128)(2,1)} %bitcast.31) | data formatting | bytes 8388608
  254.9 2.1 fusion.8
  257.0 1.4 fusion.7
  258.4 1.4 convert_bitcast_fusion
  259.8 1.8 copy.50
  261.6 2.3 all_to_all.22
  263.8 29.2 %all_to_all.29 = bf16[4,256,1024]{2,1,0:T(8,128)(2,1)S(1)} all-to-all(bf16[4,256,1024]{2,1,0:T(8,128)(2,1)} %all_to_all.22), channel_id=1, replica_groups=mesh['dp'=32,'mp'=4] {'mp'}, dimensions={0} | all-to-all | bytes 4194304 | tf_op jit(solution)/shard_map/all_to_all | solution.py:139
  293.0 2.5 copy.51
  295.5 4.1 %copy.52 = bf16[256,4096]{1,0:T(8,128)(2,1)} copy(bf16[256,4096]{0,1:T(8,128)(2,1)} %bitcast.79) | data formatting | bytes 4194304 | tf_op jit(solution)/shard_map/all_to_all | solution.py:139
  (45 shorter events, 5.1 us)
Async XLA Ops:
  6.5 53.2 %all-gather.3.cloned.1.call-start = ((), (), s32[]{:S(2)}) async-start(), calls=%async_computation.3 | async-start | bytes 4325376 | tf_op jit(solution)/shard_map/all_gather | solution.py:93
  7.3 137.1 %all-gather.5.cloned.1.call-start = ((), (), s32[]{:S(2)}) async-start(), calls=%async_computation.4 | async-start | bytes 17301504 | tf_op jit(solution)/shard_map/all_gather | solution.py:92
  9.3 50.4 %copy-start.3 = (f32[8192]{0:T(1024)S(1)}, f32[8192]{0:T(1024)}, u32[]{:S(2)}) copy-start(f32[8192]{0:T(1024)} %param.10) | copy-start | bytes 98308
  9.3 50.4 %copy-start.5 = (f32[256]{0:T(256)S(1)}, f32[256]{0:T(256)}, u32[]{:S(2)}) copy-start(f32[256]{0:T(256)} %param.14) | copy-start | bytes 3076
  71.6 72.8 %copy-start.4 = (f32[1024]{0:T(1024)S(1)}, f32[1024]{0:T(1024)}, u32[]{:S(2)}) copy-start(f32[1024]{0:T(1024)} %param.13) | copy-start | bytes 12292
  74.0 117.4 %all-to-all-start = ((bf16[32,64,256]{2,1,0:T(8,128)(2,1)}), bf16[32,64,256]{2,1,0:T(8,128)(2,1)S(1)}, u32[]{:S(2)}, u32[]{:S(2)}) async-start(bf16[32,64,256]{2,1,0:T(8,128)(2,1)} %bitcast.26), calls=%async_computation | async-start | bytes 2097152 | tf_op jit(solution)/shard_map/all_to_all | solution.py:133
  191.4 5.9 %copy-start = (s32[32,16]{0,1:T(8,128)S(1)}, s32[32,16]{0,1:T(8,128)}, u32[]{:S(2)}) copy-start(s32[32,16]{0,1:T(8,128)} %param.15) | copy-start | bytes 6148
  191.4 5.9 %copy-start.2 = (s32[32,16]{0,1:T(8,128)S(1)}, s32[32,16]{0,1:T(8,128)}, u32[]{:S(2)}) copy-start(s32[32,16]{0,1:T(8,128)} %param.16) | copy-start | bytes 6148
  191.4 5.9 %copy-start.1 = (s32[32,16]{0,1:T(8,128)S(1)}, s32[32,16]{0,1:T(8,128)}, u32[]{:S(2)}) copy-start(s32[32,16]{0,1:T(8,128)} %param.17) | copy-start | bytes 6148
  191.4 57.8 %all-to-all-start.1 = ((bf16[32,64,1024]{2,1,0:T(8,128)(2,1)}), bf16[32,64,1024]{2,1,0:T(8,128)(2,1)}, u32[]{:S(2)}, u32[]{:S(2)}) async-start(bf16[32,64,1024]{2,1,0:T(8,128)(2,1)} %bitcast.74), calls=%async_computation.1 | async-start | bytes 8388608 | tf_op jit(solution)/shard_map/all_to_all | solution.py:132
Sparse Core Ops, SparseCore 0:
  9.6 50.0 all-gather.2
  62.0 82.3 all-gather.4
where the time goes:
time: 309 us; the launch traced here: 306 us
  waiting for transfers between devices  155 us (50%)
  matrix products  42.6 us (14%)
  local copies, waits for them, and re-layouts  35.5 us (11%)
  blocking collectives  29.2 us (9%)
  other arithmetic  19.2 us (6%)
  between operations  13.7 us (4%)
  starting transfers between devices  11.2 us (4%)
    all_gather x1, waiting for transfers between devices, per_device(): query = add_rows(lax.all_gather(w_query, 'dp', axis=0, tiled=True))  65.1 us
    all_to_all x1, waiting for transfers between devices, per_device(): lax.all_to_all(outgoing(query_rot), 'dp', split_axis=0, concat_axis=0, ti...  48.7 us
    all_gather x1, waiting for transfers between devices, per_device(): keyval = add_rows(lax.all_gather(w_keyval, 'dp', axis=0, tiled=True))  39.9 us
    dot_general x2, matrix products, add_rows(): return jnp.dot(normed, piece, preferred_element_type=jnp.float32)  34.9 us
    all_to_all x1, blocking collectives, per_device(): lax.all_to_all(balanced, 'mp', split_axis=0, concat_axis=1, tiled=True)  29.2 us
    unnamed x19, local copies, waits for them, and re-layouts  17.6 us
    all_to_all x3, local copies, waits for them, and re-layouts, per_device(): lax.all_to_all(balanced, 'mp', split_axis=0, concat_axis=1, tiled=True)  8.88 us
    reduce_sum x1, other arithmetic, per_device(): mean_square = jnp.mean(widened * widened, -1, keepdims=True)  7.2 us
  transfers between devices with their start and end apart: 4, of which 3 were waited for; matrix products, arithmetic and copies ran while one was open for 25% of the time, Pallas kernels for 0%

commit v1 on v0

v1 whole, which is shorter than its diff:
```python
import jax
import jax.numpy as jnp
import numpy as np
from jax import lax
from jax.experimental import pallas as pl
from jax.experimental.pallas import tpu as pltpu
from jax.sharding import PartitionSpec as P

HD = 128
GROUP = 64
SIDE = 4
MIB = 1024 * 1024

rope_base = 1000000.0
norm_epsilon = 1e-06


def rope_tables():
    half = HD // 2
    frequency = np.float32(rope_base) ** (
        -(np.arange(half, dtype=np.float32) * np.float32(2.0)) / np.float32(HD)
    )
    within = np.arange(GROUP)
    position = np.concatenate([within % length for length in (64, 32, 16, 8)])
    angles = position.astype(np.float32)[:, None] * frequency[None, :].astype(np.float32)
    cosine, sine = np.cos(angles), np.sin(angles)
    return (
        np.concatenate([cosine, cosine], 1).astype(np.float32),
        np.concatenate([-sine, sine], 1).astype(np.float32),
    )


def device_index(y, z, core):
    return ((y % SIDE) * SIDE + (z % SIDE)) * 2 + core


def shift_pairs(first, second):
    pairs = []
    for y in range(SIDE):
        for z in range(SIDE):
            pairs.append((device_index(y, z, 0), device_index(y + first, z + second, 0)))
            pairs.append((device_index(y, z, 1), device_index(y + second, z + first, 1)))
    return pairs


def swap_pairs():
    return [
        (device_index(y, z, core), device_index(y, z, 1 - core))
        for y in range(SIDE)
        for z in range(SIDE)
        for core in range(2)
    ]


def source_table():
    table = np.zeros((32, 32), np.int32)
    for y in range(SIDE):
        for z in range(SIDE):
            for core in range(2):

                def pieces(c, second):
                    found = []
                    for first in range(SIDE):
                        if c == 0:
                            found.append(device_index(y - first, z - second, c))
                        else:
                            found.append(device_index(y - second, z - first, c))
                    return found

                other = 1 - core
                order = pieces(core, 0) + pieces(other, 0)
                order += pieces(core, 1) + pieces(core, 3) + pieces(other, 1) + pieces(other, 3)
                order += pieces(core, 2) + pieces(other, 2)
                table[device_index(y, z, core)] = order
    return table


def norm_kernel(order_ref, hidden_ref, gain_ref, early_ref, middle_ref, late_ref):
    features = hidden_ref.shape[1]
    depth = features // 32
    widened = hidden_ref[...].astype(jnp.float32)
    mean_square = jnp.sum(widened * widened, -1, keepdims=True) * (1.0 / features)
    scale = lax.rsqrt(mean_square + norm_epsilon)
    place = 0
    for ref in (early_ref, middle_ref, late_ref):
        for j in range(ref.shape[1] // depth):
            start = pl.multiple_of(order_ref[place] * depth, depth)
            block = hidden_ref[:, pl.ds(start, depth)].astype(jnp.float32)
            gain = gain_ref[:, pl.ds(start, depth)]
            ref[:, j * depth : (j + 1) * depth] = (block * scale * gain).astype(jnp.bfloat16)
            place += 1


def norm(order, hidden, gain, widths):
    rows, features = hidden.shape
    tile = 128
    return pl.pallas_call(
        norm_kernel,
        grid_spec=pltpu.PrefetchScalarGridSpec(
            num_scalar_prefetch=1,
            grid=(rows // tile,),
            in_specs=[
                pl.BlockSpec((tile, features), lambda i, order: (i, 0)),
                pl.BlockSpec((1, features), lambda i, order: (0, 0)),
            ],
            out_specs=[pl.BlockSpec((tile, w), lambda i, order: (i, 0)) for w in widths],
        ),
        out_shape=[jax.ShapeDtypeStruct((rows, w), jnp.bfloat16) for w in widths],
        compiler_params=pltpu.CompilerParams(vmem_limit_bytes=24 * MIB),
        cost_estimate=pl.CostEstimate(
            flops=6 * rows * features, bytes_accessed=4 * rows * features, transcendentals=rows
        ),
        name="norm",
    )(order, hidden, gain)


def product(x_ref, pieces):
    weights = jnp.concatenate([piece[...] for piece in pieces], axis=0)
    return jnp.dot(x_ref[...], weights, preferred_element_type=jnp.float32)


def first_kernel(x_ref, *refs):
    refs[-1][...] = product(x_ref, refs[:-1])


def add_kernel(total_ref, x_ref, *refs):
    refs[-1][...] = total_ref[...] + product(x_ref, refs[:-1])


def whole(shape):
    return pl.BlockSpec(shape, lambda i: (0,) * len(shape), pipeline_mode=pl.Buffered(1))


def matmul_cost(rows, depth, columns, more):
    return pl.CostEstimate(
        flops=2 * rows * depth * columns,
        bytes_accessed=2 * depth * (rows + columns) + 4 * more * rows * columns,
        transcendentals=0,
    )


def project(total, x, pieces):
    rows, depth = x.shape
    columns = pieces[0].shape[1]
    tile = 256
    block = pl.BlockSpec((tile, columns), lambda i: (i, 0))
    x_block = pl.BlockSpec((tile, depth), lambda i: (i, 0))
    weights = [whole(piece.shape) for piece in pieces]
    return pl.pallas_call(
        first_kernel if total is None else add_kernel,
        grid=(rows // tile,),
        in_specs=([] if total is None else [block]) + [x_block] + weights,
        out_specs=block,
        out_shape=jax.ShapeDtypeStruct((rows, columns), jnp.float32),
        input_output_aliases={} if total is None else {0: 0},
        compiler_params=pltpu.CompilerParams(vmem_limit_bytes=40 * MIB),
        cost_estimate=matmul_cost(rows, depth, columns, 1 if total is None else 2),
        name="project",
    )(*([] if total is None else [total]), x, *pieces)


def attend_kernel(
    dest_ref, length_ref, total_ref, x_ref, bias_ref, cosine_ref, sine_ref, *refs
):
    pieces, (out_ref, context, sems) = refs[:-3], refs[-3:]
    step = pl.program_id(0)
    slot = lax.rem(step, 2)
    rows, columns = total_ref.shape
    heads = columns // HD - 2
    groups = rows // GROUP

    def copies(at_step, at_slot):
        return [
            pltpu.make_async_copy(
                context.at[at_slot, pl.ds(g * GROUP, GROUP)],
                out_ref.at[dest_ref[at_step * groups + g]],
                sems.at[at_slot, g],
            )
            for g in range(groups)
        ]

    lengths = [length_ref[step * groups + g] for g in range(groups)]
    row_tables = []
    for table in (cosine_ref, sine_ref):
        parts = []
        for length in lengths:
            index = (
                (length < 64).astype(jnp.int32)
                + (length < 32).astype(jnp.int32)
                + (length < 16).astype(jnp.int32)
            )
            parts.append(table[pl.ds(pl.multiple_of(index * GROUP, GROUP), GROUP), :])
        row_tables.append(jnp.concatenate(parts, 0))
    cosine, sine = row_tables

    summed = total_ref[...] + product(x_ref, pieces) + bias_ref[...]

    def rotated(column):
        head = summed[:, column : column + HD]
        return (head * cosine + pltpu.roll(head, HD // 2, 1) * sine).astype(jnp.bfloat16)

    query = [rotated(h * HD) for h in range(heads)]
    key = rotated(heads * HD)
    value = summed[:, (heads + 1) * HD :].astype(jnp.bfloat16)

    @pl.when(step >= 2)
    def _():
        for copy in copies(step - 2, slot):
            copy.wait()

    tile = 2 * GROUP
    row = lax.broadcasted_iota(jnp.int32, (tile, tile), 0)
    column = lax.broadcasted_iota(jnp.int32, (tile, tile), 1)
    for t in range(rows // tile):
        length = jnp.where(row < GROUP, lengths[2 * t], lengths[2 * t + 1])
        allowed = (column >= (row & -length)) & (column <= row)
        span = slice(t * tile, (t + 1) * tile)
        stacked = jnp.concatenate([q[span] for q in query], 0)
        scores = lax.dot_general(
            stacked, key[span], (((1,), (1,)), ((), ())), preferred_element_type=jnp.float32
        ) * (HD ** (-0.5))
        scores = jnp.where(allowed[None], scores.reshape(heads, tile, tile), -jnp.inf)
        weights = jnp.exp(scores - jnp.max(scores, -1, keepdims=True))
        weights = weights * (1.0 / jnp.sum(weights, -1, keepdims=True))
        weights = weights.astype(jnp.bfloat16).reshape(heads * tile, tile)
        mixed = jnp.dot(weights, value[span], preferred_element_type=jnp.float32)
        mixed = mixed.astype(jnp.bfloat16)
        for h in range(heads):
            context[slot, span, h * HD : (h + 1) * HD] = mixed[h * tile : (h + 1) * tile]

    for copy in copies(step, slot):
        copy.start()

    @pl.when(step == pl.num_programs(0) - 1)
    def _():
        for copy in copies(step - 1, 1 - slot) + copies(step, slot):
            copy.wait()


def attend(dest, lengths, total, x, bias, pieces, packs):
    rows, depth = x.shape
    columns = total.shape[1]
    tile = 256
    cosine, sine = rope_tables()
    width = columns - 2 * HD

    def fixed(shape):
        return pl.BlockSpec(
            shape, lambda i, *_: (0,) * len(shape), pipeline_mode=pl.Buffered(1)
        )

    return pl.pallas_call(
        attend_kernel,
        grid_spec=pltpu.PrefetchScalarGridSpec(
            num_scalar_prefetch=2,
            grid=(rows // tile,),
            in_specs=[
                pl.BlockSpec((tile, columns), lambda i, *_: (i, 0)),
                pl.BlockSpec((tile, depth), lambda i, *_: (i, 0)),
                fixed(bias.shape),
                fixed(cosine.shape),
                fixed(sine.shape),
            ]
            + [fixed(piece.shape) for piece in pieces],
            out_specs=pl.BlockSpec(memory_space=pl.ANY),
            scratch_shapes=[
                pltpu.VMEM((2, tile, width), jnp.bfloat16),
                pltpu.SemaphoreType.DMA((2, tile // GROUP)),
            ],
        ),
        out_shape=jax.ShapeDtypeStruct((packs, GROUP, width), jnp.bfloat16),
        compiler_params=pltpu.CompilerParams(vmem_limit_bytes=48 * MIB),
        cost_estimate=matmul_cost(rows, depth, columns, 2),
        name="attend",
    )(dest, lengths, total, x, bias, cosine, sine, *pieces)


def place_kernel(source_ref, *refs):
    count = len(refs) // 2
    for given, taken in zip(refs[:count], refs[count:], strict=True):
        taken[...] = given[0]


def place(source, received, parts):
    packs, group, width = received.shape
    per_part = source.shape[0] // parts

    def given(part):
        return pl.BlockSpec(
            (1, group, width), lambda j, source: (source[part * per_part + j], 0, 0)
        )

    return pl.pallas_call(
        place_kernel,
        grid_spec=pltpu.PrefetchScalarGridSpec(
            num_scalar_prefetch=1,
            grid=(per_part,),
            in_specs=[given(part) for part in range(parts)],
            out_specs=[pl.BlockSpec((group, width), lambda j, source: (j, 0))] * parts,
        ),
        out_shape=[jax.ShapeDtypeStruct((per_part * group, width), received.dtype)] * parts,
        name="place",
    )(source, *([received] * parts))


def join_kernel(order_ref, *refs):
    width = refs[0].shape[1]
    for part, ref in enumerate(refs[:-1]):
        start = pl.multiple_of(order_ref[part] * width, width)
        refs[-1][:, pl.ds(start, width)] = ref[...]


def join(order, parts):
    rows, width = parts[0].shape
    tile = 64
    return pl.pallas_call(
        join_kernel,
        grid_spec=pltpu.PrefetchScalarGridSpec(
            num_scalar_prefetch=1,
            grid=(rows // tile,),
            in_specs=[pl.BlockSpec((tile, width), lambda i, order: (i, 0))] * len(parts),
            out_specs=pl.BlockSpec((tile, width * len(parts)), lambda i, order: (i, 0)),
        ),
        out_shape=jax.ShapeDtypeStruct((rows, width * len(parts)), parts[0].dtype),
        name="join",
    )(order, *parts)


def per_device(
    hidden_states,
    norm_gain,
    w_query,
    w_keyval,
    query_bias,
    keyval_bias,
    group_dest,
    group_offset,
    group_length,
):
    own = lax.axis_index("dp")
    plane = lax.axis_index("mp")
    planes = lax.axis_size("mp")
    packs, groups = group_dest.shape
    rows, features = hidden_states.shape

    def first(piece, by):
        return lax.ppermute(piece, "dp", shift_pairs(by, 0))

    def second(piece, by):
        return lax.ppermute(piece, "dp", shift_pairs(0, by))

    def swap(piece):
        return lax.ppermute(piece, "dp", swap_pairs())

    weights = jnp.concatenate([w_query, w_keyval], 1)
    bias = jnp.concatenate([query_bias, keyval_bias])[None]
    near = [weights, first(weights, 1), first(weights, 2), first(weights, -1)]
    ahead = [second(piece, 1) for piece in near]
    behind = [second(piece, -1) for piece in near]
    far = [second(ahead[0], 1), second(ahead[1], 1), second(behind[2], -1), second(behind[3], -1)]
    early = near + [swap(piece) for piece in near]
    middle = ahead + behind + [swap(piece) for piece in ahead + behind]
    late = far + [swap(piece) for piece in far]

    depth = weights.shape[0]
    order = lax.dynamic_index_in_dim(jnp.asarray(source_table()), own, 0, keepdims=False)
    x_early, x_middle, x_late = norm(
        order,
        hidden_states,
        norm_gain[None],
        [len(early) * depth, len(middle) * depth, len(late) * depth],
    )
    total = project(None, x_early, early)
    total = project(total, x_middle, middle)

    own_dest = lax.dynamic_index_in_dim(group_dest, own, 0, keepdims=False)
    own_length = lax.dynamic_index_in_dim(group_length, own, 0, keepdims=False)
    sent = attend(own_dest, own_length, total, x_late, bias, late, packs)
    received = lax.all_to_all(sent, "dp", split_axis=0, concat_axis=0, tiled=True)

    slot = group_offset // GROUP
    hits = (group_dest == own)[None] & (
        slot[None] == jnp.arange(groups, dtype=jnp.int32)[:, None, None]
    )
    packs_of = jnp.arange(packs, dtype=jnp.int32)[None, :, None]
    source = jnp.sum(jnp.where(hits, packs_of, 0), (1, 2)).reshape(planes, -1)
    step = jnp.arange(planes, dtype=jnp.int32)
    source = source[(plane + step) % planes].reshape(-1)
    parts = place(source, received, planes)
    arrived = [parts[0]]
    for k in range(1, planes):
        arrived.append(
            lax.ppermute(parts[k], "mp", [(i, (i + k) % planes) for i in range(planes)])
        )
    return join((plane - step) % planes, arrived)


def solution(mesh):
    return jax.shard_map(
        per_device,
        mesh=mesh,
        in_specs=(
            P("dp", None),
            P(),
            P("dp", "mp"),
            P("dp", "mp"),
            P("mp"),
            P("mp"),
            P(),
            P(),
            P(),
        ),
        out_specs=P(("dp", "mp"), None),
        check_vma=False,
    )
```

time: 309 us -> 229 us (0.74)
  Pallas kernels: 0 us -> 61 us
  waiting for transfers between devices: 155 us -> 102 us
  matrix products: 42.6 us -> 0 us
  starting transfers between devices: 11.2 us -> 41.6 us
  blocking collectives: 29.2 us -> 0 us
  other arithmetic: 19.2 us -> 1.65 us
  local copies, waits for them, and re-layouts: 35.5 us -> 20.2 us
  between operations: 13.7 us -> 0.38 us
    all_gather x2 -> x0, waiting for transfers between devices: 105 us -> none  [the longest x1 65.1 us: per_device(): query = add_rows(lax.all_gather(w_query, 'dp', axis=0, tiled=True))]
    pallas_call x0 -> x6, Pallas kernels: none -> 61 us  [the longest x2 23.3 us: project(): pl.pallas_call(first_kernel if total is None else add_kernel, grid=(rows...]
    ppermute x0 -> x34, waiting for transfers between devices: none -> 51.2 us  [the longest x3 21 us: per_device(): lax.ppermute(parts[k], 'mp', [(i, (i + k) % planes) for i in range(planes)])]
    dot_general x8 -> x0, matrix products: 42.6 us -> none  [the longest x2 34.9 us: add_rows(): return jnp.dot(normed, piece, preferred_element_type=jnp.float32)]
    ppermute x0 -> x34, starting transfers between devices: none -> 36.9 us  [the longest x16 13.7 us: swap(): return lax.ppermute(piece, 'dp', swap_pairs())]
    all_to_all x1 -> x0, blocking collectives: 29.2 us -> none  [per_device(): lax.all_to_all(balanced, 'mp', split_axis=0, concat_axis=1, tiled=True)]
    all_to_all x3 -> x0, local copies, waits for them, and re-layouts: 8.88 us -> none  [per_device(): lax.all_to_all(balanced, 'mp', split_axis=0, concat_axis=1, tiled=True)]
    reduce_sum x3 -> x1, other arithmetic: 8.96 us -> 0.39 us  [per_device(): source = jnp.sum(jnp.where(hits, packs_of, 0), (1, 2)).reshape(planes, -1)]
  transfers between devices with their start and end apart: 4 -> 35, of which waited for: 3 -> 9; matrix products, arithmetic and copies ran while one was open for 25% -> 2% of each run, Pallas kernels for 0% -> 16%
where the time goes in v1:
time: 229 us; the launch traced here: 226 us
  waiting for transfers between devices  102 us (45%)
  Pallas kernels  61 us (27%)
  starting transfers between devices  41.6 us (18%)
  local copies, waits for them, and re-layouts  20.2 us (9%)
    all_to_all x1, waiting for transfers between devices, per_device(): lax.all_to_all(sent, 'dp', split_axis=0, concat_axis=0, tiled=True)  50.5 us
    pallas_call x2, Pallas kernels, project(): pl.pallas_call(first_kernel if total is None else add_kernel, grid=(rows...  23.3 us
    ppermute x3, waiting for transfers between devices, per_device(): lax.ppermute(parts[k], 'mp', [(i, (i + k) % planes) for i in range(planes)])  21 us
    ppermute x3, waiting for transfers between devices, first(): return lax.ppermute(piece, 'dp', shift_pairs(by, 0))  16.4 us
    unnamed x73, local copies, waits for them, and re-layouts  16.4 us
    pallas_call x1, Pallas kernels, attend(): pl.pallas_call(attend_kernel, grid_spec=pltpu.PrefetchScalarGridSpec(num_...  16.1 us
    ppermute x12, waiting for transfers between devices, second(): return lax.ppermute(piece, 'dp', shift_pairs(0, by))  13.7 us
    ppermute x16, starting transfers between devices, swap(): return lax.ppermute(piece, 'dp', swap_pairs())  13.7 us
  transfers between devices with their start and end apart: 35, of which 9 were waited for; matrix products, arithmetic and copies ran while one was open for 2% of the time, Pallas kernels for 16%

profile of v1, /device:TPU:1, one launch (start us, length us, event | category | flops | bytes accessed | tf_op | source)
XLA Modules:
  0.0 226.5 jit_solution(16787085464025631958)
XLA Ops:
  0.0 1.1 constant_dynamic-update-slice_fusion.1
  1.1 0.9 constant_dynamic-update-slice_fusion.refs_0_
  2.0 2.5 %collective-permute-start = (bf16[256,1280]{1,0:T(8,128)(2,1)S(1)}, bf16[256,1280]{1,0:T(8,128)(2,1)S(1)}, u32[]{:S(2)}, u32[]{:S(2)}) collective-permute-start(bf16[256,1280]{1,0:T(8,128)(2,1)S(1)} %constant_dynamic-update-slice_fusion.refs_0_), channel_id=1, source_target_pairs={{0,32},{4,12},{8,40},{12,20},{16,48},{20,28},{24,56},{28,4},{32,64... | collective-permute-start | bytes 1966088 | tf_op jit(solution)/shard_map/ppermute | solution.py:347
  4.5 3.3 %collective-permute-start.1 = (bf16[256,1280]{1,0:T(8,128)(2,1)S(1)}, bf16[256,1280]{1,0:T(8,128)(2,1)S(1)}, u32[]{:S(2)}, u32[]{:S(2)}) collective-permute-start(bf16[256,1280]{1,0:T(8,128)(2,1)S(1)} %constant_dynamic-update-slice_fusion.refs_0_), channel_id=1, source_target_pairs={{0,64},{4,20},{8,72},{12,28},{16,80},{20,4},{24,88},{28,12},{32,96... | collective-permute-start | bytes 1966088 | tf_op jit(solution)/shard_map/ppermute | solution.py:347
  9.9 5.3 %collective-permute-done.refs_1_ = bf16[256,1280]{1,0:T(8,128)(2,1)S(1)} collective-permute-done((bf16[256,1280]{1,0:T(8,128)(2,1)S(1)}, bf16[256,1280]{1,0:T(8,128)(2,1)S(1)}, u32[]{:S(2)}, u32[]{:S(2)}) %collective-permute-start) | collective-permute-done | bytes 655392 | tf_op jit(solution)/shard_map/ppermute | solution.py:347
  15.2 3.9 %collective-permute-start.11 = (bf16[256,1280]{1,0:T(8,128)(2,1)S(1)}, bf16[256,1280]{1,0:T(8,128)(2,1)S(1)}, u32[]{:S(2)}, u32[]{:S(2)}) collective-permute-start(bf16[256,1280]{1,0:T(8,128)(2,1)S(1)} %constant_dynamic-update-slice_fusion.refs_0_), channel_id=1, source_target_pairs={{0,24},{4,100},{8,0},{12,108},{16,8},{20,116},{24,16},{28,124},{32... | collective-permute-start | bytes 1966088 | tf_op jit(solution)/shard_map/ppermute | solution.py:350
  19.1 11.1 %collective-permute-done.1.refs_2_ = bf16[256,1280]{1,0:T(8,128)(2,1)S(1)} collective-permute-done((bf16[256,1280]{1,0:T(8,128)(2,1)S(1)}, bf16[256,1280]{1,0:T(8,128)(2,1)S(1)}, u32[]{:S(2)}, u32[]{:S(2)}) %collective-permute-start.1) | collective-permute-done | bytes 655392 | tf_op jit(solution)/shard_map/ppermute | solution.py:347
  32.5 2.2 collective-permute-start.13
  39.6 3.5 %collective-permute-done.8.refs_1_ = bf16[256,1280]{1,0:T(8,128)(2,1)} collective-permute-done((bf16[256,1280]{1,0:T(8,128)(2,1)S(1)}, bf16[256,1280]{1,0:T(8,128)(2,1)}, u32[]{:S(2)}, u32[]{:S(2)}) %collective-permute-start.8) | collective-permute-done | bytes 655392 | tf_op jit(solution)/shard_map/ppermute | solution.py:350
  43.8 3.0 %collective-permute-start.15 = (bf16[256,1280]{1,0:T(8,128)(2,1)S(1)}, bf16[256,1280]{1,0:T(8,128)(2,1)S(1)}, u32[]{:S(2)}, u32[]{:S(2)}) collective-permute-start(bf16[256,1280]{1,0:T(8,128)(2,1)S(1)} %collective-permute-done.7.refs_0_), channel_id=1, source_target_pairs={{0,4},{4,0},{8,12},{12,8},{16,20},{20,16},{24,28},{28,24},{32,36},... | collective-permute-start | bytes 1966088 | tf_op jit(solution)/shard_map/ppermute | solution.py:353
  46.8 2.6 %collective-permute-done.14.refs_7_ = bf16[256,1280]{1,0:T(8,128)(2,1)} collective-permute-done((bf16[256,1280]{1,0:T(8,128)(2,1)S(1)}, bf16[256,1280]{1,0:T(8,128)(2,1)}, u32[]{:S(2)}, u32[]{:S(2)}) %collective-permute-start.14) | collective-permute-done | bytes 655392 | tf_op jit(solution)/shard_map/ppermute | solution.py:350
  49.4 2.3 %collective-permute-start.19 = (bf16[256,1280]{1,0:T(8,128)(2,1)S(1)}, bf16[256,1280]{1,0:T(8,128)(2,1)S(1)}, u32[]{:S(2)}, u32[]{:S(2)}) collective-permute-start(bf16[256,1280]{1,0:T(8,128)(2,1)S(1)} %collective-permute-done.11.refs_4_), channel_id=1, source_target_pairs={{0,4},{4,0},{8,12},{12,8},{16,20},{20,16},{24,28},{28,24},{32,36},... | collective-permute-start | bytes 1966088 | tf_op jit(solution)/shard_map/ppermute | solution.py:353
  51.7 5.4 %collective-permute-done.10.refs_3_ = bf16[256,1280]{1,0:T(8,128)(2,1)} collective-permute-done((bf16[256,1280]{1,0:T(8,128)(2,1)S(1)}, bf16[256,1280]{1,0:T(8,128)(2,1)}, u32[]{:S(2)}, u32[]{:S(2)}) %collective-permute-start.10) | collective-permute-done | bytes 655392 | tf_op jit(solution)/shard_map/ppermute | solution.py:350
  57.1 1.7 collective-permute-start.16
  58.8 0.9 copy-done.17
  61.9 2.1 collective-permute-done.23.refs_0_
  64.9 2.6 %collective-permute-start.25 = (bf16[256,1280]{1,0:T(8,128)(2,1)}, bf16[256,1280]{1,0:T(8,128)(2,1)}, u32[]{:S(2)}, u32[]{:S(2)}) collective-permute-start(bf16[256,1280]{1,0:T(8,128)(2,1)} %collective-permute-done.13.refs_6_), channel_id=1, source_target_pairs={{0,24},{4,100},{8,0},{12,108},{16,8},{20,116},{24,16},{28,124},{32... | collective-permute-start | bytes 1966088 | tf_op jit(solution)/shard_map/ppermute | solution.py:350
  69.2 3.0 %collective-permute-start.18 = (bf16[256,1280]{1,0:T(8,128)(2,1)}, bf16[256,1280]{1,0:T(8,128)(2,1)}, u32[]{:S(2)}, u32[]{:S(2)}) collective-permute-start(bf16[256,1280]{1,0:T(8,128)(2,1)} %collective-permute-done.10.refs_3_), channel_id=1, source_target_pairs={{0,4},{4,0},{8,12},{12,8},{16,20},{20,16},{24,28},{28,24},{32,36},... | collective-permute-start | bytes 1966088 | tf_op jit(solution)/shard_map/ppermute | solution.py:353
  76.2 12.6 %norm.1 = (bf16[1024,2048]{1,0:T(8,128)(2,1)S(1)}, bf16[1024,4096]{1,0:T(8,128)(2,1)S(1)}, bf16[1024,2048]{1,0:T(8,128)(2,1)S(1)}) custom-call(s32[32]{0:T(128)S(1)} %fusion.3.order_ref, bf16[1024,8192]{1,0:T(8,128)(2,1)} %hidden_ref.1, f32[1,8192]{1,0:T(1,128)S(1)} %bitcast.5), custom_call_target="tpu_custom_call" | custom-call | flops 50331648 | bytes 33554432 | tf_op jit(solution)/shard_map/norm/pallas_call | solution.py:97
  88.8 3.3 %copy-done.1 = bf16[1024,4096]{1,0:T(8,128)(2,1)} copy-done((bf16[1024,4096]{1,0:T(8,128)(2,1)}, bf16[1024,4096]{1,0:T(8,128)(2,1)S(1)}, u32[]{:S(2)}) %copy-start.1) | copy-done | bytes 8388632
  92.3 7.3 %project.2.total_ref = f32[1024,1280]{1,0:T(8,128)} custom-call(bf16[1024,2048]{1,0:T(8,128)(2,1)S(1)} %get-tuple-element.12.x_ref, bf16[256,1280]{1,0:T(8,128)(2,1)S(1)} %constant_dynamic-update-slice_fusion.refs_0_, bf16[256,1280]{1,0:T(8,128)(2,1)S(1)} %collective-permute-done.refs_1_, bf16[256,1280]{1,0:T(8,128)(2,1)S(1)} %collective-permute-done.1.refs_2_, ...), custom_call_target="tpu_custom_call" | custom-call | flops 5368709120 | bytes 14680064 | tf_op jit(solution)/shard_map/project/pallas_call | solution.py:149
  101.0 16.1 %project.3.total_ref = f32[1024,1280]{1,0:T(8,128)} custom-call(f32[1024,1280]{1,0:T(8,128)} %project.2.total_ref, bf16[1024,4096]{1,0:T(8,128)(2,1)} %copy-done.1, bf16[256,1280]{1,0:T(8,128)(2,1)S(1)} %collective-permute-done.7.refs_0_, bf16[256,1280]{1,0:T(8,128)(2,1)} %collective-permute-done.8.refs_1_, ...), custom_call_target="tpu_custom_call", output_to_operand_aliasing={{}: (0, {})} | custom-call | flops 10737418240 | bytes 29360128 | tf_op jit(solution)/shard_map/project/pallas_call | solution.py:149
  117.1 16.1 %attend.1 = bf16[32,64,1024]{2,1,0:T(8,128)(2,1)} custom-call(s32[16]{0:T(128)S(1)} %get-tuple-element.20.dest_ref, s32[16]{0:T(128)S(1)} %get-tuple-element.19.length_ref, f32[1024,1280]{1,0:T(8,128)} %project.3.total_ref, bf16[1024,2048]{1,0:T(8,128)(2,1)} %copy-done.2, f32[1,1280]{1,0:T(1,128)S(1)} %broadcast_in_dim.26.bias_ref, ...), custom_call_target="tpu_custom_call" | custom-call | flops 5368709120 | bytes 19922944 | tf_op jit(solution)/shard_map/attend/pallas_call | solution.py:252
  133.2 4.7 %all-to-all-start = ((bf16[32,64,1024]{2,1,0:T(8,128)(2,1)}), bf16[32,64,1024]{2,1,0:T(8,128)(2,1)}, u32[]{:S(2)}, u32[]{:S(2)}) async-start(bf16[32,64,1024]{2,1,0:T(8,128)(2,1)} %attend.1), calls=%async_computation | async-start | bytes 8388608 | tf_op jit(solution)/shard_map/all_to_all | solution.py:379
  139.7 50.5 %all-to-all-done.refs_0_.refs_1_.refs_2_.refs_3_ = bf16[32,64,1024]{2,1,0:T(8,128)(2,1)} async-done(((bf16[32,64,1024]{2,1,0:T(8,128)(2,1)}), bf16[32,64,1024]{2,1,0:T(8,128)(2,1)}, u32[]{:S(2)}, u32[]{:S(2)}) %all-to-all-start) | async-done | bytes 4194336 | tf_op jit(solution)/shard_map/all_to_all | solution.py:379
  190.2 4.5 %place.1 = (bf16[256,1024]{1,0:T(8,128)(2,1)}, bf16[256,1024]{1,0:T(8,128)(2,1)}, bf16[256,1024]{1,0:T(8,128)(2,1)}, bf16[256,1024]{1,0:T(8,128)(2,1)}) custom-call(s32[16]{0:T(128)} %reshape.58.source_ref, bf16[32,64,1024]{2,1,0:T(8,128)(2,1)} %all-to-all-done.refs_0_.refs_1_.refs_2_.refs_3_, ...), custom_call_target="tpu_custom_call" | custom-call | tf_op jit(solution)/shard_map/place/pallas_call | solution.py:293
  194.7 1.2 collective-permute-start.31
  195.9 2.5 %collective-permute-start.32 = (bf16[256,1024]{1,0:T(8,128)(2,1)}, bf16[256,1024]{1,0:T(8,128)(2,1)S(1)}, u32[]{:S(2)}, u32[]{:S(2)}) collective-permute-start(bf16[256,1024]{1,0:T(8,128)(2,1)} %get-tuple-element.17), channel_id=1, source_target_pairs={{0,2},{1,3},{2,0},{3,1},{4,6},{5,7},{6,4},{7,5},{8,10},{9,11},{10,... | collective-permute-start | bytes 1572872 | tf_op jit(solution)/shard_map/ppermute | solution.py:393
  198.3 1.1 collective-permute-start.33
  200.0 8.8 %collective-permute-done.31.refs_1_ = bf16[256,1024]{1,0:T(8,128)(2,1)S(1)} collective-permute-done((bf16[256,1024]{1,0:T(8,128)(2,1)}, bf16[256,1024]{1,0:T(8,128)(2,1)S(1)}, u32[]{:S(2)}, u32[]{:S(2)}) %collective-permute-start.31) | collective-permute-done | bytes 524320 | tf_op jit(solution)/shard_map/ppermute | solution.py:393
  208.8 12.2 %collective-permute-done.32.refs_2_ = bf16[256,1024]{1,0:T(8,128)(2,1)S(1)} collective-permute-done((bf16[256,1024]{1,0:T(8,128)(2,1)}, bf16[256,1024]{1,0:T(8,128)(2,1)S(1)}, u32[]{:S(2)}, u32[]{:S(2)}) %collective-permute-start.32) | collective-permute-done | bytes 524320 | tf_op jit(solution)/shard_map/ppermute | solution.py:393
  222.0 4.5 %join.1 = bf16[256,4096]{1,0:T(8,128)(2,1)} custom-call(s32[4]{0:T(128)} %and_select_fusion.1.order_ref, bf16[256,1024]{1,0:T(8,128)(2,1)} %get-tuple-element.15.refs_0_, bf16[256,1024]{1,0:T(8,128)(2,1)} %copy-done.31, bf16[256,1024]{1,0:T(8,128)(2,1)} %copy-done.32, bf16[256,1024]{1,0:T(8,128)(2,1)} %copy-done.33), custom_call_target="tpu_custom_call" | custom-call | tf_op jit(solution)/shard_map/join/pallas_call | solution.py:316
  (131 shorter events, 23.4 us)
Async XLA Ops:
  2.0 13.2 %collective-permute-start = (bf16[256,1280]{1,0:T(8,128)(2,1)S(1)}, bf16[256,1280]{1,0:T(8,128)(2,1)S(1)}, u32[]{:S(2)}, u32[]{:S(2)}) collective-permute-start(bf16[256,1280]{1,0:T(8,128)(2,1)S(1)} %constant_dynamic-update-slice_fusion.refs_0_), channel_id=1, source_target_pairs={{0,32},{4,12},{8,40},{12,20},{16,48},{20,28},{24,56},{28,4},{32,64... | collective-permute-start | bytes 1966088 | tf_op jit(solution)/shard_map/ppermute | solution.py:347
  4.5 25.6 %collective-permute-start.1 = (bf16[256,1280]{1,0:T(8,128)(2,1)S(1)}, bf16[256,1280]{1,0:T(8,128)(2,1)S(1)}, u32[]{:S(2)}, u32[]{:S(2)}) collective-permute-start(bf16[256,1280]{1,0:T(8,128)(2,1)S(1)} %constant_dynamic-update-slice_fusion.refs_0_), channel_id=1, source_target_pairs={{0,64},{4,20},{8,72},{12,28},{16,80},{20,4},{24,88},{28,12},{32,96... | collective-permute-start | bytes 1966088 | tf_op jit(solution)/shard_map/ppermute | solution.py:347
  7.8 22.8 %collective-permute-start.2 = (bf16[256,1280]{1,0:T(8,128)(2,1)S(1)}, bf16[256,1280]{1,0:T(8,128)(2,1)S(1)}, u32[]{:S(2)}, u32[]{:S(2)}) collective-permute-start(bf16[256,1280]{1,0:T(8,128)(2,1)S(1)} %constant_dynamic-update-slice_fusion.refs_0_), channel_id=1, source_target_pairs={{0,96},{4,28},{8,104},{12,4},{16,112},{20,12},{24,120},{28,20},{32... | collective-permute-start | bytes 1966088 | tf_op jit(solution)/shard_map/ppermute | solution.py:347
  8.6 22.1 %collective-permute-start.3 = (bf16[256,1280]{1,0:T(8,128)(2,1)S(1)}, bf16[256,1280]{1,0:T(8,128)(2,1)S(1)}, u32[]{:S(2)}, u32[]{:S(2)}) collective-permute-start(bf16[256,1280]{1,0:T(8,128)(2,1)S(1)} %constant_dynamic-update-slice_fusion.refs_0_), channel_id=1, source_target_pairs={{0,4},{4,0},{8,12},{12,8},{16,20},{20,16},{24,28},{28,24},{32,36},... | collective-permute-start | bytes 1966088 | tf_op jit(solution)/shard_map/ppermute | solution.py:353
  9.4 22.6 %collective-permute-start.7 = (bf16[256,1280]{1,0:T(8,128)(2,1)S(1)}, bf16[256,1280]{1,0:T(8,128)(2,1)S(1)}, u32[]{:S(2)}, u32[]{:S(2)}) collective-permute-start(bf16[256,1280]{1,0:T(8,128)(2,1)S(1)} %constant_dynamic-update-slice_fusion.refs_0_), channel_id=1, source_target_pairs={{0,8},{4,36},{8,16},{12,44},{16,24},{20,52},{24,0},{28,60},{32,40}... | collective-permute-start | bytes 1966088 | tf_op jit(solution)/shard_map/ppermute | solution.py:350
  15.2 17.3 %collective-permute-start.11 = (bf16[256,1280]{1,0:T(8,128)(2,1)S(1)}, bf16[256,1280]{1,0:T(8,128)(2,1)S(1)}, u32[]{:S(2)}, u32[]{:S(2)}) collective-permute-start(bf16[256,1280]{1,0:T(8,128)(2,1)S(1)} %constant_dynamic-update-slice_fusion.refs_0_), channel_id=1, source_target_pairs={{0,24},{4,100},{8,0},{12,108},{16,8},{20,116},{24,16},{28,124},{32... | collective-permute-start | bytes 1966088 | tf_op jit(solution)/shard_map/ppermute | solution.py:350
  32.0 11.0 %collective-permute-start.8 = (bf16[256,1280]{1,0:T(8,128)(2,1)S(1)}, bf16[256,1280]{1,0:T(8,128)(2,1)}, u32[]{:S(2)}, u32[]{:S(2)}) collective-permute-start(bf16[256,1280]{1,0:T(8,128)(2,1)S(1)} %collective-permute-done.refs_1_), channel_id=1, source_target_pairs={{0,8},{4,36},{8,16},{12,44},{16,24},{20,52},{24,0},{28,60},{32,40}... | collective-permute-start | bytes 1966088 | tf_op jit(solution)/shard_map/ppermute | solution.py:350
  32.5 11.3 %collective-permute-start.13 = (bf16[256,1280]{1,0:T(8,128)(2,1)S(1)}, bf16[256,1280]{1,0:T(8,128)(2,1)}, u32[]{:S(2)}, u32[]{:S(2)}) collective-permute-start(bf16[256,1280]{1,0:T(8,128)(2,1)S(1)} %collective-permute-done.1.refs_2_), channel_id=1, source_target_pairs={{0,24},{4,100},{8,0},{12,108},{16,8},{20,116},{24,16},{28,124},{32... | collective-permute-start | bytes 1966088 | tf_op jit(solution)/shard_map/ppermute | solution.py:350
  35.6 13.8 %collective-permute-start.14 = (bf16[256,1280]{1,0:T(8,128)(2,1)S(1)}, bf16[256,1280]{1,0:T(8,128)(2,1)}, u32[]{:S(2)}, u32[]{:S(2)}) collective-permute-start(bf16[256,1280]{1,0:T(8,128)(2,1)S(1)} %collective-permute-done.2.refs_3_), channel_id=1, source_target_pairs={{0,24},{4,100},{8,0},{12,108},{16,8},{20,116},{24,16},{28,124},{32... | collective-permute-start | bytes 1966088 | tf_op jit(solution)/shard_map/ppermute | solution.py:350
  37.1 14.5 %collective-permute-start.9 = (bf16[256,1280]{1,0:T(8,128)(2,1)S(1)}, bf16[256,1280]{1,0:T(8,128)(2,1)S(1)}, u32[]{:S(2)}, u32[]{:S(2)}) collective-permute-start(bf16[256,1280]{1,0:T(8,128)(2,1)S(1)} %collective-permute-done.1.refs_2_), channel_id=1, source_target_pairs={{0,8},{4,36},{8,16},{12,44},{16,24},{20,52},{24,0},{28,60},{32,40}... | collective-permute-start | bytes 1966088 | tf_op jit(solution)/shard_map/ppermute | solution.py:350
  38.7 18.4 %collective-permute-start.10 = (bf16[256,1280]{1,0:T(8,128)(2,1)S(1)}, bf16[256,1280]{1,0:T(8,128)(2,1)}, u32[]{:S(2)}, u32[]{:S(2)}) collective-permute-start(bf16[256,1280]{1,0:T(8,128)(2,1)S(1)} %collective-permute-done.2.refs_3_), channel_id=1, source_target_pairs={{0,8},{4,36},{8,16},{12,44},{16,24},{20,52},{24,0},{28,60},{32,40}... | collective-permute-start | bytes 1966088 | tf_op jit(solution)/shard_map/ppermute | solution.py:350
  43.1 15.7 %collective-permute-start.12 = (bf16[256,1280]{1,0:T(8,128)(2,1)S(1)}, bf16[256,1280]{1,0:T(8,128)(2,1)}, u32[]{:S(2)}, u32[]{:S(2)}) collective-permute-start(bf16[256,1280]{1,0:T(8,128)(2,1)S(1)} %collective-permute-done.refs_1_), channel_id=1, source_target_pairs={{0,24},{4,100},{8,0},{12,108},{16,8},{20,116},{24,16},{28,124},{32... | collective-permute-start | bytes 1966088 | tf_op jit(solution)/shard_map/ppermute | solution.py:350
  43.8 15.0 %collective-permute-start.15 = (bf16[256,1280]{1,0:T(8,128)(2,1)S(1)}, bf16[256,1280]{1,0:T(8,128)(2,1)S(1)}, u32[]{:S(2)}, u32[]{:S(2)}) collective-permute-start(bf16[256,1280]{1,0:T(8,128)(2,1)S(1)} %collective-permute-done.7.refs_0_), channel_id=1, source_target_pairs={{0,4},{4,0},{8,12},{12,8},{16,20},{20,16},{24,28},{28,24},{32,36},... | collective-permute-start | bytes 1966088 | tf_op jit(solution)/shard_map/ppermute | solution.py:353
  49.4 10.8 %collective-permute-start.19 = (bf16[256,1280]{1,0:T(8,128)(2,1)S(1)}, bf16[256,1280]{1,0:T(8,128)(2,1)S(1)}, u32[]{:S(2)}, u32[]{:S(2)}) collective-permute-start(bf16[256,1280]{1,0:T(8,128)(2,1)S(1)} %collective-permute-done.11.refs_4_), channel_id=1, source_target_pairs={{0,4},{4,0},{8,12},{12,8},{16,20},{20,16},{24,28},{28,24},{32,36},... | collective-permute-start | bytes 1966088 | tf_op jit(solution)/shard_map/ppermute | solution.py:353
  51.7 12.4 %collective-permute-start.23 = (bf16[256,1280]{1,0:T(8,128)(2,1)S(1)}, bf16[256,1280]{1,0:T(8,128)(2,1)S(1)}, u32[]{:S(2)}, u32[]{:S(2)}) collective-permute-start(bf16[256,1280]{1,0:T(8,128)(2,1)S(1)} %collective-permute-done.7.refs_0_), channel_id=1, source_target_pairs={{0,8},{4,36},{8,16},{12,44},{16,24},{20,52},{24,0},{28,60},{32,40}... | collective-permute-start | bytes 1966088 | tf_op jit(solution)/shard_map/ppermute | solution.py:350
  57.1 6.9 %collective-permute-start.16 = (bf16[256,1280]{1,0:T(8,128)(2,1)}, bf16[256,1280]{1,0:T(8,128)(2,1)S(1)}, u32[]{:S(2)}, u32[]{:S(2)}) collective-permute-start(bf16[256,1280]{1,0:T(8,128)(2,1)} %collective-permute-done.8.refs_1_), channel_id=1, source_target_pairs={{0,4},{4,0},{8,12},{12,8},{16,20},{20,16},{24,28},{28,24},{32,36},... | collective-permute-start | bytes 1966088 | tf_op jit(solution)/shard_map/ppermute | solution.py:353
  58.8 8.8 %collective-permute-start.21 = (bf16[256,1280]{1,0:T(8,128)(2,1)}, bf16[256,1280]{1,0:T(8,128)(2,1)S(1)}, u32[]{:S(2)}, u32[]{:S(2)}) collective-permute-start(bf16[256,1280]{1,0:T(8,128)(2,1)} %collective-permute-done.13.refs_6_), channel_id=1, source_target_pairs={{0,4},{4,0},{8,12},{12,8},{16,20},{20,16},{24,28},{28,24},{32,36},... | collective-permute-start | bytes 1966088 | tf_op jit(solution)/shard_map/ppermute | solution.py:353
  59.7 8.7 %collective-permute-start.22 = (bf16[256,1280]{1,0:T(8,128)(2,1)}, bf16[256,1280]{1,0:T(8,128)(2,1)S(1)}, u32[]{:S(2)}, u32[]{:S(2)}) collective-permute-start(bf16[256,1280]{1,0:T(8,128)(2,1)} %collective-permute-done.14.refs_7_), channel_id=1, source_target_pairs={{0,4},{4,0},{8,12},{12,8},{16,20},{20,16},{24,28},{28,24},{32,36},... | collective-permute-start | bytes 1966088 | tf_op jit(solution)/shard_map/ppermute | solution.py:353
  61.0 11.3 %collective-permute-start.17 = (bf16[256,1280]{1,0:T(8,128)(2,1)S(1)}, bf16[256,1280]{1,0:T(8,128)(2,1)S(1)}, u32[]{:S(2)}, u32[]{:S(2)}) collective-permute-start(bf16[256,1280]{1,0:T(8,128)(2,1)S(1)} %collective-permute-done.9.refs_2_), channel_id=1, source_target_pairs={{0,4},{4,0},{8,12},{12,8},{16,20},{20,16},{24,28},{28,24},{32,36},... | collective-permute-start | bytes 1966088 | tf_op jit(solution)/shard_map/ppermute | solution.py:353
  64.0 36.1 %collective-permute-start.24 = (bf16[256,1280]{1,0:T(8,128)(2,1)}, bf16[256,1280]{1,0:T(8,128)(2,1)}, u32[]{:S(2)}, u32[]{:S(2)}) collective-permute-start(bf16[256,1280]{1,0:T(8,128)(2,1)} %collective-permute-done.8.refs_1_), channel_id=1, source_target_pairs={{0,8},{4,36},{8,16},{12,44},{16,24},{20,52},{24,0},{28,60},{32,40}... | collective-permute-start | bytes 1966088 | tf_op jit(solution)/shard_map/ppermute | solution.py:350
  64.9 35.5 %collective-permute-start.25 = (bf16[256,1280]{1,0:T(8,128)(2,1)}, bf16[256,1280]{1,0:T(8,128)(2,1)}, u32[]{:S(2)}, u32[]{:S(2)}) collective-permute-start(bf16[256,1280]{1,0:T(8,128)(2,1)} %collective-permute-done.13.refs_6_), channel_id=1, source_target_pairs={{0,24},{4,100},{8,0},{12,108},{16,8},{20,116},{24,16},{28,124},{32... | collective-permute-start | bytes 1966088 | tf_op jit(solution)/shard_map/ppermute | solution.py:350
  68.4 32.3 %collective-permute-start.26 = (bf16[256,1280]{1,0:T(8,128)(2,1)}, bf16[256,1280]{1,0:T(8,128)(2,1)}, u32[]{:S(2)}, u32[]{:S(2)}) collective-permute-start(bf16[256,1280]{1,0:T(8,128)(2,1)} %collective-permute-done.14.refs_7_), channel_id=1, source_target_pairs={{0,24},{4,100},{8,0},{12,108},{16,8},{20,116},{24,16},{28,124},{32... | collective-permute-start | bytes 1966088 | tf_op jit(solution)/shard_map/ppermute | solution.py:350
  69.2 30.3 %collective-permute-start.18 = (bf16[256,1280]{1,0:T(8,128)(2,1)}, bf16[256,1280]{1,0:T(8,128)(2,1)}, u32[]{:S(2)}, u32[]{:S(2)}) collective-permute-start(bf16[256,1280]{1,0:T(8,128)(2,1)} %collective-permute-done.10.refs_3_), channel_id=1, source_target_pairs={{0,4},{4,0},{8,12},{12,8},{16,20},{20,16},{24,28},{28,24},{32,36},... | collective-permute-start | bytes 1966088 | tf_op jit(solution)/shard_map/ppermute | solution.py:353
  73.1 27.8 %collective-permute-start.20 = (bf16[256,1280]{1,0:T(8,128)(2,1)}, bf16[256,1280]{1,0:T(8,128)(2,1)}, u32[]{:S(2)}, u32[]{:S(2)}) collective-permute-start(bf16[256,1280]{1,0:T(8,128)(2,1)} %collective-permute-done.12.refs_5_), channel_id=1, source_target_pairs={{0,4},{4,0},{8,12},{12,8},{16,20},{20,16},{24,28},{28,24},{32,36},... | collective-permute-start | bytes 1966088 | tf_op jit(solution)/shard_map/ppermute | solution.py:353
  99.6 17.5 %collective-permute-start.27 = (bf16[256,1280]{1,0:T(8,128)(2,1)S(1)}, bf16[256,1280]{1,0:T(8,128)(2,1)S(1)}, u32[]{:S(2)}, u32[]{:S(2)}) collective-permute-start(bf16[256,1280]{1,0:T(8,128)(2,1)S(1)} %copy-done.14), channel_id=1, source_target_pairs={{0,4},{4,0},{8,12},{12,8},{16,20},{20,16},{24,28},{28,24},{32,36},... | collective-permute-start | bytes 1966088 | tf_op jit(solution)/shard_map/ppermute | solution.py:353
  100.1 16.9 %collective-permute-start.28 = (bf16[256,1280]{1,0:T(8,128)(2,1)}, bf16[256,1280]{1,0:T(8,128)(2,1)S(1)}, u32[]{:S(2)}, u32[]{:S(2)}) collective-permute-start(bf16[256,1280]{1,0:T(8,128)(2,1)} %collective-permute-done.24.refs_1_), channel_id=1, source_target_pairs={{0,4},{4,0},{8,12},{12,8},{16,20},{20,16},{24,28},{28,24},{32,36},... | collective-permute-start | bytes 1966088 | tf_op jit(solution)/shard_map/ppermute | solution.py:353
  100.4 16.7 %collective-permute-start.29 = (bf16[256,1280]{1,0:T(8,128)(2,1)}, bf16[256,1280]{1,0:T(8,128)(2,1)S(1)}, u32[]{:S(2)}, u32[]{:S(2)}) collective-permute-start(bf16[256,1280]{1,0:T(8,128)(2,1)} %collective-permute-done.25.refs_2_), channel_id=1, source_target_pairs={{0,4},{4,0},{8,12},{12,8},{16,20},{20,16},{24,28},{28,24},{32,36},... | collective-permute-start | bytes 1966088 | tf_op jit(solution)/shard_map/ppermute | solution.py:353
  100.7 16.4 %collective-permute-start.30 = (bf16[256,1280]{1,0:T(8,128)(2,1)}, bf16[256,1280]{1,0:T(8,128)(2,1)S(1)}, u32[]{:S(2)}, u32[]{:S(2)}) collective-permute-start(bf16[256,1280]{1,0:T(8,128)(2,1)} %collective-permute-done.26.refs_3_), channel_id=1, source_target_pairs={{0,4},{4,0},{8,12},{12,8},{16,20},{20,16},{24,28},{28,24},{32,36},... | collective-permute-start | bytes 1966088 | tf_op jit(solution)/shard_map/ppermute | solution.py:353
  133.2 57.0 %all-to-all-start = ((bf16[32,64,1024]{2,1,0:T(8,128)(2,1)}), bf16[32,64,1024]{2,1,0:T(8,128)(2,1)}, u32[]{:S(2)}, u32[]{:S(2)}) async-start(bf16[32,64,1024]{2,1,0:T(8,128)(2,1)} %attend.1), calls=%async_computation | async-start | bytes 8388608 | tf_op jit(solution)/shard_map/all_to_all | solution.py:379
  194.7 14.1 %collective-permute-start.31 = (bf16[256,1024]{1,0:T(8,128)(2,1)}, bf16[256,1024]{1,0:T(8,128)(2,1)S(1)}, u32[]{:S(2)}, u32[]{:S(2)}) collective-permute-start(bf16[256,1024]{1,0:T(8,128)(2,1)} %get-tuple-element.16), channel_id=1, source_target_pairs={{0,1},{1,2},{2,3},{3,0},{4,5},{5,6},{6,7},{7,4},{8,9},{9,10},{10,1... | collective-permute-start | bytes 1572872 | tf_op jit(solution)/shard_map/ppermute | solution.py:393
  195.9 25.1 %collective-permute-start.32 = (bf16[256,1024]{1,0:T(8,128)(2,1)}, bf16[256,1024]{1,0:T(8,128)(2,1)S(1)}, u32[]{:S(2)}, u32[]{:S(2)}) collective-permute-start(bf16[256,1024]{1,0:T(8,128)(2,1)} %get-tuple-element.17), channel_id=1, source_target_pairs={{0,2},{1,3},{2,0},{3,1},{4,6},{5,7},{6,4},{7,5},{8,10},{9,11},{10,... | collective-permute-start | bytes 1572872 | tf_op jit(solution)/shard_map/ppermute | solution.py:393
  198.3 22.6 %collective-permute-start.33 = (bf16[256,1024]{1,0:T(8,128)(2,1)}, bf16[256,1024]{1,0:T(8,128)(2,1)S(1)}, u32[]{:S(2)}, u32[]{:S(2)}) collective-permute-start(bf16[256,1024]{1,0:T(8,128)(2,1)} %get-tuple-element.18), channel_id=1, source_target_pairs={{0,3},{1,0},{2,1},{3,2},{4,7},{5,4},{6,5},{7,6},{8,11},{9,8},{10,9... | collective-permute-start | bytes 1572872 | tf_op jit(solution)/shard_map/ppermute | solution.py:393
  (39 other events, 250.5 us)

commit v2 on v1

--- a/solution.py
+++ b/solution.py
@@ -10,6 +10,7 @@
 GROUP = 64
 SIDE = 4
 MIB = 1024 * 1024
+PIECES = (6, 20, 6)
 
 rope_base = 1000000.0
 norm_epsilon = 1e-06
@@ -53,31 +54,39 @@
 
 
 def source_table():
-    table = np.zeros((32, 32), np.int32)
+    table = np.zeros((32, 64), np.int32)
     for y in range(SIDE):
         for z in range(SIDE):
             for core in range(2):
 
-                def pieces(c, second):
+                def blocks(c, offsets):
                     found = []
-                    for first in range(SIDE):
-                        if c == 0:
-                            found.append(device_index(y - first, z - second, c))
-                        else:
-                            found.append(device_index(y - second, z - first, c))
+                    for a, b, halves in offsets:
+                        held = (
+                            device_index(y - a, z - b, c)
+                            if c == 0
+                            else device_index(y - b, z - a, c)
+                        )
+                        found += [2 * held + half for half in halves]
                     return found
 
+                both, low, high = (0, 1), (0,), (1,)
+                near = [(1, 0, both), (3, 0, both), (2, 0, both)]
+                ahead = [(1, 1, both), (3, 1, both), (2, 1, both), (0, 2, low)]
+                behind = [(1, 3, both), (3, 3, both), (2, 3, both), (0, 2, high)]
+                far = [(1, 2, both), (2, 2, low), (3, 2, both), (2, 2, high)]
                 other = 1 - core
-                order = pieces(core, 0) + pieces(other, 0)
-                order += pieces(core, 1) + pieces(core, 3) + pieces(other, 1) + pieces(other, 3)
-                order += pieces(core, 2) + pieces(other, 2)
+                order = blocks(core, [(0, 0, both)] + near + [(0, 1, both), (0, 3, both)])
+                order += blocks(other, near + [(0, 1, both), (0, 3, both), (0, 0, both)])
+                order += blocks(core, ahead + behind) + blocks(other, ahead + behind)
+                order += blocks(core, far) + blocks(other, far)
                 table[device_index(y, z, core)] = order
     return table
 
 
 def norm_kernel(order_ref, hidden_ref, gain_ref, early_ref, middle_ref, late_ref):
     features = hidden_ref.shape[1]
-    depth = features // 32
+    depth = features // order_ref.shape[0]
     widened = hidden_ref[...].astype(jnp.float32)
     mean_square = jnp.sum(widened * widened, -1, keepdims=True) * (1.0 / features)
     scale = lax.rsqrt(mean_square + norm_epsilon)
@@ -153,7 +162,7 @@
         out_specs=block,
         out_shape=jax.ShapeDtypeStruct((rows, columns), jnp.float32),
         input_output_aliases={} if total is None else {0: 0},
-        compiler_params=pltpu.CompilerParams(vmem_limit_bytes=40 * MIB),
+        compiler_params=pltpu.CompilerParams(vmem_limit_bytes=44 * MIB),
         cost_estimate=matmul_cost(rows, depth, columns, 1 if total is None else 2),
         name="project",
     )(*([] if total is None else [total]), x, *pieces)
@@ -354,24 +363,34 @@
 
     weights = jnp.concatenate([w_query, w_keyval], 1)
     bias = jnp.concatenate([query_bias, keyval_bias])[None]
-    near = [weights, first(weights, 1), first(weights, 2), first(weights, -1)]
-    ahead = [second(piece, 1) for piece in near]
-    behind = [second(piece, -1) for piece in near]
-    far = [second(ahead[0], 1), second(ahead[1], 1), second(behind[2], -1), second(behind[3], -1)]
-    early = near + [swap(piece) for piece in near]
-    middle = ahead + behind + [swap(piece) for piece in ahead + behind]
+    rows_held = weights.shape[0]
+    half = rows_held // 2
+    order = lax.dynamic_index_in_dim(jnp.asarray(source_table()), own, 0, keepdims=False)
+    near = [first(weights, 1), first(weights, -1), first(weights, 2)]
+    own_ahead, own_behind = second(weights, 1), second(weights, -1)
+    x_early, x_middle, x_late = norm(
+        order, hidden_states, norm_gain[None], [count * rows_held for count in PIECES]
+    )
+
+    near, own_ahead, own_behind, x_early = lax.optimization_barrier(
+        (near, own_ahead, own_behind, x_early)
+    )
+    to_ahead = jnp.concatenate([*near, own_ahead[:half]])
+    to_behind = jnp.concatenate([*near, own_behind[half:]])
+    ahead, behind = second(to_ahead, 1), second(to_behind, -1)
+    rest = jnp.concatenate([own_ahead[half:], own_behind, weights])
+    middle = [swap(to_ahead), swap(rest)]
+    total = project(None, x_early, [weights, *near, own_ahead, own_behind])
+
+    ahead, behind, middle, total = lax.optimization_barrier((ahead, behind, middle, total))
+    far = [
+        second(jnp.concatenate([ahead[:rows_held], ahead[2 * rows_held : -half * 2]]), 1),
+        second(jnp.concatenate([behind[rows_held : 2 * rows_held], behind[-half * 2 : -half]]), -1),
+    ]
+    middle += [ahead, behind, swap(ahead), swap(behind)]
+    total = project(total, x_middle, middle)
+    far, total = lax.optimization_barrier((far, total))
     late = far + [swap(piece) for piece in far]
-
-    depth = weights.shape[0]
-    order = lax.dynamic_index_in_dim(jnp.asarray(source_table()), own, 0, keepdims=False)
-    x_early, x_middle, x_late = norm(
-        order,
-        hidden_states,
-        norm_gain[None],
-        [len(early) * depth, len(middle) * depth, len(late) * depth],
-    )
-    total = project(None, x_early, early)
-    total = project(total, x_middle, middle)
 
     own_dest = lax.dynamic_index_in_dim(group_dest, own, 0, keepdims=False)
     own_length = lax.dynamic_index_in_dim(group_length, own, 0, keepdims=False)

time: 229 us -> 207 us (0.904)
  starting transfers between devices: 41.6 us -> 29.8 us
  local copies, waits for them, and re-layouts: 20.2 us -> 12.7 us
  waiting for transfers between devices: 102 us -> 97.5 us
    ppermute x3, waiting for transfers between devices: 16.4 us -> 1.13 us  [first(): return lax.ppermute(piece, 'dp', shift_pairs(by, 0))]
    ppermute x16 -> x6, waiting for transfers between devices: 0.04 us -> 8.45 us  [swap(): return lax.ppermute(piece, 'dp', swap_pairs())]
    ppermute x16 -> x6, starting transfers between devices: 13.7 us -> 5.37 us  [swap(): return lax.ppermute(piece, 'dp', swap_pairs())]
    unnamed x73 -> x31, local copies, waits for them, and re-layouts: 16.4 us -> 8.33 us
    ppermute x12 -> x6, starting transfers between devices: 11.9 us -> 7.02 us  [second(): return lax.ppermute(piece, 'dp', shift_pairs(0, by))]
    ppermute x12 -> x6, waiting for transfers between devices: 13.7 us -> 16.6 us  [second(): return lax.ppermute(piece, 'dp', shift_pairs(0, by))]
    pallas_call x1, Pallas kernels: 16.1 us -> 13.3 us  [attend(): pl.pallas_call(attend_kernel, grid_spec=pltpu.PrefetchScalarGridSpec(num_...]
    pallas_call x2, Pallas kernels: 23.3 us -> 26 us  [project(): pl.pallas_call(first_kernel if total is None else add_kernel, grid=(rows...]
  transfers between devices with their start and end apart: 35 -> 19, of which waited for: 9 -> 9; matrix products, arithmetic and copies ran while one was open for 2% -> 2% of each run, Pallas kernels for 16% -> 19%
where the time goes in v2:
time: 207 us; the launch traced here: 204 us
  waiting for transfers between devices  97.5 us (47%)
  Pallas kernels  61.1 us (30%)
  starting transfers between devices  29.8 us (14%)
  local copies, waits for them, and re-layouts  12.7 us (6%)
  other arithmetic  2.82 us (1%)
    all_to_all x1, waiting for transfers between devices, per_device(): lax.all_to_all(sent, 'dp', split_axis=0, concat_axis=0, tiled=True)  50.5 us
    pallas_call x2, Pallas kernels, project(): pl.pallas_call(first_kernel if total is None else add_kernel, grid=(rows...  26 us
    ppermute x3, waiting for transfers between devices, per_device(): lax.ppermute(parts[k], 'mp', [(i, (i + k) % planes) for i in range(planes)])  20.9 us
    ppermute x6, waiting for transfers between devices, second(): return lax.ppermute(piece, 'dp', shift_pairs(0, by))  16.6 us
    pallas_call x1, Pallas kernels, attend(): pl.pallas_call(attend_kernel, grid_spec=pltpu.PrefetchScalarGridSpec(num_...  13.3 us
    pallas_call x1, Pallas kernels, norm(): pl.pallas_call(norm_kernel, grid_spec=pltpu.PrefetchScalarGridSpec(num_sc...  12.8 us
    ppermute x6, waiting for transfers between devices, swap(): return lax.ppermute(piece, 'dp', swap_pairs())  8.45 us
    unnamed x31, local copies, waits for them, and re-layouts  8.33 us
  transfers between devices with their start and end apart: 19, of which 9 were waited for; matrix products, arithmetic and copies ran while one was open for 2% of the time, Pallas kernels for 19%

profile of v2, /device:TPU:1, one launch (start us, length us, event | category | flops | bytes accessed | tf_op | source)
XLA Modules:
  0.0 204.1 jit_solution(5125847871461952301)
XLA Ops:
  2.0 2.5 %collective-permute-start = (bf16[256,1280]{1,0:T(8,128)(2,1)S(1)}, bf16[256,1280]{1,0:T(8,128)(2,1)S(1)}, u32[]{:S(2)}, u32[]{:S(2)}) collective-permute-start(bf16[256,1280]{1,0:T(8,128)(2,1)S(1)} %constant_dynamic-update-slice_fusion.refs_0_), channel_id=1, source_target_pairs={{0,32},{4,12},{8,40},{12,20},{16,48},{20,28},{24,56},{28,4},{32,64... | collective-permute-start | bytes 1966088 | tf_op jit(solution)/shard_map/ppermute | solution.py:356
  4.5 2.2 %collective-permute-start.1 = (bf16[256,1280]{1,0:T(8,128)(2,1)S(1)}, bf16[256,1280]{1,0:T(8,128)(2,1)S(1)}, u32[]{:S(2)}, u32[]{:S(2)}) collective-permute-start(bf16[256,1280]{1,0:T(8,128)(2,1)S(1)} %constant_dynamic-update-slice_fusion.refs_0_), channel_id=1, source_target_pairs={{0,96},{4,28},{8,104},{12,4},{16,112},{20,12},{24,120},{28,20},{32... | collective-permute-start | bytes 1966088 | tf_op jit(solution)/shard_map/ppermute | solution.py:356
  6.7 1.2 collective-permute-start.2
  8.0 1.3 collective-permute-start.3
  9.3 1.4 collective-permute-start.4
  12.1 12.8 %norm.1 = (bf16[1024,1536]{1,0:T(8,128)(2,1)S(1)}, bf16[1024,5120]{1,0:T(8,128)(2,1)S(1)}, bf16[1024,1536]{1,0:T(8,128)(2,1)S(1)}) custom-call(s32[64]{0:T(128)S(1)} %fusion.3.order_ref, bf16[1024,8192]{1,0:T(8,128)(2,1)} %hidden_ref.1, f32[1,8192]{1,0:T(1,128)S(1)} %bitcast.5), custom_call_target="tpu_custom_call" | custom-call | flops 50331648 | bytes 33554432 | tf_op jit(solution)/shard_map/norm/pallas_call | solution.py:106
  25.0 4.0 %copy-done.4 = bf16[1024,5120]{1,0:T(8,128)(2,1)} copy-done((bf16[1024,5120]{1,0:T(8,128)(2,1)}, bf16[1024,5120]{1,0:T(8,128)(2,1)S(1)}, u32[]{:S(2)}) %copy-start.4) | copy-done | bytes 10485784
  29.0 1.1 collective-permute-done.2.refs_3_
  30.2 1.1 fusion.7
  31.3 1.6 pad_maximum_fusion.2
  33.9 1.7 collective-permute-start.6
  35.6 2.1 %collective-permute-start.7 = (bf16[896,1280]{1,0:T(8,128)(2,1)S(1)}, bf16[896,1280]{1,0:T(8,128)(2,1)S(1)}, u32[]{:S(2)}, u32[]{:S(2)}) collective-permute-start(bf16[896,1280]{1,0:T(8,128)(2,1)S(1)} %get-tuple-element.48), channel_id=1, source_target_pairs={{0,4},{4,0},{8,12},{12,8},{16,20},{20,16},{24,28},{28,24},{32,36},... | collective-permute-start | bytes 6881288 | tf_op jit(solution)/shard_map/ppermute | solution.py:362
  37.9 7.0 %project.2.total_ref = f32[1024,1280]{1,0:T(8,128)} custom-call(bf16[1024,1536]{1,0:T(8,128)(2,1)S(1)} %get-tuple-element.32.x_ref, bf16[256,1280]{1,0:T(8,128)(2,1)S(1)} %constant_dynamic-update-slice_fusion.refs_0_, bf16[256,1280]{1,0:T(8,128)(2,1)S(1)} %collective-permute-done.refs_1_, bf16[256,1280]{1,0:T(8,128)(2,1)S(1)} %collective-permute-done.1.refs_2_, ...), custom_call_target="tpu_custom_call" | custom-call | flops 4026531840 | bytes 12320768 | tf_op jit(solution)/shard_map/project/pallas_call | solution.py:158
  44.9 16.6 %collective-permute-done.5.refs_2_ = bf16[896,1280]{1,0:T(8,128)(2,1)S(1)} collective-permute-done((bf16[896,1280]{1,0:T(8,128)(2,1)S(1)}, bf16[896,1280]{1,0:T(8,128)(2,1)S(1)}, u32[]{:S(2)}, u32[]{:S(2)}) %collective-permute-start.5) | collective-permute-done | bytes 2293792 | tf_op jit(solution)/shard_map/ppermute | solution.py:359
  61.4 2.4 %collective-permute-start.11 = (bf16[896,1280]{1,0:T(8,128)(2,1)S(1)}, bf16[896,1280]{1,0:T(8,128)(2,1)S(1)}, u32[]{:S(2)}, u32[]{:S(2)}) collective-permute-start(bf16[896,1280]{1,0:T(8,128)(2,1)S(1)} %collective-permute-done.5.refs_2_), channel_id=1, source_target_pairs={{0,4},{4,0},{8,12},{12,8},{16,20},{20,16},{24,28},{28,24},{32,36},... | collective-permute-start | bytes 6881288 | tf_op jit(solution)/shard_map/ppermute | solution.py:362
  64.1 1.5 collective-permute-start.10
  65.8 2.1 %collective-permute-done.11.refs_4_ = bf16[896,1280]{1,0:T(8,128)(2,1)S(1)} collective-permute-done((bf16[896,1280]{1,0:T(8,128)(2,1)S(1)}, bf16[896,1280]{1,0:T(8,128)(2,1)S(1)}, u32[]{:S(2)}, u32[]{:S(2)}) %collective-permute-start.11) | collective-permute-done | bytes 2293792 | tf_op jit(solution)/shard_map/ppermute | solution.py:362
  67.9 3.3 %collective-permute-done.12.refs_5_ = bf16[896,1280]{1,0:T(8,128)(2,1)S(1)} collective-permute-done((bf16[896,1280]{1,0:T(8,128)(2,1)S(1)}, bf16[896,1280]{1,0:T(8,128)(2,1)S(1)}, u32[]{:S(2)}, u32[]{:S(2)}) %collective-permute-start.12) | collective-permute-done | bytes 2293792 | tf_op jit(solution)/shard_map/ppermute | solution.py:362
  71.2 1.4 copy-done.14
  72.6 19.0 %project.3.total_ref = f32[1024,1280]{1,0:T(8,128)} custom-call(f32[1024,1280]{1,0:T(8,128)} %project.2.total_ref, bf16[1024,5120]{1,0:T(8,128)(2,1)} %copy-done.4, bf16[896,1280]{1,0:T(8,128)(2,1)S(1)} %collective-permute-done.7.refs_0_, bf16[640,1280]{1,0:T(8,128)(2,1)S(1)} %collective-permute-done.8.refs_1_, ...), custom_call_target="tpu_custom_call", output_to_operand_aliasing={{}: (0, {})} | custom-call | flops 13421772800 | bytes 34078720 | tf_op jit(solution)/shard_map/project/pallas_call | solution.py:158
  92.6 1.7 collective-permute-done.13.refs_2_
  94.3 1.4 collective-permute-done.14.refs_3_
  95.7 13.3 %attend.1 = bf16[32,64,1024]{2,1,0:T(8,128)(2,1)} custom-call(s32[16]{0:T(128)S(1)} %get-tuple-element.52.dest_ref, s32[16]{0:T(128)S(1)} %get-tuple-element.51.length_ref, f32[1024,1280]{1,0:T(8,128)} %project.3.total_ref, bf16[1024,1536]{1,0:T(8,128)(2,1)} %copy-done, f32[1,1280]{1,0:T(1,128)S(1)} %broadcast_in_dim.26.bias_ref, f32[256,128]{1,0:T(8,128)S(1)} %copy-done.1, ...), custom_call_target="tpu_custom_call" | custom-call | flops 4026531840 | bytes 17563648 | tf_op jit(solution)/shard_map/attend/pallas_call | solution.py:261
  109.0 6.7 %all-to-all-start = ((bf16[32,64,1024]{2,1,0:T(8,128)(2,1)}), bf16[32,64,1024]{2,1,0:T(8,128)(2,1)}, u32[]{:S(2)}, u32[]{:S(2)}) async-start(bf16[32,64,1024]{2,1,0:T(8,128)(2,1)} %attend.1), calls=%async_computation | async-start | bytes 8388608 | tf_op jit(solution)/shard_map/all_to_all | solution.py:398
  117.4 50.5 %all-to-all-done.refs_0_.refs_1_.refs_2_.refs_3_ = bf16[32,64,1024]{2,1,0:T(8,128)(2,1)} async-done(((bf16[32,64,1024]{2,1,0:T(8,128)(2,1)}), bf16[32,64,1024]{2,1,0:T(8,128)(2,1)}, u32[]{:S(2)}, u32[]{:S(2)}) %all-to-all-start) | async-done | bytes 4194336 | tf_op jit(solution)/shard_map/all_to_all | solution.py:398
  167.9 4.5 %place.1 = (bf16[256,1024]{1,0:T(8,128)(2,1)}, bf16[256,1024]{1,0:T(8,128)(2,1)}, bf16[256,1024]{1,0:T(8,128)(2,1)}, bf16[256,1024]{1,0:T(8,128)(2,1)}) custom-call(s32[16]{0:T(128)} %reshape.58.source_ref, bf16[32,64,1024]{2,1,0:T(8,128)(2,1)} %all-to-all-done.refs_0_.refs_1_.refs_2_.refs_3_, ...), custom_call_target="tpu_custom_call" | custom-call | tf_op jit(solution)/shard_map/place/pallas_call | solution.py:302
  172.4 1.2 collective-permute-start.15
  173.6 2.4 %collective-permute-start.16 = (bf16[256,1024]{1,0:T(8,128)(2,1)}, bf16[256,1024]{1,0:T(8,128)(2,1)S(1)}, u32[]{:S(2)}, u32[]{:S(2)}) collective-permute-start(bf16[256,1024]{1,0:T(8,128)(2,1)} %get-tuple-element.45), channel_id=1, source_target_pairs={{0,2},{1,3},{2,0},{3,1},{4,6},{5,7},{6,4},{7,5},{8,10},{9,11},{10,... | collective-permute-start | bytes 1572872 | tf_op jit(solution)/shard_map/ppermute | solution.py:412
  176.0 1.2 collective-permute-start.17
  177.7 8.6 %collective-permute-done.15.refs_1_ = bf16[256,1024]{1,0:T(8,128)(2,1)S(1)} collective-permute-done((bf16[256,1024]{1,0:T(8,128)(2,1)}, bf16[256,1024]{1,0:T(8,128)(2,1)S(1)}, u32[]{:S(2)}, u32[]{:S(2)}) %collective-permute-start.15) | collective-permute-done | bytes 524320 | tf_op jit(solution)/shard_map/ppermute | solution.py:412
  186.4 12.2 %collective-permute-done.16.refs_2_ = bf16[256,1024]{1,0:T(8,128)(2,1)S(1)} collective-permute-done((bf16[256,1024]{1,0:T(8,128)(2,1)}, bf16[256,1024]{1,0:T(8,128)(2,1)S(1)}, u32[]{:S(2)}, u32[]{:S(2)}) %collective-permute-start.16) | collective-permute-done | bytes 524320 | tf_op jit(solution)/shard_map/ppermute | solution.py:412
  199.6 4.5 %join.1 = bf16[256,4096]{1,0:T(8,128)(2,1)} custom-call(s32[4]{0:T(128)} %and_select_fusion.1.order_ref, bf16[256,1024]{1,0:T(8,128)(2,1)} %get-tuple-element.43.refs_0_, bf16[256,1024]{1,0:T(8,128)(2,1)} %copy-done.5, bf16[256,1024]{1,0:T(8,128)(2,1)} %copy-done.6, bf16[256,1024]{1,0:T(8,128)(2,1)} %copy-done.7), custom_call_target="tpu_custom_call" | custom-call | tf_op jit(solution)/shard_map/join/pallas_call | solution.py:325
  (67 shorter events, 9.3 us)
Async XLA Ops:
  2.0 27.0 %collective-permute-start = (bf16[256,1280]{1,0:T(8,128)(2,1)S(1)}, bf16[256,1280]{1,0:T(8,128)(2,1)S(1)}, u32[]{:S(2)}, u32[]{:S(2)}) collective-permute-start(bf16[256,1280]{1,0:T(8,128)(2,1)S(1)} %constant_dynamic-update-slice_fusion.refs_0_), channel_id=1, source_target_pairs={{0,32},{4,12},{8,40},{12,20},{16,48},{20,28},{24,56},{28,4},{32,64... | collective-permute-start | bytes 1966088 | tf_op jit(solution)/shard_map/ppermute | solution.py:356
  4.5 24.5 %collective-permute-start.1 = (bf16[256,1280]{1,0:T(8,128)(2,1)S(1)}, bf16[256,1280]{1,0:T(8,128)(2,1)S(1)}, u32[]{:S(2)}, u32[]{:S(2)}) collective-permute-start(bf16[256,1280]{1,0:T(8,128)(2,1)S(1)} %constant_dynamic-update-slice_fusion.refs_0_), channel_id=1, source_target_pairs={{0,96},{4,28},{8,104},{12,4},{16,112},{20,12},{24,120},{28,20},{32... | collective-permute-start | bytes 1966088 | tf_op jit(solution)/shard_map/ppermute | solution.py:356
  6.7 23.4 %collective-permute-start.2 = (bf16[256,1280]{1,0:T(8,128)(2,1)S(1)}, bf16[256,1280]{1,0:T(8,128)(2,1)S(1)}, u32[]{:S(2)}, u32[]{:S(2)}) collective-permute-start(bf16[256,1280]{1,0:T(8,128)(2,1)S(1)} %constant_dynamic-update-slice_fusion.refs_0_), channel_id=1, source_target_pairs={{0,64},{4,20},{8,72},{12,28},{16,80},{20,4},{24,88},{28,12},{32,96... | collective-permute-start | bytes 1966088 | tf_op jit(solution)/shard_map/ppermute | solution.py:356
  8.0 22.2 %collective-permute-start.3 = (bf16[256,1280]{1,0:T(8,128)(2,1)S(1)}, bf16[256,1280]{1,0:T(8,128)(2,1)}, u32[]{:S(2)}, u32[]{:S(2)}) collective-permute-start(bf16[256,1280]{1,0:T(8,128)(2,1)S(1)} %constant_dynamic-update-slice_fusion.refs_0_), channel_id=1, source_target_pairs={{0,8},{4,36},{8,16},{12,44},{16,24},{20,52},{24,0},{28,60},{32,40}... | collective-permute-start | bytes 1966088 | tf_op jit(solution)/shard_map/ppermute | solution.py:359
  9.3 20.9 %collective-permute-start.4 = (bf16[256,1280]{1,0:T(8,128)(2,1)S(1)}, bf16[256,1280]{1,0:T(8,128)(2,1)S(1)}, u32[]{:S(2)}, u32[]{:S(2)}) collective-permute-start(bf16[256,1280]{1,0:T(8,128)(2,1)S(1)} %constant_dynamic-update-slice_fusion.refs_0_), channel_id=1, source_target_pairs={{0,24},{4,100},{8,0},{12,108},{16,8},{20,116},{24,16},{28,124},{32... | collective-permute-start | bytes 1966088 | tf_op jit(solution)/shard_map/ppermute | solution.py:359
  25.0 4.0 %copy-start.4 = (bf16[1024,5120]{1,0:T(8,128)(2,1)}, bf16[1024,5120]{1,0:T(8,128)(2,1)S(1)}, u32[]{:S(2)}) copy-start(bf16[1024,5120]{1,0:T(8,128)(2,1)S(1)} %get-tuple-element.36.x_ref) | copy-start | bytes 31457284
  29.0 3.9 %copy-start = (bf16[1024,1536]{1,0:T(8,128)(2,1)}, bf16[1024,1536]{1,0:T(8,128)(2,1)S(1)}, u32[]{:S(2)}) copy-start(bf16[1024,1536]{1,0:T(8,128)(2,1)S(1)} %get-tuple-element.40.x_ref) | copy-start | bytes 9437188
  32.9 28.5 %collective-permute-start.5 = (bf16[896,1280]{1,0:T(8,128)(2,1)S(1)}, bf16[896,1280]{1,0:T(8,128)(2,1)S(1)}, u32[]{:S(2)}, u32[]{:S(2)}) collective-permute-start(bf16[896,1280]{1,0:T(8,128)(2,1)S(1)} %get-tuple-element.48), channel_id=1, source_target_pairs={{0,8},{4,36},{8,16},{12,44},{16,24},{20,52},{24,0},{28,60},{32,40}... | collective-permute-start | bytes 6881288 | tf_op jit(solution)/shard_map/ppermute | solution.py:359
  33.9 27.5 %collective-permute-start.6 = (bf16[896,1280]{1,0:T(8,128)(2,1)}, bf16[896,1280]{1,0:T(8,128)(2,1)S(1)}, u32[]{:S(2)}, u32[]{:S(2)}) collective-permute-start(bf16[896,1280]{1,0:T(8,128)(2,1)} %get-tuple-element.47), channel_id=1, source_target_pairs={{0,24},{4,100},{8,0},{12,108},{16,8},{20,116},{24,16},{28,124},{32... | collective-permute-start | bytes 6881288 | tf_op jit(solution)/shard_map/ppermute | solution.py:359
  35.6 25.8 %collective-permute-start.7 = (bf16[896,1280]{1,0:T(8,128)(2,1)S(1)}, bf16[896,1280]{1,0:T(8,128)(2,1)S(1)}, u32[]{:S(2)}, u32[]{:S(2)}) collective-permute-start(bf16[896,1280]{1,0:T(8,128)(2,1)S(1)} %get-tuple-element.48), channel_id=1, source_target_pairs={{0,4},{4,0},{8,12},{12,8},{16,20},{20,16},{24,28},{28,24},{32,36},... | collective-permute-start | bytes 6881288 | tf_op jit(solution)/shard_map/ppermute | solution.py:362
  37.8 7.1 %collective-permute-start.8 = (bf16[640,1280]{1,0:T(8,128)(2,1)S(1)}, bf16[640,1280]{1,0:T(8,128)(2,1)S(1)}, u32[]{:S(2)}, u32[]{:S(2)}) collective-permute-start(bf16[640,1280]{1,0:T(8,128)(2,1)S(1)} %pad_maximum_fusion.3), channel_id=1, source_target_pairs={{0,4},{4,0},{8,12},{12,8},{16,20},{20,16},{24,28},{28,24},{32,36},... | collective-permute-start | bytes 4915208 | tf_op jit(solution)/shard_map/ppermute | solution.py:362
  61.4 6.5 %collective-permute-start.11 = (bf16[896,1280]{1,0:T(8,128)(2,1)S(1)}, bf16[896,1280]{1,0:T(8,128)(2,1)S(1)}, u32[]{:S(2)}, u32[]{:S(2)}) collective-permute-start(bf16[896,1280]{1,0:T(8,128)(2,1)S(1)} %collective-permute-done.5.refs_2_), channel_id=1, source_target_pairs={{0,4},{4,0},{8,12},{12,8},{16,20},{20,16},{24,28},{28,24},{32,36},... | collective-permute-start | bytes 6881288 | tf_op jit(solution)/shard_map/ppermute | solution.py:362
  63.8 7.3 %collective-permute-start.12 = (bf16[896,1280]{1,0:T(8,128)(2,1)S(1)}, bf16[896,1280]{1,0:T(8,128)(2,1)S(1)}, u32[]{:S(2)}, u32[]{:S(2)}) collective-permute-start(bf16[896,1280]{1,0:T(8,128)(2,1)S(1)} %collective-permute-done.6.refs_3_), channel_id=1, source_target_pairs={{0,4},{4,0},{8,12},{12,8},{16,20},{20,16},{24,28},{28,24},{32,36},... | collective-permute-start | bytes 6881288 | tf_op jit(solution)/shard_map/ppermute | solution.py:362
  64.1 27.5 %collective-permute-start.10 = (bf16[384,1280]{1,0:T(8,128)(2,1)S(1)}, bf16[384,1280]{1,0:T(8,128)(2,1)S(1)}, u32[]{:S(2)}, u32[]{:S(2)}) collective-permute-start(bf16[384,1280]{1,0:T(8,128)(2,1)S(1)} %pad_maximum_fusion.5), channel_id=1, source_target_pairs={{0,24},{4,100},{8,0},{12,108},{16,8},{20,116},{24,16},{28,124},{32... | collective-permute-start | bytes 2949128 | tf_op jit(solution)/shard_map/ppermute | solution.py:359
  65.7 25.9 %collective-permute-start.9 = (bf16[384,1280]{1,0:T(8,128)(2,1)S(1)}, bf16[384,1280]{1,0:T(8,128)(2,1)S(1)}, u32[]{:S(2)}, u32[]{:S(2)}) collective-permute-start(bf16[384,1280]{1,0:T(8,128)(2,1)S(1)} %pad_maximum_fusion.4), channel_id=1, source_target_pairs={{0,8},{4,36},{8,16},{12,44},{16,24},{20,52},{24,0},{28,60},{32,40}... | collective-permute-start | bytes 2949128 | tf_op jit(solution)/shard_map/ppermute | solution.py:359
  67.9 3.3 %copy-start.13 = (bf16[896,1280]{1,0:T(8,128)(2,1)}, bf16[896,1280]{1,0:T(8,128)(2,1)S(1)}, u32[]{:S(2)}) copy-start(bf16[896,1280]{1,0:T(8,128)(2,1)S(1)} %collective-permute-done.11.refs_4_) | copy-start | bytes 6881284
  71.2 1.4 copy-start.14
  72.6 19.8 %copy-start.11 = (f32[1024]{0:T(1024)S(1)}, f32[1024]{0:T(1024)}, u32[]{:S(2)}) copy-start(f32[1024]{0:T(1024)} %param.16) | copy-start | bytes 12292
  72.6 19.8 %copy-start.12 = (f32[256]{0:T(256)S(1)}, f32[256]{0:T(256)}, u32[]{:S(2)}) copy-start(f32[256]{0:T(256)} %param.17) | copy-start | bytes 3076
  72.6 19.8 %copy-start.8 = (s32[32,16]{0,1:T(8,128)S(1)}, s32[32,16]{0,1:T(8,128)}, u32[]{:S(2)}) copy-start(s32[32,16]{0,1:T(8,128)} %param.18) | copy-start | bytes 6148
  72.6 19.8 %copy-start.9 = (s32[32,16]{0,1:T(8,128)S(1)}, s32[32,16]{0,1:T(8,128)}, u32[]{:S(2)}) copy-start(s32[32,16]{0,1:T(8,128)} %param.20) | copy-start | bytes 6148
  72.6 23.1 %copy-start.1 = (f32[256,128]{1,0:T(8,128)S(1)}, f32[256,128]{1,0:T(8,128)}, u32[]{:S(2)}) copy-start(f32[256,128]{1,0:T(8,128)} %constant.65.clone.cosine_ref) | copy-start | bytes 393220
  72.6 23.1 %copy-start.2 = (f32[256,128]{1,0:T(8,128)S(1)}, f32[256,128]{1,0:T(8,128)}, u32[]{:S(2)}) copy-start(f32[256,128]{1,0:T(8,128)} %constant.66.clone.sine_ref) | copy-start | bytes 393220
  91.6 2.6 %collective-permute-start.13 = (bf16[384,1280]{1,0:T(8,128)(2,1)S(1)}, bf16[384,1280]{1,0:T(8,128)(2,1)S(1)}, u32[]{:S(2)}, u32[]{:S(2)}) collective-permute-start(bf16[384,1280]{1,0:T(8,128)(2,1)S(1)} %collective-permute-done.9.refs_0_), channel_id=1, source_target_pairs={{0,4},{4,0},{8,12},{12,8},{16,20},{20,16},{24,28},{28,24},{32,36},... | collective-permute-start | bytes 2949128 | tf_op jit(solution)/shard_map/ppermute | solution.py:362
  92.1 3.6 %collective-permute-start.14 = (bf16[384,1280]{1,0:T(8,128)(2,1)S(1)}, bf16[384,1280]{1,0:T(8,128)(2,1)S(1)}, u32[]{:S(2)}, u32[]{:S(2)}) collective-permute-start(bf16[384,1280]{1,0:T(8,128)(2,1)S(1)} %collective-permute-done.10.refs_1_), channel_id=1, source_target_pairs={{0,4},{4,0},{8,12},{12,8},{16,20},{20,16},{24,28},{28,24},{32,36},... | collective-permute-start | bytes 2949128 | tf_op jit(solution)/shard_map/ppermute | solution.py:362
  109.0 6.7 %copy-start.10 = (s32[32,16]{0,1:T(8,128)S(1)}, s32[32,16]{0,1:T(8,128)}, u32[]{:S(2)}) copy-start(s32[32,16]{0,1:T(8,128)} %param.19) | copy-start | bytes 6148
  109.0 58.9 %all-to-all-start = ((bf16[32,64,1024]{2,1,0:T(8,128)(2,1)}), bf16[32,64,1024]{2,1,0:T(8,128)(2,1)}, u32[]{:S(2)}, u32[]{:S(2)}) async-start(bf16[32,64,1024]{2,1,0:T(8,128)(2,1)} %attend.1), calls=%async_computation | async-start | bytes 8388608 | tf_op jit(solution)/shard_map/all_to_all | solution.py:398
  172.4 14.0 %collective-permute-start.15 = (bf16[256,1024]{1,0:T(8,128)(2,1)}, bf16[256,1024]{1,0:T(8,128)(2,1)S(1)}, u32[]{:S(2)}, u32[]{:S(2)}) collective-permute-start(bf16[256,1024]{1,0:T(8,128)(2,1)} %get-tuple-element.44), channel_id=1, source_target_pairs={{0,1},{1,2},{2,3},{3,0},{4,5},{5,6},{6,7},{7,4},{8,9},{9,10},{10,1... | collective-permute-start | bytes 1572872 | tf_op jit(solution)/shard_map/ppermute | solution.py:412
  173.6 25.0 %collective-permute-start.16 = (bf16[256,1024]{1,0:T(8,128)(2,1)}, bf16[256,1024]{1,0:T(8,128)(2,1)S(1)}, u32[]{:S(2)}, u32[]{:S(2)}) collective-permute-start(bf16[256,1024]{1,0:T(8,128)(2,1)} %get-tuple-element.45), channel_id=1, source_target_pairs={{0,2},{1,3},{2,0},{3,1},{4,6},{5,7},{6,4},{7,5},{8,10},{9,11},{10,... | collective-permute-start | bytes 1572872 | tf_op jit(solution)/shard_map/ppermute | solution.py:412
  176.0 22.6 %collective-permute-start.17 = (bf16[256,1024]{1,0:T(8,128)(2,1)}, bf16[256,1024]{1,0:T(8,128)(2,1)S(1)}, u32[]{:S(2)}, u32[]{:S(2)}) collective-permute-start(bf16[256,1024]{1,0:T(8,128)(2,1)} %get-tuple-element.46), channel_id=1, source_target_pairs={{0,3},{1,0},{2,1},{3,2},{4,7},{5,4},{6,5},{7,6},{8,11},{9,8},{10,9... | collective-permute-start | bytes 1572872 | tf_op jit(solution)/shard_map/ppermute | solution.py:412
  186.4 12.2 %copy-start.5 = (bf16[256,1024]{1,0:T(8,128)(2,1)}, bf16[256,1024]{1,0:T(8,128)(2,1)S(1)}, u32[]{:S(2)}) copy-start(bf16[256,1024]{1,0:T(8,128)(2,1)S(1)} %collective-permute-done.15.refs_1_) | copy-start | bytes 1572868
  198.6 1.0 copy-start.7
  (2 other events, 1.6 us)

commit v3 on v2

v3 whole, which is shorter than its diff:
```python
import functools

import jax
import jax.numpy as jnp
import numpy as np
from jax import lax
from jax.experimental import pallas as pl
from jax.experimental.pallas import tpu as pltpu
from jax.sharding import PartitionSpec as P

HD = 128
GROUP = 64
SIDE = 4
MIB = 1024 * 1024
FIRST_HEADS = 6
PIECES = (12, 12, 4, 4)

rope_base = 1000000.0
norm_epsilon = 1e-06


def rope_tables():
    half = HD // 2
    frequency = np.float32(rope_base) ** (
        -(np.arange(half, dtype=np.float32) * np.float32(2.0)) / np.float32(HD)
    )
    within = np.arange(GROUP)
    position = np.concatenate([within % length for length in (64, 32, 16, 8)])
    angles = position.astype(np.float32)[:, None] * frequency[None, :].astype(np.float32)
    cosine, sine = np.cos(angles), np.sin(angles)
    return (
        np.concatenate([cosine, cosine], 1).astype(np.float32),
        np.concatenate([-sine, sine], 1).astype(np.float32),
    )


def device_index(y, z, core):
    return ((y % SIDE) * SIDE + (z % SIDE)) * 2 + core


def shift_pairs(first, second):
    pairs = []
    for y in range(SIDE):
        for z in range(SIDE):
            pairs.append((device_index(y, z, 0), device_index(y + first, z + second, 0)))
            pairs.append((device_index(y, z, 1), device_index(y + second, z + first, 1)))
    return pairs


def swap_pairs():
    return [
        (device_index(y, z, core), device_index(y, z, 1 - core))
        for y in range(SIDE)
        for z in range(SIDE)
        for core in range(2)
    ]


def source_table():
    table = np.zeros((32, 64), np.int32)
    for y in range(SIDE):
        for z in range(SIDE):
            for core in range(2):

                def blocks(c, offsets):
                    found = []
                    for a, b, halves in offsets:
                        held = (
                            device_index(y - a, z - b, c)
                            if c == 0
                            else device_index(y - b, z - a, c)
                        )
                        found += [2 * held + half for half in halves]
                    return found

                both, low, high = (0, 1), (0,), (1,)
                beside = [(1, 0, both), (3, 0, both), (2, 0, both)]
                straight = [(0, 0, both), (0, 1, both), (0, 3, both)]
                ahead = [(1, 1, both), (3, 1, both), (2, 1, both)]
                behind = [(1, 3, both), (3, 3, both), (2, 3, both)]
                far = [(1, 2, both), (2, 2, low), (0, 2, low)]
                far += [(3, 2, both), (2, 2, high), (0, 2, high)]
                order = []
                for offsets in (beside + straight, ahead + behind, far):
                    order += blocks(core, offsets) + blocks(1 - core, offsets)
                table[device_index(y, z, core)] = order
    return table


def scaled_columns(order_ref, place, hidden_ref, gain_ref, scale, refs):
    depth = hidden_ref.shape[1] // order_ref.shape[0]
    for ref in refs:
        for j in range(ref.shape[1] // depth):
            start = pl.multiple_of(order_ref[place] * depth, depth)
            block = hidden_ref[:, pl.ds(start, depth)].astype(jnp.float32)
            gain = gain_ref[:, pl.ds(start, depth)]
            ref[:, j * depth : (j + 1) * depth] = (block * scale * gain).astype(jnp.bfloat16)
            place += 1


def norm_kernel(order_ref, hidden_ref, gain_ref, scale_ref, *refs):
    widened = hidden_ref[...].astype(jnp.float32)
    mean_square = jnp.sum(widened * widened, -1, keepdims=True) * (1.0 / widened.shape[1])
    scale = lax.rsqrt(mean_square + norm_epsilon)
    scale_ref[...] = scale
    scaled_columns(order_ref, 0, hidden_ref, gain_ref, scale, refs)


def norm_rest_kernel(place, order_ref, hidden_ref, gain_ref, scale_ref, *refs):
    scaled_columns(order_ref, place, hidden_ref, gain_ref, scale_ref[...], refs)


def norm(order, hidden, gain, widths, scale=None, place=0):
    rows, features = hidden.shape
    tile = 128
    given = [hidden, gain] + ([] if scale is None else [scale])
    in_specs = [
        pl.BlockSpec((tile, features), lambda i, order: (i, 0)),
        pl.BlockSpec((1, features), lambda i, order: (0, 0)),
    ]
    out_specs = [pl.BlockSpec((tile, w), lambda i, order: (i, 0)) for w in widths]
    out_shape = [pltpu.HBM((rows, w), jnp.bfloat16) for w in widths]
    scale_spec = pl.BlockSpec((tile, 1), lambda i, order: (i, 0))
    if scale is None:
        out_specs = [scale_spec] + out_specs
        out_shape = [jax.ShapeDtypeStruct((rows, 1), jnp.float32)] + out_shape
    else:
        in_specs = in_specs + [scale_spec]
    return pl.pallas_call(
        norm_kernel if scale is None else functools.partial(norm_rest_kernel, place),
        grid_spec=pltpu.PrefetchScalarGridSpec(
            num_scalar_prefetch=1, grid=(rows // tile,), in_specs=in_specs, out_specs=out_specs
        ),
        out_shape=out_shape,
        compiler_params=pltpu.CompilerParams(vmem_limit_bytes=32 * MIB),
        cost_estimate=pl.CostEstimate(
            flops=6 * rows * features,
            bytes_accessed=2 * rows * (features + sum(widths)),
            transcendentals=rows,
        ),
        name="norm",
    )(order, *given)


def product(x_ref, pieces, columns=slice(None)):
    weights = jnp.concatenate([piece[:, columns] for piece in pieces], axis=0)
    return jnp.dot(x_ref[...], weights, preferred_element_type=jnp.float32)


def tile_rows(tile):
    return pl.ds(pl.multiple_of(pl.program_id(0) * tile, tile), tile)


def first_kernel(x_ref, *refs):
    refs[-1][tile_rows(x_ref.shape[0]), :] = product(x_ref, refs[:-1])


def add_kernel(total_ref, x_ref, *refs):
    rows = tile_rows(x_ref.shape[0])
    refs[-1][rows, :] = total_ref[rows, :] + product(x_ref, refs[:-1])


def matmul_cost(rows, depth, columns, more):
    return pl.CostEstimate(
        flops=2 * rows * depth * columns,
        bytes_accessed=2 * depth * (rows + columns) + 4 * more * rows * columns,
        transcendentals=0,
    )


def project(total, x, pieces):
    rows, depth = x.shape
    columns = pieces[0].shape[1]
    tile = 256
    resident = pl.BlockSpec(memory_space=pltpu.VMEM)
    x_block = pl.BlockSpec((tile, depth), lambda i: (i, 0))
    totals = [] if total is None else [total]
    return pl.pallas_call(
        add_kernel if totals else first_kernel,
        grid=(rows // tile,),
        in_specs=[resident] * len(totals) + [x_block] + [resident] * len(pieces),
        out_specs=resident,
        out_shape=jax.ShapeDtypeStruct((rows, columns), jnp.float32),
        input_output_aliases={0: 0} if totals else {},
        compiler_params=pltpu.CompilerParams(vmem_limit_bytes=20 * MIB),
        cost_estimate=matmul_cost(rows, depth, columns, 2),
        name="project",
    )(*totals, x, *pieces)


def attend_kernel(
    columns, dest_ref, length_ref, total_ref, x_ref, bias_ref, cosine_ref, sine_ref, *refs
):
    makes_keyval = columns.start == 0
    if makes_keyval:
        pieces, (out_ref, keyval_ref, context, sems) = refs[:-4], refs[-4:]
    else:
        keyval_ref, pieces, (out_ref, context, sems) = refs[0], refs[1:-3], refs[-3:]
    step = pl.program_id(0)
    slot = lax.rem(step, 2)
    rows = x_ref.shape[0]
    heads = context.shape[2] // HD
    groups = rows // GROUP

    def copies(at_step, at_slot):
        return [
            pltpu.make_async_copy(
                context.at[at_slot, pl.ds(g * GROUP, GROUP)],
                out_ref.at[dest_ref[at_step * groups + g]],
                sems.at[at_slot, g],
            )
            for g in range(groups)
        ]

    lengths = [length_ref[step * groups + g] for g in range(groups)]
    row_tables = []
    for table in (cosine_ref, sine_ref):
        parts = []
        for length in lengths:
            index = (
                (length < 64).astype(jnp.int32)
                + (length < 32).astype(jnp.int32)
                + (length < 16).astype(jnp.int32)
            )
            parts.append(table[pl.ds(pl.multiple_of(index * GROUP, GROUP), GROUP), :])
        row_tables.append(jnp.concatenate(parts, 0))
    cosine, sine = row_tables

    summed = (
        total_ref[tile_rows(rows), columns]
        + product(x_ref, pieces, columns)
        + bias_ref[:, columns]
    )

    def rotated(column):
        head = summed[:, column : column + HD]
        return (head * cosine + pltpu.roll(head, HD // 2, 1) * sine).astype(jnp.bfloat16)

    query = [rotated(h * HD) for h in range(heads)]
    if makes_keyval:
        key = rotated(heads * HD)
        value = summed[:, (heads + 1) * HD :].astype(jnp.bfloat16)
        keyval_ref[:, :HD] = key
        keyval_ref[:, HD:] = value
    else:
        key, value = keyval_ref[:, :HD], keyval_ref[:, HD:]

    @pl.when(step >= 2)
    def _():
        for copy in copies(step - 2, slot):
            copy.wait()

    tile = 2 * GROUP
    row = lax.broadcasted_iota(jnp.int32, (tile, tile), 0)
    column = lax.broadcasted_iota(jnp.int32, (tile, tile), 1)
    for t in range(rows // tile):
        length = jnp.where(row < GROUP, lengths[2 * t], lengths[2 * t + 1])
        allowed = (column >= (row & -length)) & (column <= row)
        span = slice(t * tile, (t + 1) * tile)
        stacked = jnp.concatenate([q[span] for q in query], 0)
        scores = lax.dot_general(
            stacked, key[span], (((1,), (1,)), ((), ())), preferred_element_type=jnp.float32
        ) * (HD ** (-0.5))
        scores = jnp.where(allowed[None], scores.reshape(heads, tile, tile), -jnp.inf)
        weights = jnp.exp(scores - jnp.max(scores, -1, keepdims=True))
        weights = weights * (1.0 / jnp.sum(weights, -1, keepdims=True))
        weights = weights.astype(jnp.bfloat16).reshape(heads * tile, tile)
        mixed = jnp.dot(weights, value[span], preferred_element_type=jnp.float32)
        mixed = mixed.astype(jnp.bfloat16)
        for h in range(heads):
            context[slot, span, h * HD : (h + 1) * HD] = mixed[h * tile : (h + 1) * tile]

    for copy in copies(step, slot):
        copy.start()

    @pl.when(step == pl.num_programs(0) - 1)
    def _():
        for copy in copies(step - 1, 1 - slot) + copies(step, slot):
            copy.wait()


def attend(dest, lengths, total, x, bias, keyval, pieces, packs, columns):
    rows, depth = x.shape
    tile = 256
    cosine, sine = rope_tables()
    resident = pl.BlockSpec(memory_space=pltpu.VMEM)

    def fixed(shape):
        return pl.BlockSpec(
            shape, lambda i, *_: (0,) * len(shape), pipeline_mode=pl.Buffered(1)
        )

    def by_rows(width):
        return pl.BlockSpec((tile, width), lambda i, *_: (i, 0))

    width = columns.stop - columns.start
    out_specs = [pl.BlockSpec(memory_space=pltpu.HBM)]
    if keyval is None:
        width -= 2 * HD
        out_specs.append(by_rows(2 * HD))
    out_shape = [
        pltpu.HBM((packs, GROUP, width), jnp.bfloat16),
        jax.ShapeDtypeStruct((rows, 2 * HD), jnp.bfloat16),
    ]
    keyvals = [] if keyval is None else [keyval]
    return pl.pallas_call(
        functools.partial(attend_kernel, columns),
        grid_spec=pltpu.PrefetchScalarGridSpec(
            num_scalar_prefetch=2,
            grid=(rows // tile,),
            in_specs=[
                resident,
                by_rows(depth),
                fixed(bias.shape),
                fixed(cosine.shape),
                fixed(sine.shape),
            ]
            + [by_rows(2 * HD)] * len(keyvals)
            + [resident] * len(pieces),
            out_specs=out_specs,
            scratch_shapes=[
                pltpu.VMEM((2, tile, width), jnp.bfloat16),
                pltpu.SemaphoreType.DMA((2, tile // GROUP)),
            ],
        ),
        out_shape=out_shape[: len(out_specs)],
        compiler_params=pltpu.CompilerParams(vmem_limit_bytes=24 * MIB),
        cost_estimate=matmul_cost(rows, depth, columns.stop - columns.start, 2),
        name="attend",
    )(dest, lengths, total, x, bias, cosine, sine, *keyvals, *pieces)


def place_kernel(source_ref, received_ref, *refs):
    parts, sems = refs[:-1], refs[-1]
    per_part = parts[0].shape[0] // GROUP
    copies = [
        pltpu.make_async_copy(
            received_ref.at[source_ref[k * per_part + j]],
            part.at[pl.ds(j * GROUP, GROUP)],
            sems.at[k * per_part + j],
        )
        for k, part in enumerate(parts)
        for j in range(per_part)
    ]
    for copy in copies:
        copy.start()
    for copy in copies:
        copy.wait()


def place(source, received, parts):
    packs, group, width = received.shape
    per_part = source.shape[0] // parts
    return pl.pallas_call(
        place_kernel,
        grid_spec=pltpu.PrefetchScalarGridSpec(
            num_scalar_prefetch=1,
            grid=(1,),
            in_specs=[pl.BlockSpec(memory_space=pltpu.HBM)],
            out_specs=[pl.BlockSpec(memory_space=pltpu.VMEM)] * parts,
            scratch_shapes=[pltpu.SemaphoreType.DMA((source.shape[0],))],
        ),
        out_shape=[jax.ShapeDtypeStruct((per_part * group, width), received.dtype)] * parts,
        compiler_params=pltpu.CompilerParams(vmem_limit_bytes=8 * MIB),
        name="place",
    )(source, received)


def join_kernel(step, start, order_ref, *refs):
    parts, out_ref, sems = refs[:-2], refs[-2], refs[-1]
    if start > 0:
        parts = parts[1:]
    width = parts[0].shape[1]
    copies = []
    for k, part in enumerate(parts):
        column = pl.multiple_of(order_ref[k] * step + start, HD)
        copies.append(
            pltpu.make_async_copy(part, out_ref.at[:, pl.ds(column, width)], sems.at[k])
        )
    for copy in copies:
        copy.start()
    for copy in copies:
        copy.wait()


def join(order, parts, columns, joined=None, start=0):
    rows = parts[0].shape[0]
    whole = pl.BlockSpec(memory_space=pltpu.HBM)
    given = [] if joined is None else [joined]
    return pl.pallas_call(
        functools.partial(join_kernel, columns // len(parts), start),
        grid_spec=pltpu.PrefetchScalarGridSpec(
            num_scalar_prefetch=1,
            grid=(1,),
            in_specs=[whole] * len(given)
            + [pl.BlockSpec(memory_space=pltpu.VMEM)] * len(parts),
            out_specs=whole,
            scratch_shapes=[pltpu.SemaphoreType.DMA((len(parts),))],
        ),
        out_shape=jax.ShapeDtypeStruct((rows, columns), parts[0].dtype),
        input_output_aliases={1: 0} if given else {},
        compiler_params=pltpu.CompilerParams(vmem_limit_bytes=8 * MIB),
        name="join",
    )(order, *given, *parts)


def per_device(
    hidden_states,
    norm_gain,
    w_query,
    w_keyval,
    query_bias,
    keyval_bias,
    group_dest,
    group_offset,
    group_length,
):
    own = lax.axis_index("dp")
    plane = lax.axis_index("mp")
    planes = lax.axis_size("mp")
    packs, groups = group_dest.shape
    rows, features = hidden_states.shape

    def first(piece, by):
        return lax.ppermute(piece, "dp", shift_pairs(by, 0))

    def second(piece, by):
        return lax.ppermute(piece, "dp", shift_pairs(0, by))

    def swap(piece):
        return lax.ppermute(piece, "dp", swap_pairs())

    cut = FIRST_HEADS * HD
    weights = jnp.concatenate([w_query[:, :cut], w_keyval, w_query[:, cut:]], 1)
    bias = jnp.concatenate([query_bias[:cut], keyval_bias, query_bias[cut:]])[None]
    rows_held = weights.shape[0]
    half = rows_held // 2
    order = lax.dynamic_index_in_dim(jnp.asarray(source_table()), own, 0, keepdims=False)
    near = [first(weights, 1), first(weights, -1), first(weights, 2)]
    own_ahead, own_behind = second(weights, 1), second(weights, -1)
    widths = [count * rows_held for count in PIECES]
    gain = norm_gain[None]
    scale, x_early = norm(order, hidden_states, gain, widths[:1])

    near, own_ahead, own_behind, x_early, scale = lax.optimization_barrier(
        (near, own_ahead, own_behind, x_early, scale)
    )
    beside = jnp.concatenate(near)
    straight = jnp.concatenate([weights, own_ahead, own_behind])
    ahead, behind = second(beside, 1), second(beside, -1)
    total = project(None, x_early, [beside, straight, swap(beside), swap(straight)])
    x_middle, x_far, x_last = norm(
        order, hidden_states, gain, widths[1:], scale, widths[0] // half
    )

    ahead, behind, total, x_middle, x_far, x_last = lax.optimization_barrier(
        (ahead, behind, total, x_middle, x_far, x_last)
    )
    far = [
        second(
            jnp.concatenate(
                [ahead[:rows_held], ahead[2 * rows_held : -half], own_ahead[:half]]
            ),
            1,
        ),
        second(
            jnp.concatenate(
                [behind[rows_held : 2 * rows_held], behind[-half:], own_behind[half:]]
            ),
            -1,
        ),
    ]
    total = project(total, x_middle, [ahead, behind, swap(ahead), swap(behind)])
    far, total = lax.optimization_barrier((far, total))
    last = [swap(piece) for piece in far]
    total = project(total, x_far, far)

    own_dest = lax.dynamic_index_in_dim(group_dest, own, 0, keepdims=False)
    own_length = lax.dynamic_index_in_dim(group_length, own, 0, keepdims=False)
    middle = cut + w_keyval.shape[1]
    given = (own_dest, own_length, total, x_last, bias)
    first_sent, keyval = attend(*given, None, last, packs, slice(0, middle))
    (second_sent,) = attend(*given, keyval, last, packs, slice(middle, weights.shape[1]))

    slot = group_offset // GROUP
    hits = (group_dest == own)[None] & (
        slot[None] == jnp.arange(groups, dtype=jnp.int32)[:, None, None]
    )
    packs_of = jnp.arange(packs, dtype=jnp.int32)[None, :, None]
    source = jnp.sum(jnp.where(hits, packs_of, 0), (1, 2)).reshape(planes, -1)
    step = jnp.arange(planes, dtype=jnp.int32)
    source = source[(plane + step) % planes].reshape(-1)
    joins = (plane - step) % planes

    def exchanged(sent):
        received = lax.all_to_all(sent, "dp", split_axis=0, concat_axis=0, tiled=True)
        parts = place(source, received, planes)
        return [parts[0]] + [
            lax.ppermute(parts[k], "mp", [(i, (i + k) % planes) for i in range(planes)])
            for k in range(1, planes)
        ]

    columns = planes * w_query.shape[1]
    joined = join(joins, exchanged(first_sent), columns)
    return join(joins, exchanged(second_sent), columns, joined, cut)


def solution(mesh):
    return jax.shard_map(
        per_device,
        mesh=mesh,
        in_specs=(
            P("dp", None),
            P(),
            P("dp", "mp"),
            P("dp", "mp"),
            P("mp"),
            P("mp"),
            P(),
            P(),
            P(),
        ),
        out_specs=P(("dp", "mp"), None),
        check_vma=False,
    )
```

time: 207 us -> 182 us (0.88); the launches traced: 204 us -> 182 us
  waiting for transfers between devices: 97.5 us -> 57.9 us
  local copies, waits for them, and re-layouts: 12.7 us -> 24.4 us
  starting transfers between devices: 29.8 us -> 37.8 us
    all_to_all x1 -> x2, waiting for transfers between devices: 50.5 us -> 33 us  [exchanged(): lax.all_to_all(sent, 'dp', split_axis=0, concat_axis=0, tiled=True)]
    ppermute x3 -> x6, waiting for transfers between devices: 20.9 us -> 6.68 us  [exchanged(): lax.ppermute(parts[k], 'mp', [(i, (i + k) % planes) for i in range(planes)])]
    unnamed x31 -> x52, local copies, waits for them, and re-layouts: 8.33 us -> 18.8 us
    ppermute x6, waiting for transfers between devices: 16.6 us -> 9.13 us  [second(): return lax.ppermute(piece, 'dp', shift_pairs(0, by))]
    ppermute x3 -> x6, starting transfers between devices: 4.82 us -> 9.77 us  [exchanged(): lax.ppermute(parts[k], 'mp', [(i, (i + k) % planes) for i in range(planes)])]
    ppermute x6, waiting for transfers between devices: 8.45 us -> 3.68 us  [swap(): return lax.ppermute(piece, 'dp', swap_pairs())]
    ppermute x3, waiting for transfers between devices: 1.13 us -> 5.41 us  [first(): return lax.ppermute(piece, 'dp', shift_pairs(by, 0))]
    pallas_call x5 -> x9, Pallas kernels: 56.6 us -> 53.7 us  [the longest x3 22 us: project(): pl.pallas_call(add_kernel if totals else first_kernel, grid=(rows // tile...]
  transfers between devices with their start and end apart: 19 -> 23, of which waited for: 9 -> 12; matrix products, arithmetic and copies ran while one was open for 2% -> 1% of each run, Pallas kernels for 19% -> 27%
where the time goes in v3:
time: 182 us
  Pallas kernels  59.2 us (33%)
  waiting for transfers between devices  57.9 us (32%)
  starting transfers between devices  37.8 us (21%)
  local copies, waits for them, and re-layouts  24.4 us (13%)
    all_to_all x2, waiting for transfers between devices, exchanged(): lax.all_to_all(sent, 'dp', split_axis=0, concat_axis=0, tiled=True)  33 us
    pallas_call x3, Pallas kernels, project(): pl.pallas_call(add_kernel if totals else first_kernel, grid=(rows // tile...  22 us
    unnamed x52, local copies, waits for them, and re-layouts  18.8 us
    pallas_call x2, Pallas kernels, norm(): pl.pallas_call(norm_kernel if scale is None else functools.partial(norm_r...  14.5 us
    pallas_call x2, Pallas kernels, attend(): pl.pallas_call(functools.partial(attend_kernel, columns), grid_spec=pltpu...  14.1 us
    ppermute x6, starting transfers between devices, exchanged(): lax.ppermute(parts[k], 'mp', [(i, (i + k) % planes) for i in range(planes)])  9.77 us
    ppermute x6, waiting for transfers between devices, second(): return lax.ppermute(piece, 'dp', shift_pairs(0, by))  9.13 us
    all_to_all x2, starting transfers between devices, exchanged(): lax.all_to_all(sent, 'dp', split_axis=0, concat_axis=0, tiled=True)  9.06 us
  transfers between devices with their start and end apart: 23, of which 12 were waited for; matrix products, arithmetic and copies ran while one was open for 1% of the time, Pallas kernels for 27%

profile of v3, /device:TPU:1, one launch (start us, length us, event | category | flops | bytes accessed | tf_op | source)
XLA Modules:
  0.0 181.6 jit_solution(2139256586498918813)
XLA Ops:
  2.9 2.5 %collective-permute-start = (bf16[256,1280]{1,0:T(8,128)(2,1)S(1)}, bf16[256,1280]{1,0:T(8,128)(2,1)S(1)}, u32[]{:S(2)}, u32[]{:S(2)}) collective-permute-start(bf16[256,1280]{1,0:T(8,128)(2,1)S(1)} %pad_maximum_fusion.3), channel_id=1, source_target_pairs={{0,32},{4,12},{8,40},{12,20},{16,48},{20,28},{24,56},{28,4},{32,64... | collective-permute-start | bytes 1966088 | tf_op jit(solution)/shard_map/ppermute | solution.py:425
  5.4 2.2 %collective-permute-start.1 = (bf16[256,1280]{1,0:T(8,128)(2,1)S(1)}, bf16[256,1280]{1,0:T(8,128)(2,1)}, u32[]{:S(2)}, u32[]{:S(2)}) collective-permute-start(bf16[256,1280]{1,0:T(8,128)(2,1)S(1)} %pad_maximum_fusion.3), channel_id=1, source_target_pairs={{0,96},{4,28},{8,104},{12,4},{16,112},{20,12},{24,120},{28,20},{32... | collective-permute-start | bytes 1966088 | tf_op jit(solution)/shard_map/ppermute | solution.py:425
  12.3 5.8 %copy-done = bf16[1024,8192]{1,0:T(8,128)(2,1)S(1)} copy-done((bf16[1024,8192]{1,0:T(8,128)(2,1)S(1)}, bf16[1024,8192]{1,0:T(8,128)(2,1)}, u32[]{:S(2)}) %copy-start) | copy-done | bytes 16777240
  18.1 7.7 %norm.2 = (f32[1024,1]{1,0:T(8,128)S(1)}, bf16[1024,3072]{1,0:T(8,128)(2,1)}) custom-call(s32[64]{0:T(128)S(1)} %fusion.3.order_ref, bf16[1024,8192]{1,0:T(8,128)(2,1)S(1)} %copy-done, f32[1,8192]{1,0:T(1,128)S(1)} %bitcast.6), custom_call_target="tpu_custom_call" | custom-call | flops 50331648 | bytes 23068672 | tf_op jit(solution)/shard_map/norm/pallas_call | solution.py:129
  25.8 5.4 %collective-permute-done.2 = bf16[256,1280]{1,0:T(8,128)(2,1)} collective-permute-done((bf16[256,1280]{1,0:T(8,128)(2,1)S(1)}, bf16[256,1280]{1,0:T(8,128)(2,1)}, u32[]{:S(2)}, u32[]{:S(2)}) %collective-permute-start.2) | collective-permute-done | bytes 655392 | tf_op jit(solution)/shard_map/ppermute | solution.py:425
  31.3 1.6 constant_dynamic-update-slice_fusion.1
  37.6 6.8 %norm.3 = (bf16[1024,3072]{1,0:T(8,128)(2,1)}, bf16[1024,1024]{1,0:T(8,128)(2,1)}, bf16[1024,1024]{1,0:T(8,128)(2,1)}) custom-call(s32[64]{0:T(128)S(1)} %fusion.3.order_ref, bf16[1024,8192]{1,0:T(8,128)(2,1)S(1)} %copy-done, f32[1,8192]{1,0:T(1,128)S(1)} %bitcast.7, f32[1024,1]{1,0:T(8,128)S(1)} %get-tuple-element.44.scale_ref), custom_call_target="tpu_custom_call" | custom-call | flops 50331648 | bytes 27262976 | tf_op jit(solution)/shard_map/norm/pallas_call | solution.py:129
  44.4 2.8 %copy-done.16 = bf16[1024,3072]{1,0:T(8,128)(2,1)S(1)} copy-done((bf16[1024,3072]{1,0:T(8,128)(2,1)S(1)}, bf16[1024,3072]{1,0:T(8,128)(2,1)}, u32[]{:S(2)}) %copy-start.16) | copy-done | bytes 6291480
  47.2 9.0 %project.3.total_ref = f32[1024,1280]{1,0:T(8,128)S(1)} custom-call(bf16[1024,3072]{1,0:T(8,128)(2,1)S(1)} %copy-done.16, bf16[768,1280]{1,0:T(8,128)(2,1)S(1)} %constant_dynamic-update-slice_fusion.refs_0_, bf16[768,1280]{1,0:T(8,128)(2,1)S(1)} %pad_maximum_fusion.refs_1_, bf16[768,1280]{1,0:T(8,128)(2,1)S(1)} %collective-permute-done.7.refs_2_, ...), custom_call_target="tpu_custom_call" | custom-call | flops 8053063680 | bytes 24641536 | tf_op jit(solution)/shard_map/project/pallas_call | solution.py:178
  56.1 3.8 %collective-permute-done.5.refs_0_ = bf16[768,1280]{1,0:T(8,128)(2,1)S(1)} collective-permute-done((bf16[768,1280]{1,0:T(8,128)(2,1)S(1)}, bf16[768,1280]{1,0:T(8,128)(2,1)S(1)}, u32[]{:S(2)}, u32[]{:S(2)}) %collective-permute-start.5) | collective-permute-done | bytes 1966112 | tf_op jit(solution)/shard_map/ppermute | solution.py:428
  59.9 2.1 %collective-permute-start.11 = (bf16[768,1280]{1,0:T(8,128)(2,1)S(1)}, bf16[768,1280]{1,0:T(8,128)(2,1)S(1)}, u32[]{:S(2)}, u32[]{:S(2)}) collective-permute-start(bf16[768,1280]{1,0:T(8,128)(2,1)S(1)} %collective-permute-done.5.refs_0_), channel_id=1, source_target_pairs={{0,4},{4,0},{8,12},{12,8},{16,20},{20,16},{24,28},{28,24},{32,36},... | collective-permute-start | bytes 5898248 | tf_op jit(solution)/shard_map/ppermute | solution.py:431
  63.0 1.7 collective-permute-start.10
  65.6 2.8 %collective-permute-done.12.refs_3_ = bf16[768,1280]{1,0:T(8,128)(2,1)S(1)} collective-permute-done((bf16[768,1280]{1,0:T(8,128)(2,1)S(1)}, bf16[768,1280]{1,0:T(8,128)(2,1)S(1)}, u32[]{:S(2)}, u32[]{:S(2)}) %collective-permute-start.12) | collective-permute-done | bytes 1966112 | tf_op jit(solution)/shard_map/ppermute | solution.py:431
  68.4 9.2 %project.4.total_ref = f32[1024,1280]{1,0:T(8,128)S(1)} custom-call(f32[1024,1280]{1,0:T(8,128)S(1)} %project.3.total_ref, bf16[1024,3072]{1,0:T(8,128)(2,1)S(1)} %copy-done.15, bf16[768,1280]{1,0:T(8,128)(2,1)S(1)} %collective-permute-done.5.refs_0_, bf16[768,1280]{1,0:T(8,128)(2,1)S(1)} %collective-permute-done.6.refs_1_, ...), custom_call_target="tpu_custom_call", output_to_operand_aliasing={{}: (0, {})} | custom-call | flops 8053063680 | bytes 24641536 | tf_op jit(solution)/shard_map/project/pallas_call | solution.py:178
  77.5 2.3 %collective-permute-done.10.refs_1_ = bf16[512,1280]{1,0:T(8,128)(2,1)S(1)} collective-permute-done((bf16[512,1280]{1,0:T(8,128)(2,1)S(1)}, bf16[512,1280]{1,0:T(8,128)(2,1)S(1)}, u32[]{:S(2)}, u32[]{:S(2)}) %collective-permute-start.10) | collective-permute-done | bytes 1310752 | tf_op jit(solution)/shard_map/ppermute | solution.py:428
  79.8 3.1 %collective-permute-done.9.refs_0_ = bf16[512,1280]{1,0:T(8,128)(2,1)S(1)} collective-permute-done((bf16[512,1280]{1,0:T(8,128)(2,1)S(1)}, bf16[512,1280]{1,0:T(8,128)(2,1)S(1)}, u32[]{:S(2)}, u32[]{:S(2)}) %collective-permute-start.9) | collective-permute-done | bytes 1310752 | tf_op jit(solution)/shard_map/ppermute | solution.py:428
  82.9 3.0 %collective-permute-start.13 = (bf16[512,1280]{1,0:T(8,128)(2,1)S(1)}, bf16[512,1280]{1,0:T(8,128)(2,1)S(1)}, u32[]{:S(2)}, u32[]{:S(2)}) collective-permute-start(bf16[512,1280]{1,0:T(8,128)(2,1)S(1)} %collective-permute-done.9.refs_0_), channel_id=1, source_target_pairs={{0,4},{4,0},{8,12},{12,8},{16,20},{20,16},{24,28},{28,24},{32,36},... | collective-permute-start | bytes 3932168 | tf_op jit(solution)/shard_map/ppermute | solution.py:431
  86.2 3.9 %project.5.total_ref = f32[1024,1280]{1,0:T(8,128)S(1)} custom-call(f32[1024,1280]{1,0:T(8,128)S(1)} %project.4.total_ref, bf16[1024,1024]{1,0:T(8,128)(2,1)S(1)} %copy-done.9, bf16[512,1280]{1,0:T(8,128)(2,1)S(1)} %collective-permute-done.9.refs_0_, bf16[512,1280]{1,0:T(8,128)(2,1)S(1)} %collective-permute-done.10.refs_1_), custom_call_target="tpu_custom_call", output_to_operand_aliasing={{}: (0, {})} | custom-call | flops 2684354560 | bytes 15204352 | tf_op jit(solution)/shard_map/project/pallas_call | solution.py:178
  90.4 7.9 %attend.2 = (bf16[32,64,768]{2,1,0:T(8,128)(2,1)}, bf16[1024,256]{1,0:T(8,128)(2,1)S(1)}) custom-call(s32[16]{0:T(128)S(1)} %get-tuple-element.68.dest_ref, s32[16]{0:T(128)S(1)} %get-tuple-element.67.length_ref, f32[1024,1280]{1,0:T(8,128)S(1)} %project.5.total_ref, bf16[1024,1024]{1,0:T(8,128)(2,1)S(1)} %copy-done.3, ...), custom_call_target="tpu_custom_call" | custom-call | flops 2147483648 | bytes 12582912 | tf_op jit(solution)/shard_map/attend/pallas_call | solution.py:306
  99.2 4.1 %all-to-all-start = ((bf16[32,64,768]{2,1,0:T(8,128)(2,1)}), bf16[32,64,768]{2,1,0:T(8,128)(2,1)S(1)}, u32[]{:S(2)}, u32[]{:S(2)}) async-start(bf16[32,64,768]{2,1,0:T(8,128)(2,1)} %get-tuple-element.57), calls=%async_computation | async-start | bytes 6291456 | tf_op jit(solution)/shard_map/all_to_all | solution.py:496
  103.3 2.5 %copy-done.2 = f32[1024,1280]{1,0:T(8,128)S(1)} copy-done((f32[1024,1280]{1,0:T(8,128)S(1)}, f32[1024,1280]{1,0:T(8,128)}, u32[]{:S(2)}) %copy-start.2) | copy-done | bytes 5242904
  111.0 6.2 %attend.3 = bf16[32,64,256]{2,1,0:T(8,128)(2,1)} custom-call(s32[16]{0:T(128)S(1)} %get-tuple-element.68.dest_ref, s32[16]{0:T(128)S(1)} %get-tuple-element.67.length_ref, f32[1024,1280]{1,0:T(8,128)S(1)} %copy-done.2, bf16[1024,1024]{1,0:T(8,128)(2,1)S(1)} %copy-done.4, f32[1,1280]{1,0:T(1,128)S(1)} %broadcast_in_dim.26.bias_ref, ...), custom_call_target="tpu_custom_call" | custom-call | flops 536870912 | bytes 4718592 | tf_op jit(solution)/shard_map/attend/pallas_call | solution.py:306
  117.2 25.9 %all-to-all-done.received_ref = bf16[32,64,768]{2,1,0:T(8,128)(2,1)S(1)} async-done(((bf16[32,64,768]{2,1,0:T(8,128)(2,1)}), bf16[32,64,768]{2,1,0:T(8,128)(2,1)S(1)}, u32[]{:S(2)}, u32[]{:S(2)}) %all-to-all-start) | async-done | bytes 3145760 | tf_op jit(solution)/shard_map/all_to_all | solution.py:496
  143.1 5.0 %all-to-all-start.1 = ((bf16[32,64,256]{2,1,0:T(8,128)(2,1)}), bf16[32,64,256]{2,1,0:T(8,128)(2,1)}, u32[]{:S(2)}, u32[]{:S(2)}) async-start(bf16[32,64,256]{2,1,0:T(8,128)(2,1)} %attend.3), calls=%async_computation.1 | async-start | bytes 2097152 | tf_op jit(solution)/shard_map/all_to_all | solution.py:496
  149.3 3.8 %place.2 = (bf16[256,768]{1,0:T(8,128)(2,1)S(1)}, bf16[256,768]{1,0:T(8,128)(2,1)}, bf16[256,768]{1,0:T(8,128)(2,1)}, bf16[256,768]{1,0:T(8,128)(2,1)}) custom-call(s32[16]{0:T(128)S(1)} %reshape.58.source_ref, bf16[32,64,768]{2,1,0:T(8,128)(2,1)S(1)} %all-to-all-done.received_ref), custom_call_target="tpu_custom_call" | custom-call | tf_op jit(solution)/shard_map/place/pallas_call | solution.py:354
  154.4 2.4 %collective-permute-start.16 = (bf16[256,768]{1,0:T(8,128)(2,1)}, bf16[256,768]{1,0:T(8,128)(2,1)S(1)}, u32[]{:S(2)}, u32[]{:S(2)}) collective-permute-start(bf16[256,768]{1,0:T(8,128)(2,1)} %get-tuple-element.60), channel_id=1, source_target_pairs={{0,2},{1,3},{2,0},{3,1},{4,6},{5,7},{6,4},{7,5},{8,10},{9,11},{10,... | collective-permute-start | bytes 1179656 | tf_op jit(solution)/shard_map/ppermute | solution.py:499
  158.0 7.1 %all-to-all-done.1.received_ref = bf16[32,64,256]{2,1,0:T(8,128)(2,1)} async-done(((bf16[32,64,256]{2,1,0:T(8,128)(2,1)}), bf16[32,64,256]{2,1,0:T(8,128)(2,1)}, u32[]{:S(2)}, u32[]{:S(2)}) %all-to-all-start.1) | async-done | bytes 1048608 | tf_op jit(solution)/shard_map/all_to_all | solution.py:496
  165.1 1.7 place.3
  168.0 2.4 %collective-permute-start.19 = (bf16[256,256]{1,0:T(8,128)(2,1)S(1)}, bf16[256,256]{1,0:T(8,128)(2,1)S(1)}, u32[]{:S(2)}, u32[]{:S(2)}) collective-permute-start(bf16[256,256]{1,0:T(8,128)(2,1)S(1)} %get-tuple-element.65), channel_id=1, source_target_pairs={{0,2},{1,3},{2,0},{3,1},{4,6},{5,7},{6,4},{7,5},{8,10},{9,11},{10,... | collective-permute-start | bytes 393224 | tf_op jit(solution)/shard_map/ppermute | solution.py:499
  171.7 2.8 %collective-permute-done.16.refs_2_ = bf16[256,768]{1,0:T(8,128)(2,1)S(1)} collective-permute-done((bf16[256,768]{1,0:T(8,128)(2,1)}, bf16[256,768]{1,0:T(8,128)(2,1)S(1)}, u32[]{:S(2)}, u32[]{:S(2)}) %collective-permute-start.16) | collective-permute-done | bytes 393248 | tf_op jit(solution)/shard_map/ppermute | solution.py:499
  174.4 1.7 join.2.refs_0_
  176.2 2.4 %collective-permute-done.18.refs_2_ = bf16[256,256]{1,0:T(8,128)(2,1)S(1)} collective-permute-done((bf16[256,256]{1,0:T(8,128)(2,1)S(1)}, bf16[256,256]{1,0:T(8,128)(2,1)S(1)}, u32[]{:S(2)}, u32[]{:S(2)}) %collective-permute-start.18) | collective-permute-done | bytes 131104 | tf_op jit(solution)/shard_map/ppermute | solution.py:499
  (106 shorter events, 29.7 us)
Async XLA Ops:
  0.0 12.3 %copy-start.14 = (f32[8192]{0:T(1024)S(1)}, f32[8192]{0:T(1024)}, u32[]{:S(2)}) copy-start(f32[8192]{0:T(1024)} %param.15) | copy-start | bytes 98308
  2.9 22.8 %collective-permute-start = (bf16[256,1280]{1,0:T(8,128)(2,1)S(1)}, bf16[256,1280]{1,0:T(8,128)(2,1)S(1)}, u32[]{:S(2)}, u32[]{:S(2)}) collective-permute-start(bf16[256,1280]{1,0:T(8,128)(2,1)S(1)} %pad_maximum_fusion.3), channel_id=1, source_target_pairs={{0,32},{4,12},{8,40},{12,20},{16,48},{20,28},{24,56},{28,4},{32,64... | collective-permute-start | bytes 1966088 | tf_op jit(solution)/shard_map/ppermute | solution.py:425
  5.4 20.3 %collective-permute-start.1 = (bf16[256,1280]{1,0:T(8,128)(2,1)S(1)}, bf16[256,1280]{1,0:T(8,128)(2,1)}, u32[]{:S(2)}, u32[]{:S(2)}) collective-permute-start(bf16[256,1280]{1,0:T(8,128)(2,1)S(1)} %pad_maximum_fusion.3), channel_id=1, source_target_pairs={{0,96},{4,28},{8,104},{12,4},{16,112},{20,12},{24,120},{28,20},{32... | collective-permute-start | bytes 1966088 | tf_op jit(solution)/shard_map/ppermute | solution.py:425
  7.7 23.5 %collective-permute-start.2 = (bf16[256,1280]{1,0:T(8,128)(2,1)S(1)}, bf16[256,1280]{1,0:T(8,128)(2,1)}, u32[]{:S(2)}, u32[]{:S(2)}) collective-permute-start(bf16[256,1280]{1,0:T(8,128)(2,1)S(1)} %pad_maximum_fusion.3), channel_id=1, source_target_pairs={{0,64},{4,20},{8,72},{12,28},{16,80},{20,4},{24,88},{28,12},{32,96... | collective-permute-start | bytes 1966088 | tf_op jit(solution)/shard_map/ppermute | solution.py:425
  8.9 22.3 %collective-permute-start.3 = (bf16[256,1280]{1,0:T(8,128)(2,1)S(1)}, bf16[256,1280]{1,0:T(8,128)(2,1)S(1)}, u32[]{:S(2)}, u32[]{:S(2)}) collective-permute-start(bf16[256,1280]{1,0:T(8,128)(2,1)S(1)} %pad_maximum_fusion.3), channel_id=1, source_target_pairs={{0,8},{4,36},{8,16},{12,44},{16,24},{20,52},{24,0},{28,60},{32,40}... | collective-permute-start | bytes 1966088 | tf_op jit(solution)/shard_map/ppermute | solution.py:428
  10.2 21.0 %collective-permute-start.4 = (bf16[256,1280]{1,0:T(8,128)(2,1)S(1)}, bf16[256,1280]{1,0:T(8,128)(2,1)S(1)}, u32[]{:S(2)}, u32[]{:S(2)}) collective-permute-start(bf16[256,1280]{1,0:T(8,128)(2,1)S(1)} %pad_maximum_fusion.3), channel_id=1, source_target_pairs={{0,24},{4,100},{8,0},{12,108},{16,8},{20,116},{24,16},{28,124},{32... | collective-permute-start | bytes 1966088 | tf_op jit(solution)/shard_map/ppermute | solution.py:428
  31.2 30.8 %copy-start.17 = (bf16[256,1280]{1,0:T(8,128)(2,1)}, bf16[256,1280]{1,0:T(8,128)(2,1)S(1)}, u32[]{:S(2)}) copy-start(bf16[256,1280]{1,0:T(8,128)(2,1)S(1)} %collective-permute-done.3) | copy-start | bytes 1966084
  31.2 30.8 %copy-start.18 = (bf16[256,1280]{1,0:T(8,128)(2,1)}, bf16[256,1280]{1,0:T(8,128)(2,1)S(1)}, u32[]{:S(2)}) copy-start(bf16[256,1280]{1,0:T(8,128)(2,1)S(1)} %collective-permute-done.4) | copy-start | bytes 1966084
  34.0 10.4 %collective-permute-start.7 = (bf16[768,1280]{1,0:T(8,128)(2,1)S(1)}, bf16[768,1280]{1,0:T(8,128)(2,1)S(1)}, u32[]{:S(2)}, u32[]{:S(2)}) collective-permute-start(bf16[768,1280]{1,0:T(8,128)(2,1)S(1)} %constant_dynamic-update-slice_fusion.refs_0_), channel_id=1, source_target_pairs={{0,4},{4,0},{8,12},{12,8},{16,20},{20,16},{24,28},{28,24},{32,36},... | collective-permute-start | bytes 5898248 | tf_op jit(solution)/shard_map/ppermute | solution.py:431
  34.7 9.7 %collective-permute-start.8 = (bf16[768,1280]{1,0:T(8,128)(2,1)S(1)}, bf16[768,1280]{1,0:T(8,128)(2,1)S(1)}, u32[]{:S(2)}, u32[]{:S(2)}) collective-permute-start(bf16[768,1280]{1,0:T(8,128)(2,1)S(1)} %pad_maximum_fusion.refs_1_), channel_id=1, source_target_pairs={{0,4},{4,0},{8,12},{12,8},{16,20},{20,16},{24,28},{28,24},{32,36},... | collective-permute-start | bytes 5898248 | tf_op jit(solution)/shard_map/ppermute | solution.py:431
  34.8 25.0 %collective-permute-start.5 = (bf16[768,1280]{1,0:T(8,128)(2,1)S(1)}, bf16[768,1280]{1,0:T(8,128)(2,1)S(1)}, u32[]{:S(2)}, u32[]{:S(2)}) collective-permute-start(bf16[768,1280]{1,0:T(8,128)(2,1)S(1)} %constant_dynamic-update-slice_fusion.refs_0_), channel_id=1, source_target_pairs={{0,8},{4,36},{8,16},{12,44},{16,24},{20,52},{24,0},{28,60},{32,40}... | collective-permute-start | bytes 5898248 | tf_op jit(solution)/shard_map/ppermute | solution.py:428
  36.0 23.8 %collective-permute-start.6 = (bf16[768,1280]{1,0:T(8,128)(2,1)S(1)}, bf16[768,1280]{1,0:T(8,128)(2,1)S(1)}, u32[]{:S(2)}, u32[]{:S(2)}) collective-permute-start(bf16[768,1280]{1,0:T(8,128)(2,1)S(1)} %constant_dynamic-update-slice_fusion.refs_0_), channel_id=1, source_target_pairs={{0,24},{4,100},{8,0},{12,108},{16,8},{20,116},{24,16},{28,124},{32... | collective-permute-start | bytes 5898248 | tf_op jit(solution)/shard_map/ppermute | solution.py:428
  59.9 5.7 %collective-permute-start.11 = (bf16[768,1280]{1,0:T(8,128)(2,1)S(1)}, bf16[768,1280]{1,0:T(8,128)(2,1)S(1)}, u32[]{:S(2)}, u32[]{:S(2)}) collective-permute-start(bf16[768,1280]{1,0:T(8,128)(2,1)S(1)} %collective-permute-done.5.refs_0_), channel_id=1, source_target_pairs={{0,4},{4,0},{8,12},{12,8},{16,20},{20,16},{24,28},{28,24},{32,36},... | collective-permute-start | bytes 5898248 | tf_op jit(solution)/shard_map/ppermute | solution.py:431
  62.0 6.4 %collective-permute-start.12 = (bf16[768,1280]{1,0:T(8,128)(2,1)S(1)}, bf16[768,1280]{1,0:T(8,128)(2,1)S(1)}, u32[]{:S(2)}, u32[]{:S(2)}) collective-permute-start(bf16[768,1280]{1,0:T(8,128)(2,1)S(1)} %collective-permute-done.6.refs_1_), channel_id=1, source_target_pairs={{0,4},{4,0},{8,12},{12,8},{16,20},{20,16},{24,28},{28,24},{32,36},... | collective-permute-start | bytes 5898248 | tf_op jit(solution)/shard_map/ppermute | solution.py:431
  63.0 16.8 %collective-permute-start.10 = (bf16[512,1280]{1,0:T(8,128)(2,1)S(1)}, bf16[512,1280]{1,0:T(8,128)(2,1)S(1)}, u32[]{:S(2)}, u32[]{:S(2)}) collective-permute-start(bf16[512,1280]{1,0:T(8,128)(2,1)S(1)} %pad_maximum_fusion.2), channel_id=1, source_target_pairs={{0,24},{4,100},{8,0},{12,108},{16,8},{20,116},{24,16},{28,124},{32... | collective-permute-start | bytes 3932168 | tf_op jit(solution)/shard_map/ppermute | solution.py:428
  64.8 21.1 %copy-start.23 = (f32[1024]{0:T(1024)S(1)}, f32[1024]{0:T(1024)}, u32[]{:S(2)}) copy-start(f32[1024]{0:T(1024)} %param.18) | copy-start | bytes 12292
  64.8 21.1 %copy-start.24 = (f32[256]{0:T(256)S(1)}, f32[256]{0:T(256)}, u32[]{:S(2)}) copy-start(f32[256]{0:T(256)} %param.19) | copy-start | bytes 3076
  64.8 21.1 %copy-start.20 = (s32[32,16]{0,1:T(8,128)S(1)}, s32[32,16]{0,1:T(8,128)}, u32[]{:S(2)}) copy-start(s32[32,16]{0,1:T(8,128)} %param.20) | copy-start | bytes 6148
  64.8 21.1 %copy-start.21 = (s32[32,16]{0,1:T(8,128)S(1)}, s32[32,16]{0,1:T(8,128)}, u32[]{:S(2)}) copy-start(s32[32,16]{0,1:T(8,128)} %param.22) | copy-start | bytes 6148
  64.9 21.3 %copy-start.9 = (bf16[1024,1024]{1,0:T(8,128)(2,1)S(1)}, bf16[1024,1024]{1,0:T(8,128)(2,1)}, u32[]{:S(2)}) copy-start(bf16[1024,1024]{1,0:T(8,128)(2,1)} %get-tuple-element.53.x_ref) | copy-start | bytes 6291460
  64.9 18.0 %collective-permute-start.9 = (bf16[512,1280]{1,0:T(8,128)(2,1)S(1)}, bf16[512,1280]{1,0:T(8,128)(2,1)S(1)}, u32[]{:S(2)}, u32[]{:S(2)}) collective-permute-start(bf16[512,1280]{1,0:T(8,128)(2,1)S(1)} %pad_maximum_fusion.1), channel_id=1, source_target_pairs={{0,8},{4,36},{8,16},{12,44},{16,24},{20,52},{24,0},{28,60},{32,40}... | collective-permute-start | bytes 3932168 | tf_op jit(solution)/shard_map/ppermute | solution.py:428
  82.9 7.2 %collective-permute-start.13 = (bf16[512,1280]{1,0:T(8,128)(2,1)S(1)}, bf16[512,1280]{1,0:T(8,128)(2,1)S(1)}, u32[]{:S(2)}, u32[]{:S(2)}) collective-permute-start(bf16[512,1280]{1,0:T(8,128)(2,1)S(1)} %collective-permute-done.9.refs_0_), channel_id=1, source_target_pairs={{0,4},{4,0},{8,12},{12,8},{16,20},{20,16},{24,28},{28,24},{32,36},... | collective-permute-start | bytes 3932168 | tf_op jit(solution)/shard_map/ppermute | solution.py:431
  85.9 4.5 %collective-permute-start.14 = (bf16[512,1280]{1,0:T(8,128)(2,1)S(1)}, bf16[512,1280]{1,0:T(8,128)(2,1)S(1)}, u32[]{:S(2)}, u32[]{:S(2)}) collective-permute-start(bf16[512,1280]{1,0:T(8,128)(2,1)S(1)} %collective-permute-done.10.refs_1_), channel_id=1, source_target_pairs={{0,4},{4,0},{8,12},{12,8},{16,20},{20,16},{24,28},{28,24},{32,36},... | collective-permute-start | bytes 3932168 | tf_op jit(solution)/shard_map/ppermute | solution.py:431
  99.2 44.0 %all-to-all-start = ((bf16[32,64,768]{2,1,0:T(8,128)(2,1)}), bf16[32,64,768]{2,1,0:T(8,128)(2,1)S(1)}, u32[]{:S(2)}, u32[]{:S(2)}) async-start(bf16[32,64,768]{2,1,0:T(8,128)(2,1)} %get-tuple-element.57), calls=%async_computation | async-start | bytes 6291456 | tf_op jit(solution)/shard_map/all_to_all | solution.py:496
  117.2 30.9 %copy-start.22 = (s32[32,16]{0,1:T(8,128)S(1)}, s32[32,16]{0,1:T(8,128)}, u32[]{:S(2)}) copy-start(s32[32,16]{0,1:T(8,128)} %param.21) | copy-start | bytes 6148
  143.1 21.9 %all-to-all-start.1 = ((bf16[32,64,256]{2,1,0:T(8,128)(2,1)}), bf16[32,64,256]{2,1,0:T(8,128)(2,1)}, u32[]{:S(2)}, u32[]{:S(2)}) async-start(bf16[32,64,256]{2,1,0:T(8,128)(2,1)} %attend.3), calls=%async_computation.1 | async-start | bytes 2097152 | tf_op jit(solution)/shard_map/all_to_all | solution.py:496
  153.1 17.4 %collective-permute-start.15 = (bf16[256,768]{1,0:T(8,128)(2,1)}, bf16[256,768]{1,0:T(8,128)(2,1)S(1)}, u32[]{:S(2)}, u32[]{:S(2)}) collective-permute-start(bf16[256,768]{1,0:T(8,128)(2,1)} %get-tuple-element.59), channel_id=1, source_target_pairs={{0,1},{1,2},{2,3},{3,0},{4,5},{5,6},{6,7},{7,4},{8,9},{9,10},{10,1... | collective-permute-start | bytes 1179656 | tf_op jit(solution)/shard_map/ppermute | solution.py:499
  154.4 20.1 %collective-permute-start.16 = (bf16[256,768]{1,0:T(8,128)(2,1)}, bf16[256,768]{1,0:T(8,128)(2,1)S(1)}, u32[]{:S(2)}, u32[]{:S(2)}) collective-permute-start(bf16[256,768]{1,0:T(8,128)(2,1)} %get-tuple-element.60), channel_id=1, source_target_pairs={{0,2},{1,3},{2,0},{3,1},{4,6},{5,7},{6,4},{7,5},{8,10},{9,11},{10,... | collective-permute-start | bytes 1179656 | tf_op jit(solution)/shard_map/ppermute | solution.py:499
  156.8 17.6 %collective-permute-start.17 = (bf16[256,768]{1,0:T(8,128)(2,1)}, bf16[256,768]{1,0:T(8,128)(2,1)S(1)}, u32[]{:S(2)}, u32[]{:S(2)}) collective-permute-start(bf16[256,768]{1,0:T(8,128)(2,1)} %get-tuple-element.61), channel_id=1, source_target_pairs={{0,3},{1,0},{2,1},{3,2},{4,7},{5,4},{6,5},{7,6},{8,11},{9,8},{10,9... | collective-permute-start | bytes 1179656 | tf_op jit(solution)/shard_map/ppermute | solution.py:499
  166.8 11.8 %collective-permute-start.18 = (bf16[256,256]{1,0:T(8,128)(2,1)S(1)}, bf16[256,256]{1,0:T(8,128)(2,1)S(1)}, u32[]{:S(2)}, u32[]{:S(2)}) collective-permute-start(bf16[256,256]{1,0:T(8,128)(2,1)S(1)} %get-tuple-element.64), channel_id=1, source_target_pairs={{0,1},{1,2},{2,3},{3,0},{4,5},{5,6},{6,7},{7,4},{8,9},{9,10},{10,1... | collective-permute-start | bytes 393224 | tf_op jit(solution)/shard_map/ppermute | solution.py:499
  168.0 12.0 %collective-permute-start.19 = (bf16[256,256]{1,0:T(8,128)(2,1)S(1)}, bf16[256,256]{1,0:T(8,128)(2,1)S(1)}, u32[]{:S(2)}, u32[]{:S(2)}) collective-permute-start(bf16[256,256]{1,0:T(8,128)(2,1)S(1)} %get-tuple-element.65), channel_id=1, source_target_pairs={{0,2},{1,3},{2,0},{3,1},{4,6},{5,7},{6,4},{7,5},{8,10},{9,11},{10,... | collective-permute-start | bytes 393224 | tf_op jit(solution)/shard_map/ppermute | solution.py:499
  170.5 9.6 %collective-permute-start.20 = (bf16[256,256]{1,0:T(8,128)(2,1)S(1)}, bf16[256,256]{1,0:T(8,128)(2,1)S(1)}, u32[]{:S(2)}, u32[]{:S(2)}) collective-permute-start(bf16[256,256]{1,0:T(8,128)(2,1)S(1)} %get-tuple-element.66), channel_id=1, source_target_pairs={{0,3},{1,0},{2,1},{3,2},{4,7},{5,4},{6,5},{7,6},{8,11},{9,8},{10,9... | collective-permute-start | bytes 393224 | tf_op jit(solution)/shard_map/ppermute | solution.py:499
  (18 other events, 67.6 us)

commit v4 on v3

--- a/solution.py
+++ b/solution.py
@@ -13,7 +13,7 @@
 SIDE = 4
 MIB = 1024 * 1024
 FIRST_HEADS = 6
-PIECES = (12, 12, 4, 4)
+PIECES = (6, 12, 6, 4, 4)
 
 rope_base = 1000000.0
 norm_epsilon = 1e-06
@@ -74,17 +74,54 @@
                     return found
 
                 both, low, high = (0, 1), (0,), (1,)
-                beside = [(1, 0, both), (3, 0, both), (2, 0, both)]
-                straight = [(0, 0, both), (0, 1, both), (0, 3, both)]
-                ahead = [(1, 1, both), (3, 1, both), (2, 1, both)]
-                behind = [(1, 3, both), (3, 3, both), (2, 3, both)]
+                near = [(1, 0, both), (3, 0, both), (2, 0, both)]
+                near += [(0, 0, both), (0, 1, both), (0, 3, both)]
+                corners = [(1, 1, both), (3, 1, both), (2, 1, both)]
+                corners += [(1, 3, both), (3, 3, both), (2, 3, both)]
                 far = [(1, 2, both), (2, 2, low), (0, 2, low)]
                 far += [(3, 2, both), (2, 2, high), (0, 2, high)]
                 order = []
-                for offsets in (beside + straight, ahead + behind, far):
+                for offsets in (near, corners, far):
                     order += blocks(core, offsets) + blocks(1 - core, offsets)
                 table[device_index(y, z, core)] = order
     return table
+
+
+def beside_kernel(query_ref, keyval_ref, out_ref, sems):
+    cut = FIRST_HEADS * HD
+    middle = cut + keyval_ref.shape[1]
+    copies = [
+        pltpu.make_async_copy(
+            query_ref.at[:, pl.ds(0, cut)], out_ref.at[:, pl.ds(0, cut)], sems.at[0]
+        ),
+        pltpu.make_async_copy(
+            keyval_ref, out_ref.at[:, pl.ds(cut, middle - cut)], sems.at[1]
+        ),
+        pltpu.make_async_copy(
+            query_ref.at[:, pl.ds(cut, query_ref.shape[1] - cut)],
+            out_ref.at[:, pl.ds(middle, out_ref.shape[1] - middle)],
+            sems.at[2],
+        ),
+    ]
+    for copy in copies:
+        copy.start()
+    for copy in copies:
+        copy.wait()
+
+
+def side_by_side(w_query, w_keyval):
+    rows = w_query.shape[0]
+    return pl.pallas_call(
+        beside_kernel,
+        in_specs=[pl.BlockSpec(memory_space=pltpu.HBM)] * 2,
+        out_specs=pl.BlockSpec(memory_space=pltpu.VMEM),
+        out_shape=jax.ShapeDtypeStruct(
+            (rows, w_query.shape[1] + w_keyval.shape[1]), w_query.dtype
+        ),
+        scratch_shapes=[pltpu.SemaphoreType.DMA((3,))],
+        compiler_params=pltpu.CompilerParams(vmem_limit_bytes=4 * MIB),
+        name="side_by_side",
+    )(w_query, w_keyval)
 
 
 def scaled_columns(order_ref, place, hidden_ref, gain_ref, scale, refs):
@@ -330,35 +367,24 @@
     )(dest, lengths, total, x, bias, cosine, sine, *keyvals, *pieces)
 
 
-def place_kernel(source_ref, received_ref, *refs):
-    parts, sems = refs[:-1], refs[-1]
+def place_kernel(source_ref, received_ref, *parts):
     per_part = parts[0].shape[0] // GROUP
-    copies = [
-        pltpu.make_async_copy(
-            received_ref.at[source_ref[k * per_part + j]],
-            part.at[pl.ds(j * GROUP, GROUP)],
-            sems.at[k * per_part + j],
-        )
-        for k, part in enumerate(parts)
-        for j in range(per_part)
-    ]
-    for copy in copies:
-        copy.start()
-    for copy in copies:
-        copy.wait()
+    for k, part in enumerate(parts):
+        for j in range(per_part):
+            part[j * GROUP : (j + 1) * GROUP, :] = received_ref[source_ref[k * per_part + j]]
 
 
 def place(source, received, parts):
     packs, group, width = received.shape
     per_part = source.shape[0] // parts
+    resident = pl.BlockSpec(memory_space=pltpu.VMEM)
     return pl.pallas_call(
         place_kernel,
         grid_spec=pltpu.PrefetchScalarGridSpec(
             num_scalar_prefetch=1,
             grid=(1,),
-            in_specs=[pl.BlockSpec(memory_space=pltpu.HBM)],
-            out_specs=[pl.BlockSpec(memory_space=pltpu.VMEM)] * parts,
-            scratch_shapes=[pltpu.SemaphoreType.DMA((source.shape[0],))],
+            in_specs=[resident],
+            out_specs=[resident] * parts,
         ),
         out_shape=[jax.ShapeDtypeStruct((per_part * group, width), received.dtype)] * parts,
         compiler_params=pltpu.CompilerParams(vmem_limit_bytes=8 * MIB),
@@ -402,6 +428,10 @@
         compiler_params=pltpu.CompilerParams(vmem_limit_bytes=8 * MIB),
         name="join",
     )(order, *given, *parts)
+
+
+def held_until(value, *others):
+    return lax.optimization_barrier((value, *others))[0]
 
 
 def per_device(
@@ -430,31 +460,45 @@
     def swap(piece):
         return lax.ppermute(piece, "dp", swap_pairs())
 
+    own_dest = lax.dynamic_index_in_dim(group_dest, own, 0, keepdims=False)
+    own_length = lax.dynamic_index_in_dim(group_length, own, 0, keepdims=False)
+    slot = group_offset // GROUP
+    hits = (group_dest == own)[None] & (
+        slot[None] == jnp.arange(groups, dtype=jnp.int32)[:, None, None]
+    )
+    packs_of = jnp.arange(packs, dtype=jnp.int32)[None, :, None]
+    source = jnp.sum(jnp.where(hits, packs_of, 0), (1, 2)).reshape(planes, -1)
+    step = jnp.arange(planes, dtype=jnp.int32)
+    source = source[(plane + step) % planes].reshape(-1)
+    joins = (plane - step) % planes
+    plan = own_dest, own_length, source, joins
+
     cut = FIRST_HEADS * HD
-    weights = jnp.concatenate([w_query[:, :cut], w_keyval, w_query[:, cut:]], 1)
+    weights = side_by_side(w_query, w_keyval)
     bias = jnp.concatenate([query_bias[:cut], keyval_bias, query_bias[cut:]])[None]
     rows_held = weights.shape[0]
     half = rows_held // 2
     order = lax.dynamic_index_in_dim(jnp.asarray(source_table()), own, 0, keepdims=False)
-    near = [first(weights, 1), first(weights, -1), first(weights, 2)]
-    own_ahead, own_behind = second(weights, 1), second(weights, -1)
     widths = [count * rows_held for count in PIECES]
     gain = norm_gain[None]
-    scale, x_early = norm(order, hidden_states, gain, widths[:1])
-
-    near, own_ahead, own_behind, x_early, scale = lax.optimization_barrier(
-        (near, own_ahead, own_behind, x_early, scale)
-    )
-    beside = jnp.concatenate(near)
+
+    near = [first(weights, 1), first(weights, -1), first(weights, 2)]
+    near += [second(weights, 1), second(weights, -1)]
+    scale, x_near = norm(order, hidden_states, gain, widths[:1])
+    near, scale, x_near, plan, bias = lax.optimization_barrier((near, scale, x_near, plan, bias))
+    own_dest, own_length, source, joins = plan
+
+    own_ahead, own_behind = near[3:]
+    beside = jnp.concatenate(near[:3])
+    ahead, behind = second(beside, 1), second(beside, -1)
+    x_middle, x_corners, x_far, x_last = norm(
+        order, hidden_states, gain, widths[1:], scale, widths[0] // half
+    )
     straight = jnp.concatenate([weights, own_ahead, own_behind])
-    ahead, behind = second(beside, 1), second(beside, -1)
-    total = project(None, x_early, [beside, straight, swap(beside), swap(straight)])
-    x_middle, x_far, x_last = norm(
-        order, hidden_states, gain, widths[1:], scale, widths[0] // half
-    )
-
-    ahead, behind, total, x_middle, x_far, x_last = lax.optimization_barrier(
-        (ahead, behind, total, x_middle, x_far, x_last)
+    total = project(None, x_near, [beside, straight])
+
+    ahead, behind, total, x_middle, x_corners, x_far, x_last = lax.optimization_barrier(
+        (ahead, behind, total, x_middle, x_corners, x_far, x_last)
     )
     far = [
         second(
@@ -470,27 +514,17 @@
             -1,
         ),
     ]
-    total = project(total, x_middle, [ahead, behind, swap(ahead), swap(behind)])
+    near = [swap(held_until(piece, ahead)) for piece in (beside, straight)]
+    total = project(total, x_middle, [*near, ahead, behind])
+    total = project(total, x_corners, [swap(ahead), swap(behind)])
     far, total = lax.optimization_barrier((far, total))
     last = [swap(piece) for piece in far]
     total = project(total, x_far, far)
 
-    own_dest = lax.dynamic_index_in_dim(group_dest, own, 0, keepdims=False)
-    own_length = lax.dynamic_index_in_dim(group_length, own, 0, keepdims=False)
     middle = cut + w_keyval.shape[1]
     given = (own_dest, own_length, total, x_last, bias)
     first_sent, keyval = attend(*given, None, last, packs, slice(0, middle))
     (second_sent,) = attend(*given, keyval, last, packs, slice(middle, weights.shape[1]))
-
-    slot = group_offset // GROUP
-    hits = (group_dest == own)[None] & (
-        slot[None] == jnp.arange(groups, dtype=jnp.int32)[:, None, None]
-    )
-    packs_of = jnp.arange(packs, dtype=jnp.int32)[None, :, None]
-    source = jnp.sum(jnp.where(hits, packs_of, 0), (1, 2)).reshape(planes, -1)
-    step = jnp.arange(planes, dtype=jnp.int32)
-    source = source[(plane + step) % planes].reshape(-1)
-    joins = (plane - step) % planes
 
     def exchanged(sent):
         received = lax.all_to_all(sent, "dp", split_axis=0, concat_axis=0, tiled=True)

time: 182 us -> 177 us (0.973)
  waiting for transfers between devices: 57.9 us -> 51.6 us
    ppermute x3, waiting for transfers between devices: 5.41 us -> 1.04 us  [first(): return lax.ppermute(piece, 'dp', shift_pairs(by, 0))]
    all_to_all x2, waiting for transfers between devices: 33 us -> 36.4 us  [exchanged(): lax.all_to_all(sent, 'dp', split_axis=0, concat_axis=0, tiled=True)]
    ppermute x6, waiting for transfers between devices: 6.68 us -> 3.42 us  [exchanged(): lax.ppermute(parts[k], 'mp', [(i, (i + k) % planes) for i in range(planes)])]
    pallas_call x2, Pallas kernels: 5.48 us -> 3.46 us  [place(): pl.pallas_call(place_kernel, grid_spec=pltpu.PrefetchScalarGridSpec(num_s...]
    slice x2 -> x0, local copies, waits for them, and re-layouts: 1.95 us -> none  [per_device(): weights = jnp.concatenate([w_query[:, :cut], w_keyval, w_query[:, cut:]], 1)]
    pallas_call x3 -> x4, Pallas kernels: 22 us -> 23.1 us  [project(): pl.pallas_call(add_kernel if totals else first_kernel, grid=(rows // tile...]
    unnamed x52 -> x48, local copies, waits for them, and re-layouts: 18.8 us -> 19.2 us
  transfers between devices with their start and end apart: 23 -> 23, of which waited for: 12 -> 10; matrix products, arithmetic and copies ran while one was open for 1% -> 3% of each run, Pallas kernels for 27% -> 28%
where the time goes in v4:
time: 177 us; the launch traced here: 176 us
  Pallas kernels  58.2 us (33%)
  waiting for transfers between devices  51.6 us (29%)
  starting transfers between devices  38.6 us (22%)
  local copies, waits for them, and re-layouts  24.6 us (14%)
  other arithmetic  2.83 us (2%)
    all_to_all x2, waiting for transfers between devices, exchanged(): lax.all_to_all(sent, 'dp', split_axis=0, concat_axis=0, tiled=True)  36.4 us
    pallas_call x4, Pallas kernels, project(): pl.pallas_call(add_kernel if totals else first_kernel, grid=(rows // tile...  23.1 us
    unnamed x48, local copies, waits for them, and re-layouts  19.2 us
    pallas_call x2, Pallas kernels, attend(): pl.pallas_call(functools.partial(attend_kernel, columns), grid_spec=pltpu...  14.3 us
    pallas_call x2, Pallas kernels, norm(): pl.pallas_call(norm_kernel if scale is None else functools.partial(norm_r...  14.1 us
    ppermute x6, starting transfers between devices, exchanged(): lax.ppermute(parts[k], 'mp', [(i, (i + k) % planes) for i in range(planes)])  9.7 us
    all_to_all x2, starting transfers between devices, exchanged(): lax.all_to_all(sent, 'dp', split_axis=0, concat_axis=0, tiled=True)  9.05 us
    ppermute x6, starting transfers between devices, second(): return lax.ppermute(piece, 'dp', shift_pairs(0, by))  8.32 us
  transfers between devices with their start and end apart: 23, of which 10 were waited for; matrix products, arithmetic and copies ran while one was open for 3% of the time, Pallas kernels for 28%

profile of v4, /device:TPU:1, one launch (start us, length us, event | category | flops | bytes accessed | tf_op | source)
XLA Modules:
  0.0 176.3 jit_solution(6269494946842843567)
XLA Ops:
  2.0 2.5 %collective-permute-start = (bf16[256,1280]{1,0:T(8,128)(2,1)S(1)}, bf16[256,1280]{1,0:T(8,128)(2,1)S(1)}, u32[]{:S(2)}, u32[]{:S(2)}) collective-permute-start(bf16[256,1280]{1,0:T(8,128)(2,1)S(1)} %side_by_side.1), channel_id=1, source_target_pairs={{0,32},{4,12},{8,40},{12,20},{16,48},{20,28},{24,56},{28,4},{32,64... | collective-permute-start | bytes 1966088 | tf_op jit(solution)/shard_map/ppermute | solution.py:455
  4.6 2.2 %collective-permute-start.1 = (bf16[256,1280]{1,0:T(8,128)(2,1)S(1)}, bf16[256,1280]{1,0:T(8,128)(2,1)S(1)}, u32[]{:S(2)}, u32[]{:S(2)}) collective-permute-start(bf16[256,1280]{1,0:T(8,128)(2,1)S(1)} %side_by_side.1), channel_id=1, source_target_pairs={{0,96},{4,28},{8,104},{12,4},{16,112},{20,12},{24,120},{28,20},{32... | collective-permute-start | bytes 1966088 | tf_op jit(solution)/shard_map/ppermute | solution.py:455
  9.3 1.4 collective-permute-start.4
  16.3 5.8 %copy-done.2 = bf16[1024,8192]{1,0:T(8,128)(2,1)S(1)} copy-done((bf16[1024,8192]{1,0:T(8,128)(2,1)S(1)}, bf16[1024,8192]{1,0:T(8,128)(2,1)}, u32[]{:S(2)}) %copy-start.2) | copy-done | bytes 16777240
  22.8 6.4 %norm.2 = (f32[1024,1]{1,0:T(8,128)S(1)}, bf16[1024,1536]{1,0:T(8,128)(2,1)}) custom-call(s32[64]{0:T(128)S(1)} %fusion.3.order_ref, bf16[1024,8192]{1,0:T(8,128)(2,1)S(1)} %copy-done.2, f32[1,8192]{1,0:T(1,128)S(1)} %bitcast.6), custom_call_target="tpu_custom_call" | custom-call | flops 50331648 | bytes 19922944 | tf_op jit(solution)/shard_map/norm/pallas_call | solution.py:166
  30.4 1.5 constant_dynamic-update-slice_fusion.refs_0_
  33.0 1.7 collective-permute-start.6
  34.7 7.7 %norm.3 = (bf16[1024,3072]{1,0:T(8,128)(2,1)}, bf16[1024,1536]{1,0:T(8,128)(2,1)}, bf16[1024,1024]{1,0:T(8,128)(2,1)}, bf16[1024,1024]{1,0:T(8,128)(2,1)}) custom-call(s32[64]{0:T(128)S(1)} %fusion.3.order_ref, bf16[1024,8192]{1,0:T(8,128)(2,1)S(1)} %copy-done.2, f32[1,8192]{1,0:T(1,128)S(1)} %bitcast.7, f32[1024,1]{1,0:T(8,128)S(1)} %get-tuple-element.57.scale_ref), custom_call_target="tpu_custom_call" | custom-call | flops 50331648 | bytes 30408704 | tf_op jit(solution)/shard_map/norm/pallas_call | solution.py:166
  42.5 2.0 %copy-done.18 = bf16[1024,1536]{1,0:T(8,128)(2,1)S(1)} copy-done((bf16[1024,1536]{1,0:T(8,128)(2,1)S(1)}, bf16[1024,1536]{1,0:T(8,128)(2,1)}, u32[]{:S(2)}) %copy-start.18) | copy-done | bytes 3145752
  44.6 4.7 %project.4.total_ref = f32[1024,1280]{1,0:T(8,128)S(1)} custom-call(bf16[1024,1536]{1,0:T(8,128)(2,1)S(1)} %copy-done.18, bf16[768,1280]{1,0:T(8,128)(2,1)S(1)} %constant_dynamic-update-slice_fusion.refs_0_, bf16[768,1280]{1,0:T(8,128)(2,1)S(1)} %pad_maximum_fusion.refs_1_), custom_call_target="tpu_custom_call" | custom-call | flops 4026531840 | bytes 17563648 | tf_op jit(solution)/shard_map/project/pallas_call | solution.py:215
  49.3 7.7 %collective-permute-done.5.refs_2_ = bf16[768,1280]{1,0:T(8,128)(2,1)S(1)} collective-permute-done((bf16[768,1280]{1,0:T(8,128)(2,1)S(1)}, bf16[768,1280]{1,0:T(8,128)(2,1)S(1)}, u32[]{:S(2)}, u32[]{:S(2)}) %collective-permute-start.5) | collective-permute-done | bytes 1966112 | tf_op jit(solution)/shard_map/ppermute | solution.py:458
  57.0 2.2 %collective-permute-start.10 = (bf16[768,1280]{1,0:T(8,128)(2,1)S(1)}, bf16[768,1280]{1,0:T(8,128)(2,1)S(1)}, u32[]{:S(2)}, u32[]{:S(2)}) collective-permute-start(bf16[768,1280]{1,0:T(8,128)(2,1)S(1)} %pad_maximum_fusion.refs_1_), channel_id=1, source_target_pairs={{0,4},{4,0},{8,12},{12,8},{16,20},{20,16},{24,28},{28,24},{32,36},... | collective-permute-start | bytes 5898248 | tf_op jit(solution)/shard_map/ppermute | solution.py:461
  60.7 1.7 collective-permute-start.8
  63.9 1.7 collective-permute-done.9.refs_0_
  65.6 9.5 %project.5.total_ref = f32[1024,1280]{1,0:T(8,128)S(1)} custom-call(f32[1024,1280]{1,0:T(8,128)S(1)} %project.4.total_ref, bf16[1024,3072]{1,0:T(8,128)(2,1)S(1)} %bitcast.9, bf16[768,1280]{1,0:T(8,128)(2,1)S(1)} %collective-permute-done.9.refs_0_, bf16[768,1280]{1,0:T(8,128)(2,1)S(1)} %collective-permute-done.10.refs_1_, ...), custom_call_target="tpu_custom_call", output_to_operand_aliasing={{}: (0, {})} | custom-call | flops 8053063680 | bytes 24641536 | tf_op jit(solution)/shard_map/project/pallas_call | solution.py:215
  75.1 5.2 %project.6.total_ref = f32[1024,1280]{1,0:T(8,128)S(1)} custom-call(f32[1024,1280]{1,0:T(8,128)S(1)} %project.5.total_ref, bf16[1024,1536]{1,0:T(8,128)(2,1)S(1)} %copy-done.9, bf16[768,1280]{1,0:T(8,128)(2,1)S(1)} %collective-permute-done.11.refs_0_, bf16[768,1280]{1,0:T(8,128)(2,1)S(1)} %collective-permute-done.12.refs_1_), custom_call_target="tpu_custom_call", output_to_operand_aliasing={{}: (0, {})} | custom-call | flops 4026531840 | bytes 17563648 | tf_op jit(solution)/shard_map/project/pallas_call | solution.py:215
  80.7 2.9 %collective-permute-start.13 = (bf16[512,1280]{1,0:T(8,128)(2,1)S(1)}, bf16[512,1280]{1,0:T(8,128)(2,1)S(1)}, u32[]{:S(2)}, u32[]{:S(2)}) collective-permute-start(bf16[512,1280]{1,0:T(8,128)(2,1)S(1)} %collective-permute-done.7.refs_0_), channel_id=1, source_target_pairs={{0,4},{4,0},{8,12},{12,8},{16,20},{20,16},{24,28},{28,24},{32,36},... | collective-permute-start | bytes 3932168 | tf_op jit(solution)/shard_map/ppermute | solution.py:461
  83.6 3.7 %project.7.total_ref = f32[1024,1280]{1,0:T(8,128)S(1)} custom-call(f32[1024,1280]{1,0:T(8,128)S(1)} %project.6.total_ref, bf16[1024,1024]{1,0:T(8,128)(2,1)S(1)} %copy-done.10, bf16[512,1280]{1,0:T(8,128)(2,1)S(1)} %collective-permute-done.7.refs_0_, bf16[512,1280]{1,0:T(8,128)(2,1)S(1)} %collective-permute-done.8.refs_1_), custom_call_target="tpu_custom_call", output_to_operand_aliasing={{}: (0, {})} | custom-call | flops 2684354560 | bytes 15204352 | tf_op jit(solution)/shard_map/project/pallas_call | solution.py:215
  88.2 8.0 %attend.2 = (bf16[32,64,768]{2,1,0:T(8,128)(2,1)}, bf16[1024,256]{1,0:T(8,128)(2,1)S(1)}) custom-call(s32[16]{0:T(128)S(1)} %get-tuple-element.49.dest_ref, s32[16]{0:T(128)S(1)} %get-tuple-element.50.length_ref, f32[1024,1280]{1,0:T(8,128)S(1)} %project.7.total_ref, bf16[1024,1024]{1,0:T(8,128)(2,1)S(1)} %copy-done.3, ...), custom_call_target="tpu_custom_call" | custom-call | flops 2147483648 | bytes 12582912 | tf_op jit(solution)/shard_map/attend/pallas_call | solution.py:343
  97.1 4.1 %all-to-all-start = ((bf16[32,64,768]{2,1,0:T(8,128)(2,1)}), bf16[32,64,768]{2,1,0:T(8,128)(2,1)S(1)}, u32[]{:S(2)}, u32[]{:S(2)}) async-start(bf16[32,64,768]{2,1,0:T(8,128)(2,1)} %get-tuple-element.75), calls=%async_computation | async-start | bytes 6291456 | tf_op jit(solution)/shard_map/all_to_all | solution.py:530
  101.2 2.5 %copy-done.1 = f32[1024,1280]{1,0:T(8,128)S(1)} copy-done((f32[1024,1280]{1,0:T(8,128)S(1)}, f32[1024,1280]{1,0:T(8,128)}, u32[]{:S(2)}) %copy-start.1) | copy-done | bytes 5242904
  103.7 1.6 copy-done.4
  108.9 6.2 %attend.3 = bf16[32,64,256]{2,1,0:T(8,128)(2,1)} custom-call(s32[16]{0:T(128)S(1)} %get-tuple-element.49.dest_ref, s32[16]{0:T(128)S(1)} %get-tuple-element.50.length_ref, f32[1024,1280]{1,0:T(8,128)S(1)} %copy-done.1, bf16[1024,1024]{1,0:T(8,128)(2,1)S(1)} %copy-done.4, f32[1,1280]{1,0:T(1,128)S(1)} %broadcast_in_dim.26.bias_ref, ...), custom_call_target="tpu_custom_call" | custom-call | flops 536870912 | bytes 4718592 | tf_op jit(solution)/shard_map/attend/pallas_call | solution.py:343
  115.1 25.9 %all-to-all-done.received_ref = bf16[32,64,768]{2,1,0:T(8,128)(2,1)S(1)} async-done(((bf16[32,64,768]{2,1,0:T(8,128)(2,1)}), bf16[32,64,768]{2,1,0:T(8,128)(2,1)S(1)}, u32[]{:S(2)}, u32[]{:S(2)}) %all-to-all-start) | async-done | bytes 3145760 | tf_op jit(solution)/shard_map/all_to_all | solution.py:530
  141.0 5.0 %all-to-all-start.1 = ((bf16[32,64,256]{2,1,0:T(8,128)(2,1)}), bf16[32,64,256]{2,1,0:T(8,128)(2,1)}, u32[]{:S(2)}, u32[]{:S(2)}) async-start(bf16[32,64,256]{2,1,0:T(8,128)(2,1)} %attend.3), calls=%async_computation.1 | async-start | bytes 2097152 | tf_op jit(solution)/shard_map/all_to_all | solution.py:530
  146.0 1.7 place.2
  148.9 2.4 %collective-permute-start.16 = (bf16[256,768]{1,0:T(8,128)(2,1)}, bf16[256,768]{1,0:T(8,128)(2,1)S(1)}, u32[]{:S(2)}, u32[]{:S(2)}) collective-permute-start(bf16[256,768]{1,0:T(8,128)(2,1)} %get-tuple-element.78), channel_id=1, source_target_pairs={{0,2},{1,3},{2,0},{3,1},{4,6},{5,7},{6,4},{7,5},{8,10},{9,11},{10,... | collective-permute-start | bytes 1179656 | tf_op jit(solution)/shard_map/ppermute | solution.py:533
  152.5 10.5 %all-to-all-done.1.received_ref = bf16[32,64,256]{2,1,0:T(8,128)(2,1)} async-done(((bf16[32,64,256]{2,1,0:T(8,128)(2,1)}), bf16[32,64,256]{2,1,0:T(8,128)(2,1)}, u32[]{:S(2)}, u32[]{:S(2)}) %all-to-all-start.1) | async-done | bytes 1048608 | tf_op jit(solution)/shard_map/all_to_all | solution.py:530
  163.0 1.8 %place.3 = (bf16[256,256]{1,0:T(8,128)(2,1)S(1)}, bf16[256,256]{1,0:T(8,128)(2,1)S(1)}, bf16[256,256]{1,0:T(8,128)(2,1)S(1)}, bf16[256,256]{1,0:T(8,128)(2,1)S(1)}) custom-call(s32[16]{0:T(128)S(1)} %reshape.58.source_ref, bf16[32,64,256]{2,1,0:T(8,128)(2,1)} %all-to-all-done.1.received_ref), custom_call_target="tpu_custom_call" | custom-call | tf_op jit(solution)/shard_map/place/pallas_call | solution.py:381
  166.1 2.4 %collective-permute-start.19 = (bf16[256,256]{1,0:T(8,128)(2,1)S(1)}, bf16[256,256]{1,0:T(8,128)(2,1)S(1)}, u32[]{:S(2)}, u32[]{:S(2)}) collective-permute-start(bf16[256,256]{1,0:T(8,128)(2,1)S(1)} %get-tuple-element.83), channel_id=1, source_target_pairs={{0,2},{1,3},{2,0},{3,1},{4,6},{5,7},{6,4},{7,5},{8,10},{9,11},{10,... | collective-permute-start | bytes 393224 | tf_op jit(solution)/shard_map/ppermute | solution.py:533
  169.7 1.7 join.2.refs_0_
  172.8 2.0 %collective-permute-done.19.refs_3_ = bf16[256,256]{1,0:T(8,128)(2,1)S(1)} collective-permute-done((bf16[256,256]{1,0:T(8,128)(2,1)S(1)}, bf16[256,256]{1,0:T(8,128)(2,1)S(1)}, u32[]{:S(2)}, u32[]{:S(2)}) %collective-permute-start.19) | collective-permute-done | bytes 131104 | tf_op jit(solution)/shard_map/ppermute | solution.py:533
  (102 shorter events, 29.4 us)
Async XLA Ops:
  2.0 27.2 %collective-permute-start = (bf16[256,1280]{1,0:T(8,128)(2,1)S(1)}, bf16[256,1280]{1,0:T(8,128)(2,1)S(1)}, u32[]{:S(2)}, u32[]{:S(2)}) collective-permute-start(bf16[256,1280]{1,0:T(8,128)(2,1)S(1)} %side_by_side.1), channel_id=1, source_target_pairs={{0,32},{4,12},{8,40},{12,20},{16,48},{20,28},{24,56},{28,4},{32,64... | collective-permute-start | bytes 1966088 | tf_op jit(solution)/shard_map/ppermute | solution.py:455
  4.6 24.7 %collective-permute-start.1 = (bf16[256,1280]{1,0:T(8,128)(2,1)S(1)}, bf16[256,1280]{1,0:T(8,128)(2,1)S(1)}, u32[]{:S(2)}, u32[]{:S(2)}) collective-permute-start(bf16[256,1280]{1,0:T(8,128)(2,1)S(1)} %side_by_side.1), channel_id=1, source_target_pairs={{0,96},{4,28},{8,104},{12,4},{16,112},{20,12},{24,120},{28,20},{32... | collective-permute-start | bytes 1966088 | tf_op jit(solution)/shard_map/ppermute | solution.py:455
  6.8 23.5 %collective-permute-start.2 = (bf16[256,1280]{1,0:T(8,128)(2,1)S(1)}, bf16[256,1280]{1,0:T(8,128)(2,1)}, u32[]{:S(2)}, u32[]{:S(2)}) collective-permute-start(bf16[256,1280]{1,0:T(8,128)(2,1)S(1)} %side_by_side.1), channel_id=1, source_target_pairs={{0,64},{4,20},{8,72},{12,28},{16,80},{20,4},{24,88},{28,12},{32,96... | collective-permute-start | bytes 1966088 | tf_op jit(solution)/shard_map/ppermute | solution.py:455
  8.0 22.3 %collective-permute-start.3 = (bf16[256,1280]{1,0:T(8,128)(2,1)S(1)}, bf16[256,1280]{1,0:T(8,128)(2,1)S(1)}, u32[]{:S(2)}, u32[]{:S(2)}) collective-permute-start(bf16[256,1280]{1,0:T(8,128)(2,1)S(1)} %side_by_side.1), channel_id=1, source_target_pairs={{0,8},{4,36},{8,16},{12,44},{16,24},{20,52},{24,0},{28,60},{32,40}... | collective-permute-start | bytes 1966088 | tf_op jit(solution)/shard_map/ppermute | solution.py:458
  9.3 21.0 %collective-permute-start.4 = (bf16[256,1280]{1,0:T(8,128)(2,1)S(1)}, bf16[256,1280]{1,0:T(8,128)(2,1)S(1)}, u32[]{:S(2)}, u32[]{:S(2)}) collective-permute-start(bf16[256,1280]{1,0:T(8,128)(2,1)S(1)} %side_by_side.1), channel_id=1, source_target_pairs={{0,24},{4,100},{8,0},{12,108},{16,8},{20,116},{24,16},{28,124},{32... | collective-permute-start | bytes 1966088 | tf_op jit(solution)/shard_map/ppermute | solution.py:458
  30.3 29.4 %copy-start.19 = (bf16[256,1280]{1,0:T(8,128)(2,1)}, bf16[256,1280]{1,0:T(8,128)(2,1)S(1)}, u32[]{:S(2)}) copy-start(bf16[256,1280]{1,0:T(8,128)(2,1)S(1)} %collective-permute-done.3) | copy-start | bytes 1966084
  30.3 29.4 %copy-start.20 = (bf16[256,1280]{1,0:T(8,128)(2,1)}, bf16[256,1280]{1,0:T(8,128)(2,1)S(1)}, u32[]{:S(2)}) copy-start(bf16[256,1280]{1,0:T(8,128)(2,1)S(1)} %collective-permute-done.4) | copy-start | bytes 1966084
  31.9 25.1 %collective-permute-start.5 = (bf16[768,1280]{1,0:T(8,128)(2,1)S(1)}, bf16[768,1280]{1,0:T(8,128)(2,1)S(1)}, u32[]{:S(2)}, u32[]{:S(2)}) collective-permute-start(bf16[768,1280]{1,0:T(8,128)(2,1)S(1)} %constant_dynamic-update-slice_fusion.refs_0_), channel_id=1, source_target_pairs={{0,8},{4,36},{8,16},{12,44},{16,24},{20,52},{24,0},{28,60},{32,40}... | collective-permute-start | bytes 5898248 | tf_op jit(solution)/shard_map/ppermute | solution.py:458
  33.0 24.0 %collective-permute-start.6 = (bf16[768,1280]{1,0:T(8,128)(2,1)S(1)}, bf16[768,1280]{1,0:T(8,128)(2,1)S(1)}, u32[]{:S(2)}, u32[]{:S(2)}) collective-permute-start(bf16[768,1280]{1,0:T(8,128)(2,1)S(1)} %constant_dynamic-update-slice_fusion.refs_0_), channel_id=1, source_target_pairs={{0,24},{4,100},{8,0},{12,108},{16,8},{20,116},{24,16},{28,124},{32... | collective-permute-start | bytes 5898248 | tf_op jit(solution)/shard_map/ppermute | solution.py:458
  42.4 23.2 %slice-start = ((s8[6291456]{0:T(1024)(128)(4,1)}), s8[4194304]{0:T(1024)(128)(4,1)S(1)}, s32[]{:S(2)}) async-start(s8[6291456]{0:T(1024)(128)(4,1)} %bitcast.8), calls=%async_computation.2 | async-start | bytes 8388608
  44.6 21.0 %slice-start.1 = ((s8[6291456]{0:T(1024)(128)(4,1)}), s8[2097152]{0:T(1024)(128)(4,1)S(1)}, s32[]{:S(2)}) async-start(s8[6291456]{0:T(1024)(128)(4,1)} %bitcast.8), calls=%async_computation.3 | async-start | bytes 4194304
  57.0 5.8 %collective-permute-start.10 = (bf16[768,1280]{1,0:T(8,128)(2,1)S(1)}, bf16[768,1280]{1,0:T(8,128)(2,1)S(1)}, u32[]{:S(2)}, u32[]{:S(2)}) collective-permute-start(bf16[768,1280]{1,0:T(8,128)(2,1)S(1)} %pad_maximum_fusion.refs_1_), channel_id=1, source_target_pairs={{0,4},{4,0},{8,12},{12,8},{16,20},{20,16},{24,28},{28,24},{32,36},... | collective-permute-start | bytes 5898248 | tf_op jit(solution)/shard_map/ppermute | solution.py:461
  59.2 6.4 %collective-permute-start.9 = (bf16[768,1280]{1,0:T(8,128)(2,1)S(1)}, bf16[768,1280]{1,0:T(8,128)(2,1)S(1)}, u32[]{:S(2)}, u32[]{:S(2)}) collective-permute-start(bf16[768,1280]{1,0:T(8,128)(2,1)S(1)} %constant_dynamic-update-slice_fusion.refs_0_), channel_id=1, source_target_pairs={{0,4},{4,0},{8,12},{12,8},{16,20},{20,16},{24,28},{28,24},{32,36},... | collective-permute-start | bytes 5898248 | tf_op jit(solution)/shard_map/ppermute | solution.py:461
  59.2 15.9 %collective-permute-start.11 = (bf16[768,1280]{1,0:T(8,128)(2,1)S(1)}, bf16[768,1280]{1,0:T(8,128)(2,1)S(1)}, u32[]{:S(2)}, u32[]{:S(2)}) collective-permute-start(bf16[768,1280]{1,0:T(8,128)(2,1)S(1)} %collective-permute-done.5.refs_2_), channel_id=1, source_target_pairs={{0,4},{4,0},{8,12},{12,8},{16,20},{20,16},{24,28},{28,24},{32,36},... | collective-permute-start | bytes 5898248 | tf_op jit(solution)/shard_map/ppermute | solution.py:461
  59.7 15.4 %collective-permute-start.12 = (bf16[768,1280]{1,0:T(8,128)(2,1)S(1)}, bf16[768,1280]{1,0:T(8,128)(2,1)S(1)}, u32[]{:S(2)}, u32[]{:S(2)}) collective-permute-start(bf16[768,1280]{1,0:T(8,128)(2,1)S(1)} %collective-permute-done.6.refs_3_), channel_id=1, source_target_pairs={{0,4},{4,0},{8,12},{12,8},{16,20},{20,16},{24,28},{28,24},{32,36},... | collective-permute-start | bytes 5898248 | tf_op jit(solution)/shard_map/ppermute | solution.py:461
  60.7 19.6 %collective-permute-start.8 = (bf16[512,1280]{1,0:T(8,128)(2,1)S(1)}, bf16[512,1280]{1,0:T(8,128)(2,1)S(1)}, u32[]{:S(2)}, u32[]{:S(2)}) collective-permute-start(bf16[512,1280]{1,0:T(8,128)(2,1)S(1)} %pad_maximum_fusion.2), channel_id=1, source_target_pairs={{0,24},{4,100},{8,0},{12,108},{16,8},{20,116},{24,16},{28,124},{32... | collective-permute-start | bytes 3932168 | tf_op jit(solution)/shard_map/ppermute | solution.py:458
  62.8 18.0 %collective-permute-start.7 = (bf16[512,1280]{1,0:T(8,128)(2,1)S(1)}, bf16[512,1280]{1,0:T(8,128)(2,1)S(1)}, u32[]{:S(2)}, u32[]{:S(2)}) collective-permute-start(bf16[512,1280]{1,0:T(8,128)(2,1)S(1)} %pad_maximum_fusion.1), channel_id=1, source_target_pairs={{0,8},{4,36},{8,16},{12,44},{16,24},{20,52},{24,0},{28,60},{32,40}... | collective-permute-start | bytes 3932168 | tf_op jit(solution)/shard_map/ppermute | solution.py:458
  65.6 9.5 %copy-start.9 = (bf16[1024,1536]{1,0:T(8,128)(2,1)S(1)}, bf16[1024,1536]{1,0:T(8,128)(2,1)}, u32[]{:S(2)}) copy-start(bf16[1024,1536]{1,0:T(8,128)(2,1)} %get-tuple-element.68.x_ref) | copy-start | bytes 9437188
  75.1 8.6 %copy-start.10 = (bf16[1024,1024]{1,0:T(8,128)(2,1)S(1)}, bf16[1024,1024]{1,0:T(8,128)(2,1)}, u32[]{:S(2)}) copy-start(bf16[1024,1024]{1,0:T(8,128)(2,1)} %get-tuple-element.70.x_ref) | copy-start | bytes 6291460
  80.7 6.7 %collective-permute-start.13 = (bf16[512,1280]{1,0:T(8,128)(2,1)S(1)}, bf16[512,1280]{1,0:T(8,128)(2,1)S(1)}, u32[]{:S(2)}, u32[]{:S(2)}) collective-permute-start(bf16[512,1280]{1,0:T(8,128)(2,1)S(1)} %collective-permute-done.7.refs_0_), channel_id=1, source_target_pairs={{0,4},{4,0},{8,12},{12,8},{16,20},{20,16},{24,28},{28,24},{32,36},... | collective-permute-start | bytes 3932168 | tf_op jit(solution)/shard_map/ppermute | solution.py:461
  83.6 4.5 %collective-permute-start.14 = (bf16[512,1280]{1,0:T(8,128)(2,1)S(1)}, bf16[512,1280]{1,0:T(8,128)(2,1)S(1)}, u32[]{:S(2)}, u32[]{:S(2)}) collective-permute-start(bf16[512,1280]{1,0:T(8,128)(2,1)S(1)} %collective-permute-done.8.refs_1_), channel_id=1, source_target_pairs={{0,4},{4,0},{8,12},{12,8},{16,20},{20,16},{24,28},{28,24},{32,36},... | collective-permute-start | bytes 3932168 | tf_op jit(solution)/shard_map/ppermute | solution.py:461
  87.4 8.8 %copy-start = (f32[1024,1280]{1,0:T(8,128)}, f32[1024,1280]{1,0:T(8,128)S(1)}, u32[]{:S(2)}) copy-start(f32[1024,1280]{1,0:T(8,128)S(1)} %project.7.total_ref) | copy-start | bytes 15728644
  87.4 8.8 %copy-start.5 = (bf16[512,1280]{1,0:T(8,128)(2,1)}, bf16[512,1280]{1,0:T(8,128)(2,1)S(1)}, u32[]{:S(2)}) copy-start(bf16[512,1280]{1,0:T(8,128)(2,1)S(1)} %collective-permute-done.13.refs_0_.refs_1_) | copy-start | bytes 3932164
  88.2 8.1 %copy-start.7 = (bf16[512,1280]{1,0:T(8,128)(2,1)}, bf16[512,1280]{1,0:T(8,128)(2,1)S(1)}, u32[]{:S(2)}) copy-start(bf16[512,1280]{1,0:T(8,128)(2,1)S(1)} %collective-permute-done.14.refs_1_.refs_2_) | copy-start | bytes 3932164
  97.1 44.0 %all-to-all-start = ((bf16[32,64,768]{2,1,0:T(8,128)(2,1)}), bf16[32,64,768]{2,1,0:T(8,128)(2,1)S(1)}, u32[]{:S(2)}, u32[]{:S(2)}) async-start(bf16[32,64,768]{2,1,0:T(8,128)(2,1)} %get-tuple-element.75), calls=%async_computation | async-start | bytes 6291456 | tf_op jit(solution)/shard_map/all_to_all | solution.py:530
  141.0 21.9 %all-to-all-start.1 = ((bf16[32,64,256]{2,1,0:T(8,128)(2,1)}), bf16[32,64,256]{2,1,0:T(8,128)(2,1)}, u32[]{:S(2)}, u32[]{:S(2)}) async-start(bf16[32,64,256]{2,1,0:T(8,128)(2,1)} %attend.3), calls=%async_computation.1 | async-start | bytes 2097152 | tf_op jit(solution)/shard_map/all_to_all | solution.py:530
  147.7 20.8 %collective-permute-start.15 = (bf16[256,768]{1,0:T(8,128)(2,1)}, bf16[256,768]{1,0:T(8,128)(2,1)S(1)}, u32[]{:S(2)}, u32[]{:S(2)}) collective-permute-start(bf16[256,768]{1,0:T(8,128)(2,1)} %get-tuple-element.77), channel_id=1, source_target_pairs={{0,1},{1,2},{2,3},{3,0},{4,5},{5,6},{6,7},{7,4},{8,9},{9,10},{10,1... | collective-permute-start | bytes 1179656 | tf_op jit(solution)/shard_map/ppermute | solution.py:533
  148.9 20.8 %collective-permute-start.16 = (bf16[256,768]{1,0:T(8,128)(2,1)}, bf16[256,768]{1,0:T(8,128)(2,1)S(1)}, u32[]{:S(2)}, u32[]{:S(2)}) collective-permute-start(bf16[256,768]{1,0:T(8,128)(2,1)} %get-tuple-element.78), channel_id=1, source_target_pairs={{0,2},{1,3},{2,0},{3,1},{4,6},{5,7},{6,4},{7,5},{8,10},{9,11},{10,... | collective-permute-start | bytes 1179656 | tf_op jit(solution)/shard_map/ppermute | solution.py:533
  151.3 18.3 %collective-permute-start.17 = (bf16[256,768]{1,0:T(8,128)(2,1)}, bf16[256,768]{1,0:T(8,128)(2,1)S(1)}, u32[]{:S(2)}, u32[]{:S(2)}) collective-permute-start(bf16[256,768]{1,0:T(8,128)(2,1)} %get-tuple-element.79), channel_id=1, source_target_pairs={{0,3},{1,0},{2,1},{3,2},{4,7},{5,4},{6,5},{7,6},{8,11},{9,8},{10,9... | collective-permute-start | bytes 1179656 | tf_op jit(solution)/shard_map/ppermute | solution.py:533
  164.8 8.0 %collective-permute-start.18 = (bf16[256,256]{1,0:T(8,128)(2,1)S(1)}, bf16[256,256]{1,0:T(8,128)(2,1)S(1)}, u32[]{:S(2)}, u32[]{:S(2)}) collective-permute-start(bf16[256,256]{1,0:T(8,128)(2,1)S(1)} %get-tuple-element.82), channel_id=1, source_target_pairs={{0,1},{1,2},{2,3},{3,0},{4,5},{5,6},{6,7},{7,4},{8,9},{9,10},{10,1... | collective-permute-start | bytes 393224 | tf_op jit(solution)/shard_map/ppermute | solution.py:533
  166.1 8.8 %collective-permute-start.19 = (bf16[256,256]{1,0:T(8,128)(2,1)S(1)}, bf16[256,256]{1,0:T(8,128)(2,1)S(1)}, u32[]{:S(2)}, u32[]{:S(2)}) collective-permute-start(bf16[256,256]{1,0:T(8,128)(2,1)S(1)} %get-tuple-element.83), channel_id=1, source_target_pairs={{0,2},{1,3},{2,0},{3,1},{4,6},{5,7},{6,4},{7,5},{8,10},{9,11},{10,... | collective-permute-start | bytes 393224 | tf_op jit(solution)/shard_map/ppermute | solution.py:533
  168.5 6.3 %collective-permute-start.20 = (bf16[256,256]{1,0:T(8,128)(2,1)S(1)}, bf16[256,256]{1,0:T(8,128)(2,1)S(1)}, u32[]{:S(2)}, u32[]{:S(2)}) collective-permute-start(bf16[256,256]{1,0:T(8,128)(2,1)S(1)} %get-tuple-element.84), channel_id=1, source_target_pairs={{0,3},{1,0},{2,1},{3,2},{4,7},{5,4},{6,5},{7,6},{8,11},{9,8},{10,9... | collective-permute-start | bytes 393224 | tf_op jit(solution)/shard_map/ppermute | solution.py:533
  (16 other events, 46.2 us)

commit v5 on v4

--- a/solution.py
+++ b/solution.py
@@ -119,7 +119,7 @@
             (rows, w_query.shape[1] + w_keyval.shape[1]), w_query.dtype
         ),
         scratch_shapes=[pltpu.SemaphoreType.DMA((3,))],
-        compiler_params=pltpu.CompilerParams(vmem_limit_bytes=4 * MIB),
+        compiler_params=pltpu.CompilerParams(vmem_limit_bytes=58 * MIB),
         name="side_by_side",
     )(w_query, w_keyval)
 
@@ -169,7 +169,7 @@
             num_scalar_prefetch=1, grid=(rows // tile,), in_specs=in_specs, out_specs=out_specs
         ),
         out_shape=out_shape,
-        compiler_params=pltpu.CompilerParams(vmem_limit_bytes=32 * MIB),
+        compiler_params=pltpu.CompilerParams(vmem_limit_bytes=18 * MIB),
         cost_estimate=pl.CostEstimate(
             flops=6 * rows * features,
             bytes_accessed=2 * rows * (features + sum(widths)),
@@ -318,7 +318,7 @@
 
 def attend(dest, lengths, total, x, bias, keyval, pieces, packs, columns):
     rows, depth = x.shape
-    tile = 256
+    tile = 512
     cosine, sine = rope_tables()
     resident = pl.BlockSpec(memory_space=pltpu.VMEM)
 
@@ -361,7 +361,7 @@
             ],
         ),
         out_shape=out_shape[: len(out_specs)],
-        compiler_params=pltpu.CompilerParams(vmem_limit_bytes=24 * MIB),
+        compiler_params=pltpu.CompilerParams(vmem_limit_bytes=28 * MIB),
         cost_estimate=matmul_cost(rows, depth, columns.stop - columns.start, 2),
         name="attend",
     )(dest, lengths, total, x, bias, cosine, sine, *keyvals, *pieces)
@@ -497,19 +497,19 @@
     straight = jnp.concatenate([weights, own_ahead, own_behind])
     total = project(None, x_near, [beside, straight])
 
-    ahead, behind, total, x_middle, x_corners, x_far, x_last = lax.optimization_barrier(
-        (ahead, behind, total, x_middle, x_corners, x_far, x_last)
+    ahead, behind, straight, total, x_middle, x_corners, x_far, x_last = lax.optimization_barrier(
+        (ahead, behind, straight, total, x_middle, x_corners, x_far, x_last)
     )
     far = [
         second(
             jnp.concatenate(
-                [ahead[:rows_held], ahead[2 * rows_held : -half], own_ahead[:half]]
+                [ahead[:rows_held], ahead[2 * rows_held : -half], straight[rows_held : rows_held + half]]
             ),
             1,
         ),
         second(
             jnp.concatenate(
-                [behind[rows_held : 2 * rows_held], behind[-half:], own_behind[half:]]
+                [behind[rows_held : 2 * rows_held], behind[-half:], straight[-half:]]
             ),
             -1,
         ),

time: 177 us -> 174 us (0.983)
  local copies, waits for them, and re-layouts: 24.6 us -> 18.5 us
  waiting for transfers between devices: 51.6 us -> 55.2 us
    unnamed x48 -> x42, local copies, waits for them, and re-layouts: 19.2 us -> 15.2 us
    ppermute x6, waiting for transfers between devices: 8.06 us -> 10.3 us  [second(): return lax.ppermute(piece, 'dp', shift_pairs(0, by))]
    pallas_call x1, Pallas kernels: 0.09 us -> 1.96 us  [side_by_side(): pl.pallas_call(beside_kernel, in_specs=[pl.BlockSpec(memory_space=pltpu.H...]
where the time goes in v5:
time: 174 us; the launch traced here: 173 us
  Pallas kernels  58.1 us (33%)
  waiting for transfers between devices  55.2 us (32%)
  starting transfers between devices  38.3 us (22%)
  local copies, waits for them, and re-layouts  18.5 us (11%)
  other arithmetic  2.83 us (2%)
    all_to_all x2, waiting for transfers between devices, exchanged(): lax.all_to_all(sent, 'dp', split_axis=0, concat_axis=0, tiled=True)  36.9 us
    pallas_call x4, Pallas kernels, project(): pl.pallas_call(add_kernel if totals else first_kernel, grid=(rows // tile...  22.9 us
    unnamed x42, local copies, waits for them, and re-layouts  15.2 us
    pallas_call x2, Pallas kernels, norm(): pl.pallas_call(norm_kernel if scale is None else functools.partial(norm_r...  14.2 us
    pallas_call x2, Pallas kernels, attend(): pl.pallas_call(functools.partial(attend_kernel, columns), grid_spec=pltpu...  12.6 us
    ppermute x6, waiting for transfers between devices, second(): return lax.ppermute(piece, 'dp', shift_pairs(0, by))  10.3 us
    ppermute x6, starting transfers between devices, exchanged(): lax.ppermute(parts[k], 'mp', [(i, (i + k) % planes) for i in range(planes)])  9.7 us
    all_to_all x2, starting transfers between devices, exchanged(): lax.all_to_all(sent, 'dp', split_axis=0, concat_axis=0, tiled=True)  9.55 us
  transfers between devices with their start and end apart: 23, of which 10 were waited for; matrix products, arithmetic and copies ran while one was open for 3% of the time, Pallas kernels for 28%

profile of v5, /device:TPU:1, one launch (start us, length us, event | category | flops | bytes accessed | tf_op | source)
XLA Modules:
  0.0 173.5 jit_solution(3025622067841235760)
XLA Ops:
  0.0 2.0 %side_by_side.1 = bf16[256,1280]{1,0:T(8,128)(2,1)} custom-call(bf16[256,1024]{1,0:T(8,128)(2,1)} %query_ref.1, bf16[256,256]{1,0:T(8,128)(2,1)} %keyval_ref.1), custom_call_target="tpu_custom_call" | custom-call | tf_op jit(solution)/shard_map/side_by_side/pallas_call | solution.py:114
  2.0 2.5 %collective-permute-start = (bf16[256,1280]{1,0:T(8,128)(2,1)}, bf16[256,1280]{1,0:T(8,128)(2,1)S(1)}, u32[]{:S(2)}, u32[]{:S(2)}) collective-permute-start(bf16[256,1280]{1,0:T(8,128)(2,1)} %side_by_side.1), channel_id=1, source_target_pairs={{0,32},{4,12},{8,40},{12,20},{16,48},{20,28},{24,56},{28,4},{32,64... | collective-permute-start | bytes 1966088 | tf_op jit(solution)/shard_map/ppermute | solution.py:455
  4.5 2.2 %collective-permute-start.1 = (bf16[256,1280]{1,0:T(8,128)(2,1)}, bf16[256,1280]{1,0:T(8,128)(2,1)S(1)}, u32[]{:S(2)}, u32[]{:S(2)}) collective-permute-start(bf16[256,1280]{1,0:T(8,128)(2,1)} %side_by_side.1), channel_id=1, source_target_pairs={{0,96},{4,28},{8,104},{12,4},{16,112},{20,12},{24,120},{28,20},{32... | collective-permute-start | bytes 1966088 | tf_op jit(solution)/shard_map/ppermute | solution.py:455
  9.2 1.4 collective-permute-start.4
  16.2 5.8 %copy-done.2 = bf16[1024,8192]{1,0:T(8,128)(2,1)S(1)} copy-done((bf16[1024,8192]{1,0:T(8,128)(2,1)S(1)}, bf16[1024,8192]{1,0:T(8,128)(2,1)}, u32[]{:S(2)}) %copy-start.2) | copy-done | bytes 16777240
  22.8 6.4 %norm.2 = (f32[1024,1]{1,0:T(8,128)S(1)}, bf16[1024,1536]{1,0:T(8,128)(2,1)}) custom-call(s32[64]{0:T(128)S(1)} %fusion.3.order_ref, bf16[1024,8192]{1,0:T(8,128)(2,1)S(1)} %copy-done.2, f32[1,8192]{1,0:T(1,128)S(1)} %bitcast.6), custom_call_target="tpu_custom_call" | custom-call | flops 50331648 | bytes 19922944 | tf_op jit(solution)/shard_map/norm/pallas_call | solution.py:166
  31.6 1.7 collective-permute-start.6
  33.2 7.7 %norm.3 = (bf16[1024,3072]{1,0:T(8,128)(2,1)}, bf16[1024,1536]{1,0:T(8,128)(2,1)}, bf16[1024,1024]{1,0:T(8,128)(2,1)}, bf16[1024,1024]{1,0:T(8,128)(2,1)}) custom-call(s32[64]{0:T(128)S(1)} %fusion.3.order_ref, bf16[1024,8192]{1,0:T(8,128)(2,1)S(1)} %copy-done.2, f32[1,8192]{1,0:T(1,128)S(1)} %bitcast.7, f32[1024,1]{1,0:T(8,128)S(1)} %get-tuple-element.58.scale_ref), custom_call_target="tpu_custom_call" | custom-call | flops 50331648 | bytes 30408704 | tf_op jit(solution)/shard_map/norm/pallas_call | solution.py:166
  41.1 4.8 %project.4.total_ref = f32[1024,1280]{1,0:T(8,128)S(1)} custom-call(bf16[1024,1536]{1,0:T(8,128)(2,1)S(1)} %copy-done.16, bf16[768,1280]{1,0:T(8,128)(2,1)S(1)} %constant_dynamic-update-slice_fusion.refs_0_, bf16[768,1280]{1,0:T(8,128)(2,1)S(1)} %pad_maximum_fusion.refs_1_), custom_call_target="tpu_custom_call" | custom-call | flops 4026531840 | bytes 17563648 | tf_op jit(solution)/shard_map/project/pallas_call | solution.py:215
  45.9 9.6 %collective-permute-done.5.refs_2_ = bf16[768,1280]{1,0:T(8,128)(2,1)S(1)} collective-permute-done((bf16[768,1280]{1,0:T(8,128)(2,1)S(1)}, bf16[768,1280]{1,0:T(8,128)(2,1)S(1)}, u32[]{:S(2)}, u32[]{:S(2)}) %collective-permute-start.5) | collective-permute-done | bytes 1966112 | tf_op jit(solution)/shard_map/ppermute | solution.py:458
  55.6 2.2 %collective-permute-start.10 = (bf16[768,1280]{1,0:T(8,128)(2,1)S(1)}, bf16[768,1280]{1,0:T(8,128)(2,1)S(1)}, u32[]{:S(2)}, u32[]{:S(2)}) collective-permute-start(bf16[768,1280]{1,0:T(8,128)(2,1)S(1)} %pad_maximum_fusion.refs_1_), channel_id=1, source_target_pairs={{0,4},{4,0},{8,12},{12,8},{16,20},{20,16},{24,28},{28,24},{32,36},... | collective-permute-start | bytes 5898248 | tf_op jit(solution)/shard_map/ppermute | solution.py:461
  58.5 1.7 collective-permute-start.8
  62.5 1.7 collective-permute-done.9.refs_0_
  64.1 9.2 %project.5.total_ref = f32[1024,1280]{1,0:T(8,128)S(1)} custom-call(f32[1024,1280]{1,0:T(8,128)S(1)} %project.4.total_ref, bf16[1024,3072]{1,0:T(8,128)(2,1)S(1)} %bitcast.9, bf16[768,1280]{1,0:T(8,128)(2,1)S(1)} %collective-permute-done.9.refs_0_, bf16[768,1280]{1,0:T(8,128)(2,1)S(1)} %collective-permute-done.10.refs_1_, ...), custom_call_target="tpu_custom_call", output_to_operand_aliasing={{}: (0, {})} | custom-call | flops 8053063680 | bytes 24641536 | tf_op jit(solution)/shard_map/project/pallas_call | solution.py:215
  73.4 5.2 %project.6.total_ref = f32[1024,1280]{1,0:T(8,128)S(1)} custom-call(f32[1024,1280]{1,0:T(8,128)S(1)} %project.5.total_ref, bf16[1024,1536]{1,0:T(8,128)(2,1)S(1)} %copy-done.9, bf16[768,1280]{1,0:T(8,128)(2,1)S(1)} %collective-permute-done.11.refs_0_, bf16[768,1280]{1,0:T(8,128)(2,1)S(1)} %collective-permute-done.12.refs_1_), custom_call_target="tpu_custom_call", output_to_operand_aliasing={{}: (0, {})} | custom-call | flops 4026531840 | bytes 17563648 | tf_op jit(solution)/shard_map/project/pallas_call | solution.py:215
  79.3 2.1 %collective-permute-start.13 = (bf16[512,1280]{1,0:T(8,128)(2,1)S(1)}, bf16[512,1280]{1,0:T(8,128)(2,1)S(1)}, u32[]{:S(2)}, u32[]{:S(2)}) collective-permute-start(bf16[512,1280]{1,0:T(8,128)(2,1)S(1)} %collective-permute-done.7.refs_0_), channel_id=1, source_target_pairs={{0,4},{4,0},{8,12},{12,8},{16,20},{20,16},{24,28},{28,24},{32,36},... | collective-permute-start | bytes 3932168 | tf_op jit(solution)/shard_map/ppermute | solution.py:461
  81.4 3.7 %project.7.total_ref = f32[1024,1280]{1,0:T(8,128)S(1)} custom-call(f32[1024,1280]{1,0:T(8,128)S(1)} %project.6.total_ref, bf16[1024,1024]{1,0:T(8,128)(2,1)S(1)} %copy-done.10, bf16[512,1280]{1,0:T(8,128)(2,1)S(1)} %collective-permute-done.7.refs_0_, bf16[512,1280]{1,0:T(8,128)(2,1)S(1)} %collective-permute-done.8.refs_1_), custom_call_target="tpu_custom_call", output_to_operand_aliasing={{}: (0, {})} | custom-call | flops 2684354560 | bytes 15204352 | tf_op jit(solution)/shard_map/project/pallas_call | solution.py:215
  86.0 7.0 %attend.2 = (bf16[32,64,768]{2,1,0:T(8,128)(2,1)}, bf16[1024,256]{1,0:T(8,128)(2,1)S(1)}) custom-call(s32[16]{0:T(128)S(1)} %get-tuple-element.50.dest_ref, s32[16]{0:T(128)S(1)} %get-tuple-element.51.length_ref, f32[1024,1280]{1,0:T(8,128)S(1)} %project.7.total_ref, bf16[1024,1024]{1,0:T(8,128)(2,1)S(1)} %copy-done.3, ...), custom_call_target="tpu_custom_call" | custom-call | flops 2147483648 | bytes 12582912 | tf_op jit(solution)/shard_map/attend/pallas_call | solution.py:343
  93.8 4.5 %all-to-all-start = ((bf16[32,64,768]{2,1,0:T(8,128)(2,1)}), bf16[32,64,768]{2,1,0:T(8,128)(2,1)S(1)}, u32[]{:S(2)}, u32[]{:S(2)}) async-start(bf16[32,64,768]{2,1,0:T(8,128)(2,1)} %get-tuple-element.77), calls=%async_computation | async-start | bytes 6291456 | tf_op jit(solution)/shard_map/all_to_all | solution.py:530
  98.4 2.5 %copy-done.1 = f32[1024,1280]{1,0:T(8,128)S(1)} copy-done((f32[1024,1280]{1,0:T(8,128)S(1)}, f32[1024,1280]{1,0:T(8,128)}, u32[]{:S(2)}) %copy-start.1) | copy-done | bytes 5242904
  100.8 1.6 copy-done.4
  106.1 5.6 %attend.3 = bf16[32,64,256]{2,1,0:T(8,128)(2,1)} custom-call(s32[16]{0:T(128)S(1)} %get-tuple-element.50.dest_ref, s32[16]{0:T(128)S(1)} %get-tuple-element.51.length_ref, f32[1024,1280]{1,0:T(8,128)S(1)} %copy-done.1, bf16[1024,1024]{1,0:T(8,128)(2,1)S(1)} %copy-done.4, f32[1,1280]{1,0:T(1,128)S(1)} %broadcast_in_dim.26.bias_ref, ...), custom_call_target="tpu_custom_call" | custom-call | flops 536870912 | bytes 4718592 | tf_op jit(solution)/shard_map/attend/pallas_call | solution.py:343
  111.7 26.4 %all-to-all-done.received_ref = bf16[32,64,768]{2,1,0:T(8,128)(2,1)S(1)} async-done(((bf16[32,64,768]{2,1,0:T(8,128)(2,1)}), bf16[32,64,768]{2,1,0:T(8,128)(2,1)S(1)}, u32[]{:S(2)}, u32[]{:S(2)}) %all-to-all-start) | async-done | bytes 3145760 | tf_op jit(solution)/shard_map/all_to_all | solution.py:530
  138.1 5.0 %all-to-all-start.1 = ((bf16[32,64,256]{2,1,0:T(8,128)(2,1)}), bf16[32,64,256]{2,1,0:T(8,128)(2,1)}, u32[]{:S(2)}, u32[]{:S(2)}) async-start(bf16[32,64,256]{2,1,0:T(8,128)(2,1)} %attend.3), calls=%async_computation.1 | async-start | bytes 2097152 | tf_op jit(solution)/shard_map/all_to_all | solution.py:530
  143.2 1.6 place.2
  146.0 2.5 %collective-permute-start.16 = (bf16[256,768]{1,0:T(8,128)(2,1)}, bf16[256,768]{1,0:T(8,128)(2,1)S(1)}, u32[]{:S(2)}, u32[]{:S(2)}) collective-permute-start(bf16[256,768]{1,0:T(8,128)(2,1)} %get-tuple-element.80), channel_id=1, source_target_pairs={{0,2},{1,3},{2,0},{3,1},{4,6},{5,7},{6,4},{7,5},{8,10},{9,11},{10,... | collective-permute-start | bytes 1179656 | tf_op jit(solution)/shard_map/ppermute | solution.py:533
  149.6 10.5 %all-to-all-done.1.received_ref = bf16[32,64,256]{2,1,0:T(8,128)(2,1)} async-done(((bf16[32,64,256]{2,1,0:T(8,128)(2,1)}), bf16[32,64,256]{2,1,0:T(8,128)(2,1)}, u32[]{:S(2)}, u32[]{:S(2)}) %all-to-all-start.1) | async-done | bytes 1048608 | tf_op jit(solution)/shard_map/all_to_all | solution.py:530
  160.1 1.8 %place.3 = (bf16[256,256]{1,0:T(8,128)(2,1)S(1)}, bf16[256,256]{1,0:T(8,128)(2,1)S(1)}, bf16[256,256]{1,0:T(8,128)(2,1)S(1)}, bf16[256,256]{1,0:T(8,128)(2,1)S(1)}) custom-call(s32[16]{0:T(128)S(1)} %reshape.58.source_ref, bf16[32,64,256]{2,1,0:T(8,128)(2,1)} %all-to-all-done.1.received_ref), custom_call_target="tpu_custom_call" | custom-call | tf_op jit(solution)/shard_map/place/pallas_call | solution.py:381
  163.2 2.5 %collective-permute-start.19 = (bf16[256,256]{1,0:T(8,128)(2,1)S(1)}, bf16[256,256]{1,0:T(8,128)(2,1)S(1)}, u32[]{:S(2)}, u32[]{:S(2)}) collective-permute-start(bf16[256,256]{1,0:T(8,128)(2,1)S(1)} %get-tuple-element.85), channel_id=1, source_target_pairs={{0,2},{1,3},{2,0},{3,1},{4,6},{5,7},{6,4},{7,5},{8,10},{9,11},{10,... | collective-permute-start | bytes 393224 | tf_op jit(solution)/shard_map/ppermute | solution.py:533
  166.8 1.7 join.2.refs_0_
  169.9 2.1 %collective-permute-done.19.refs_3_ = bf16[256,256]{1,0:T(8,128)(2,1)S(1)} collective-permute-done((bf16[256,256]{1,0:T(8,128)(2,1)S(1)}, bf16[256,256]{1,0:T(8,128)(2,1)S(1)}, u32[]{:S(2)}, u32[]{:S(2)}) %collective-permute-start.19) | collective-permute-done | bytes 131104 | tf_op jit(solution)/shard_map/ppermute | solution.py:533
  172.0 1.4 join.3
  (93 shorter events, 26.4 us)
Async XLA Ops:
  2.0 27.3 %collective-permute-start = (bf16[256,1280]{1,0:T(8,128)(2,1)}, bf16[256,1280]{1,0:T(8,128)(2,1)S(1)}, u32[]{:S(2)}, u32[]{:S(2)}) collective-permute-start(bf16[256,1280]{1,0:T(8,128)(2,1)} %side_by_side.1), channel_id=1, source_target_pairs={{0,32},{4,12},{8,40},{12,20},{16,48},{20,28},{24,56},{28,4},{32,64... | collective-permute-start | bytes 1966088 | tf_op jit(solution)/shard_map/ppermute | solution.py:455
  4.5 24.7 %collective-permute-start.1 = (bf16[256,1280]{1,0:T(8,128)(2,1)}, bf16[256,1280]{1,0:T(8,128)(2,1)S(1)}, u32[]{:S(2)}, u32[]{:S(2)}) collective-permute-start(bf16[256,1280]{1,0:T(8,128)(2,1)} %side_by_side.1), channel_id=1, source_target_pairs={{0,96},{4,28},{8,104},{12,4},{16,112},{20,12},{24,120},{28,20},{32... | collective-permute-start | bytes 1966088 | tf_op jit(solution)/shard_map/ppermute | solution.py:455
  6.7 23.6 %collective-permute-start.2 = (bf16[256,1280]{1,0:T(8,128)(2,1)}, bf16[256,1280]{1,0:T(8,128)(2,1)S(1)}, u32[]{:S(2)}, u32[]{:S(2)}) collective-permute-start(bf16[256,1280]{1,0:T(8,128)(2,1)} %side_by_side.1), channel_id=1, source_target_pairs={{0,64},{4,20},{8,72},{12,28},{16,80},{20,4},{24,88},{28,12},{32,96... | collective-permute-start | bytes 1966088 | tf_op jit(solution)/shard_map/ppermute | solution.py:455
  7.9 22.4 %collective-permute-start.3 = (bf16[256,1280]{1,0:T(8,128)(2,1)}, bf16[256,1280]{1,0:T(8,128)(2,1)S(1)}, u32[]{:S(2)}, u32[]{:S(2)}) collective-permute-start(bf16[256,1280]{1,0:T(8,128)(2,1)} %side_by_side.1), channel_id=1, source_target_pairs={{0,8},{4,36},{8,16},{12,44},{16,24},{20,52},{24,0},{28,60},{32,40}... | collective-permute-start | bytes 1966088 | tf_op jit(solution)/shard_map/ppermute | solution.py:458
  9.2 21.1 %collective-permute-start.4 = (bf16[256,1280]{1,0:T(8,128)(2,1)}, bf16[256,1280]{1,0:T(8,128)(2,1)S(1)}, u32[]{:S(2)}, u32[]{:S(2)}) collective-permute-start(bf16[256,1280]{1,0:T(8,128)(2,1)} %side_by_side.1), channel_id=1, source_target_pairs={{0,24},{4,100},{8,0},{12,108},{16,8},{20,116},{24,16},{28,124},{32... | collective-permute-start | bytes 1966088 | tf_op jit(solution)/shard_map/ppermute | solution.py:458
  30.5 10.5 %copy-start.17 = (bf16[256,1280]{1,0:T(8,128)(2,1)S(1)}, bf16[256,1280]{1,0:T(8,128)(2,1)}, u32[]{:S(2)}) copy-start(bf16[256,1280]{1,0:T(8,128)(2,1)} %side_by_side.1) | copy-start | bytes 1966084
  30.5 25.1 %collective-permute-start.5 = (bf16[768,1280]{1,0:T(8,128)(2,1)S(1)}, bf16[768,1280]{1,0:T(8,128)(2,1)S(1)}, u32[]{:S(2)}, u32[]{:S(2)}) collective-permute-start(bf16[768,1280]{1,0:T(8,128)(2,1)S(1)} %constant_dynamic-update-slice_fusion.refs_0_), channel_id=1, source_target_pairs={{0,8},{4,36},{8,16},{12,44},{16,24},{20,52},{24,0},{28,60},{32,40}... | collective-permute-start | bytes 5898248 | tf_op jit(solution)/shard_map/ppermute | solution.py:458
  31.6 24.0 %collective-permute-start.6 = (bf16[768,1280]{1,0:T(8,128)(2,1)S(1)}, bf16[768,1280]{1,0:T(8,128)(2,1)S(1)}, u32[]{:S(2)}, u32[]{:S(2)}) collective-permute-start(bf16[768,1280]{1,0:T(8,128)(2,1)S(1)} %constant_dynamic-update-slice_fusion.refs_0_), channel_id=1, source_target_pairs={{0,24},{4,100},{8,0},{12,108},{16,8},{20,116},{24,16},{28,124},{32... | collective-permute-start | bytes 5898248 | tf_op jit(solution)/shard_map/ppermute | solution.py:458
  33.2 7.9 %copy-start.16 = (bf16[1024,1536]{1,0:T(8,128)(2,1)S(1)}, bf16[1024,1536]{1,0:T(8,128)(2,1)}, u32[]{:S(2)}) copy-start(bf16[1024,1536]{1,0:T(8,128)(2,1)} %get-tuple-element.57.x_ref) | copy-start | bytes 9437188
  41.0 23.2 %slice-start = ((s8[6291456]{0:T(1024)(128)(4,1)}), s8[4194304]{0:T(1024)(128)(4,1)S(1)}, s32[]{:S(2)}) async-start(s8[6291456]{0:T(1024)(128)(4,1)} %bitcast.8), calls=%async_computation.2 | async-start | bytes 8388608
  41.1 23.0 %slice-start.1 = ((s8[6291456]{0:T(1024)(128)(4,1)}), s8[2097152]{0:T(1024)(128)(4,1)S(1)}, s32[]{:S(2)}) async-start(s8[6291456]{0:T(1024)(128)(4,1)} %bitcast.8), calls=%async_computation.3 | async-start | bytes 4194304
  55.6 5.8 %collective-permute-start.10 = (bf16[768,1280]{1,0:T(8,128)(2,1)S(1)}, bf16[768,1280]{1,0:T(8,128)(2,1)S(1)}, u32[]{:S(2)}, u32[]{:S(2)}) collective-permute-start(bf16[768,1280]{1,0:T(8,128)(2,1)S(1)} %pad_maximum_fusion.refs_1_), channel_id=1, source_target_pairs={{0,4},{4,0},{8,12},{12,8},{16,20},{20,16},{24,28},{28,24},{32,36},... | collective-permute-start | bytes 5898248 | tf_op jit(solution)/shard_map/ppermute | solution.py:461
  57.7 6.4 %collective-permute-start.9 = (bf16[768,1280]{1,0:T(8,128)(2,1)S(1)}, bf16[768,1280]{1,0:T(8,128)(2,1)S(1)}, u32[]{:S(2)}, u32[]{:S(2)}) collective-permute-start(bf16[768,1280]{1,0:T(8,128)(2,1)S(1)} %constant_dynamic-update-slice_fusion.refs_0_), channel_id=1, source_target_pairs={{0,4},{4,0},{8,12},{12,8},{16,20},{20,16},{24,28},{28,24},{32,36},... | collective-permute-start | bytes 5898248 | tf_op jit(solution)/shard_map/ppermute | solution.py:461
  57.7 15.7 %collective-permute-start.11 = (bf16[768,1280]{1,0:T(8,128)(2,1)S(1)}, bf16[768,1280]{1,0:T(8,128)(2,1)S(1)}, u32[]{:S(2)}, u32[]{:S(2)}) collective-permute-start(bf16[768,1280]{1,0:T(8,128)(2,1)S(1)} %collective-permute-done.5.refs_2_), channel_id=1, source_target_pairs={{0,4},{4,0},{8,12},{12,8},{16,20},{20,16},{24,28},{28,24},{32,36},... | collective-permute-start | bytes 5898248 | tf_op jit(solution)/shard_map/ppermute | solution.py:461
  58.2 15.2 %collective-permute-start.12 = (bf16[768,1280]{1,0:T(8,128)(2,1)S(1)}, bf16[768,1280]{1,0:T(8,128)(2,1)S(1)}, u32[]{:S(2)}, u32[]{:S(2)}) collective-permute-start(bf16[768,1280]{1,0:T(8,128)(2,1)S(1)} %collective-permute-done.6.refs_3_), channel_id=1, source_target_pairs={{0,4},{4,0},{8,12},{12,8},{16,20},{20,16},{24,28},{28,24},{32,36},... | collective-permute-start | bytes 5898248 | tf_op jit(solution)/shard_map/ppermute | solution.py:461
  58.5 20.1 %collective-permute-start.8 = (bf16[512,1280]{1,0:T(8,128)(2,1)S(1)}, bf16[512,1280]{1,0:T(8,128)(2,1)S(1)}, u32[]{:S(2)}, u32[]{:S(2)}) collective-permute-start(bf16[512,1280]{1,0:T(8,128)(2,1)S(1)} %pad_maximum_fusion.2), channel_id=1, source_target_pairs={{0,24},{4,100},{8,0},{12,108},{16,8},{20,116},{24,16},{28,124},{32... | collective-permute-start | bytes 3932168 | tf_op jit(solution)/shard_map/ppermute | solution.py:458
  61.3 18.0 %collective-permute-start.7 = (bf16[512,1280]{1,0:T(8,128)(2,1)S(1)}, bf16[512,1280]{1,0:T(8,128)(2,1)S(1)}, u32[]{:S(2)}, u32[]{:S(2)}) collective-permute-start(bf16[512,1280]{1,0:T(8,128)(2,1)S(1)} %pad_maximum_fusion.1), channel_id=1, source_target_pairs={{0,8},{4,36},{8,16},{12,44},{16,24},{20,52},{24,0},{28,60},{32,40}... | collective-permute-start | bytes 3932168 | tf_op jit(solution)/shard_map/ppermute | solution.py:458
  64.1 9.3 %copy-start.9 = (bf16[1024,1536]{1,0:T(8,128)(2,1)S(1)}, bf16[1024,1536]{1,0:T(8,128)(2,1)}, u32[]{:S(2)}) copy-start(bf16[1024,1536]{1,0:T(8,128)(2,1)} %get-tuple-element.70.x_ref) | copy-start | bytes 9437188
  73.4 8.1 %copy-start.10 = (bf16[1024,1024]{1,0:T(8,128)(2,1)S(1)}, bf16[1024,1024]{1,0:T(8,128)(2,1)}, u32[]{:S(2)}) copy-start(bf16[1024,1024]{1,0:T(8,128)(2,1)} %get-tuple-element.72.x_ref) | copy-start | bytes 6291460
  78.6 7.3 %copy-start.3 = (bf16[1024,1024]{1,0:T(8,128)(2,1)S(1)}, bf16[1024,1024]{1,0:T(8,128)(2,1)}, u32[]{:S(2)}) copy-start(bf16[1024,1024]{1,0:T(8,128)(2,1)} %get-tuple-element.75.x_ref) | copy-start | bytes 6291460
  79.3 5.9 %collective-permute-start.13 = (bf16[512,1280]{1,0:T(8,128)(2,1)S(1)}, bf16[512,1280]{1,0:T(8,128)(2,1)S(1)}, u32[]{:S(2)}, u32[]{:S(2)}) collective-permute-start(bf16[512,1280]{1,0:T(8,128)(2,1)S(1)} %collective-permute-done.7.refs_0_), channel_id=1, source_target_pairs={{0,4},{4,0},{8,12},{12,8},{16,20},{20,16},{24,28},{28,24},{32,36},... | collective-permute-start | bytes 3932168 | tf_op jit(solution)/shard_map/ppermute | solution.py:461
  81.4 4.5 %collective-permute-start.14 = (bf16[512,1280]{1,0:T(8,128)(2,1)S(1)}, bf16[512,1280]{1,0:T(8,128)(2,1)S(1)}, u32[]{:S(2)}, u32[]{:S(2)}) collective-permute-start(bf16[512,1280]{1,0:T(8,128)(2,1)S(1)} %collective-permute-done.8.refs_1_), channel_id=1, source_target_pairs={{0,4},{4,0},{8,12},{12,8},{16,20},{20,16},{24,28},{28,24},{32,36},... | collective-permute-start | bytes 3932168 | tf_op jit(solution)/shard_map/ppermute | solution.py:461
  85.1 7.8 %copy-start = (f32[1024,1280]{1,0:T(8,128)}, f32[1024,1280]{1,0:T(8,128)S(1)}, u32[]{:S(2)}) copy-start(f32[1024,1280]{1,0:T(8,128)S(1)} %project.7.total_ref) | copy-start | bytes 15728644
  85.2 7.8 %copy-start.5 = (bf16[512,1280]{1,0:T(8,128)(2,1)}, bf16[512,1280]{1,0:T(8,128)(2,1)S(1)}, u32[]{:S(2)}) copy-start(bf16[512,1280]{1,0:T(8,128)(2,1)S(1)} %collective-permute-done.13.refs_0_.refs_1_) | copy-start | bytes 3932164
  93.8 44.3 %all-to-all-start = ((bf16[32,64,768]{2,1,0:T(8,128)(2,1)}), bf16[32,64,768]{2,1,0:T(8,128)(2,1)S(1)}, u32[]{:S(2)}, u32[]{:S(2)}) async-start(bf16[32,64,768]{2,1,0:T(8,128)(2,1)} %get-tuple-element.77), calls=%async_computation | async-start | bytes 6291456 | tf_op jit(solution)/shard_map/all_to_all | solution.py:530
  138.1 22.0 %all-to-all-start.1 = ((bf16[32,64,256]{2,1,0:T(8,128)(2,1)}), bf16[32,64,256]{2,1,0:T(8,128)(2,1)}, u32[]{:S(2)}, u32[]{:S(2)}) async-start(bf16[32,64,256]{2,1,0:T(8,128)(2,1)} %attend.3), calls=%async_computation.1 | async-start | bytes 2097152 | tf_op jit(solution)/shard_map/all_to_all | solution.py:530
  144.8 20.9 %collective-permute-start.15 = (bf16[256,768]{1,0:T(8,128)(2,1)}, bf16[256,768]{1,0:T(8,128)(2,1)S(1)}, u32[]{:S(2)}, u32[]{:S(2)}) collective-permute-start(bf16[256,768]{1,0:T(8,128)(2,1)} %get-tuple-element.79), channel_id=1, source_target_pairs={{0,1},{1,2},{2,3},{3,0},{4,5},{5,6},{6,7},{7,4},{8,9},{9,10},{10,1... | collective-permute-start | bytes 1179656 | tf_op jit(solution)/shard_map/ppermute | solution.py:533
  146.0 20.8 %collective-permute-start.16 = (bf16[256,768]{1,0:T(8,128)(2,1)}, bf16[256,768]{1,0:T(8,128)(2,1)S(1)}, u32[]{:S(2)}, u32[]{:S(2)}) collective-permute-start(bf16[256,768]{1,0:T(8,128)(2,1)} %get-tuple-element.80), channel_id=1, source_target_pairs={{0,2},{1,3},{2,0},{3,1},{4,6},{5,7},{6,4},{7,5},{8,10},{9,11},{10,... | collective-permute-start | bytes 1179656 | tf_op jit(solution)/shard_map/ppermute | solution.py:533
  148.4 18.4 %collective-permute-start.17 = (bf16[256,768]{1,0:T(8,128)(2,1)}, bf16[256,768]{1,0:T(8,128)(2,1)S(1)}, u32[]{:S(2)}, u32[]{:S(2)}) collective-permute-start(bf16[256,768]{1,0:T(8,128)(2,1)} %get-tuple-element.81), channel_id=1, source_target_pairs={{0,3},{1,0},{2,1},{3,2},{4,7},{5,4},{6,5},{7,6},{8,11},{9,8},{10,9... | collective-permute-start | bytes 1179656 | tf_op jit(solution)/shard_map/ppermute | solution.py:533
  161.9 7.9 %collective-permute-start.18 = (bf16[256,256]{1,0:T(8,128)(2,1)S(1)}, bf16[256,256]{1,0:T(8,128)(2,1)S(1)}, u32[]{:S(2)}, u32[]{:S(2)}) collective-permute-start(bf16[256,256]{1,0:T(8,128)(2,1)S(1)} %get-tuple-element.84), channel_id=1, source_target_pairs={{0,1},{1,2},{2,3},{3,0},{4,5},{5,6},{6,7},{7,4},{8,9},{9,10},{10,1... | collective-permute-start | bytes 393224 | tf_op jit(solution)/shard_map/ppermute | solution.py:533
  163.2 8.8 %collective-permute-start.19 = (bf16[256,256]{1,0:T(8,128)(2,1)S(1)}, bf16[256,256]{1,0:T(8,128)(2,1)S(1)}, u32[]{:S(2)}, u32[]{:S(2)}) collective-permute-start(bf16[256,256]{1,0:T(8,128)(2,1)S(1)} %get-tuple-element.85), channel_id=1, source_target_pairs={{0,2},{1,3},{2,0},{3,1},{4,6},{5,7},{6,4},{7,5},{8,10},{9,11},{10,... | collective-permute-start | bytes 393224 | tf_op jit(solution)/shard_map/ppermute | solution.py:533
  165.7 6.3 %collective-permute-start.20 = (bf16[256,256]{1,0:T(8,128)(2,1)S(1)}, bf16[256,256]{1,0:T(8,128)(2,1)S(1)}, u32[]{:S(2)}, u32[]{:S(2)}) collective-permute-start(bf16[256,256]{1,0:T(8,128)(2,1)S(1)} %get-tuple-element.86), channel_id=1, source_target_pairs={{0,3},{1,0},{2,1},{3,2},{4,7},{5,4},{6,5},{7,6},{8,11},{9,8},{10,9... | collective-permute-start | bytes 393224 | tf_op jit(solution)/shard_map/ppermute | solution.py:533
  (11 other events, 36.8 us)

commit v6 on v5

--- a/solution.py
+++ b/solution.py
@@ -233,23 +233,11 @@
         pieces, (out_ref, keyval_ref, context, sems) = refs[:-4], refs[-4:]
     else:
         keyval_ref, pieces, (out_ref, context, sems) = refs[0], refs[1:-3], refs[-3:]
-    step = pl.program_id(0)
-    slot = lax.rem(step, 2)
     rows = x_ref.shape[0]
-    heads = context.shape[2] // HD
+    heads = context.shape[1] // HD
     groups = rows // GROUP
 
-    def copies(at_step, at_slot):
-        return [
-            pltpu.make_async_copy(
-                context.at[at_slot, pl.ds(g * GROUP, GROUP)],
-                out_ref.at[dest_ref[at_step * groups + g]],
-                sems.at[at_slot, g],
-            )
-            for g in range(groups)
-        ]
-
-    lengths = [length_ref[step * groups + g] for g in range(groups)]
+    lengths = [length_ref[g] for g in range(groups)]
     row_tables = []
     for table in (cosine_ref, sine_ref):
         parts = []
@@ -264,7 +252,7 @@
     cosine, sine = row_tables
 
     summed = (
-        total_ref[tile_rows(rows), columns]
+        total_ref[:, columns]
         + product(x_ref, pieces, columns)
         + bias_ref[:, columns]
     )
@@ -282,11 +270,7 @@
     else:
         key, value = keyval_ref[:, :HD], keyval_ref[:, HD:]
 
-    @pl.when(step >= 2)
-    def _():
-        for copy in copies(step - 2, slot):
-            copy.wait()
-
+    copies = []
     tile = 2 * GROUP
     row = lax.broadcasted_iota(jnp.int32, (tile, tile), 0)
     column = lax.broadcasted_iota(jnp.int32, (tile, tile), 1)
@@ -305,20 +289,19 @@
         mixed = jnp.dot(weights, value[span], preferred_element_type=jnp.float32)
         mixed = mixed.astype(jnp.bfloat16)
         for h in range(heads):
-            context[slot, span, h * HD : (h + 1) * HD] = mixed[h * tile : (h + 1) * tile]
-
-    for copy in copies(step, slot):
-        copy.start()
-
-    @pl.when(step == pl.num_programs(0) - 1)
-    def _():
-        for copy in copies(step - 1, 1 - slot) + copies(step, slot):
-            copy.wait()
+            context[span, h * HD : (h + 1) * HD] = mixed[h * tile : (h + 1) * tile]
+        for g in (2 * t, 2 * t + 1):
+            copy = pltpu.make_async_copy(
+                context.at[pl.ds(g * GROUP, GROUP)], out_ref.at[dest_ref[g]], sems.at[g]
+            )
+            copy.start()
+            copies.append(copy)
+    for copy in copies:
+        copy.wait()
 
 
 def attend(dest, lengths, total, x, bias, keyval, pieces, packs, columns):
     rows, depth = x.shape
-    tile = 512
     cosine, sine = rope_tables()
     resident = pl.BlockSpec(memory_space=pltpu.VMEM)
 
@@ -328,7 +311,7 @@
         )
 
     def by_rows(width):
-        return pl.BlockSpec((tile, width), lambda i, *_: (i, 0))
+        return pl.BlockSpec((rows, width), lambda i, *_: (i, 0))
 
     width = columns.stop - columns.start
     out_specs = [pl.BlockSpec(memory_space=pltpu.HBM)]
@@ -344,7 +327,7 @@
         functools.partial(attend_kernel, columns),
         grid_spec=pltpu.PrefetchScalarGridSpec(
             num_scalar_prefetch=2,
-            grid=(rows // tile,),
+            grid=(1,),
             in_specs=[
                 resident,
                 by_rows(depth),
@@ -356,8 +339,8 @@
             + [resident] * len(pieces),
             out_specs=out_specs,
             scratch_shapes=[
-                pltpu.VMEM((2, tile, width), jnp.bfloat16),
-                pltpu.SemaphoreType.DMA((2, tile // GROUP)),
+                pltpu.VMEM((rows, width), jnp.bfloat16),
+                pltpu.SemaphoreType.DMA((rows // GROUP,)),
             ],
         ),
         out_shape=out_shape[: len(out_specs)],
@@ -470,7 +453,7 @@
     source = jnp.sum(jnp.where(hits, packs_of, 0), (1, 2)).reshape(planes, -1)
     step = jnp.arange(planes, dtype=jnp.int32)
     source = source[(plane + step) % planes].reshape(-1)
-    joins = (plane - step) % planes
+    joins = (plane - jnp.array([0, 2, 1, 3], jnp.int32)) % planes
     plan = own_dest, own_length, source, joins
 
     cut = FIRST_HEADS * HD
@@ -531,7 +514,7 @@
         parts = place(source, received, planes)
         return [parts[0]] + [
             lax.ppermute(parts[k], "mp", [(i, (i + k) % planes) for i in range(planes)])
-            for k in range(1, planes)
+            for k in (2, 1, 3)
         ]
 
     columns = planes * w_query.shape[1]

time: 174 us -> 173 us (level)
    unnamed x42 -> x44, local copies, waits for them, and re-layouts: 15.2 us -> 15.2 us
  transfers between devices with their start and end apart: 23 -> 23, of which waited for: 10 -> 9; matrix products, arithmetic and copies ran while one was open for 3% -> 4% of each run, Pallas kernels for 28% -> 27%
where the time goes in v6:
time: 173 us; the launch traced here: 172 us
  Pallas kernels  56.9 us (33%)
  waiting for transfers between devices  53.9 us (31%)
  starting transfers between devices  39.6 us (23%)
  local copies, waits for them, and re-layouts  18.5 us (11%)
  other arithmetic  2.83 us (2%)
    all_to_all x2, waiting for transfers between devices, exchanged(): lax.all_to_all(sent, 'dp', split_axis=0, concat_axis=0, tiled=True)  37.1 us
    pallas_call x4, Pallas kernels, project(): pl.pallas_call(add_kernel if totals else first_kernel, grid=(rows // tile...  23.2 us
    unnamed x44, local copies, waits for them, and re-layouts  15.2 us
    pallas_call x2, Pallas kernels, norm(): pl.pallas_call(norm_kernel if scale is None else functools.partial(norm_r...  14.2 us
    pallas_call x2, Pallas kernels, attend(): pl.pallas_call(functools.partial(attend_kernel, columns), grid_spec=pltpu...  11 us
    ppermute x6, starting transfers between devices, exchanged(): lax.ppermute(parts[k], 'mp', [(i, (i + k) % planes) for i in range(planes)])  10.9 us
    ppermute x6, waiting for transfers between devices, second(): return lax.ppermute(piece, 'dp', shift_pairs(0, by))  10 us
    all_to_all x2, starting transfers between devices, exchanged(): lax.all_to_all(sent, 'dp', split_axis=0, concat_axis=0, tiled=True)  9.58 us
  transfers between devices with their start and end apart: 23, of which 9 were waited for; matrix products, arithmetic and copies ran while one was open for 4% of the time, Pallas kernels for 27%

profile of v6, /device:TPU:1, one launch (start us, length us, event | category | flops | bytes accessed | tf_op | source)
XLA Modules:
  0.0 172.3 jit_solution(16776539688423921031)
XLA Ops:
  0.0 2.0 %side_by_side.1 = bf16[256,1280]{1,0:T(8,128)(2,1)} custom-call(bf16[256,1024]{1,0:T(8,128)(2,1)} %query_ref.1, bf16[256,256]{1,0:T(8,128)(2,1)} %keyval_ref.1), custom_call_target="tpu_custom_call" | custom-call | tf_op jit(solution)/shard_map/side_by_side/pallas_call | solution.py:114
  2.0 2.5 %collective-permute-start = (bf16[256,1280]{1,0:T(8,128)(2,1)}, bf16[256,1280]{1,0:T(8,128)(2,1)S(1)}, u32[]{:S(2)}, u32[]{:S(2)}) collective-permute-start(bf16[256,1280]{1,0:T(8,128)(2,1)} %side_by_side.1), channel_id=1, source_target_pairs={{0,32},{4,12},{8,40},{12,20},{16,48},{20,28},{24,56},{28,4},{32,64... | collective-permute-start | bytes 1966088 | tf_op jit(solution)/shard_map/ppermute | solution.py:438
  4.5 2.2 %collective-permute-start.1 = (bf16[256,1280]{1,0:T(8,128)(2,1)}, bf16[256,1280]{1,0:T(8,128)(2,1)S(1)}, u32[]{:S(2)}, u32[]{:S(2)}) collective-permute-start(bf16[256,1280]{1,0:T(8,128)(2,1)} %side_by_side.1), channel_id=1, source_target_pairs={{0,96},{4,28},{8,104},{12,4},{16,112},{20,12},{24,120},{28,20},{32... | collective-permute-start | bytes 1966088 | tf_op jit(solution)/shard_map/ppermute | solution.py:438
  16.2 5.8 %copy-done.2 = bf16[1024,8192]{1,0:T(8,128)(2,1)S(1)} copy-done((bf16[1024,8192]{1,0:T(8,128)(2,1)S(1)}, bf16[1024,8192]{1,0:T(8,128)(2,1)}, u32[]{:S(2)}) %copy-start.2) | copy-done | bytes 16777240
  22.8 6.4 %norm.2 = (f32[1024,1]{1,0:T(8,128)S(1)}, bf16[1024,1536]{1,0:T(8,128)(2,1)}) custom-call(s32[64]{0:T(128)S(1)} %fusion.4.order_ref, bf16[1024,8192]{1,0:T(8,128)(2,1)S(1)} %copy-done.2, f32[1,8192]{1,0:T(1,128)S(1)} %bitcast.6), custom_call_target="tpu_custom_call" | custom-call | flops 50331648 | bytes 19922944 | tf_op jit(solution)/shard_map/norm/pallas_call | solution.py:166
  31.6 1.7 collective-permute-start.6
  33.3 7.8 %norm.3 = (bf16[1024,3072]{1,0:T(8,128)(2,1)}, bf16[1024,1536]{1,0:T(8,128)(2,1)}, bf16[1024,1024]{1,0:T(8,128)(2,1)}, bf16[1024,1024]{1,0:T(8,128)(2,1)}) custom-call(s32[64]{0:T(128)S(1)} %fusion.4.order_ref, bf16[1024,8192]{1,0:T(8,128)(2,1)S(1)} %copy-done.2, f32[1,8192]{1,0:T(1,128)S(1)} %bitcast.7, f32[1024,1]{1,0:T(8,128)S(1)} %get-tuple-element.58.scale_ref), custom_call_target="tpu_custom_call" | custom-call | flops 50331648 | bytes 30408704 | tf_op jit(solution)/shard_map/norm/pallas_call | solution.py:166
  41.2 4.8 %project.4.total_ref = f32[1024,1280]{1,0:T(8,128)S(1)} custom-call(bf16[1024,1536]{1,0:T(8,128)(2,1)S(1)} %copy-done.16, bf16[768,1280]{1,0:T(8,128)(2,1)S(1)} %constant_dynamic-update-slice_fusion.refs_0_, bf16[768,1280]{1,0:T(8,128)(2,1)S(1)} %pad_maximum_fusion.refs_1_), custom_call_target="tpu_custom_call" | custom-call | flops 4026531840 | bytes 17563648 | tf_op jit(solution)/shard_map/project/pallas_call | solution.py:215
  46.0 9.6 %collective-permute-done.5.refs_2_ = bf16[768,1280]{1,0:T(8,128)(2,1)S(1)} collective-permute-done((bf16[768,1280]{1,0:T(8,128)(2,1)S(1)}, bf16[768,1280]{1,0:T(8,128)(2,1)S(1)}, u32[]{:S(2)}, u32[]{:S(2)}) %collective-permute-start.5) | collective-permute-done | bytes 1966112 | tf_op jit(solution)/shard_map/ppermute | solution.py:441
  55.6 2.2 %collective-permute-start.10 = (bf16[768,1280]{1,0:T(8,128)(2,1)S(1)}, bf16[768,1280]{1,0:T(8,128)(2,1)S(1)}, u32[]{:S(2)}, u32[]{:S(2)}) collective-permute-start(bf16[768,1280]{1,0:T(8,128)(2,1)S(1)} %pad_maximum_fusion.refs_1_), channel_id=1, source_target_pairs={{0,4},{4,0},{8,12},{12,8},{16,20},{20,16},{24,28},{28,24},{32,36},... | collective-permute-start | bytes 5898248 | tf_op jit(solution)/shard_map/ppermute | solution.py:444
  58.6 1.7 collective-permute-start.8
  62.5 1.7 collective-permute-done.9.refs_0_
  64.2 9.5 %project.5.total_ref = f32[1024,1280]{1,0:T(8,128)S(1)} custom-call(f32[1024,1280]{1,0:T(8,128)S(1)} %project.4.total_ref, bf16[1024,3072]{1,0:T(8,128)(2,1)S(1)} %bitcast.9, bf16[768,1280]{1,0:T(8,128)(2,1)S(1)} %collective-permute-done.9.refs_0_, bf16[768,1280]{1,0:T(8,128)(2,1)S(1)} %collective-permute-done.10.refs_1_, ...), custom_call_target="tpu_custom_call", output_to_operand_aliasing={{}: (0, {})} | custom-call | flops 8053063680 | bytes 24641536 | tf_op jit(solution)/shard_map/project/pallas_call | solution.py:215
  73.7 5.2 %project.6.total_ref = f32[1024,1280]{1,0:T(8,128)S(1)} custom-call(f32[1024,1280]{1,0:T(8,128)S(1)} %project.5.total_ref, bf16[1024,1536]{1,0:T(8,128)(2,1)S(1)} %copy-done.9, bf16[768,1280]{1,0:T(8,128)(2,1)S(1)} %collective-permute-done.11.refs_0_, bf16[768,1280]{1,0:T(8,128)(2,1)S(1)} %collective-permute-done.12.refs_1_), custom_call_target="tpu_custom_call", output_to_operand_aliasing={{}: (0, {})} | custom-call | flops 4026531840 | bytes 17563648 | tf_op jit(solution)/shard_map/project/pallas_call | solution.py:215
  79.3 2.1 %collective-permute-start.13 = (bf16[512,1280]{1,0:T(8,128)(2,1)S(1)}, bf16[512,1280]{1,0:T(8,128)(2,1)S(1)}, u32[]{:S(2)}, u32[]{:S(2)}) collective-permute-start(bf16[512,1280]{1,0:T(8,128)(2,1)S(1)} %collective-permute-done.7.refs_0_), channel_id=1, source_target_pairs={{0,4},{4,0},{8,12},{12,8},{16,20},{20,16},{24,28},{28,24},{32,36},... | collective-permute-start | bytes 3932168 | tf_op jit(solution)/shard_map/ppermute | solution.py:444
  81.4 3.8 %project.7.total_ref = f32[1024,1280]{1,0:T(8,128)S(1)} custom-call(f32[1024,1280]{1,0:T(8,128)S(1)} %project.6.total_ref, bf16[1024,1024]{1,0:T(8,128)(2,1)S(1)} %copy-done.10, bf16[512,1280]{1,0:T(8,128)(2,1)S(1)} %collective-permute-done.7.refs_0_, bf16[512,1280]{1,0:T(8,128)(2,1)S(1)} %collective-permute-done.8.refs_1_), custom_call_target="tpu_custom_call", output_to_operand_aliasing={{}: (0, {})} | custom-call | flops 2684354560 | bytes 15204352 | tf_op jit(solution)/shard_map/project/pallas_call | solution.py:215
  86.0 6.2 %attend.2 = (bf16[32,64,768]{2,1,0:T(8,128)(2,1)}, bf16[1024,256]{1,0:T(8,128)(2,1)S(1)}) custom-call(s32[16]{0:T(128)S(1)} %get-tuple-element.50.dest_ref, s32[16]{0:T(128)S(1)} %get-tuple-element.51.length_ref, f32[1024,1280]{1,0:T(8,128)S(1)} %project.7.total_ref, bf16[1024,1024]{1,0:T(8,128)(2,1)S(1)} %copy-done.3, ...), custom_call_target="tpu_custom_call" | custom-call | flops 2147483648 | bytes 12582912 | tf_op jit(solution)/shard_map/attend/pallas_call | solution.py:326
  93.0 4.5 %all-to-all-start = ((bf16[32,64,768]{2,1,0:T(8,128)(2,1)}), bf16[32,64,768]{2,1,0:T(8,128)(2,1)S(1)}, u32[]{:S(2)}, u32[]{:S(2)}) async-start(bf16[32,64,768]{2,1,0:T(8,128)(2,1)} %get-tuple-element.77), calls=%async_computation | async-start | bytes 6291456 | tf_op jit(solution)/shard_map/all_to_all | solution.py:513
  97.6 2.5 %copy-done.1 = f32[1024,1280]{1,0:T(8,128)S(1)} copy-done((f32[1024,1280]{1,0:T(8,128)S(1)}, f32[1024,1280]{1,0:T(8,128)}, u32[]{:S(2)}) %copy-start.1) | copy-done | bytes 5242904
  100.1 1.6 copy-done.4
  105.3 4.8 %attend.3 = bf16[32,64,256]{2,1,0:T(8,128)(2,1)} custom-call(s32[16]{0:T(128)S(1)} %get-tuple-element.50.dest_ref, s32[16]{0:T(128)S(1)} %get-tuple-element.51.length_ref, f32[1024,1280]{1,0:T(8,128)S(1)} %copy-done.1, bf16[1024,1024]{1,0:T(8,128)(2,1)S(1)} %copy-done.4, f32[1,1280]{1,0:T(1,128)S(1)} %broadcast_in_dim.26.bias_ref, ...), custom_call_target="tpu_custom_call" | custom-call | flops 536870912 | bytes 4718592 | tf_op jit(solution)/shard_map/attend/pallas_call | solution.py:326
  110.2 27.2 %all-to-all-done.received_ref = bf16[32,64,768]{2,1,0:T(8,128)(2,1)S(1)} async-done(((bf16[32,64,768]{2,1,0:T(8,128)(2,1)}), bf16[32,64,768]{2,1,0:T(8,128)(2,1)S(1)}, u32[]{:S(2)}, u32[]{:S(2)}) %all-to-all-start) | async-done | bytes 3145760 | tf_op jit(solution)/shard_map/all_to_all | solution.py:513
  137.4 5.0 %all-to-all-start.1 = ((bf16[32,64,256]{2,1,0:T(8,128)(2,1)}), bf16[32,64,256]{2,1,0:T(8,128)(2,1)}, u32[]{:S(2)}, u32[]{:S(2)}) async-start(bf16[32,64,256]{2,1,0:T(8,128)(2,1)} %attend.3), calls=%async_computation.1 | async-start | bytes 2097152 | tf_op jit(solution)/shard_map/all_to_all | solution.py:513
  142.4 1.6 place.2
  144.0 2.7 %collective-permute-start.15 = (bf16[256,768]{1,0:T(8,128)(2,1)}, bf16[256,768]{1,0:T(8,128)(2,1)S(1)}, u32[]{:S(2)}, u32[]{:S(2)}) collective-permute-start(bf16[256,768]{1,0:T(8,128)(2,1)} %get-tuple-element.79), channel_id=1, source_target_pairs={{0,2},{1,3},{2,0},{3,1},{4,6},{5,7},{6,4},{7,5},{8,10},{9,11},{10,... | collective-permute-start | bytes 1179656 | tf_op jit(solution)/shard_map/ppermute | solution.py:516
  147.1 2.4 %collective-permute-start.17 = (bf16[256,768]{1,0:T(8,128)(2,1)}, bf16[256,768]{1,0:T(8,128)(2,1)S(1)}, u32[]{:S(2)}, u32[]{:S(2)}) collective-permute-start(bf16[256,768]{1,0:T(8,128)(2,1)} %get-tuple-element.81), channel_id=1, source_target_pairs={{0,3},{1,0},{2,1},{3,2},{4,7},{5,4},{6,5},{7,6},{8,11},{9,8},{10,9... | collective-permute-start | bytes 1179656 | tf_op jit(solution)/shard_map/ppermute | solution.py:516
  149.5 9.9 %all-to-all-done.1.received_ref = bf16[32,64,256]{2,1,0:T(8,128)(2,1)} async-done(((bf16[32,64,256]{2,1,0:T(8,128)(2,1)}), bf16[32,64,256]{2,1,0:T(8,128)(2,1)}, u32[]{:S(2)}, u32[]{:S(2)}) %all-to-all-start.1) | async-done | bytes 1048608 | tf_op jit(solution)/shard_map/all_to_all | solution.py:513
  159.4 1.8 %place.3 = (bf16[256,256]{1,0:T(8,128)(2,1)S(1)}, bf16[256,256]{1,0:T(8,128)(2,1)S(1)}, bf16[256,256]{1,0:T(8,128)(2,1)S(1)}, bf16[256,256]{1,0:T(8,128)(2,1)S(1)}) custom-call(s32[16]{0:T(128)S(1)} %reshape.58.source_ref, bf16[32,64,256]{2,1,0:T(8,128)(2,1)} %all-to-all-done.1.received_ref), custom_call_target="tpu_custom_call" | custom-call | tf_op jit(solution)/shard_map/place/pallas_call | solution.py:364
  161.2 2.8 %collective-permute-start.18 = (bf16[256,256]{1,0:T(8,128)(2,1)S(1)}, bf16[256,256]{1,0:T(8,128)(2,1)S(1)}, u32[]{:S(2)}, u32[]{:S(2)}) collective-permute-start(bf16[256,256]{1,0:T(8,128)(2,1)S(1)} %get-tuple-element.84), channel_id=1, source_target_pairs={{0,2},{1,3},{2,0},{3,1},{4,6},{5,7},{6,4},{7,5},{8,10},{9,11},{10,... | collective-permute-start | bytes 393224 | tf_op jit(solution)/shard_map/ppermute | solution.py:516
  164.3 2.4 %collective-permute-start.20 = (bf16[256,256]{1,0:T(8,128)(2,1)S(1)}, bf16[256,256]{1,0:T(8,128)(2,1)S(1)}, u32[]{:S(2)}, u32[]{:S(2)}) collective-permute-start(bf16[256,256]{1,0:T(8,128)(2,1)S(1)} %get-tuple-element.86), channel_id=1, source_target_pairs={{0,3},{1,0},{2,1},{3,2},{4,7},{5,4},{6,5},{7,6},{8,11},{9,8},{10,9... | collective-permute-start | bytes 393224 | tf_op jit(solution)/shard_map/ppermute | solution.py:516
  166.7 1.7 join.2.refs_0_
  168.4 2.3 %collective-permute-done.19.refs_3_ = bf16[256,256]{1,0:T(8,128)(2,1)S(1)} collective-permute-done((bf16[256,256]{1,0:T(8,128)(2,1)S(1)}, bf16[256,256]{1,0:T(8,128)(2,1)S(1)}, u32[]{:S(2)}, u32[]{:S(2)}) %collective-permute-start.19) | collective-permute-done | bytes 131104 | tf_op jit(solution)/shard_map/ppermute | solution.py:516
  (95 shorter events, 23.4 us)
Async XLA Ops:
  2.0 27.2 %collective-permute-start = (bf16[256,1280]{1,0:T(8,128)(2,1)}, bf16[256,1280]{1,0:T(8,128)(2,1)S(1)}, u32[]{:S(2)}, u32[]{:S(2)}) collective-permute-start(bf16[256,1280]{1,0:T(8,128)(2,1)} %side_by_side.1), channel_id=1, source_target_pairs={{0,32},{4,12},{8,40},{12,20},{16,48},{20,28},{24,56},{28,4},{32,64... | collective-permute-start | bytes 1966088 | tf_op jit(solution)/shard_map/ppermute | solution.py:438
  4.5 24.7 %collective-permute-start.1 = (bf16[256,1280]{1,0:T(8,128)(2,1)}, bf16[256,1280]{1,0:T(8,128)(2,1)S(1)}, u32[]{:S(2)}, u32[]{:S(2)}) collective-permute-start(bf16[256,1280]{1,0:T(8,128)(2,1)} %side_by_side.1), channel_id=1, source_target_pairs={{0,96},{4,28},{8,104},{12,4},{16,112},{20,12},{24,120},{28,20},{32... | collective-permute-start | bytes 1966088 | tf_op jit(solution)/shard_map/ppermute | solution.py:438
  6.7 23.6 %collective-permute-start.2 = (bf16[256,1280]{1,0:T(8,128)(2,1)}, bf16[256,1280]{1,0:T(8,128)(2,1)S(1)}, u32[]{:S(2)}, u32[]{:S(2)}) collective-permute-start(bf16[256,1280]{1,0:T(8,128)(2,1)} %side_by_side.1), channel_id=1, source_target_pairs={{0,64},{4,20},{8,72},{12,28},{16,80},{20,4},{24,88},{28,12},{32,96... | collective-permute-start | bytes 1966088 | tf_op jit(solution)/shard_map/ppermute | solution.py:438
  7.9 22.4 %collective-permute-start.3 = (bf16[256,1280]{1,0:T(8,128)(2,1)}, bf16[256,1280]{1,0:T(8,128)(2,1)S(1)}, u32[]{:S(2)}, u32[]{:S(2)}) collective-permute-start(bf16[256,1280]{1,0:T(8,128)(2,1)} %side_by_side.1), channel_id=1, source_target_pairs={{0,8},{4,36},{8,16},{12,44},{16,24},{20,52},{24,0},{28,60},{32,40}... | collective-permute-start | bytes 1966088 | tf_op jit(solution)/shard_map/ppermute | solution.py:441
  9.2 21.1 %collective-permute-start.4 = (bf16[256,1280]{1,0:T(8,128)(2,1)}, bf16[256,1280]{1,0:T(8,128)(2,1)S(1)}, u32[]{:S(2)}, u32[]{:S(2)}) collective-permute-start(bf16[256,1280]{1,0:T(8,128)(2,1)} %side_by_side.1), channel_id=1, source_target_pairs={{0,24},{4,100},{8,0},{12,108},{16,8},{20,116},{24,16},{28,124},{32... | collective-permute-start | bytes 1966088 | tf_op jit(solution)/shard_map/ppermute | solution.py:441
  30.5 10.5 %copy-start.17 = (bf16[256,1280]{1,0:T(8,128)(2,1)S(1)}, bf16[256,1280]{1,0:T(8,128)(2,1)}, u32[]{:S(2)}) copy-start(bf16[256,1280]{1,0:T(8,128)(2,1)} %side_by_side.1) | copy-start | bytes 1966084
  30.5 25.1 %collective-permute-start.5 = (bf16[768,1280]{1,0:T(8,128)(2,1)S(1)}, bf16[768,1280]{1,0:T(8,128)(2,1)S(1)}, u32[]{:S(2)}, u32[]{:S(2)}) collective-permute-start(bf16[768,1280]{1,0:T(8,128)(2,1)S(1)} %constant_dynamic-update-slice_fusion.refs_0_), channel_id=1, source_target_pairs={{0,8},{4,36},{8,16},{12,44},{16,24},{20,52},{24,0},{28,60},{32,40}... | collective-permute-start | bytes 5898248 | tf_op jit(solution)/shard_map/ppermute | solution.py:441
  31.6 24.0 %collective-permute-start.6 = (bf16[768,1280]{1,0:T(8,128)(2,1)S(1)}, bf16[768,1280]{1,0:T(8,128)(2,1)S(1)}, u32[]{:S(2)}, u32[]{:S(2)}) collective-permute-start(bf16[768,1280]{1,0:T(8,128)(2,1)S(1)} %constant_dynamic-update-slice_fusion.refs_0_), channel_id=1, source_target_pairs={{0,24},{4,100},{8,0},{12,108},{16,8},{20,116},{24,16},{28,124},{32... | collective-permute-start | bytes 5898248 | tf_op jit(solution)/shard_map/ppermute | solution.py:441
  33.3 7.9 %copy-start.16 = (bf16[1024,1536]{1,0:T(8,128)(2,1)S(1)}, bf16[1024,1536]{1,0:T(8,128)(2,1)}, u32[]{:S(2)}) copy-start(bf16[1024,1536]{1,0:T(8,128)(2,1)} %get-tuple-element.57.x_ref) | copy-start | bytes 9437188
  41.0 23.1 %slice-start = ((s8[6291456]{0:T(1024)(128)(4,1)}), s8[4194304]{0:T(1024)(128)(4,1)S(1)}, s32[]{:S(2)}) async-start(s8[6291456]{0:T(1024)(128)(4,1)} %bitcast.8), calls=%async_computation.2 | async-start | bytes 8388608
  41.2 23.0 %slice-start.1 = ((s8[6291456]{0:T(1024)(128)(4,1)}), s8[2097152]{0:T(1024)(128)(4,1)S(1)}, s32[]{:S(2)}) async-start(s8[6291456]{0:T(1024)(128)(4,1)} %bitcast.8), calls=%async_computation.3 | async-start | bytes 4194304
  55.6 5.8 %collective-permute-start.10 = (bf16[768,1280]{1,0:T(8,128)(2,1)S(1)}, bf16[768,1280]{1,0:T(8,128)(2,1)S(1)}, u32[]{:S(2)}, u32[]{:S(2)}) collective-permute-start(bf16[768,1280]{1,0:T(8,128)(2,1)S(1)} %pad_maximum_fusion.refs_1_), channel_id=1, source_target_pairs={{0,4},{4,0},{8,12},{12,8},{16,20},{20,16},{24,28},{28,24},{32,36},... | collective-permute-start | bytes 5898248 | tf_op jit(solution)/shard_map/ppermute | solution.py:444
  57.7 6.4 %collective-permute-start.9 = (bf16[768,1280]{1,0:T(8,128)(2,1)S(1)}, bf16[768,1280]{1,0:T(8,128)(2,1)S(1)}, u32[]{:S(2)}, u32[]{:S(2)}) collective-permute-start(bf16[768,1280]{1,0:T(8,128)(2,1)S(1)} %constant_dynamic-update-slice_fusion.refs_0_), channel_id=1, source_target_pairs={{0,4},{4,0},{8,12},{12,8},{16,20},{20,16},{24,28},{28,24},{32,36},... | collective-permute-start | bytes 5898248 | tf_op jit(solution)/shard_map/ppermute | solution.py:444
  57.7 15.9 %collective-permute-start.11 = (bf16[768,1280]{1,0:T(8,128)(2,1)S(1)}, bf16[768,1280]{1,0:T(8,128)(2,1)S(1)}, u32[]{:S(2)}, u32[]{:S(2)}) collective-permute-start(bf16[768,1280]{1,0:T(8,128)(2,1)S(1)} %collective-permute-done.5.refs_2_), channel_id=1, source_target_pairs={{0,4},{4,0},{8,12},{12,8},{16,20},{20,16},{24,28},{28,24},{32,36},... | collective-permute-start | bytes 5898248 | tf_op jit(solution)/shard_map/ppermute | solution.py:444
  58.2 15.4 %collective-permute-start.12 = (bf16[768,1280]{1,0:T(8,128)(2,1)S(1)}, bf16[768,1280]{1,0:T(8,128)(2,1)S(1)}, u32[]{:S(2)}, u32[]{:S(2)}) collective-permute-start(bf16[768,1280]{1,0:T(8,128)(2,1)S(1)} %collective-permute-done.6.refs_3_), channel_id=1, source_target_pairs={{0,4},{4,0},{8,12},{12,8},{16,20},{20,16},{24,28},{28,24},{32,36},... | collective-permute-start | bytes 5898248 | tf_op jit(solution)/shard_map/ppermute | solution.py:444
  58.6 20.3 %collective-permute-start.8 = (bf16[512,1280]{1,0:T(8,128)(2,1)S(1)}, bf16[512,1280]{1,0:T(8,128)(2,1)S(1)}, u32[]{:S(2)}, u32[]{:S(2)}) collective-permute-start(bf16[512,1280]{1,0:T(8,128)(2,1)S(1)} %pad_maximum_fusion.2), channel_id=1, source_target_pairs={{0,24},{4,100},{8,0},{12,108},{16,8},{20,116},{24,16},{28,124},{32... | collective-permute-start | bytes 3932168 | tf_op jit(solution)/shard_map/ppermute | solution.py:441
  61.3 18.0 %collective-permute-start.7 = (bf16[512,1280]{1,0:T(8,128)(2,1)S(1)}, bf16[512,1280]{1,0:T(8,128)(2,1)S(1)}, u32[]{:S(2)}, u32[]{:S(2)}) collective-permute-start(bf16[512,1280]{1,0:T(8,128)(2,1)S(1)} %pad_maximum_fusion.1), channel_id=1, source_target_pairs={{0,8},{4,36},{8,16},{12,44},{16,24},{20,52},{24,0},{28,60},{32,40}... | collective-permute-start | bytes 3932168 | tf_op jit(solution)/shard_map/ppermute | solution.py:441
  64.2 9.5 %copy-start.9 = (bf16[1024,1536]{1,0:T(8,128)(2,1)S(1)}, bf16[1024,1536]{1,0:T(8,128)(2,1)}, u32[]{:S(2)}) copy-start(bf16[1024,1536]{1,0:T(8,128)(2,1)} %get-tuple-element.70.x_ref) | copy-start | bytes 9437188
  73.6 7.8 %copy-start.10 = (bf16[1024,1024]{1,0:T(8,128)(2,1)S(1)}, bf16[1024,1024]{1,0:T(8,128)(2,1)}, u32[]{:S(2)}) copy-start(bf16[1024,1024]{1,0:T(8,128)(2,1)} %get-tuple-element.72.x_ref) | copy-start | bytes 6291460
  78.9 7.1 %copy-start.3 = (bf16[1024,1024]{1,0:T(8,128)(2,1)S(1)}, bf16[1024,1024]{1,0:T(8,128)(2,1)}, u32[]{:S(2)}) copy-start(bf16[1024,1024]{1,0:T(8,128)(2,1)} %get-tuple-element.75.x_ref) | copy-start | bytes 6291460
  78.9 7.1 %copy-start.13 = (f32[256,128]{1,0:T(8,128)S(1)}, f32[256,128]{1,0:T(8,128)}, u32[]{:S(2)}) copy-start(f32[256,128]{1,0:T(8,128)} %constant.68.clone.cosine_ref) | copy-start | bytes 393220
  78.9 7.1 %copy-start.14 = (f32[256,128]{1,0:T(8,128)S(1)}, f32[256,128]{1,0:T(8,128)}, u32[]{:S(2)}) copy-start(f32[256,128]{1,0:T(8,128)} %constant.69.clone.sine_ref) | copy-start | bytes 393220
  79.3 5.9 %collective-permute-start.13 = (bf16[512,1280]{1,0:T(8,128)(2,1)S(1)}, bf16[512,1280]{1,0:T(8,128)(2,1)S(1)}, u32[]{:S(2)}, u32[]{:S(2)}) collective-permute-start(bf16[512,1280]{1,0:T(8,128)(2,1)S(1)} %collective-permute-done.7.refs_0_), channel_id=1, source_target_pairs={{0,4},{4,0},{8,12},{12,8},{16,20},{20,16},{24,28},{28,24},{32,36},... | collective-permute-start | bytes 3932168 | tf_op jit(solution)/shard_map/ppermute | solution.py:444
  81.4 4.5 %collective-permute-start.14 = (bf16[512,1280]{1,0:T(8,128)(2,1)S(1)}, bf16[512,1280]{1,0:T(8,128)(2,1)S(1)}, u32[]{:S(2)}, u32[]{:S(2)}) collective-permute-start(bf16[512,1280]{1,0:T(8,128)(2,1)S(1)} %collective-permute-done.8.refs_1_), channel_id=1, source_target_pairs={{0,4},{4,0},{8,12},{12,8},{16,20},{20,16},{24,28},{28,24},{32,36},... | collective-permute-start | bytes 3932168 | tf_op jit(solution)/shard_map/ppermute | solution.py:444
  93.0 44.3 %all-to-all-start = ((bf16[32,64,768]{2,1,0:T(8,128)(2,1)}), bf16[32,64,768]{2,1,0:T(8,128)(2,1)S(1)}, u32[]{:S(2)}, u32[]{:S(2)}) async-start(bf16[32,64,768]{2,1,0:T(8,128)(2,1)} %get-tuple-element.77), calls=%async_computation | async-start | bytes 6291456 | tf_op jit(solution)/shard_map/all_to_all | solution.py:513
  137.4 22.0 %all-to-all-start.1 = ((bf16[32,64,256]{2,1,0:T(8,128)(2,1)}), bf16[32,64,256]{2,1,0:T(8,128)(2,1)}, u32[]{:S(2)}, u32[]{:S(2)}) async-start(bf16[32,64,256]{2,1,0:T(8,128)(2,1)} %attend.3), calls=%async_computation.1 | async-start | bytes 2097152 | tf_op jit(solution)/shard_map/all_to_all | solution.py:513
  144.0 20.3 %collective-permute-start.15 = (bf16[256,768]{1,0:T(8,128)(2,1)}, bf16[256,768]{1,0:T(8,128)(2,1)S(1)}, u32[]{:S(2)}, u32[]{:S(2)}) collective-permute-start(bf16[256,768]{1,0:T(8,128)(2,1)} %get-tuple-element.79), channel_id=1, source_target_pairs={{0,2},{1,3},{2,0},{3,1},{4,6},{5,7},{6,4},{7,5},{8,10},{9,11},{10,... | collective-permute-start | bytes 1179656 | tf_op jit(solution)/shard_map/ppermute | solution.py:516
  146.8 19.9 %collective-permute-start.16 = (bf16[256,768]{1,0:T(8,128)(2,1)}, bf16[256,768]{1,0:T(8,128)(2,1)S(1)}, u32[]{:S(2)}, u32[]{:S(2)}) collective-permute-start(bf16[256,768]{1,0:T(8,128)(2,1)} %get-tuple-element.80), channel_id=1, source_target_pairs={{0,1},{1,2},{2,3},{3,0},{4,5},{5,6},{6,7},{7,4},{8,9},{9,10},{10,1... | collective-permute-start | bytes 1179656 | tf_op jit(solution)/shard_map/ppermute | solution.py:516
  147.1 19.6 %collective-permute-start.17 = (bf16[256,768]{1,0:T(8,128)(2,1)}, bf16[256,768]{1,0:T(8,128)(2,1)S(1)}, u32[]{:S(2)}, u32[]{:S(2)}) collective-permute-start(bf16[256,768]{1,0:T(8,128)(2,1)} %get-tuple-element.81), channel_id=1, source_target_pairs={{0,3},{1,0},{2,1},{3,2},{4,7},{5,4},{6,5},{7,6},{8,11},{9,8},{10,9... | collective-permute-start | bytes 1179656 | tf_op jit(solution)/shard_map/ppermute | solution.py:516
  161.2 7.2 %collective-permute-start.18 = (bf16[256,256]{1,0:T(8,128)(2,1)S(1)}, bf16[256,256]{1,0:T(8,128)(2,1)S(1)}, u32[]{:S(2)}, u32[]{:S(2)}) collective-permute-start(bf16[256,256]{1,0:T(8,128)(2,1)S(1)} %get-tuple-element.84), channel_id=1, source_target_pairs={{0,2},{1,3},{2,0},{3,1},{4,6},{5,7},{6,4},{7,5},{8,10},{9,11},{10,... | collective-permute-start | bytes 393224 | tf_op jit(solution)/shard_map/ppermute | solution.py:516
  164.0 6.8 %collective-permute-start.19 = (bf16[256,256]{1,0:T(8,128)(2,1)S(1)}, bf16[256,256]{1,0:T(8,128)(2,1)S(1)}, u32[]{:S(2)}, u32[]{:S(2)}) collective-permute-start(bf16[256,256]{1,0:T(8,128)(2,1)S(1)} %get-tuple-element.85), channel_id=1, source_target_pairs={{0,1},{1,2},{2,3},{3,0},{4,5},{5,6},{6,7},{7,4},{8,9},{9,10},{10,1... | collective-permute-start | bytes 393224 | tf_op jit(solution)/shard_map/ppermute | solution.py:516
  164.3 6.4 %collective-permute-start.20 = (bf16[256,256]{1,0:T(8,128)(2,1)S(1)}, bf16[256,256]{1,0:T(8,128)(2,1)S(1)}, u32[]{:S(2)}, u32[]{:S(2)}) collective-permute-start(bf16[256,256]{1,0:T(8,128)(2,1)S(1)} %get-tuple-element.86), channel_id=1, source_target_pairs={{0,3},{1,0},{2,1},{3,2},{4,7},{5,4},{6,5},{7,6},{8,11},{9,8},{10,9... | collective-permute-start | bytes 393224 | tf_op jit(solution)/shard_map/ppermute | solution.py:516
  (12 other events, 41.7 us)

commit v7 on v6

--- a/solution.py
+++ b/solution.py
@@ -13,7 +13,7 @@
 SIDE = 4
 MIB = 1024 * 1024
 FIRST_HEADS = 6
-PIECES = (6, 12, 6, 4, 4)
+PIECES = (6, 6, 6, 6, 4, 4)
 
 rope_base = 1000000.0
 norm_epsilon = 1e-06
@@ -78,8 +78,8 @@
                 near += [(0, 0, both), (0, 1, both), (0, 3, both)]
                 corners = [(1, 1, both), (3, 1, both), (2, 1, both)]
                 corners += [(1, 3, both), (3, 3, both), (2, 3, both)]
-                far = [(1, 2, both), (2, 2, low), (0, 2, low)]
-                far += [(3, 2, both), (2, 2, high), (0, 2, high)]
+                far = [(3, 2, both), (2, 2, high), (0, 2, high)]
+                far += [(1, 2, both), (2, 2, low), (0, 2, low)]
                 order = []
                 for offsets in (near, corners, far):
                     order += blocks(core, offsets) + blocks(1 - core, offsets)
@@ -205,7 +205,10 @@
     )
 
 
-def project(total, x, pieces):
+SHORT = pl.CostEstimate(flops=1024, bytes_accessed=1024, transcendentals=0)
+
+
+def project(total, x, pieces, cost=None):
     rows, depth = x.shape
     columns = pieces[0].shape[1]
     tile = 256
@@ -220,7 +223,7 @@
         out_shape=jax.ShapeDtypeStruct((rows, columns), jnp.float32),
         input_output_aliases={0: 0} if totals else {},
         compiler_params=pltpu.CompilerParams(vmem_limit_bytes=20 * MIB),
-        cost_estimate=matmul_cost(rows, depth, columns, 2),
+        cost_estimate=cost or matmul_cost(rows, depth, columns, 2),
         name="project",
     )(*totals, x, *pieces)
 
@@ -474,32 +477,38 @@
     own_ahead, own_behind = near[3:]
     beside = jnp.concatenate(near[:3])
     ahead, behind = second(beside, 1), second(beside, -1)
-    x_middle, x_corners, x_far, x_last = norm(
+    x_middle, x_corners, x_swapped, x_far, x_last = norm(
         order, hidden_states, gain, widths[1:], scale, widths[0] // half
     )
     straight = jnp.concatenate([weights, own_ahead, own_behind])
     total = project(None, x_near, [beside, straight])
-
-    ahead, behind, straight, total, x_middle, x_corners, x_far, x_last = lax.optimization_barrier(
-        (ahead, behind, straight, total, x_middle, x_corners, x_far, x_last)
+    pairs = [beside[: 2 * rows_held], jnp.concatenate([near[2], weights]), straight[rows_held:]]
+    pairs = [swap(held_until(piece, total)) for piece in pairs]
+    total = project(total, x_middle, pairs, SHORT)
+
+    ahead, behind, straight, total, x_corners, x_swapped, x_far, x_last = lax.optimization_barrier(
+        (ahead, behind, straight, total, x_corners, x_swapped, x_far, x_last)
     )
     far = [
-        second(
-            jnp.concatenate(
-                [ahead[:rows_held], ahead[2 * rows_held : -half], straight[rows_held : rows_held + half]]
-            ),
-            1,
-        ),
         second(
             jnp.concatenate(
                 [behind[rows_held : 2 * rows_held], behind[-half:], straight[-half:]]
             ),
             -1,
         ),
+        second(
+            jnp.concatenate(
+                [
+                    ahead[:rows_held],
+                    ahead[2 * rows_held : -half],
+                    straight[rows_held : rows_held + half],
+                ]
+            ),
+            1,
+        ),
     ]
-    near = [swap(held_until(piece, ahead)) for piece in (beside, straight)]
-    total = project(total, x_middle, [*near, ahead, behind])
-    total = project(total, x_corners, [swap(ahead), swap(behind)])
+    total = project(total, x_corners, [ahead, behind])
+    total = project(total, x_swapped, [swap(ahead), swap(behind)])
     far, total = lax.optimization_barrier((far, total))
     last = [swap(piece) for piece in far]
     total = project(total, x_far, far)

time: 173 us -> 172 us (level)
  waiting for transfers between devices: 53.9 us -> 46.2 us
  starting transfers between devices: 39.6 us -> 43.3 us
  local copies, waits for them, and re-layouts: 18.5 us -> 20.4 us
    ppermute x6, waiting for transfers between devices: 10 us -> 4.92 us  [second(): return lax.ppermute(piece, 'dp', shift_pairs(0, by))]
    ppermute x6 -> x7, waiting for transfers between devices: 3.38 us -> 0.72 us  [swap(): return lax.ppermute(piece, 'dp', swap_pairs())]
    ppermute x6 -> x7, starting transfers between devices: 4.82 us -> 6.97 us  [swap(): return lax.ppermute(piece, 'dp', swap_pairs())]
    unnamed x44 -> x52, local copies, waits for them, and re-layouts: 15.2 us -> 17.1 us
    pallas_call x4 -> x5, Pallas kernels: 23.2 us -> 24.1 us  [project(): pl.pallas_call(add_kernel if totals else first_kernel, grid=(rows // tile...]
  transfers between devices with their start and end apart: 23 -> 24, of which waited for: 9 -> 8; matrix products, arithmetic and copies ran while one was open for 4% -> 4% of each run, Pallas kernels for 27% -> 28%
where the time goes in v7:
time: 172 us; the launch traced here: 171 us
  Pallas kernels  57.1 us (33%)
  waiting for transfers between devices  46.2 us (27%)
  starting transfers between devices  43.3 us (25%)
  local copies, waits for them, and re-layouts  20.4 us (12%)
  other arithmetic  3.09 us (2%)
    all_to_all x2, waiting for transfers between devices, exchanged(): lax.all_to_all(sent, 'dp', split_axis=0, concat_axis=0, tiled=True)  37.1 us
    pallas_call x5, Pallas kernels, project(): pl.pallas_call(add_kernel if totals else first_kernel, grid=(rows // tile...  24.1 us
    unnamed x52, local copies, waits for them, and re-layouts  17.1 us
    pallas_call x2, Pallas kernels, norm(): pl.pallas_call(norm_kernel if scale is None else functools.partial(norm_r...  13.4 us
    all_to_all x2, starting transfers between devices, exchanged(): lax.all_to_all(sent, 'dp', split_axis=0, concat_axis=0, tiled=True)  11.1 us
    pallas_call x2, Pallas kernels, attend(): pl.pallas_call(functools.partial(attend_kernel, columns), grid_spec=pltpu...  11 us
    ppermute x6, starting transfers between devices, exchanged(): lax.ppermute(parts[k], 'mp', [(i, (i + k) % planes) for i in range(planes)])  10.9 us
    ppermute x6, starting transfers between devices, second(): return lax.ppermute(piece, 'dp', shift_pairs(0, by))  8.3 us
  transfers between devices with their start and end apart: 24, of which 8 were waited for; matrix products, arithmetic and copies ran while one was open for 4% of the time, Pallas kernels for 28%

profile of v7, /device:TPU:1, one launch (start us, length us, event | category | flops | bytes accessed | tf_op | source)
XLA Modules:
  0.0 170.7 jit_solution(1334212558975280025)
XLA Ops:
  0.0 1.9 %side_by_side.1 = bf16[256,1280]{1,0:T(8,128)(2,1)} custom-call(bf16[256,1024]{1,0:T(8,128)(2,1)} %query_ref.1, bf16[256,256]{1,0:T(8,128)(2,1)} %keyval_ref.1), custom_call_target="tpu_custom_call" | custom-call | tf_op jit(solution)/shard_map/side_by_side/pallas_call | solution.py:114
  2.0 2.5 %collective-permute-start = (bf16[256,1280]{1,0:T(8,128)(2,1)}, bf16[256,1280]{1,0:T(8,128)(2,1)S(1)}, u32[]{:S(2)}, u32[]{:S(2)}) collective-permute-start(bf16[256,1280]{1,0:T(8,128)(2,1)} %side_by_side.1), channel_id=1, source_target_pairs={{0,32},{4,12},{8,40},{12,20},{16,48},{20,28},{24,56},{28,4},{32,64... | collective-permute-start | bytes 1966088 | tf_op jit(solution)/shard_map/ppermute | solution.py:441
  4.5 2.2 %collective-permute-start.1 = (bf16[256,1280]{1,0:T(8,128)(2,1)}, bf16[256,1280]{1,0:T(8,128)(2,1)S(1)}, u32[]{:S(2)}, u32[]{:S(2)}) collective-permute-start(bf16[256,1280]{1,0:T(8,128)(2,1)} %side_by_side.1), channel_id=1, source_target_pairs={{0,96},{4,28},{8,104},{12,4},{16,112},{20,12},{24,120},{28,20},{32... | collective-permute-start | bytes 1966088 | tf_op jit(solution)/shard_map/ppermute | solution.py:441
  16.2 5.8 %copy-done.2 = bf16[1024,8192]{1,0:T(8,128)(2,1)S(1)} copy-done((bf16[1024,8192]{1,0:T(8,128)(2,1)S(1)}, bf16[1024,8192]{1,0:T(8,128)(2,1)}, u32[]{:S(2)}) %copy-start.2) | copy-done | bytes 16777240
  22.8 6.4 %norm.2 = (f32[1024,1]{1,0:T(8,128)S(1)}, bf16[1024,1536]{1,0:T(8,128)(2,1)}) custom-call(s32[64]{0:T(128)S(1)} %fusion.4.order_ref, bf16[1024,8192]{1,0:T(8,128)(2,1)S(1)} %copy-done.2, f32[1,8192]{1,0:T(1,128)S(1)} %bitcast.8), custom_call_target="tpu_custom_call" | custom-call | flops 50331648 | bytes 19922944 | tf_op jit(solution)/shard_map/norm/pallas_call | solution.py:166
  31.6 1.7 collective-permute-start.6
  33.4 4.8 %project.5.total_ref = f32[1024,1280]{1,0:T(8,128)S(1)} custom-call(bf16[1024,1536]{1,0:T(8,128)(2,1)S(1)} %copy-done.18, bf16[768,1280]{1,0:T(8,128)(2,1)S(1)} %constant_dynamic-update-slice_fusion.refs_0_, bf16[768,1280]{1,0:T(8,128)(2,1)S(1)} %pad_maximum_fusion.refs_1_), custom_call_target="tpu_custom_call" | custom-call | flops 4026531840 | bytes 17563648 | tf_op jit(solution)/shard_map/project/pallas_call | solution.py:218
  38.3 2.0 %collective-permute-start.9 = (bf16[512,1280]{1,0:T(8,128)(2,1)S(1)}, bf16[512,1280]{1,0:T(8,128)(2,1)S(1)}, u32[]{:S(2)}, u32[]{:S(2)}) collective-permute-start(bf16[512,1280]{1,0:T(8,128)(2,1)S(1)} %pad_maximum_fusion.3), channel_id=1, source_target_pairs={{0,4},{4,0},{8,12},{12,8},{16,20},{20,16},{24,28},{28,24},{32,36},... | collective-permute-start | bytes 3932168 | tf_op jit(solution)/shard_map/ppermute | solution.py:447
  41.2 7.1 %norm.3 = (bf16[1024,1536]{1,0:T(8,128)(2,1)}, bf16[1024,1536]{1,0:T(8,128)(2,1)}, bf16[1024,1536]{1,0:T(8,128)(2,1)}, bf16[1024,1024]{1,0:T(8,128)(2,1)}, bf16[1024,1024]{1,0:T(8,128)(2,1)}) custom-call(s32[64]{0:T(128)S(1)} %fusion.4.order_ref, bf16[1024,8192]{1,0:T(8,128)(2,1)S(1)} %bitcast.7, f32[1,8192]{1,0:T(1,128)S(1)} %bitcast.9, ...), custom_call_target="tpu_custom_call" | custom-call | flops 50331648 | bytes 30408704 | tf_op jit(solution)/shard_map/norm/pallas_call | solution.py:166
  48.3 1.9 %copy-done.11 = bf16[1024,1536]{1,0:T(8,128)(2,1)S(1)} copy-done((bf16[1024,1536]{1,0:T(8,128)(2,1)S(1)}, bf16[1024,1536]{1,0:T(8,128)(2,1)}, u32[]{:S(2)}) %copy-start.11) | copy-done | bytes 3145752
  50.2 5.2 %project.6.total_ref = f32[1024,1280]{1,0:T(8,128)S(1)} custom-call(f32[1024,1280]{1,0:T(8,128)S(1)} %project.5.total_ref, bf16[1024,1536]{1,0:T(8,128)(2,1)S(1)} %copy-done.11, bf16[512,1280]{1,0:T(8,128)(2,1)S(1)} %collective-permute-done.7.refs_0_, bf16[512,1280]{1,0:T(8,128)(2,1)S(1)} %collective-permute-done.8.refs_1_, ...), custom_call_target="tpu_custom_call", output_to_operand_aliasing={{}: (0, {})} | custom-call | flops 1024 | bytes 1024 | tf_op jit(solution)/shard_map/project/pallas_call | solution.py:218
  55.6 2.2 %collective-permute-start.12 = (bf16[768,1280]{1,0:T(8,128)(2,1)S(1)}, bf16[768,1280]{1,0:T(8,128)(2,1)S(1)}, u32[]{:S(2)}, u32[]{:S(2)}) collective-permute-start(bf16[768,1280]{1,0:T(8,128)(2,1)S(1)} %collective-permute-done.5.refs_0_), channel_id=1, source_target_pairs={{0,4},{4,0},{8,12},{12,8},{16,20},{20,16},{24,28},{28,24},{32,36},... | collective-permute-start | bytes 5898248 | tf_op jit(solution)/shard_map/ppermute | solution.py:447
  61.1 5.2 %project.7.total_ref = f32[1024,1280]{1,0:T(8,128)S(1)} custom-call(f32[1024,1280]{1,0:T(8,128)S(1)} %project.6.total_ref, bf16[1024,1536]{1,0:T(8,128)(2,1)S(1)} %copy-done.10, bf16[768,1280]{1,0:T(8,128)(2,1)S(1)} %collective-permute-done.5.refs_0_, bf16[768,1280]{1,0:T(8,128)(2,1)S(1)} %collective-permute-done.6.refs_1_), custom_call_target="tpu_custom_call", output_to_operand_aliasing={{}: (0, {})} | custom-call | flops 4026531840 | bytes 17563648 | tf_op jit(solution)/shard_map/project/pallas_call | solution.py:218
  66.3 5.2 %project.8.total_ref = f32[1024,1280]{1,0:T(8,128)S(1)} custom-call(f32[1024,1280]{1,0:T(8,128)S(1)} %project.7.total_ref, bf16[1024,1536]{1,0:T(8,128)(2,1)S(1)} %copy-done.9, bf16[768,1280]{1,0:T(8,128)(2,1)S(1)} %collective-permute-done.12.refs_0_, bf16[768,1280]{1,0:T(8,128)(2,1)S(1)} %collective-permute-done.13.refs_1_), custom_call_target="tpu_custom_call", output_to_operand_aliasing={{}: (0, {})} | custom-call | flops 4026531840 | bytes 17563648 | tf_op jit(solution)/shard_map/project/pallas_call | solution.py:218
  71.5 4.6 %collective-permute-done.11.refs_1_ = bf16[512,1280]{1,0:T(8,128)(2,1)S(1)} collective-permute-done((bf16[512,1280]{1,0:T(8,128)(2,1)S(1)}, bf16[512,1280]{1,0:T(8,128)(2,1)S(1)}, u32[]{:S(2)}, u32[]{:S(2)}) %collective-permute-start.11) | collective-permute-done | bytes 1310752 | tf_op jit(solution)/shard_map/ppermute | solution.py:444
  76.3 2.0 %collective-permute-start.14 = (bf16[512,1280]{1,0:T(8,128)(2,1)S(1)}, bf16[512,1280]{1,0:T(8,128)(2,1)S(1)}, u32[]{:S(2)}, u32[]{:S(2)}) collective-permute-start(bf16[512,1280]{1,0:T(8,128)(2,1)S(1)} %collective-permute-done.10.refs_0_), channel_id=1, source_target_pairs={{0,4},{4,0},{8,12},{12,8},{16,20},{20,16},{24,28},{28,24},{32,36},... | collective-permute-start | bytes 3932168 | tf_op jit(solution)/shard_map/ppermute | solution.py:447
  78.3 3.8 %project.9.total_ref = f32[1024,1280]{1,0:T(8,128)S(1)} custom-call(f32[1024,1280]{1,0:T(8,128)S(1)} %project.8.total_ref, bf16[1024,1024]{1,0:T(8,128)(2,1)S(1)} %copy-done.12, bf16[512,1280]{1,0:T(8,128)(2,1)S(1)} %collective-permute-done.10.refs_0_, bf16[512,1280]{1,0:T(8,128)(2,1)S(1)} %collective-permute-done.11.refs_1_), custom_call_target="tpu_custom_call", output_to_operand_aliasing={{}: (0, {})} | custom-call | flops 2684354560 | bytes 15204352 | tf_op jit(solution)/shard_map/project/pallas_call | solution.py:218
  82.8 6.2 %attend.2 = (bf16[32,64,768]{2,1,0:T(8,128)(2,1)}, bf16[1024,256]{1,0:T(8,128)(2,1)S(1)}) custom-call(s32[16]{0:T(128)S(1)} %get-tuple-element.52.dest_ref, s32[16]{0:T(128)S(1)} %get-tuple-element.53.length_ref, f32[1024,1280]{1,0:T(8,128)S(1)} %project.9.total_ref, bf16[1024,1024]{1,0:T(8,128)(2,1)S(1)} %copy-done.3, ...), custom_call_target="tpu_custom_call" | custom-call | flops 2147483648 | bytes 12582912 | tf_op jit(solution)/shard_map/attend/pallas_call | solution.py:329
  89.9 6.1 %all-to-all-start = ((bf16[32,64,768]{2,1,0:T(8,128)(2,1)}), bf16[32,64,768]{2,1,0:T(8,128)(2,1)S(1)}, u32[]{:S(2)}, u32[]{:S(2)}) async-start(bf16[32,64,768]{2,1,0:T(8,128)(2,1)} %get-tuple-element.81), calls=%async_computation | async-start | bytes 6291456 | tf_op jit(solution)/shard_map/all_to_all | solution.py:522
  96.0 2.5 %copy-done.1 = f32[1024,1280]{1,0:T(8,128)S(1)} copy-done((f32[1024,1280]{1,0:T(8,128)S(1)}, f32[1024,1280]{1,0:T(8,128)}, u32[]{:S(2)}) %copy-start.1) | copy-done | bytes 5242904
  103.7 4.8 %attend.3 = bf16[32,64,256]{2,1,0:T(8,128)(2,1)} custom-call(s32[16]{0:T(128)S(1)} %get-tuple-element.52.dest_ref, s32[16]{0:T(128)S(1)} %get-tuple-element.53.length_ref, f32[1024,1280]{1,0:T(8,128)S(1)} %copy-done.1, bf16[1024,1024]{1,0:T(8,128)(2,1)S(1)} %copy-done.4, f32[1,1280]{1,0:T(1,128)S(1)} %broadcast_in_dim.26.bias_ref, ...), custom_call_target="tpu_custom_call" | custom-call | flops 536870912 | bytes 4718592 | tf_op jit(solution)/shard_map/attend/pallas_call | solution.py:329
  108.6 27.2 %all-to-all-done.received_ref = bf16[32,64,768]{2,1,0:T(8,128)(2,1)S(1)} async-done(((bf16[32,64,768]{2,1,0:T(8,128)(2,1)}), bf16[32,64,768]{2,1,0:T(8,128)(2,1)S(1)}, u32[]{:S(2)}, u32[]{:S(2)}) %all-to-all-start) | async-done | bytes 3145760 | tf_op jit(solution)/shard_map/all_to_all | solution.py:522
  135.7 5.0 %all-to-all-start.1 = ((bf16[32,64,256]{2,1,0:T(8,128)(2,1)}), bf16[32,64,256]{2,1,0:T(8,128)(2,1)}, u32[]{:S(2)}, u32[]{:S(2)}) async-start(bf16[32,64,256]{2,1,0:T(8,128)(2,1)} %attend.3), calls=%async_computation.1 | async-start | bytes 2097152 | tf_op jit(solution)/shard_map/all_to_all | solution.py:522
  140.8 1.7 place.2
  142.5 2.7 %collective-permute-start.16 = (bf16[256,768]{1,0:T(8,128)(2,1)}, bf16[256,768]{1,0:T(8,128)(2,1)S(1)}, u32[]{:S(2)}, u32[]{:S(2)}) collective-permute-start(bf16[256,768]{1,0:T(8,128)(2,1)} %get-tuple-element.83), channel_id=1, source_target_pairs={{0,2},{1,3},{2,0},{3,1},{4,6},{5,7},{6,4},{7,5},{8,10},{9,11},{10,... | collective-permute-start | bytes 1179656 | tf_op jit(solution)/shard_map/ppermute | solution.py:525
  145.5 2.4 %collective-permute-start.18 = (bf16[256,768]{1,0:T(8,128)(2,1)}, bf16[256,768]{1,0:T(8,128)(2,1)S(1)}, u32[]{:S(2)}, u32[]{:S(2)}) collective-permute-start(bf16[256,768]{1,0:T(8,128)(2,1)} %get-tuple-element.85), channel_id=1, source_target_pairs={{0,3},{1,0},{2,1},{3,2},{4,7},{5,4},{6,5},{7,6},{8,11},{9,8},{10,9... | collective-permute-start | bytes 1179656 | tf_op jit(solution)/shard_map/ppermute | solution.py:525
  147.9 9.9 %all-to-all-done.1.received_ref = bf16[32,64,256]{2,1,0:T(8,128)(2,1)} async-done(((bf16[32,64,256]{2,1,0:T(8,128)(2,1)}), bf16[32,64,256]{2,1,0:T(8,128)(2,1)}, u32[]{:S(2)}, u32[]{:S(2)}) %all-to-all-start.1) | async-done | bytes 1048608 | tf_op jit(solution)/shard_map/all_to_all | solution.py:522
  157.7 1.8 %place.3 = (bf16[256,256]{1,0:T(8,128)(2,1)S(1)}, bf16[256,256]{1,0:T(8,128)(2,1)S(1)}, bf16[256,256]{1,0:T(8,128)(2,1)S(1)}, bf16[256,256]{1,0:T(8,128)(2,1)S(1)}) custom-call(s32[16]{0:T(128)S(1)} %reshape.58.source_ref, bf16[32,64,256]{2,1,0:T(8,128)(2,1)} %all-to-all-done.1.received_ref), custom_call_target="tpu_custom_call" | custom-call | tf_op jit(solution)/shard_map/place/pallas_call | solution.py:367
  159.6 2.8 %collective-permute-start.19 = (bf16[256,256]{1,0:T(8,128)(2,1)S(1)}, bf16[256,256]{1,0:T(8,128)(2,1)S(1)}, u32[]{:S(2)}, u32[]{:S(2)}) collective-permute-start(bf16[256,256]{1,0:T(8,128)(2,1)S(1)} %get-tuple-element.88), channel_id=1, source_target_pairs={{0,2},{1,3},{2,0},{3,1},{4,6},{5,7},{6,4},{7,5},{8,10},{9,11},{10,... | collective-permute-start | bytes 393224 | tf_op jit(solution)/shard_map/ppermute | solution.py:525
  162.7 2.4 %collective-permute-start.21 = (bf16[256,256]{1,0:T(8,128)(2,1)S(1)}, bf16[256,256]{1,0:T(8,128)(2,1)S(1)}, u32[]{:S(2)}, u32[]{:S(2)}) collective-permute-start(bf16[256,256]{1,0:T(8,128)(2,1)S(1)} %get-tuple-element.90), channel_id=1, source_target_pairs={{0,3},{1,0},{2,1},{3,2},{4,7},{5,4},{6,5},{7,6},{8,11},{9,8},{10,9... | collective-permute-start | bytes 393224 | tf_op jit(solution)/shard_map/ppermute | solution.py:525
  165.1 1.7 %join.2.refs_0_ = bf16[256,4096]{1,0:T(8,128)(2,1)} custom-call(s32[4]{0:T(128)S(1)} %and_select_fusion.order_ref, bf16[256,768]{1,0:T(8,128)(2,1)S(1)} %get-tuple-element.82.refs_0_, bf16[256,768]{1,0:T(8,128)(2,1)S(1)} %collective-permute-done.16.refs_1_, bf16[256,768]{1,0:T(8,128)(2,1)S(1)} %collective-permute-done.17.refs_2_, ...), custom_call_target="tpu_custom_call" | custom-call | tf_op jit(solution)/shard_map/join/pallas_call | solution.py:402
  166.8 2.3 %collective-permute-done.20.refs_3_ = bf16[256,256]{1,0:T(8,128)(2,1)S(1)} collective-permute-done((bf16[256,256]{1,0:T(8,128)(2,1)S(1)}, bf16[256,256]{1,0:T(8,128)(2,1)S(1)}, u32[]{:S(2)}, u32[]{:S(2)}) %collective-permute-start.20) | collective-permute-done | bytes 131104 | tf_op jit(solution)/shard_map/ppermute | solution.py:525
  (109 shorter events, 26.1 us)
Async XLA Ops:
  2.0 27.2 %collective-permute-start = (bf16[256,1280]{1,0:T(8,128)(2,1)}, bf16[256,1280]{1,0:T(8,128)(2,1)S(1)}, u32[]{:S(2)}, u32[]{:S(2)}) collective-permute-start(bf16[256,1280]{1,0:T(8,128)(2,1)} %side_by_side.1), channel_id=1, source_target_pairs={{0,32},{4,12},{8,40},{12,20},{16,48},{20,28},{24,56},{28,4},{32,64... | collective-permute-start | bytes 1966088 | tf_op jit(solution)/shard_map/ppermute | solution.py:441
  4.5 24.7 %collective-permute-start.1 = (bf16[256,1280]{1,0:T(8,128)(2,1)}, bf16[256,1280]{1,0:T(8,128)(2,1)S(1)}, u32[]{:S(2)}, u32[]{:S(2)}) collective-permute-start(bf16[256,1280]{1,0:T(8,128)(2,1)} %side_by_side.1), channel_id=1, source_target_pairs={{0,96},{4,28},{8,104},{12,4},{16,112},{20,12},{24,120},{28,20},{32... | collective-permute-start | bytes 1966088 | tf_op jit(solution)/shard_map/ppermute | solution.py:441
  6.7 23.6 %collective-permute-start.2 = (bf16[256,1280]{1,0:T(8,128)(2,1)}, bf16[256,1280]{1,0:T(8,128)(2,1)S(1)}, u32[]{:S(2)}, u32[]{:S(2)}) collective-permute-start(bf16[256,1280]{1,0:T(8,128)(2,1)} %side_by_side.1), channel_id=1, source_target_pairs={{0,64},{4,20},{8,72},{12,28},{16,80},{20,4},{24,88},{28,12},{32,96... | collective-permute-start | bytes 1966088 | tf_op jit(solution)/shard_map/ppermute | solution.py:441
  7.9 22.4 %collective-permute-start.3 = (bf16[256,1280]{1,0:T(8,128)(2,1)}, bf16[256,1280]{1,0:T(8,128)(2,1)S(1)}, u32[]{:S(2)}, u32[]{:S(2)}) collective-permute-start(bf16[256,1280]{1,0:T(8,128)(2,1)} %side_by_side.1), channel_id=1, source_target_pairs={{0,8},{4,36},{8,16},{12,44},{16,24},{20,52},{24,0},{28,60},{32,40}... | collective-permute-start | bytes 1966088 | tf_op jit(solution)/shard_map/ppermute | solution.py:444
  9.2 21.1 %collective-permute-start.4 = (bf16[256,1280]{1,0:T(8,128)(2,1)}, bf16[256,1280]{1,0:T(8,128)(2,1)S(1)}, u32[]{:S(2)}, u32[]{:S(2)}) collective-permute-start(bf16[256,1280]{1,0:T(8,128)(2,1)} %side_by_side.1), channel_id=1, source_target_pairs={{0,24},{4,100},{8,0},{12,108},{16,8},{20,116},{24,16},{28,124},{32... | collective-permute-start | bytes 1966088 | tf_op jit(solution)/shard_map/ppermute | solution.py:444
  22.8 10.5 %copy-start.19 = (bf16[256,1280]{1,0:T(8,128)(2,1)S(1)}, bf16[256,1280]{1,0:T(8,128)(2,1)}, u32[]{:S(2)}) copy-start(bf16[256,1280]{1,0:T(8,128)(2,1)} %side_by_side.1) | copy-start | bytes 1966084
  30.3 10.8 %slice-start = ((s8[16777216]{0:T(1024)(128)(4,1)}), s8[4194304]{0:T(1024)(128)(4,1)S(1)}, s32[]{:S(2)}) async-start(s8[16777216]{0:T(1024)(128)(4,1)} %bitcast.6), calls=%async_computation.2 | async-start | bytes 8388608
  30.5 10.7 %slice-start.1 = ((s8[16777216]{0:T(1024)(128)(4,1)}), s8[4194304]{0:T(1024)(128)(4,1)S(1)}, s32[]{:S(2)}) async-start(s8[16777216]{0:T(1024)(128)(4,1)} %bitcast.6), calls=%async_computation.3 | async-start | bytes 8388608
  30.5 25.1 %collective-permute-start.5 = (bf16[768,1280]{1,0:T(8,128)(2,1)S(1)}, bf16[768,1280]{1,0:T(8,128)(2,1)S(1)}, u32[]{:S(2)}, u32[]{:S(2)}) collective-permute-start(bf16[768,1280]{1,0:T(8,128)(2,1)S(1)} %constant_dynamic-update-slice_fusion.refs_0_), channel_id=1, source_target_pairs={{0,8},{4,36},{8,16},{12,44},{16,24},{20,52},{24,0},{28,60},{32,40}... | collective-permute-start | bytes 5898248 | tf_op jit(solution)/shard_map/ppermute | solution.py:444
  31.6 24.0 %collective-permute-start.6 = (bf16[768,1280]{1,0:T(8,128)(2,1)S(1)}, bf16[768,1280]{1,0:T(8,128)(2,1)S(1)}, u32[]{:S(2)}, u32[]{:S(2)}) collective-permute-start(bf16[768,1280]{1,0:T(8,128)(2,1)S(1)} %constant_dynamic-update-slice_fusion.refs_0_), channel_id=1, source_target_pairs={{0,24},{4,100},{8,0},{12,108},{16,8},{20,116},{24,16},{28,124},{32... | collective-permute-start | bytes 5898248 | tf_op jit(solution)/shard_map/ppermute | solution.py:444
  33.4 7.8 %slice-start.2 = ((s8[16777216]{0:T(1024)(128)(4,1)}), s8[4194304]{0:T(1024)(128)(4,1)S(1)}, s32[]{:S(2)}) async-start(s8[16777216]{0:T(1024)(128)(4,1)} %bitcast.6), calls=%async_computation.4 | async-start | bytes 8388608
  38.3 10.0 %collective-permute-start.9 = (bf16[512,1280]{1,0:T(8,128)(2,1)S(1)}, bf16[512,1280]{1,0:T(8,128)(2,1)S(1)}, u32[]{:S(2)}, u32[]{:S(2)}) collective-permute-start(bf16[512,1280]{1,0:T(8,128)(2,1)S(1)} %pad_maximum_fusion.3), channel_id=1, source_target_pairs={{0,4},{4,0},{8,12},{12,8},{16,20},{20,16},{24,28},{28,24},{32,36},... | collective-permute-start | bytes 3932168 | tf_op jit(solution)/shard_map/ppermute | solution.py:447
  40.4 7.9 %collective-permute-start.7 = (bf16[512,1280]{1,0:T(8,128)(2,1)S(1)}, bf16[512,1280]{1,0:T(8,128)(2,1)S(1)}, u32[]{:S(2)}, u32[]{:S(2)}) collective-permute-start(bf16[512,1280]{1,0:T(8,128)(2,1)S(1)} %pad_maximum_fusion.1), channel_id=1, source_target_pairs={{0,4},{4,0},{8,12},{12,8},{16,20},{20,16},{24,28},{28,24},{32,36},... | collective-permute-start | bytes 3932168 | tf_op jit(solution)/shard_map/ppermute | solution.py:447
  40.6 7.7 %collective-permute-start.8 = (bf16[512,1280]{1,0:T(8,128)(2,1)S(1)}, bf16[512,1280]{1,0:T(8,128)(2,1)S(1)}, u32[]{:S(2)}, u32[]{:S(2)}) collective-permute-start(bf16[512,1280]{1,0:T(8,128)(2,1)S(1)} %pad_maximum_fusion.2), channel_id=1, source_target_pairs={{0,4},{4,0},{8,12},{12,8},{16,20},{20,16},{24,28},{28,24},{32,36},... | collective-permute-start | bytes 3932168 | tf_op jit(solution)/shard_map/ppermute | solution.py:447
  55.6 10.7 %collective-permute-start.12 = (bf16[768,1280]{1,0:T(8,128)(2,1)S(1)}, bf16[768,1280]{1,0:T(8,128)(2,1)S(1)}, u32[]{:S(2)}, u32[]{:S(2)}) collective-permute-start(bf16[768,1280]{1,0:T(8,128)(2,1)S(1)} %collective-permute-done.5.refs_0_), channel_id=1, source_target_pairs={{0,4},{4,0},{8,12},{12,8},{16,20},{20,16},{24,28},{28,24},{32,36},... | collective-permute-start | bytes 5898248 | tf_op jit(solution)/shard_map/ppermute | solution.py:447
  57.8 8.5 %collective-permute-start.13 = (bf16[768,1280]{1,0:T(8,128)(2,1)S(1)}, bf16[768,1280]{1,0:T(8,128)(2,1)S(1)}, u32[]{:S(2)}, u32[]{:S(2)}) collective-permute-start(bf16[768,1280]{1,0:T(8,128)(2,1)S(1)} %collective-permute-done.6.refs_1_), channel_id=1, source_target_pairs={{0,4},{4,0},{8,12},{12,8},{16,20},{20,16},{24,28},{28,24},{32,36},... | collective-permute-start | bytes 5898248 | tf_op jit(solution)/shard_map/ppermute | solution.py:447
  58.1 18.0 %collective-permute-start.11 = (bf16[512,1280]{1,0:T(8,128)(2,1)S(1)}, bf16[512,1280]{1,0:T(8,128)(2,1)S(1)}, u32[]{:S(2)}, u32[]{:S(2)}) collective-permute-start(bf16[512,1280]{1,0:T(8,128)(2,1)S(1)} %pad_maximum_fusion.5), channel_id=1, source_target_pairs={{0,8},{4,36},{8,16},{12,44},{16,24},{20,52},{24,0},{28,60},{32,40}... | collective-permute-start | bytes 3932168 | tf_op jit(solution)/shard_map/ppermute | solution.py:444
  59.4 16.8 %collective-permute-start.10 = (bf16[512,1280]{1,0:T(8,128)(2,1)S(1)}, bf16[512,1280]{1,0:T(8,128)(2,1)S(1)}, u32[]{:S(2)}, u32[]{:S(2)}) collective-permute-start(bf16[512,1280]{1,0:T(8,128)(2,1)S(1)} %pad_maximum_fusion.4), channel_id=1, source_target_pairs={{0,24},{4,100},{8,0},{12,108},{16,8},{20,116},{24,16},{28,124},{32... | collective-permute-start | bytes 3932168 | tf_op jit(solution)/shard_map/ppermute | solution.py:444
  66.3 12.0 %copy-start.12 = (bf16[1024,1024]{1,0:T(8,128)(2,1)S(1)}, bf16[1024,1024]{1,0:T(8,128)(2,1)}, u32[]{:S(2)}) copy-start(bf16[1024,1024]{1,0:T(8,128)(2,1)} %get-tuple-element.76.x_ref) | copy-start | bytes 6291460
  71.5 11.3 %copy-start.3 = (bf16[1024,1024]{1,0:T(8,128)(2,1)S(1)}, bf16[1024,1024]{1,0:T(8,128)(2,1)}, u32[]{:S(2)}) copy-start(bf16[1024,1024]{1,0:T(8,128)(2,1)} %get-tuple-element.79.x_ref) | copy-start | bytes 6291460
  71.5 11.3 %copy-start.15 = (f32[256,128]{1,0:T(8,128)S(1)}, f32[256,128]{1,0:T(8,128)}, u32[]{:S(2)}) copy-start(f32[256,128]{1,0:T(8,128)} %constant.68.clone.cosine_ref) | copy-start | bytes 393220
  71.5 11.3 %copy-start.16 = (f32[256,128]{1,0:T(8,128)S(1)}, f32[256,128]{1,0:T(8,128)}, u32[]{:S(2)}) copy-start(f32[256,128]{1,0:T(8,128)} %constant.69.clone.sine_ref) | copy-start | bytes 393220
  76.3 5.8 %collective-permute-start.14 = (bf16[512,1280]{1,0:T(8,128)(2,1)S(1)}, bf16[512,1280]{1,0:T(8,128)(2,1)S(1)}, u32[]{:S(2)}, u32[]{:S(2)}) collective-permute-start(bf16[512,1280]{1,0:T(8,128)(2,1)S(1)} %collective-permute-done.10.refs_0_), channel_id=1, source_target_pairs={{0,4},{4,0},{8,12},{12,8},{16,20},{20,16},{24,28},{28,24},{32,36},... | collective-permute-start | bytes 3932168 | tf_op jit(solution)/shard_map/ppermute | solution.py:447
  78.3 4.5 %collective-permute-start.15 = (bf16[512,1280]{1,0:T(8,128)(2,1)S(1)}, bf16[512,1280]{1,0:T(8,128)(2,1)S(1)}, u32[]{:S(2)}, u32[]{:S(2)}) collective-permute-start(bf16[512,1280]{1,0:T(8,128)(2,1)S(1)} %collective-permute-done.11.refs_1_), channel_id=1, source_target_pairs={{0,4},{4,0},{8,12},{12,8},{16,20},{20,16},{24,28},{28,24},{32,36},... | collective-permute-start | bytes 3932168 | tf_op jit(solution)/shard_map/ppermute | solution.py:447
  89.9 45.9 %all-to-all-start = ((bf16[32,64,768]{2,1,0:T(8,128)(2,1)}), bf16[32,64,768]{2,1,0:T(8,128)(2,1)S(1)}, u32[]{:S(2)}, u32[]{:S(2)}) async-start(bf16[32,64,768]{2,1,0:T(8,128)(2,1)} %get-tuple-element.81), calls=%async_computation | async-start | bytes 6291456 | tf_op jit(solution)/shard_map/all_to_all | solution.py:522
  135.7 22.0 %all-to-all-start.1 = ((bf16[32,64,256]{2,1,0:T(8,128)(2,1)}), bf16[32,64,256]{2,1,0:T(8,128)(2,1)}, u32[]{:S(2)}, u32[]{:S(2)}) async-start(bf16[32,64,256]{2,1,0:T(8,128)(2,1)} %attend.3), calls=%async_computation.1 | async-start | bytes 2097152 | tf_op jit(solution)/shard_map/all_to_all | solution.py:522
  142.5 20.2 %collective-permute-start.16 = (bf16[256,768]{1,0:T(8,128)(2,1)}, bf16[256,768]{1,0:T(8,128)(2,1)S(1)}, u32[]{:S(2)}, u32[]{:S(2)}) collective-permute-start(bf16[256,768]{1,0:T(8,128)(2,1)} %get-tuple-element.83), channel_id=1, source_target_pairs={{0,2},{1,3},{2,0},{3,1},{4,6},{5,7},{6,4},{7,5},{8,10},{9,11},{10,... | collective-permute-start | bytes 1179656 | tf_op jit(solution)/shard_map/ppermute | solution.py:525
  145.2 19.9 %collective-permute-start.17 = (bf16[256,768]{1,0:T(8,128)(2,1)}, bf16[256,768]{1,0:T(8,128)(2,1)S(1)}, u32[]{:S(2)}, u32[]{:S(2)}) collective-permute-start(bf16[256,768]{1,0:T(8,128)(2,1)} %get-tuple-element.84), channel_id=1, source_target_pairs={{0,1},{1,2},{2,3},{3,0},{4,5},{5,6},{6,7},{7,4},{8,9},{9,10},{10,1... | collective-permute-start | bytes 1179656 | tf_op jit(solution)/shard_map/ppermute | solution.py:525
  145.5 19.5 %collective-permute-start.18 = (bf16[256,768]{1,0:T(8,128)(2,1)}, bf16[256,768]{1,0:T(8,128)(2,1)S(1)}, u32[]{:S(2)}, u32[]{:S(2)}) collective-permute-start(bf16[256,768]{1,0:T(8,128)(2,1)} %get-tuple-element.85), channel_id=1, source_target_pairs={{0,3},{1,0},{2,1},{3,2},{4,7},{5,4},{6,5},{7,6},{8,11},{9,8},{10,9... | collective-permute-start | bytes 1179656 | tf_op jit(solution)/shard_map/ppermute | solution.py:525
  159.6 7.2 %collective-permute-start.19 = (bf16[256,256]{1,0:T(8,128)(2,1)S(1)}, bf16[256,256]{1,0:T(8,128)(2,1)S(1)}, u32[]{:S(2)}, u32[]{:S(2)}) collective-permute-start(bf16[256,256]{1,0:T(8,128)(2,1)S(1)} %get-tuple-element.88), channel_id=1, source_target_pairs={{0,2},{1,3},{2,0},{3,1},{4,6},{5,7},{6,4},{7,5},{8,10},{9,11},{10,... | collective-permute-start | bytes 393224 | tf_op jit(solution)/shard_map/ppermute | solution.py:525
  162.4 6.8 %collective-permute-start.20 = (bf16[256,256]{1,0:T(8,128)(2,1)S(1)}, bf16[256,256]{1,0:T(8,128)(2,1)S(1)}, u32[]{:S(2)}, u32[]{:S(2)}) collective-permute-start(bf16[256,256]{1,0:T(8,128)(2,1)S(1)} %get-tuple-element.89), channel_id=1, source_target_pairs={{0,1},{1,2},{2,3},{3,0},{4,5},{5,6},{6,7},{7,4},{8,9},{9,10},{10,1... | collective-permute-start | bytes 393224 | tf_op jit(solution)/shard_map/ppermute | solution.py:525
  162.7 6.4 %collective-permute-start.21 = (bf16[256,256]{1,0:T(8,128)(2,1)S(1)}, bf16[256,256]{1,0:T(8,128)(2,1)S(1)}, u32[]{:S(2)}, u32[]{:S(2)}) collective-permute-start(bf16[256,256]{1,0:T(8,128)(2,1)S(1)} %get-tuple-element.90), channel_id=1, source_target_pairs={{0,3},{1,0},{2,1},{3,2},{4,7},{5,4},{6,5},{7,6},{8,11},{9,8},{10,9... | collective-permute-start | bytes 393224 | tf_op jit(solution)/shard_map/ppermute | solution.py:525
  (17 other events, 57.7 us)

commit v8 on v7

--- a/solution.py
+++ b/solution.py
@@ -179,8 +179,8 @@
     )(order, *given)
 
 
-def product(x_ref, pieces, columns=slice(None)):
-    weights = jnp.concatenate([piece[:, columns] for piece in pieces], axis=0)
+def product(x_ref, pieces):
+    weights = jnp.concatenate([piece[...] for piece in pieces], axis=0)
     return jnp.dot(x_ref[...], weights, preferred_element_type=jnp.float32)
 
 
@@ -211,7 +211,7 @@
 def project(total, x, pieces, cost=None):
     rows, depth = x.shape
     columns = pieces[0].shape[1]
-    tile = 256
+    tile = 512
     resident = pl.BlockSpec(memory_space=pltpu.VMEM)
     x_block = pl.BlockSpec((tile, depth), lambda i: (i, 0))
     totals = [] if total is None else [total]
@@ -256,7 +256,7 @@
 
     summed = (
         total_ref[:, columns]
-        + product(x_ref, pieces, columns)
+        + product(x_ref, pieces)
         + bias_ref[:, columns]
     )
 
@@ -510,12 +510,13 @@
     total = project(total, x_corners, [ahead, behind])
     total = project(total, x_swapped, [swap(ahead), swap(behind)])
     far, total = lax.optimization_barrier((far, total))
-    last = [swap(piece) for piece in far]
+    middle = cut + w_keyval.shape[1]
+    last = [swap(piece[:, :middle]) for piece in far]
     total = project(total, x_far, far)
 
-    middle = cut + w_keyval.shape[1]
     given = (own_dest, own_length, total, x_last, bias)
     first_sent, keyval = attend(*given, None, last, packs, slice(0, middle))
+    last = [swap(held_until(piece[:, middle:], keyval)) for piece in far]
     (second_sent,) = attend(*given, keyval, last, packs, slice(middle, weights.shape[1]))
 
     def exchanged(sent):

time: 172 us -> 171 us (level)
  Pallas kernels: 57.1 us -> 55.1 us
    unnamed x52 -> x50, local copies, waits for them, and re-layouts: 17.1 us -> 14.5 us
    slice x0 -> x4, local copies, waits for them, and re-layouts: none -> 2.19 us  [the longest x2 1.94 us: per_device(): last = [swap(held_until(piece[:, middle:], keyval)) for piece in far]]
    pallas_call x5, Pallas kernels: 24.1 us -> 22.2 us  [project(): pl.pallas_call(add_kernel if totals else first_kernel, grid=(rows // tile...]
    ppermute x7 -> x9, starting transfers between devices: 6.97 us -> 7.77 us  [swap(): return lax.ppermute(piece, 'dp', swap_pairs())]
  transfers between devices with their start and end apart: 24 -> 26, of which waited for: 8 -> 9; matrix products, arithmetic and copies ran while one was open for 4% -> 5% of each run, Pallas kernels for 28% -> 27%
where the time goes in v8:
time: 171 us; the launch traced here: 170 us
  Pallas kernels  55.1 us (32%)
  waiting for transfers between devices  47.2 us (28%)
  starting transfers between devices  44.5 us (26%)
  local copies, waits for them, and re-layouts  19.9 us (12%)
  other arithmetic  3.09 us (2%)
    all_to_all x2, waiting for transfers between devices, exchanged(): lax.all_to_all(sent, 'dp', split_axis=0, concat_axis=0, tiled=True)  35.8 us
    pallas_call x5, Pallas kernels, project(): pl.pallas_call(add_kernel if totals else first_kernel, grid=(rows // tile...  22.2 us
    unnamed x50, local copies, waits for them, and re-layouts  14.5 us
    pallas_call x2, Pallas kernels, norm(): pl.pallas_call(norm_kernel if scale is None else functools.partial(norm_r...  13.5 us
    all_to_all x2, starting transfers between devices, exchanged(): lax.all_to_all(sent, 'dp', split_axis=0, concat_axis=0, tiled=True)  11.3 us
    pallas_call x2, Pallas kernels, attend(): pl.pallas_call(functools.partial(attend_kernel, columns), grid_spec=pltpu...  10.9 us
    ppermute x6, starting transfers between devices, exchanged(): lax.ppermute(parts[k], 'mp', [(i, (i + k) % planes) for i in range(planes)])  10.9 us
    ppermute x6, starting transfers between devices, second(): return lax.ppermute(piece, 'dp', shift_pairs(0, by))  8.48 us
  transfers between devices with their start and end apart: 26, of which 9 were waited for; matrix products, arithmetic and copies ran while one was open for 5% of the time, Pallas kernels for 27%

profile of v8, /device:TPU:1, one launch (start us, length us, event | category | flops | bytes accessed | tf_op | source)
XLA Modules:
  0.0 170.4 jit_solution(10087642227063759860)
XLA Ops:
  0.0 1.9 %side_by_side.1 = bf16[256,1280]{1,0:T(8,128)(2,1)} custom-call(bf16[256,1024]{1,0:T(8,128)(2,1)} %query_ref.1, bf16[256,256]{1,0:T(8,128)(2,1)} %keyval_ref.1), custom_call_target="tpu_custom_call" | custom-call | tf_op jit(solution)/shard_map/side_by_side/pallas_call | solution.py:114
  2.0 2.5 %collective-permute-start = (bf16[256,1280]{1,0:T(8,128)(2,1)}, bf16[256,1280]{1,0:T(8,128)(2,1)S(1)}, u32[]{:S(2)}, u32[]{:S(2)}) collective-permute-start(bf16[256,1280]{1,0:T(8,128)(2,1)} %side_by_side.1), channel_id=1, source_target_pairs={{0,32},{4,12},{8,40},{12,20},{16,48},{20,28},{24,56},{28,4},{32,64... | collective-permute-start | bytes 1966088 | tf_op jit(solution)/shard_map/ppermute | solution.py:441
  4.5 2.2 %collective-permute-start.1 = (bf16[256,1280]{1,0:T(8,128)(2,1)}, bf16[256,1280]{1,0:T(8,128)(2,1)S(1)}, u32[]{:S(2)}, u32[]{:S(2)}) collective-permute-start(bf16[256,1280]{1,0:T(8,128)(2,1)} %side_by_side.1), channel_id=1, source_target_pairs={{0,96},{4,28},{8,104},{12,4},{16,112},{20,12},{24,120},{28,20},{32... | collective-permute-start | bytes 1966088 | tf_op jit(solution)/shard_map/ppermute | solution.py:441
  16.2 5.8 %copy-done.2 = bf16[1024,8192]{1,0:T(8,128)(2,1)S(1)} copy-done((bf16[1024,8192]{1,0:T(8,128)(2,1)S(1)}, bf16[1024,8192]{1,0:T(8,128)(2,1)}, u32[]{:S(2)}) %copy-start.2) | copy-done | bytes 16777240
  22.8 6.4 %norm.2 = (f32[1024,1]{1,0:T(8,128)S(1)}, bf16[1024,1536]{1,0:T(8,128)(2,1)}) custom-call(s32[64]{0:T(128)S(1)} %fusion.4.order_ref, bf16[1024,8192]{1,0:T(8,128)(2,1)S(1)} %copy-done.2, f32[1,8192]{1,0:T(1,128)S(1)} %bitcast.8), custom_call_target="tpu_custom_call" | custom-call | flops 50331648 | bytes 19922944 | tf_op jit(solution)/shard_map/norm/pallas_call | solution.py:166
  31.6 1.7 collective-permute-start.6
  33.4 4.4 %project.5.total_ref = f32[1024,1280]{1,0:T(8,128)S(1)} custom-call(bf16[1024,1536]{1,0:T(8,128)(2,1)S(1)} %copy-done.17, bf16[768,1280]{1,0:T(8,128)(2,1)S(1)} %constant_dynamic-update-slice_fusion.refs_0_, bf16[768,1280]{1,0:T(8,128)(2,1)S(1)} %pad_maximum_fusion.refs_1_), custom_call_target="tpu_custom_call" | custom-call | flops 4026531840 | bytes 17563648 | tf_op jit(solution)/shard_map/project/pallas_call | solution.py:218
  37.9 2.0 %collective-permute-start.9 = (bf16[512,1280]{1,0:T(8,128)(2,1)S(1)}, bf16[512,1280]{1,0:T(8,128)(2,1)S(1)}, u32[]{:S(2)}, u32[]{:S(2)}) collective-permute-start(bf16[512,1280]{1,0:T(8,128)(2,1)S(1)} %pad_maximum_fusion.3), channel_id=1, source_target_pairs={{0,4},{4,0},{8,12},{12,8},{16,20},{20,16},{24,28},{28,24},{32,36},... | collective-permute-start | bytes 3932168 | tf_op jit(solution)/shard_map/ppermute | solution.py:447
  40.9 7.1 %norm.3 = (bf16[1024,1536]{1,0:T(8,128)(2,1)}, bf16[1024,1536]{1,0:T(8,128)(2,1)}, bf16[1024,1536]{1,0:T(8,128)(2,1)}, bf16[1024,1024]{1,0:T(8,128)(2,1)}, bf16[1024,1024]{1,0:T(8,128)(2,1)}) custom-call(s32[64]{0:T(128)S(1)} %fusion.4.order_ref, bf16[1024,8192]{1,0:T(8,128)(2,1)S(1)} %bitcast.7, f32[1,8192]{1,0:T(1,128)S(1)} %bitcast.9, ...), custom_call_target="tpu_custom_call" | custom-call | flops 50331648 | bytes 30408704 | tf_op jit(solution)/shard_map/norm/pallas_call | solution.py:166
  48.0 1.9 %copy-done.9 = bf16[1024,1536]{1,0:T(8,128)(2,1)S(1)} copy-done((bf16[1024,1536]{1,0:T(8,128)(2,1)S(1)}, bf16[1024,1536]{1,0:T(8,128)(2,1)}, u32[]{:S(2)}) %copy-start.9) | copy-done | bytes 3145752
  49.8 4.8 %project.6.total_ref = f32[1024,1280]{1,0:T(8,128)S(1)} custom-call(f32[1024,1280]{1,0:T(8,128)S(1)} %project.5.total_ref, bf16[1024,1536]{1,0:T(8,128)(2,1)S(1)} %copy-done.9, bf16[512,1280]{1,0:T(8,128)(2,1)S(1)} %collective-permute-done.7.refs_0_, bf16[512,1280]{1,0:T(8,128)(2,1)S(1)} %collective-permute-done.8.refs_1_, ...), custom_call_target="tpu_custom_call", output_to_operand_aliasing={{}: (0, {})} | custom-call | flops 1024 | bytes 1024 | tf_op jit(solution)/shard_map/project/pallas_call | solution.py:218
  55.6 2.2 %collective-permute-start.12 = (bf16[768,1280]{1,0:T(8,128)(2,1)S(1)}, bf16[768,1280]{1,0:T(8,128)(2,1)S(1)}, u32[]{:S(2)}, u32[]{:S(2)}) collective-permute-start(bf16[768,1280]{1,0:T(8,128)(2,1)S(1)} %collective-permute-done.5.refs_0_), channel_id=1, source_target_pairs={{0,4},{4,0},{8,12},{12,8},{16,20},{20,16},{24,28},{28,24},{32,36},... | collective-permute-start | bytes 5898248 | tf_op jit(solution)/shard_map/ppermute | solution.py:447
  59.4 1.8 %collective-permute-start.10 = (bf16[512,1280]{1,0:T(8,128)(2,1)S(1)}, bf16[512,1280]{1,0:T(8,128)(2,1)S(1)}, u32[]{:S(2)}, u32[]{:S(2)}) collective-permute-start(bf16[512,1280]{1,0:T(8,128)(2,1)S(1)} %pad_maximum_fusion.4), channel_id=1, source_target_pairs={{0,24},{4,100},{8,0},{12,108},{16,8},{20,116},{24,16},{28,124},{32... | collective-permute-start | bytes 3932168 | tf_op jit(solution)/shard_map/ppermute | solution.py:444
  61.2 4.8 %project.7.total_ref = f32[1024,1280]{1,0:T(8,128)S(1)} custom-call(f32[1024,1280]{1,0:T(8,128)S(1)} %project.6.total_ref, bf16[1024,1536]{1,0:T(8,128)(2,1)S(1)} %copy-done.8, bf16[768,1280]{1,0:T(8,128)(2,1)S(1)} %collective-permute-done.5.refs_0_, bf16[768,1280]{1,0:T(8,128)(2,1)S(1)} %collective-permute-done.6.refs_1_), custom_call_target="tpu_custom_call", output_to_operand_aliasing={{}: (0, {})} | custom-call | flops 4026531840 | bytes 17563648 | tf_op jit(solution)/shard_map/project/pallas_call | solution.py:218
  66.0 4.8 %project.8.total_ref = f32[1024,1280]{1,0:T(8,128)S(1)} custom-call(f32[1024,1280]{1,0:T(8,128)S(1)} %project.7.total_ref, bf16[1024,1536]{1,0:T(8,128)(2,1)S(1)} %copy-done.7, bf16[768,1280]{1,0:T(8,128)(2,1)S(1)} %collective-permute-done.12.refs_0_, bf16[768,1280]{1,0:T(8,128)(2,1)S(1)} %collective-permute-done.13.refs_1_), custom_call_target="tpu_custom_call", output_to_operand_aliasing={{}: (0, {})} | custom-call | flops 4026531840 | bytes 17563648 | tf_op jit(solution)/shard_map/project/pallas_call | solution.py:218
  70.9 5.3 %collective-permute-done.11.refs_1_ = bf16[512,1280]{1,0:T(8,128)(2,1)S(1)} collective-permute-done((bf16[512,1280]{1,0:T(8,128)(2,1)S(1)}, bf16[512,1280]{1,0:T(8,128)(2,1)S(1)}, u32[]{:S(2)}, u32[]{:S(2)}) %collective-permute-start.11) | collective-permute-done | bytes 1310752 | tf_op jit(solution)/shard_map/ppermute | solution.py:444
  76.6 2.1 %collective-permute-start.14 = (bf16[512,1024]{1,0:T(8,128)(2,1)S(1)}, bf16[512,1024]{1,0:T(8,128)(2,1)S(1)}, u32[]{:S(2)}, u32[]{:S(2)}) collective-permute-start(bf16[512,1024]{1,0:T(8,128)(2,1)S(1)} %slice.48), channel_id=1, source_target_pairs={{0,4},{4,0},{8,12},{12,8},{16,20},{20,16},{24,28},{28,24},{32,36},... | collective-permute-start | bytes 3145736 | tf_op jit(solution)/shard_map/ppermute | solution.py:447
  79.0 3.4 %project.9.total_ref = f32[1024,1280]{1,0:T(8,128)S(1)} custom-call(f32[1024,1280]{1,0:T(8,128)S(1)} %project.8.total_ref, bf16[1024,1024]{1,0:T(8,128)(2,1)S(1)} %copy-done.10, bf16[512,1280]{1,0:T(8,128)(2,1)S(1)} %collective-permute-done.10.refs_0_, bf16[512,1280]{1,0:T(8,128)(2,1)S(1)} %collective-permute-done.11.refs_1_), custom_call_target="tpu_custom_call", output_to_operand_aliasing={{}: (0, {})} | custom-call | flops 2684354560 | bytes 15204352 | tf_op jit(solution)/shard_map/project/pallas_call | solution.py:218
  82.5 6.1 %attend.2 = (bf16[32,64,768]{2,1,0:T(8,128)(2,1)}, bf16[1024,256]{1,0:T(8,128)(2,1)S(1)}) custom-call(s32[16]{0:T(128)S(1)} %get-tuple-element.54.dest_ref, s32[16]{0:T(128)S(1)} %get-tuple-element.55.length_ref, f32[1024,1280]{1,0:T(8,128)S(1)} %project.9.total_ref, bf16[1024,1024]{1,0:T(8,128)(2,1)S(1)} %copy-done.3, ...), custom_call_target="tpu_custom_call" | custom-call | flops 2147483648 | bytes 12582912 | tf_op jit(solution)/shard_map/attend/pallas_call | solution.py:329
  89.4 6.3 %all-to-all-start = ((bf16[32,64,768]{2,1,0:T(8,128)(2,1)}), bf16[32,64,768]{2,1,0:T(8,128)(2,1)S(1)}, u32[]{:S(2)}, u32[]{:S(2)}) async-start(bf16[32,64,768]{2,1,0:T(8,128)(2,1)} %get-tuple-element.83), calls=%async_computation | async-start | bytes 6291456 | tf_op jit(solution)/shard_map/all_to_all | solution.py:523
  99.7 2.5 %copy-done.1 = f32[1024,1280]{1,0:T(8,128)S(1)} copy-done((f32[1024,1280]{1,0:T(8,128)S(1)}, f32[1024,1280]{1,0:T(8,128)}, u32[]{:S(2)}) %copy-start.1) | copy-done | bytes 5242904
  104.8 4.8 %attend.3 = bf16[32,64,256]{2,1,0:T(8,128)(2,1)} custom-call(s32[16]{0:T(128)S(1)} %get-tuple-element.54.dest_ref, s32[16]{0:T(128)S(1)} %get-tuple-element.55.length_ref, f32[1024,1280]{1,0:T(8,128)S(1)} %copy-done.1, bf16[1024,1024]{1,0:T(8,128)(2,1)S(1)} %copy-done.4, f32[1,1280]{1,0:T(1,128)S(1)} %broadcast_in_dim.26.bias_ref, ...), custom_call_target="tpu_custom_call" | custom-call | flops 536870912 | bytes 4718592 | tf_op jit(solution)/shard_map/attend/pallas_call | solution.py:329
  109.6 25.9 %all-to-all-done.received_ref = bf16[32,64,768]{2,1,0:T(8,128)(2,1)S(1)} async-done(((bf16[32,64,768]{2,1,0:T(8,128)(2,1)}), bf16[32,64,768]{2,1,0:T(8,128)(2,1)S(1)}, u32[]{:S(2)}, u32[]{:S(2)}) %all-to-all-start) | async-done | bytes 3145760 | tf_op jit(solution)/shard_map/all_to_all | solution.py:523
  135.5 5.0 %all-to-all-start.1 = ((bf16[32,64,256]{2,1,0:T(8,128)(2,1)}), bf16[32,64,256]{2,1,0:T(8,128)(2,1)}, u32[]{:S(2)}, u32[]{:S(2)}) async-start(bf16[32,64,256]{2,1,0:T(8,128)(2,1)} %attend.3), calls=%async_computation.1 | async-start | bytes 2097152 | tf_op jit(solution)/shard_map/all_to_all | solution.py:523
  142.2 2.7 %collective-permute-start.16 = (bf16[256,768]{1,0:T(8,128)(2,1)}, bf16[256,768]{1,0:T(8,128)(2,1)S(1)}, u32[]{:S(2)}, u32[]{:S(2)}) collective-permute-start(bf16[256,768]{1,0:T(8,128)(2,1)} %get-tuple-element.85), channel_id=1, source_target_pairs={{0,2},{1,3},{2,0},{3,1},{4,6},{5,7},{6,4},{7,5},{8,10},{9,11},{10,... | collective-permute-start | bytes 1179656 | tf_op jit(solution)/shard_map/ppermute | solution.py:526
  145.3 2.4 %collective-permute-start.18 = (bf16[256,768]{1,0:T(8,128)(2,1)}, bf16[256,768]{1,0:T(8,128)(2,1)S(1)}, u32[]{:S(2)}, u32[]{:S(2)}) collective-permute-start(bf16[256,768]{1,0:T(8,128)(2,1)} %get-tuple-element.87), channel_id=1, source_target_pairs={{0,3},{1,0},{2,1},{3,2},{4,7},{5,4},{6,5},{7,6},{8,11},{9,8},{10,9... | collective-permute-start | bytes 1179656 | tf_op jit(solution)/shard_map/ppermute | solution.py:526
  147.6 9.9 %all-to-all-done.1.received_ref = bf16[32,64,256]{2,1,0:T(8,128)(2,1)} async-done(((bf16[32,64,256]{2,1,0:T(8,128)(2,1)}), bf16[32,64,256]{2,1,0:T(8,128)(2,1)}, u32[]{:S(2)}, u32[]{:S(2)}) %all-to-all-start.1) | async-done | bytes 1048608 | tf_op jit(solution)/shard_map/all_to_all | solution.py:523
  157.5 1.8 %place.3 = (bf16[256,256]{1,0:T(8,128)(2,1)S(1)}, bf16[256,256]{1,0:T(8,128)(2,1)S(1)}, bf16[256,256]{1,0:T(8,128)(2,1)S(1)}, bf16[256,256]{1,0:T(8,128)(2,1)S(1)}) custom-call(s32[16]{0:T(128)S(1)} %reshape.58.source_ref, bf16[32,64,256]{2,1,0:T(8,128)(2,1)} %all-to-all-done.1.received_ref), custom_call_target="tpu_custom_call" | custom-call | tf_op jit(solution)/shard_map/place/pallas_call | solution.py:367
  159.3 2.8 %collective-permute-start.21 = (bf16[256,256]{1,0:T(8,128)(2,1)S(1)}, bf16[256,256]{1,0:T(8,128)(2,1)S(1)}, u32[]{:S(2)}, u32[]{:S(2)}) collective-permute-start(bf16[256,256]{1,0:T(8,128)(2,1)S(1)} %get-tuple-element.92), channel_id=1, source_target_pairs={{0,2},{1,3},{2,0},{3,1},{4,6},{5,7},{6,4},{7,5},{8,10},{9,11},{10,... | collective-permute-start | bytes 393224 | tf_op jit(solution)/shard_map/ppermute | solution.py:526
  162.4 2.4 %collective-permute-start.23 = (bf16[256,256]{1,0:T(8,128)(2,1)S(1)}, bf16[256,256]{1,0:T(8,128)(2,1)S(1)}, u32[]{:S(2)}, u32[]{:S(2)}) collective-permute-start(bf16[256,256]{1,0:T(8,128)(2,1)S(1)} %get-tuple-element.94), channel_id=1, source_target_pairs={{0,3},{1,0},{2,1},{3,2},{4,7},{5,4},{6,5},{7,6},{8,11},{9,8},{10,9... | collective-permute-start | bytes 393224 | tf_op jit(solution)/shard_map/ppermute | solution.py:526
  164.8 1.7 %join.2.refs_0_ = bf16[256,4096]{1,0:T(8,128)(2,1)} custom-call(s32[4]{0:T(128)S(1)} %and_select_fusion.order_ref, bf16[256,768]{1,0:T(8,128)(2,1)S(1)} %get-tuple-element.84.refs_0_, bf16[256,768]{1,0:T(8,128)(2,1)S(1)} %collective-permute-done.16.refs_1_, bf16[256,768]{1,0:T(8,128)(2,1)S(1)} %collective-permute-done.17.refs_2_, ...), custom_call_target="tpu_custom_call" | custom-call | tf_op jit(solution)/shard_map/join/pallas_call | solution.py:402
  166.5 2.3 %collective-permute-done.22.refs_3_ = bf16[256,256]{1,0:T(8,128)(2,1)S(1)} collective-permute-done((bf16[256,256]{1,0:T(8,128)(2,1)S(1)}, bf16[256,256]{1,0:T(8,128)(2,1)S(1)}, u32[]{:S(2)}, u32[]{:S(2)}) %collective-permute-start.22) | collective-permute-done | bytes 131104 | tf_op jit(solution)/shard_map/ppermute | solution.py:526
  (115 shorter events, 28.0 us)
Async XLA Ops:
  2.0 27.2 %collective-permute-start = (bf16[256,1280]{1,0:T(8,128)(2,1)}, bf16[256,1280]{1,0:T(8,128)(2,1)S(1)}, u32[]{:S(2)}, u32[]{:S(2)}) collective-permute-start(bf16[256,1280]{1,0:T(8,128)(2,1)} %side_by_side.1), channel_id=1, source_target_pairs={{0,32},{4,12},{8,40},{12,20},{16,48},{20,28},{24,56},{28,4},{32,64... | collective-permute-start | bytes 1966088 | tf_op jit(solution)/shard_map/ppermute | solution.py:441
  4.5 24.7 %collective-permute-start.1 = (bf16[256,1280]{1,0:T(8,128)(2,1)}, bf16[256,1280]{1,0:T(8,128)(2,1)S(1)}, u32[]{:S(2)}, u32[]{:S(2)}) collective-permute-start(bf16[256,1280]{1,0:T(8,128)(2,1)} %side_by_side.1), channel_id=1, source_target_pairs={{0,96},{4,28},{8,104},{12,4},{16,112},{20,12},{24,120},{28,20},{32... | collective-permute-start | bytes 1966088 | tf_op jit(solution)/shard_map/ppermute | solution.py:441
  6.7 23.6 %collective-permute-start.2 = (bf16[256,1280]{1,0:T(8,128)(2,1)}, bf16[256,1280]{1,0:T(8,128)(2,1)S(1)}, u32[]{:S(2)}, u32[]{:S(2)}) collective-permute-start(bf16[256,1280]{1,0:T(8,128)(2,1)} %side_by_side.1), channel_id=1, source_target_pairs={{0,64},{4,20},{8,72},{12,28},{16,80},{20,4},{24,88},{28,12},{32,96... | collective-permute-start | bytes 1966088 | tf_op jit(solution)/shard_map/ppermute | solution.py:441
  7.9 22.4 %collective-permute-start.3 = (bf16[256,1280]{1,0:T(8,128)(2,1)}, bf16[256,1280]{1,0:T(8,128)(2,1)S(1)}, u32[]{:S(2)}, u32[]{:S(2)}) collective-permute-start(bf16[256,1280]{1,0:T(8,128)(2,1)} %side_by_side.1), channel_id=1, source_target_pairs={{0,8},{4,36},{8,16},{12,44},{16,24},{20,52},{24,0},{28,60},{32,40}... | collective-permute-start | bytes 1966088 | tf_op jit(solution)/shard_map/ppermute | solution.py:444
  9.2 21.1 %collective-permute-start.4 = (bf16[256,1280]{1,0:T(8,128)(2,1)}, bf16[256,1280]{1,0:T(8,128)(2,1)S(1)}, u32[]{:S(2)}, u32[]{:S(2)}) collective-permute-start(bf16[256,1280]{1,0:T(8,128)(2,1)} %side_by_side.1), channel_id=1, source_target_pairs={{0,24},{4,100},{8,0},{12,108},{16,8},{20,116},{24,16},{28,124},{32... | collective-permute-start | bytes 1966088 | tf_op jit(solution)/shard_map/ppermute | solution.py:444
  22.7 6.4 %copy-start.19 = (s32[4]{0:T(128)S(1)}, s32[4]{0:T(128)}, u32[]{:S(2)}) copy-start(s32[4]{0:T(128)} %constant.70) | copy-start | bytes 52
  22.8 10.5 %copy-start.18 = (bf16[256,1280]{1,0:T(8,128)(2,1)S(1)}, bf16[256,1280]{1,0:T(8,128)(2,1)}, u32[]{:S(2)}) copy-start(bf16[256,1280]{1,0:T(8,128)(2,1)} %side_by_side.1) | copy-start | bytes 1966084
  30.3 10.5 %slice-start = ((s8[16777216]{0:T(1024)(128)(4,1)}), s8[4194304]{0:T(1024)(128)(4,1)S(1)}, s32[]{:S(2)}) async-start(s8[16777216]{0:T(1024)(128)(4,1)} %bitcast.6), calls=%async_computation.2 | async-start | bytes 8388608
  30.5 10.3 %slice-start.1 = ((s8[16777216]{0:T(1024)(128)(4,1)}), s8[4194304]{0:T(1024)(128)(4,1)S(1)}, s32[]{:S(2)}) async-start(s8[16777216]{0:T(1024)(128)(4,1)} %bitcast.6), calls=%async_computation.3 | async-start | bytes 8388608
  30.5 25.1 %collective-permute-start.5 = (bf16[768,1280]{1,0:T(8,128)(2,1)S(1)}, bf16[768,1280]{1,0:T(8,128)(2,1)S(1)}, u32[]{:S(2)}, u32[]{:S(2)}) collective-permute-start(bf16[768,1280]{1,0:T(8,128)(2,1)S(1)} %constant_dynamic-update-slice_fusion.refs_0_), channel_id=1, source_target_pairs={{0,8},{4,36},{8,16},{12,44},{16,24},{20,52},{24,0},{28,60},{32,40}... | collective-permute-start | bytes 5898248 | tf_op jit(solution)/shard_map/ppermute | solution.py:444
  31.6 24.0 %collective-permute-start.6 = (bf16[768,1280]{1,0:T(8,128)(2,1)S(1)}, bf16[768,1280]{1,0:T(8,128)(2,1)S(1)}, u32[]{:S(2)}, u32[]{:S(2)}) collective-permute-start(bf16[768,1280]{1,0:T(8,128)(2,1)S(1)} %constant_dynamic-update-slice_fusion.refs_0_), channel_id=1, source_target_pairs={{0,24},{4,100},{8,0},{12,108},{16,8},{20,116},{24,16},{28,124},{32... | collective-permute-start | bytes 5898248 | tf_op jit(solution)/shard_map/ppermute | solution.py:444
  33.4 7.4 %slice-start.2 = ((s8[16777216]{0:T(1024)(128)(4,1)}), s8[4194304]{0:T(1024)(128)(4,1)S(1)}, s32[]{:S(2)}) async-start(s8[16777216]{0:T(1024)(128)(4,1)} %bitcast.6), calls=%async_computation.4 | async-start | bytes 8388608
  37.9 10.0 %collective-permute-start.9 = (bf16[512,1280]{1,0:T(8,128)(2,1)S(1)}, bf16[512,1280]{1,0:T(8,128)(2,1)S(1)}, u32[]{:S(2)}, u32[]{:S(2)}) collective-permute-start(bf16[512,1280]{1,0:T(8,128)(2,1)S(1)} %pad_maximum_fusion.3), channel_id=1, source_target_pairs={{0,4},{4,0},{8,12},{12,8},{16,20},{20,16},{24,28},{28,24},{32,36},... | collective-permute-start | bytes 3932168 | tf_op jit(solution)/shard_map/ppermute | solution.py:447
  40.1 7.9 %collective-permute-start.7 = (bf16[512,1280]{1,0:T(8,128)(2,1)S(1)}, bf16[512,1280]{1,0:T(8,128)(2,1)S(1)}, u32[]{:S(2)}, u32[]{:S(2)}) collective-permute-start(bf16[512,1280]{1,0:T(8,128)(2,1)S(1)} %pad_maximum_fusion.1), channel_id=1, source_target_pairs={{0,4},{4,0},{8,12},{12,8},{16,20},{20,16},{24,28},{28,24},{32,36},... | collective-permute-start | bytes 3932168 | tf_op jit(solution)/shard_map/ppermute | solution.py:447
  40.3 7.7 %collective-permute-start.8 = (bf16[512,1280]{1,0:T(8,128)(2,1)S(1)}, bf16[512,1280]{1,0:T(8,128)(2,1)S(1)}, u32[]{:S(2)}, u32[]{:S(2)}) collective-permute-start(bf16[512,1280]{1,0:T(8,128)(2,1)S(1)} %pad_maximum_fusion.2), channel_id=1, source_target_pairs={{0,4},{4,0},{8,12},{12,8},{16,20},{20,16},{24,28},{28,24},{32,36},... | collective-permute-start | bytes 3932168 | tf_op jit(solution)/shard_map/ppermute | solution.py:447
  55.6 10.5 %collective-permute-start.12 = (bf16[768,1280]{1,0:T(8,128)(2,1)S(1)}, bf16[768,1280]{1,0:T(8,128)(2,1)S(1)}, u32[]{:S(2)}, u32[]{:S(2)}) collective-permute-start(bf16[768,1280]{1,0:T(8,128)(2,1)S(1)} %collective-permute-done.5.refs_0_), channel_id=1, source_target_pairs={{0,4},{4,0},{8,12},{12,8},{16,20},{20,16},{24,28},{28,24},{32,36},... | collective-permute-start | bytes 5898248 | tf_op jit(solution)/shard_map/ppermute | solution.py:447
  57.8 8.2 %collective-permute-start.13 = (bf16[768,1280]{1,0:T(8,128)(2,1)S(1)}, bf16[768,1280]{1,0:T(8,128)(2,1)S(1)}, u32[]{:S(2)}, u32[]{:S(2)}) collective-permute-start(bf16[768,1280]{1,0:T(8,128)(2,1)S(1)} %collective-permute-done.6.refs_1_), channel_id=1, source_target_pairs={{0,4},{4,0},{8,12},{12,8},{16,20},{20,16},{24,28},{28,24},{32,36},... | collective-permute-start | bytes 5898248 | tf_op jit(solution)/shard_map/ppermute | solution.py:447
  58.1 18.0 %collective-permute-start.11 = (bf16[512,1280]{1,0:T(8,128)(2,1)S(1)}, bf16[512,1280]{1,0:T(8,128)(2,1)S(1)}, u32[]{:S(2)}, u32[]{:S(2)}) collective-permute-start(bf16[512,1280]{1,0:T(8,128)(2,1)S(1)} %pad_maximum_fusion.5), channel_id=1, source_target_pairs={{0,8},{4,36},{8,16},{12,44},{16,24},{20,52},{24,0},{28,60},{32,40}... | collective-permute-start | bytes 3932168 | tf_op jit(solution)/shard_map/ppermute | solution.py:444
  59.4 17.0 %collective-permute-start.10 = (bf16[512,1280]{1,0:T(8,128)(2,1)S(1)}, bf16[512,1280]{1,0:T(8,128)(2,1)S(1)}, u32[]{:S(2)}, u32[]{:S(2)}) collective-permute-start(bf16[512,1280]{1,0:T(8,128)(2,1)S(1)} %pad_maximum_fusion.4), channel_id=1, source_target_pairs={{0,24},{4,100},{8,0},{12,108},{16,8},{20,116},{24,16},{28,124},{32... | collective-permute-start | bytes 3932168 | tf_op jit(solution)/shard_map/ppermute | solution.py:444
  70.9 8.1 %copy-start.10 = (bf16[1024,1024]{1,0:T(8,128)(2,1)S(1)}, bf16[1024,1024]{1,0:T(8,128)(2,1)}, u32[]{:S(2)}) copy-start(bf16[1024,1024]{1,0:T(8,128)(2,1)} %get-tuple-element.78.x_ref) | copy-start | bytes 6291460
  76.6 5.8 %collective-permute-start.14 = (bf16[512,1024]{1,0:T(8,128)(2,1)S(1)}, bf16[512,1024]{1,0:T(8,128)(2,1)S(1)}, u32[]{:S(2)}, u32[]{:S(2)}) collective-permute-start(bf16[512,1024]{1,0:T(8,128)(2,1)S(1)} %slice.48), channel_id=1, source_target_pairs={{0,4},{4,0},{8,12},{12,8},{16,20},{20,16},{24,28},{28,24},{32,36},... | collective-permute-start | bytes 3145736 | tf_op jit(solution)/shard_map/ppermute | solution.py:447
  78.8 3.6 %collective-permute-start.15 = (bf16[512,1024]{1,0:T(8,128)(2,1)S(1)}, bf16[512,1024]{1,0:T(8,128)(2,1)S(1)}, u32[]{:S(2)}, u32[]{:S(2)}) collective-permute-start(bf16[512,1024]{1,0:T(8,128)(2,1)S(1)} %slice.49), channel_id=1, source_target_pairs={{0,4},{4,0},{8,12},{12,8},{16,20},{20,16},{24,28},{28,24},{32,36},... | collective-permute-start | bytes 3145736 | tf_op jit(solution)/shard_map/ppermute | solution.py:447
  89.4 46.1 %all-to-all-start = ((bf16[32,64,768]{2,1,0:T(8,128)(2,1)}), bf16[32,64,768]{2,1,0:T(8,128)(2,1)S(1)}, u32[]{:S(2)}, u32[]{:S(2)}) async-start(bf16[32,64,768]{2,1,0:T(8,128)(2,1)} %get-tuple-element.83), calls=%async_computation | async-start | bytes 6291456 | tf_op jit(solution)/shard_map/all_to_all | solution.py:523
  97.7 1.6 collective-permute-start.20
  98.0 1.7 collective-permute-start.19
  135.5 22.0 %all-to-all-start.1 = ((bf16[32,64,256]{2,1,0:T(8,128)(2,1)}), bf16[32,64,256]{2,1,0:T(8,128)(2,1)}, u32[]{:S(2)}, u32[]{:S(2)}) async-start(bf16[32,64,256]{2,1,0:T(8,128)(2,1)} %attend.3), calls=%async_computation.1 | async-start | bytes 2097152 | tf_op jit(solution)/shard_map/all_to_all | solution.py:523
  142.2 20.2 %collective-permute-start.16 = (bf16[256,768]{1,0:T(8,128)(2,1)}, bf16[256,768]{1,0:T(8,128)(2,1)S(1)}, u32[]{:S(2)}, u32[]{:S(2)}) collective-permute-start(bf16[256,768]{1,0:T(8,128)(2,1)} %get-tuple-element.85), channel_id=1, source_target_pairs={{0,2},{1,3},{2,0},{3,1},{4,6},{5,7},{6,4},{7,5},{8,10},{9,11},{10,... | collective-permute-start | bytes 1179656 | tf_op jit(solution)/shard_map/ppermute | solution.py:526
  145.0 19.9 %collective-permute-start.17 = (bf16[256,768]{1,0:T(8,128)(2,1)}, bf16[256,768]{1,0:T(8,128)(2,1)S(1)}, u32[]{:S(2)}, u32[]{:S(2)}) collective-permute-start(bf16[256,768]{1,0:T(8,128)(2,1)} %get-tuple-element.86), channel_id=1, source_target_pairs={{0,1},{1,2},{2,3},{3,0},{4,5},{5,6},{6,7},{7,4},{8,9},{9,10},{10,1... | collective-permute-start | bytes 1179656 | tf_op jit(solution)/shard_map/ppermute | solution.py:526
  145.3 19.5 %collective-permute-start.18 = (bf16[256,768]{1,0:T(8,128)(2,1)}, bf16[256,768]{1,0:T(8,128)(2,1)S(1)}, u32[]{:S(2)}, u32[]{:S(2)}) collective-permute-start(bf16[256,768]{1,0:T(8,128)(2,1)} %get-tuple-element.87), channel_id=1, source_target_pairs={{0,3},{1,0},{2,1},{3,2},{4,7},{5,4},{6,5},{7,6},{8,11},{9,8},{10,9... | collective-permute-start | bytes 1179656 | tf_op jit(solution)/shard_map/ppermute | solution.py:526
  159.3 7.2 %collective-permute-start.21 = (bf16[256,256]{1,0:T(8,128)(2,1)S(1)}, bf16[256,256]{1,0:T(8,128)(2,1)S(1)}, u32[]{:S(2)}, u32[]{:S(2)}) collective-permute-start(bf16[256,256]{1,0:T(8,128)(2,1)S(1)} %get-tuple-element.92), channel_id=1, source_target_pairs={{0,2},{1,3},{2,0},{3,1},{4,6},{5,7},{6,4},{7,5},{8,10},{9,11},{10,... | collective-permute-start | bytes 393224 | tf_op jit(solution)/shard_map/ppermute | solution.py:526
  162.1 6.8 %collective-permute-start.22 = (bf16[256,256]{1,0:T(8,128)(2,1)S(1)}, bf16[256,256]{1,0:T(8,128)(2,1)S(1)}, u32[]{:S(2)}, u32[]{:S(2)}) collective-permute-start(bf16[256,256]{1,0:T(8,128)(2,1)S(1)} %get-tuple-element.93), channel_id=1, source_target_pairs={{0,1},{1,2},{2,3},{3,0},{4,5},{5,6},{6,7},{7,4},{8,9},{9,10},{10,1... | collective-permute-start | bytes 393224 | tf_op jit(solution)/shard_map/ppermute | solution.py:526
  162.4 6.4 %collective-permute-start.23 = (bf16[256,256]{1,0:T(8,128)(2,1)S(1)}, bf16[256,256]{1,0:T(8,128)(2,1)S(1)}, u32[]{:S(2)}, u32[]{:S(2)}) collective-permute-start(bf16[256,256]{1,0:T(8,128)(2,1)S(1)} %get-tuple-element.94), channel_id=1, source_target_pairs={{0,3},{1,0},{2,1},{3,2},{4,7},{5,4},{6,5},{7,6},{8,11},{9,8},{10,9... | collective-permute-start | bytes 393224 | tf_op jit(solution)/shard_map/ppermute | solution.py:526
  (18 other events, 51.5 us)

commit v9 on v8

--- a/solution.py
+++ b/solution.py
@@ -471,7 +471,7 @@
     near = [first(weights, 1), first(weights, -1), first(weights, 2)]
     near += [second(weights, 1), second(weights, -1)]
     scale, x_near = norm(order, hidden_states, gain, widths[:1])
-    near, scale, x_near, plan, bias = lax.optimization_barrier((near, scale, x_near, plan, bias))
+    near, scale, x_near, plan = lax.optimization_barrier((near, scale, x_near, plan))
     own_dest, own_length, source, joins = plan
 
     own_ahead, own_behind = near[3:]

time: 171 us -> 171 us (level)
    unnamed x50 -> x54, local copies, waits for them, and re-layouts: 14.5 us -> 14.5 us
  transfers between devices with their start and end apart: 26 -> 26, of which waited for: 9 -> 9; matrix products, arithmetic and copies ran while one was open for 5% -> 4% of each run, Pallas kernels for 27% -> 27%
where the time goes in v9:
time: 171 us
  Pallas kernels  55.1 us (32%)
  waiting for transfers between devices  48.6 us (28%)
  starting transfers between devices  44.4 us (26%)
  local copies, waits for them, and re-layouts  19.2 us (11%)
  other arithmetic  2.39 us (1%)
    all_to_all x2, waiting for transfers between devices, exchanged(): lax.all_to_all(sent, 'dp', split_axis=0, concat_axis=0, tiled=True)  35.8 us
    pallas_call x5, Pallas kernels, project(): pl.pallas_call(add_kernel if totals else first_kernel, grid=(rows // tile...  22.3 us
    unnamed x54, local copies, waits for them, and re-layouts  14.5 us
    pallas_call x2, Pallas kernels, norm(): pl.pallas_call(norm_kernel if scale is None else functools.partial(norm_r...  13.4 us
    all_to_all x2, starting transfers between devices, exchanged(): lax.all_to_all(sent, 'dp', split_axis=0, concat_axis=0, tiled=True)  11.3 us
    ppermute x6, starting transfers between devices, exchanged(): lax.ppermute(parts[k], 'mp', [(i, (i + k) % planes) for i in range(planes)])  10.9 us
    pallas_call x2, Pallas kernels, attend(): pl.pallas_call(functools.partial(attend_kernel, columns), grid_spec=pltpu...  10.9 us
    ppermute x6, starting transfers between devices, second(): return lax.ppermute(piece, 'dp', shift_pairs(0, by))  8.48 us
  transfers between devices with their start and end apart: 26, of which 9 were waited for; matrix products, arithmetic and copies ran while one was open for 4% of the time, Pallas kernels for 27%

profile of v9, /device:TPU:1, one launch (start us, length us, event | category | flops | bytes accessed | tf_op | source)
XLA Modules:
  0.0 170.5 jit_solution(5359207480537750494)
XLA Ops:
  0.0 1.9 %side_by_side.1 = bf16[256,1280]{1,0:T(8,128)(2,1)} custom-call(bf16[256,1024]{1,0:T(8,128)(2,1)} %query_ref.1, bf16[256,256]{1,0:T(8,128)(2,1)} %keyval_ref.1), custom_call_target="tpu_custom_call" | custom-call | tf_op jit(solution)/shard_map/side_by_side/pallas_call | solution.py:114
  2.0 2.5 %collective-permute-start = (bf16[256,1280]{1,0:T(8,128)(2,1)}, bf16[256,1280]{1,0:T(8,128)(2,1)S(1)}, u32[]{:S(2)}, u32[]{:S(2)}) collective-permute-start(bf16[256,1280]{1,0:T(8,128)(2,1)} %side_by_side.1), channel_id=1, source_target_pairs={{0,32},{4,12},{8,40},{12,20},{16,48},{20,28},{24,56},{28,4},{32,64... | collective-permute-start | bytes 1966088 | tf_op jit(solution)/shard_map/ppermute | solution.py:441
  4.5 2.2 %collective-permute-start.1 = (bf16[256,1280]{1,0:T(8,128)(2,1)}, bf16[256,1280]{1,0:T(8,128)(2,1)S(1)}, u32[]{:S(2)}, u32[]{:S(2)}) collective-permute-start(bf16[256,1280]{1,0:T(8,128)(2,1)} %side_by_side.1), channel_id=1, source_target_pairs={{0,96},{4,28},{8,104},{12,4},{16,112},{20,12},{24,120},{28,20},{32... | collective-permute-start | bytes 1966088 | tf_op jit(solution)/shard_map/ppermute | solution.py:441
  14.8 5.8 %copy-done.2 = bf16[1024,8192]{1,0:T(8,128)(2,1)S(1)} copy-done((bf16[1024,8192]{1,0:T(8,128)(2,1)S(1)}, bf16[1024,8192]{1,0:T(8,128)(2,1)}, u32[]{:S(2)}) %copy-start.2) | copy-done | bytes 16777240
  21.3 6.3 %norm.2 = (f32[1024,1]{1,0:T(8,128)S(1)}, bf16[1024,1536]{1,0:T(8,128)(2,1)}) custom-call(s32[64]{0:T(128)S(1)} %fusion.4.order_ref, bf16[1024,8192]{1,0:T(8,128)(2,1)S(1)} %copy-done.2, f32[1,8192]{1,0:T(1,128)S(1)} %bitcast.8), custom_call_target="tpu_custom_call" | custom-call | flops 50331648 | bytes 19922944 | tf_op jit(solution)/shard_map/norm/pallas_call | solution.py:166
  27.7 2.6 %collective-permute-done.2 = bf16[256,1280]{1,0:T(8,128)(2,1)S(1)} collective-permute-done((bf16[256,1280]{1,0:T(8,128)(2,1)}, bf16[256,1280]{1,0:T(8,128)(2,1)S(1)}, u32[]{:S(2)}, u32[]{:S(2)}) %collective-permute-start.2) | collective-permute-done | bytes 655392 | tf_op jit(solution)/shard_map/ppermute | solution.py:441
  33.4 4.4 %project.5.total_ref = f32[1024,1280]{1,0:T(8,128)S(1)} custom-call(bf16[1024,1536]{1,0:T(8,128)(2,1)S(1)} %copy-done.17, bf16[768,1280]{1,0:T(8,128)(2,1)S(1)} %constant_dynamic-update-slice_fusion.refs_0_, bf16[768,1280]{1,0:T(8,128)(2,1)S(1)} %pad_maximum_fusion.refs_1_), custom_call_target="tpu_custom_call" | custom-call | flops 4026531840 | bytes 17563648 | tf_op jit(solution)/shard_map/project/pallas_call | solution.py:218
  37.9 2.0 %collective-permute-start.9 = (bf16[512,1280]{1,0:T(8,128)(2,1)S(1)}, bf16[512,1280]{1,0:T(8,128)(2,1)S(1)}, u32[]{:S(2)}, u32[]{:S(2)}) collective-permute-start(bf16[512,1280]{1,0:T(8,128)(2,1)S(1)} %pad_maximum_fusion.3), channel_id=1, source_target_pairs={{0,4},{4,0},{8,12},{12,8},{16,20},{20,16},{24,28},{28,24},{32,36},... | collective-permute-start | bytes 3932168 | tf_op jit(solution)/shard_map/ppermute | solution.py:447
  40.9 7.1 %norm.3 = (bf16[1024,1536]{1,0:T(8,128)(2,1)}, bf16[1024,1536]{1,0:T(8,128)(2,1)}, bf16[1024,1536]{1,0:T(8,128)(2,1)}, bf16[1024,1024]{1,0:T(8,128)(2,1)}, bf16[1024,1024]{1,0:T(8,128)(2,1)}) custom-call(s32[64]{0:T(128)S(1)} %fusion.4.order_ref, bf16[1024,8192]{1,0:T(8,128)(2,1)S(1)} %bitcast.7, f32[1,8192]{1,0:T(1,128)S(1)} %bitcast.9, ...), custom_call_target="tpu_custom_call" | custom-call | flops 50331648 | bytes 30408704 | tf_op jit(solution)/shard_map/norm/pallas_call | solution.py:166
  48.0 1.9 %copy-done.9 = bf16[1024,1536]{1,0:T(8,128)(2,1)S(1)} copy-done((bf16[1024,1536]{1,0:T(8,128)(2,1)S(1)}, bf16[1024,1536]{1,0:T(8,128)(2,1)}, u32[]{:S(2)}) %copy-start.9) | copy-done | bytes 3145752
  49.9 4.8 %project.6.total_ref = f32[1024,1280]{1,0:T(8,128)S(1)} custom-call(f32[1024,1280]{1,0:T(8,128)S(1)} %project.5.total_ref, bf16[1024,1536]{1,0:T(8,128)(2,1)S(1)} %copy-done.9, bf16[512,1280]{1,0:T(8,128)(2,1)S(1)} %collective-permute-done.7.refs_0_, bf16[512,1280]{1,0:T(8,128)(2,1)S(1)} %collective-permute-done.8.refs_1_, ...), custom_call_target="tpu_custom_call", output_to_operand_aliasing={{}: (0, {})} | custom-call | flops 1024 | bytes 1024 | tf_op jit(solution)/shard_map/project/pallas_call | solution.py:218
  55.6 2.2 %collective-permute-start.12 = (bf16[768,1280]{1,0:T(8,128)(2,1)S(1)}, bf16[768,1280]{1,0:T(8,128)(2,1)S(1)}, u32[]{:S(2)}, u32[]{:S(2)}) collective-permute-start(bf16[768,1280]{1,0:T(8,128)(2,1)S(1)} %collective-permute-done.5.refs_0_), channel_id=1, source_target_pairs={{0,4},{4,0},{8,12},{12,8},{16,20},{20,16},{24,28},{28,24},{32,36},... | collective-permute-start | bytes 5898248 | tf_op jit(solution)/shard_map/ppermute | solution.py:447
  59.4 1.8 %collective-permute-start.10 = (bf16[512,1280]{1,0:T(8,128)(2,1)S(1)}, bf16[512,1280]{1,0:T(8,128)(2,1)S(1)}, u32[]{:S(2)}, u32[]{:S(2)}) collective-permute-start(bf16[512,1280]{1,0:T(8,128)(2,1)S(1)} %pad_maximum_fusion.4), channel_id=1, source_target_pairs={{0,24},{4,100},{8,0},{12,108},{16,8},{20,116},{24,16},{28,124},{32... | collective-permute-start | bytes 3932168 | tf_op jit(solution)/shard_map/ppermute | solution.py:444
  61.2 4.8 %project.7.total_ref = f32[1024,1280]{1,0:T(8,128)S(1)} custom-call(f32[1024,1280]{1,0:T(8,128)S(1)} %project.6.total_ref, bf16[1024,1536]{1,0:T(8,128)(2,1)S(1)} %copy-done.8, bf16[768,1280]{1,0:T(8,128)(2,1)S(1)} %collective-permute-done.5.refs_0_, bf16[768,1280]{1,0:T(8,128)(2,1)S(1)} %collective-permute-done.6.refs_1_), custom_call_target="tpu_custom_call", output_to_operand_aliasing={{}: (0, {})} | custom-call | flops 4026531840 | bytes 17563648 | tf_op jit(solution)/shard_map/project/pallas_call | solution.py:218
  66.0 4.8 %project.8.total_ref = f32[1024,1280]{1,0:T(8,128)S(1)} custom-call(f32[1024,1280]{1,0:T(8,128)S(1)} %project.7.total_ref, bf16[1024,1536]{1,0:T(8,128)(2,1)S(1)} %copy-done.7, bf16[768,1280]{1,0:T(8,128)(2,1)S(1)} %collective-permute-done.12.refs_0_, bf16[768,1280]{1,0:T(8,128)(2,1)S(1)} %collective-permute-done.13.refs_1_), custom_call_target="tpu_custom_call", output_to_operand_aliasing={{}: (0, {})} | custom-call | flops 4026531840 | bytes 17563648 | tf_op jit(solution)/shard_map/project/pallas_call | solution.py:218
  70.9 5.3 %collective-permute-done.11.refs_1_ = bf16[512,1280]{1,0:T(8,128)(2,1)S(1)} collective-permute-done((bf16[512,1280]{1,0:T(8,128)(2,1)S(1)}, bf16[512,1280]{1,0:T(8,128)(2,1)S(1)}, u32[]{:S(2)}, u32[]{:S(2)}) %collective-permute-start.11) | collective-permute-done | bytes 1310752 | tf_op jit(solution)/shard_map/ppermute | solution.py:444
  76.6 2.1 %collective-permute-start.14 = (bf16[512,1024]{1,0:T(8,128)(2,1)S(1)}, bf16[512,1024]{1,0:T(8,128)(2,1)S(1)}, u32[]{:S(2)}, u32[]{:S(2)}) collective-permute-start(bf16[512,1024]{1,0:T(8,128)(2,1)S(1)} %slice.48), channel_id=1, source_target_pairs={{0,4},{4,0},{8,12},{12,8},{16,20},{20,16},{24,28},{28,24},{32,36},... | collective-permute-start | bytes 3145736 | tf_op jit(solution)/shard_map/ppermute | solution.py:447
  79.0 3.5 %project.9.total_ref = f32[1024,1280]{1,0:T(8,128)S(1)} custom-call(f32[1024,1280]{1,0:T(8,128)S(1)} %project.8.total_ref, bf16[1024,1024]{1,0:T(8,128)(2,1)S(1)} %copy-done.10, bf16[512,1280]{1,0:T(8,128)(2,1)S(1)} %collective-permute-done.10.refs_0_, bf16[512,1280]{1,0:T(8,128)(2,1)S(1)} %collective-permute-done.11.refs_1_), custom_call_target="tpu_custom_call", output_to_operand_aliasing={{}: (0, {})} | custom-call | flops 2684354560 | bytes 15204352 | tf_op jit(solution)/shard_map/project/pallas_call | solution.py:218
  82.6 6.1 %attend.2 = (bf16[32,64,768]{2,1,0:T(8,128)(2,1)}, bf16[1024,256]{1,0:T(8,128)(2,1)S(1)}) custom-call(s32[16]{0:T(128)S(1)} %get-tuple-element.53.dest_ref, s32[16]{0:T(128)S(1)} %get-tuple-element.54.length_ref, f32[1024,1280]{1,0:T(8,128)S(1)} %project.9.total_ref, bf16[1024,1024]{1,0:T(8,128)(2,1)S(1)} %copy-done.3, ...), custom_call_target="tpu_custom_call" | custom-call | flops 2147483648 | bytes 12582912 | tf_op jit(solution)/shard_map/attend/pallas_call | solution.py:329
  89.6 6.2 %all-to-all-start = ((bf16[32,64,768]{2,1,0:T(8,128)(2,1)}), bf16[32,64,768]{2,1,0:T(8,128)(2,1)S(1)}, u32[]{:S(2)}, u32[]{:S(2)}) async-start(bf16[32,64,768]{2,1,0:T(8,128)(2,1)} %get-tuple-element.81), calls=%async_computation | async-start | bytes 6291456 | tf_op jit(solution)/shard_map/all_to_all | solution.py:523
  99.7 2.5 %copy-done.1 = f32[1024,1280]{1,0:T(8,128)S(1)} copy-done((f32[1024,1280]{1,0:T(8,128)S(1)}, f32[1024,1280]{1,0:T(8,128)}, u32[]{:S(2)}) %copy-start.1) | copy-done | bytes 5242904
  104.9 4.8 %attend.3 = bf16[32,64,256]{2,1,0:T(8,128)(2,1)} custom-call(s32[16]{0:T(128)S(1)} %get-tuple-element.53.dest_ref, s32[16]{0:T(128)S(1)} %get-tuple-element.54.length_ref, f32[1024,1280]{1,0:T(8,128)S(1)} %copy-done.1, bf16[1024,1024]{1,0:T(8,128)(2,1)S(1)} %copy-done.4, f32[1,1280]{1,0:T(1,128)S(1)} %broadcast_in_dim.26.bias_ref, ...), custom_call_target="tpu_custom_call" | custom-call | flops 536870912 | bytes 4718592 | tf_op jit(solution)/shard_map/attend/pallas_call | solution.py:329
  109.7 25.9 %all-to-all-done.received_ref = bf16[32,64,768]{2,1,0:T(8,128)(2,1)S(1)} async-done(((bf16[32,64,768]{2,1,0:T(8,128)(2,1)}), bf16[32,64,768]{2,1,0:T(8,128)(2,1)S(1)}, u32[]{:S(2)}, u32[]{:S(2)}) %all-to-all-start) | async-done | bytes 3145760 | tf_op jit(solution)/shard_map/all_to_all | solution.py:523
  135.6 5.0 %all-to-all-start.1 = ((bf16[32,64,256]{2,1,0:T(8,128)(2,1)}), bf16[32,64,256]{2,1,0:T(8,128)(2,1)}, u32[]{:S(2)}, u32[]{:S(2)}) async-start(bf16[32,64,256]{2,1,0:T(8,128)(2,1)} %attend.3), calls=%async_computation.1 | async-start | bytes 2097152 | tf_op jit(solution)/shard_map/all_to_all | solution.py:523
  142.3 2.7 %collective-permute-start.16 = (bf16[256,768]{1,0:T(8,128)(2,1)}, bf16[256,768]{1,0:T(8,128)(2,1)S(1)}, u32[]{:S(2)}, u32[]{:S(2)}) collective-permute-start(bf16[256,768]{1,0:T(8,128)(2,1)} %get-tuple-element.83), channel_id=1, source_target_pairs={{0,2},{1,3},{2,0},{3,1},{4,6},{5,7},{6,4},{7,5},{8,10},{9,11},{10,... | collective-permute-start | bytes 1179656 | tf_op jit(solution)/shard_map/ppermute | solution.py:526
  145.3 2.4 %collective-permute-start.18 = (bf16[256,768]{1,0:T(8,128)(2,1)}, bf16[256,768]{1,0:T(8,128)(2,1)S(1)}, u32[]{:S(2)}, u32[]{:S(2)}) collective-permute-start(bf16[256,768]{1,0:T(8,128)(2,1)} %get-tuple-element.85), channel_id=1, source_target_pairs={{0,3},{1,0},{2,1},{3,2},{4,7},{5,4},{6,5},{7,6},{8,11},{9,8},{10,9... | collective-permute-start | bytes 1179656 | tf_op jit(solution)/shard_map/ppermute | solution.py:526
  147.7 9.9 %all-to-all-done.1.received_ref = bf16[32,64,256]{2,1,0:T(8,128)(2,1)} async-done(((bf16[32,64,256]{2,1,0:T(8,128)(2,1)}), bf16[32,64,256]{2,1,0:T(8,128)(2,1)}, u32[]{:S(2)}, u32[]{:S(2)}) %all-to-all-start.1) | async-done | bytes 1048608 | tf_op jit(solution)/shard_map/all_to_all | solution.py:523
  157.6 1.8 %place.3 = (bf16[256,256]{1,0:T(8,128)(2,1)S(1)}, bf16[256,256]{1,0:T(8,128)(2,1)S(1)}, bf16[256,256]{1,0:T(8,128)(2,1)S(1)}, bf16[256,256]{1,0:T(8,128)(2,1)S(1)}) custom-call(s32[16]{0:T(128)S(1)} %reshape.58.source_ref, bf16[32,64,256]{2,1,0:T(8,128)(2,1)} %all-to-all-done.1.received_ref), custom_call_target="tpu_custom_call" | custom-call | tf_op jit(solution)/shard_map/place/pallas_call | solution.py:367
  159.4 2.8 %collective-permute-start.21 = (bf16[256,256]{1,0:T(8,128)(2,1)S(1)}, bf16[256,256]{1,0:T(8,128)(2,1)S(1)}, u32[]{:S(2)}, u32[]{:S(2)}) collective-permute-start(bf16[256,256]{1,0:T(8,128)(2,1)S(1)} %get-tuple-element.90), channel_id=1, source_target_pairs={{0,2},{1,3},{2,0},{3,1},{4,6},{5,7},{6,4},{7,5},{8,10},{9,11},{10,... | collective-permute-start | bytes 393224 | tf_op jit(solution)/shard_map/ppermute | solution.py:526
  162.5 2.4 %collective-permute-start.23 = (bf16[256,256]{1,0:T(8,128)(2,1)S(1)}, bf16[256,256]{1,0:T(8,128)(2,1)S(1)}, u32[]{:S(2)}, u32[]{:S(2)}) collective-permute-start(bf16[256,256]{1,0:T(8,128)(2,1)S(1)} %get-tuple-element.92), channel_id=1, source_target_pairs={{0,3},{1,0},{2,1},{3,2},{4,7},{5,4},{6,5},{7,6},{8,11},{9,8},{10,9... | collective-permute-start | bytes 393224 | tf_op jit(solution)/shard_map/ppermute | solution.py:526
  164.9 1.7 %join.2.refs_0_ = bf16[256,4096]{1,0:T(8,128)(2,1)} custom-call(s32[4]{0:T(128)S(1)} %and_select_fusion.order_ref, bf16[256,768]{1,0:T(8,128)(2,1)S(1)} %get-tuple-element.82.refs_0_, bf16[256,768]{1,0:T(8,128)(2,1)S(1)} %collective-permute-done.16.refs_1_, bf16[256,768]{1,0:T(8,128)(2,1)S(1)} %collective-permute-done.17.refs_2_, ...), custom_call_target="tpu_custom_call" | custom-call | tf_op jit(solution)/shard_map/join/pallas_call | solution.py:402
  166.6 2.3 %collective-permute-done.22.refs_3_ = bf16[256,256]{1,0:T(8,128)(2,1)S(1)} collective-permute-done((bf16[256,256]{1,0:T(8,128)(2,1)S(1)}, bf16[256,256]{1,0:T(8,128)(2,1)S(1)}, u32[]{:S(2)}, u32[]{:S(2)}) %collective-permute-start.22) | collective-permute-done | bytes 131104 | tf_op jit(solution)/shard_map/ppermute | solution.py:526
  (119 shorter events, 27.1 us)
Async XLA Ops:
  2.0 25.7 %collective-permute-start = (bf16[256,1280]{1,0:T(8,128)(2,1)}, bf16[256,1280]{1,0:T(8,128)(2,1)S(1)}, u32[]{:S(2)}, u32[]{:S(2)}) collective-permute-start(bf16[256,1280]{1,0:T(8,128)(2,1)} %side_by_side.1), channel_id=1, source_target_pairs={{0,32},{4,12},{8,40},{12,20},{16,48},{20,28},{24,56},{28,4},{32,64... | collective-permute-start | bytes 1966088 | tf_op jit(solution)/shard_map/ppermute | solution.py:441
  4.5 23.2 %collective-permute-start.1 = (bf16[256,1280]{1,0:T(8,128)(2,1)}, bf16[256,1280]{1,0:T(8,128)(2,1)S(1)}, u32[]{:S(2)}, u32[]{:S(2)}) collective-permute-start(bf16[256,1280]{1,0:T(8,128)(2,1)} %side_by_side.1), channel_id=1, source_target_pairs={{0,96},{4,28},{8,104},{12,4},{16,112},{20,12},{24,120},{28,20},{32... | collective-permute-start | bytes 1966088 | tf_op jit(solution)/shard_map/ppermute | solution.py:441
  6.7 23.6 %collective-permute-start.2 = (bf16[256,1280]{1,0:T(8,128)(2,1)}, bf16[256,1280]{1,0:T(8,128)(2,1)S(1)}, u32[]{:S(2)}, u32[]{:S(2)}) collective-permute-start(bf16[256,1280]{1,0:T(8,128)(2,1)} %side_by_side.1), channel_id=1, source_target_pairs={{0,64},{4,20},{8,72},{12,28},{16,80},{20,4},{24,88},{28,12},{32,96... | collective-permute-start | bytes 1966088 | tf_op jit(solution)/shard_map/ppermute | solution.py:441
  7.9 22.4 %collective-permute-start.3 = (bf16[256,1280]{1,0:T(8,128)(2,1)}, bf16[256,1280]{1,0:T(8,128)(2,1)S(1)}, u32[]{:S(2)}, u32[]{:S(2)}) collective-permute-start(bf16[256,1280]{1,0:T(8,128)(2,1)} %side_by_side.1), channel_id=1, source_target_pairs={{0,8},{4,36},{8,16},{12,44},{16,24},{20,52},{24,0},{28,60},{32,40}... | collective-permute-start | bytes 1966088 | tf_op jit(solution)/shard_map/ppermute | solution.py:444
  9.2 21.1 %collective-permute-start.4 = (bf16[256,1280]{1,0:T(8,128)(2,1)}, bf16[256,1280]{1,0:T(8,128)(2,1)S(1)}, u32[]{:S(2)}, u32[]{:S(2)}) collective-permute-start(bf16[256,1280]{1,0:T(8,128)(2,1)} %side_by_side.1), channel_id=1, source_target_pairs={{0,24},{4,100},{8,0},{12,108},{16,8},{20,116},{24,16},{28,124},{32... | collective-permute-start | bytes 1966088 | tf_op jit(solution)/shard_map/ppermute | solution.py:444
  21.3 11.9 %copy-start.18 = (bf16[256,1280]{1,0:T(8,128)(2,1)S(1)}, bf16[256,1280]{1,0:T(8,128)(2,1)}, u32[]{:S(2)}) copy-start(bf16[256,1280]{1,0:T(8,128)(2,1)} %side_by_side.1) | copy-start | bytes 1966084
  30.3 10.5 %slice-start = ((s8[16777216]{0:T(1024)(128)(4,1)}), s8[4194304]{0:T(1024)(128)(4,1)S(1)}, s32[]{:S(2)}) async-start(s8[16777216]{0:T(1024)(128)(4,1)} %bitcast.6), calls=%async_computation.2 | async-start | bytes 8388608
  30.5 10.3 %slice-start.1 = ((s8[16777216]{0:T(1024)(128)(4,1)}), s8[4194304]{0:T(1024)(128)(4,1)S(1)}, s32[]{:S(2)}) async-start(s8[16777216]{0:T(1024)(128)(4,1)} %bitcast.6), calls=%async_computation.3 | async-start | bytes 8388608
  30.5 25.1 %collective-permute-start.5 = (bf16[768,1280]{1,0:T(8,128)(2,1)S(1)}, bf16[768,1280]{1,0:T(8,128)(2,1)S(1)}, u32[]{:S(2)}, u32[]{:S(2)}) collective-permute-start(bf16[768,1280]{1,0:T(8,128)(2,1)S(1)} %constant_dynamic-update-slice_fusion.refs_0_), channel_id=1, source_target_pairs={{0,8},{4,36},{8,16},{12,44},{16,24},{20,52},{24,0},{28,60},{32,40}... | collective-permute-start | bytes 5898248 | tf_op jit(solution)/shard_map/ppermute | solution.py:444
  31.6 24.0 %collective-permute-start.6 = (bf16[768,1280]{1,0:T(8,128)(2,1)S(1)}, bf16[768,1280]{1,0:T(8,128)(2,1)S(1)}, u32[]{:S(2)}, u32[]{:S(2)}) collective-permute-start(bf16[768,1280]{1,0:T(8,128)(2,1)S(1)} %constant_dynamic-update-slice_fusion.refs_0_), channel_id=1, source_target_pairs={{0,24},{4,100},{8,0},{12,108},{16,8},{20,116},{24,16},{28,124},{32... | collective-permute-start | bytes 5898248 | tf_op jit(solution)/shard_map/ppermute | solution.py:444
  37.9 10.0 %collective-permute-start.9 = (bf16[512,1280]{1,0:T(8,128)(2,1)S(1)}, bf16[512,1280]{1,0:T(8,128)(2,1)S(1)}, u32[]{:S(2)}, u32[]{:S(2)}) collective-permute-start(bf16[512,1280]{1,0:T(8,128)(2,1)S(1)} %pad_maximum_fusion.3), channel_id=1, source_target_pairs={{0,4},{4,0},{8,12},{12,8},{16,20},{20,16},{24,28},{28,24},{32,36},... | collective-permute-start | bytes 3932168 | tf_op jit(solution)/shard_map/ppermute | solution.py:447
  40.1 7.9 %collective-permute-start.7 = (bf16[512,1280]{1,0:T(8,128)(2,1)S(1)}, bf16[512,1280]{1,0:T(8,128)(2,1)S(1)}, u32[]{:S(2)}, u32[]{:S(2)}) collective-permute-start(bf16[512,1280]{1,0:T(8,128)(2,1)S(1)} %pad_maximum_fusion.1), channel_id=1, source_target_pairs={{0,4},{4,0},{8,12},{12,8},{16,20},{20,16},{24,28},{28,24},{32,36},... | collective-permute-start | bytes 3932168 | tf_op jit(solution)/shard_map/ppermute | solution.py:447
  40.3 7.7 %collective-permute-start.8 = (bf16[512,1280]{1,0:T(8,128)(2,1)S(1)}, bf16[512,1280]{1,0:T(8,128)(2,1)S(1)}, u32[]{:S(2)}, u32[]{:S(2)}) collective-permute-start(bf16[512,1280]{1,0:T(8,128)(2,1)S(1)} %pad_maximum_fusion.2), channel_id=1, source_target_pairs={{0,4},{4,0},{8,12},{12,8},{16,20},{20,16},{24,28},{28,24},{32,36},... | collective-permute-start | bytes 3932168 | tf_op jit(solution)/shard_map/ppermute | solution.py:447
  55.6 10.5 %collective-permute-start.12 = (bf16[768,1280]{1,0:T(8,128)(2,1)S(1)}, bf16[768,1280]{1,0:T(8,128)(2,1)S(1)}, u32[]{:S(2)}, u32[]{:S(2)}) collective-permute-start(bf16[768,1280]{1,0:T(8,128)(2,1)S(1)} %collective-permute-done.5.refs_0_), channel_id=1, source_target_pairs={{0,4},{4,0},{8,12},{12,8},{16,20},{20,16},{24,28},{28,24},{32,36},... | collective-permute-start | bytes 5898248 | tf_op jit(solution)/shard_map/ppermute | solution.py:447
  57.8 8.2 %collective-permute-start.13 = (bf16[768,1280]{1,0:T(8,128)(2,1)S(1)}, bf16[768,1280]{1,0:T(8,128)(2,1)S(1)}, u32[]{:S(2)}, u32[]{:S(2)}) collective-permute-start(bf16[768,1280]{1,0:T(8,128)(2,1)S(1)} %collective-permute-done.6.refs_1_), channel_id=1, source_target_pairs={{0,4},{4,0},{8,12},{12,8},{16,20},{20,16},{24,28},{28,24},{32,36},... | collective-permute-start | bytes 5898248 | tf_op jit(solution)/shard_map/ppermute | solution.py:447
  58.1 18.0 %collective-permute-start.11 = (bf16[512,1280]{1,0:T(8,128)(2,1)S(1)}, bf16[512,1280]{1,0:T(8,128)(2,1)S(1)}, u32[]{:S(2)}, u32[]{:S(2)}) collective-permute-start(bf16[512,1280]{1,0:T(8,128)(2,1)S(1)} %pad_maximum_fusion.5), channel_id=1, source_target_pairs={{0,8},{4,36},{8,16},{12,44},{16,24},{20,52},{24,0},{28,60},{32,40}... | collective-permute-start | bytes 3932168 | tf_op jit(solution)/shard_map/ppermute | solution.py:444
  59.4 17.0 %collective-permute-start.10 = (bf16[512,1280]{1,0:T(8,128)(2,1)S(1)}, bf16[512,1280]{1,0:T(8,128)(2,1)S(1)}, u32[]{:S(2)}, u32[]{:S(2)}) collective-permute-start(bf16[512,1280]{1,0:T(8,128)(2,1)S(1)} %pad_maximum_fusion.4), channel_id=1, source_target_pairs={{0,24},{4,100},{8,0},{12,108},{16,8},{20,116},{24,16},{28,124},{32... | collective-permute-start | bytes 3932168 | tf_op jit(solution)/shard_map/ppermute | solution.py:444
  70.8 8.1 %copy-start.19 = (f32[1024]{0:T(1024)S(1)}, f32[1024]{0:T(1024)}, u32[]{:S(2)}) copy-start(f32[1024]{0:T(1024)} %param.19) | copy-start | bytes 12292
  70.9 8.1 %copy-start.20 = (f32[256]{0:T(256)S(1)}, f32[256]{0:T(256)}, u32[]{:S(2)}) copy-start(f32[256]{0:T(256)} %param.20) | copy-start | bytes 3076
  70.9 8.1 %copy-start.10 = (bf16[1024,1024]{1,0:T(8,128)(2,1)S(1)}, bf16[1024,1024]{1,0:T(8,128)(2,1)}, u32[]{:S(2)}) copy-start(bf16[1024,1024]{1,0:T(8,128)(2,1)} %get-tuple-element.77.x_ref) | copy-start | bytes 6291460
  76.6 6.0 %collective-permute-start.14 = (bf16[512,1024]{1,0:T(8,128)(2,1)S(1)}, bf16[512,1024]{1,0:T(8,128)(2,1)S(1)}, u32[]{:S(2)}, u32[]{:S(2)}) collective-permute-start(bf16[512,1024]{1,0:T(8,128)(2,1)S(1)} %slice.48), channel_id=1, source_target_pairs={{0,4},{4,0},{8,12},{12,8},{16,20},{20,16},{24,28},{28,24},{32,36},... | collective-permute-start | bytes 3145736 | tf_op jit(solution)/shard_map/ppermute | solution.py:447
  78.8 3.8 %collective-permute-start.15 = (bf16[512,1024]{1,0:T(8,128)(2,1)S(1)}, bf16[512,1024]{1,0:T(8,128)(2,1)S(1)}, u32[]{:S(2)}, u32[]{:S(2)}) collective-permute-start(bf16[512,1024]{1,0:T(8,128)(2,1)S(1)} %slice.49), channel_id=1, source_target_pairs={{0,4},{4,0},{8,12},{12,8},{16,20},{20,16},{24,28},{28,24},{32,36},... | collective-permute-start | bytes 3145736 | tf_op jit(solution)/shard_map/ppermute | solution.py:447
  89.6 46.0 %all-to-all-start = ((bf16[32,64,768]{2,1,0:T(8,128)(2,1)}), bf16[32,64,768]{2,1,0:T(8,128)(2,1)S(1)}, u32[]{:S(2)}, u32[]{:S(2)}) async-start(bf16[32,64,768]{2,1,0:T(8,128)(2,1)} %get-tuple-element.81), calls=%async_computation | async-start | bytes 6291456 | tf_op jit(solution)/shard_map/all_to_all | solution.py:523
  97.7 1.6 collective-permute-start.20
  98.1 1.7 collective-permute-start.19
  135.6 22.0 %all-to-all-start.1 = ((bf16[32,64,256]{2,1,0:T(8,128)(2,1)}), bf16[32,64,256]{2,1,0:T(8,128)(2,1)}, u32[]{:S(2)}, u32[]{:S(2)}) async-start(bf16[32,64,256]{2,1,0:T(8,128)(2,1)} %attend.3), calls=%async_computation.1 | async-start | bytes 2097152 | tf_op jit(solution)/shard_map/all_to_all | solution.py:523
  142.3 20.2 %collective-permute-start.16 = (bf16[256,768]{1,0:T(8,128)(2,1)}, bf16[256,768]{1,0:T(8,128)(2,1)S(1)}, u32[]{:S(2)}, u32[]{:S(2)}) collective-permute-start(bf16[256,768]{1,0:T(8,128)(2,1)} %get-tuple-element.83), channel_id=1, source_target_pairs={{0,2},{1,3},{2,0},{3,1},{4,6},{5,7},{6,4},{7,5},{8,10},{9,11},{10,... | collective-permute-start | bytes 1179656 | tf_op jit(solution)/shard_map/ppermute | solution.py:526
  145.0 19.9 %collective-permute-start.17 = (bf16[256,768]{1,0:T(8,128)(2,1)}, bf16[256,768]{1,0:T(8,128)(2,1)S(1)}, u32[]{:S(2)}, u32[]{:S(2)}) collective-permute-start(bf16[256,768]{1,0:T(8,128)(2,1)} %get-tuple-element.84), channel_id=1, source_target_pairs={{0,1},{1,2},{2,3},{3,0},{4,5},{5,6},{6,7},{7,4},{8,9},{9,10},{10,1... | collective-permute-start | bytes 1179656 | tf_op jit(solution)/shard_map/ppermute | solution.py:526
  145.3 19.6 %collective-permute-start.18 = (bf16[256,768]{1,0:T(8,128)(2,1)}, bf16[256,768]{1,0:T(8,128)(2,1)S(1)}, u32[]{:S(2)}, u32[]{:S(2)}) collective-permute-start(bf16[256,768]{1,0:T(8,128)(2,1)} %get-tuple-element.85), channel_id=1, source_target_pairs={{0,3},{1,0},{2,1},{3,2},{4,7},{5,4},{6,5},{7,6},{8,11},{9,8},{10,9... | collective-permute-start | bytes 1179656 | tf_op jit(solution)/shard_map/ppermute | solution.py:526
  159.4 7.2 %collective-permute-start.21 = (bf16[256,256]{1,0:T(8,128)(2,1)S(1)}, bf16[256,256]{1,0:T(8,128)(2,1)S(1)}, u32[]{:S(2)}, u32[]{:S(2)}) collective-permute-start(bf16[256,256]{1,0:T(8,128)(2,1)S(1)} %get-tuple-element.90), channel_id=1, source_target_pairs={{0,2},{1,3},{2,0},{3,1},{4,6},{5,7},{6,4},{7,5},{8,10},{9,11},{10,... | collective-permute-start | bytes 393224 | tf_op jit(solution)/shard_map/ppermute | solution.py:526
  162.2 6.8 %collective-permute-start.22 = (bf16[256,256]{1,0:T(8,128)(2,1)S(1)}, bf16[256,256]{1,0:T(8,128)(2,1)S(1)}, u32[]{:S(2)}, u32[]{:S(2)}) collective-permute-start(bf16[256,256]{1,0:T(8,128)(2,1)S(1)} %get-tuple-element.91), channel_id=1, source_target_pairs={{0,1},{1,2},{2,3},{3,0},{4,5},{5,6},{6,7},{7,4},{8,9},{9,10},{10,1... | collective-permute-start | bytes 393224 | tf_op jit(solution)/shard_map/ppermute | solution.py:526
  162.5 6.4 %collective-permute-start.23 = (bf16[256,256]{1,0:T(8,128)(2,1)S(1)}, bf16[256,256]{1,0:T(8,128)(2,1)S(1)}, u32[]{:S(2)}, u32[]{:S(2)}) collective-permute-start(bf16[256,256]{1,0:T(8,128)(2,1)S(1)} %get-tuple-element.92), channel_id=1, source_target_pairs={{0,3},{1,0},{2,1},{3,2},{4,7},{5,4},{6,5},{7,6},{8,11},{9,8},{10,9... | collective-permute-start | bytes 393224 | tf_op jit(solution)/shard_map/ppermute | solution.py:526
  (20 other events, 65.2 us)
